TPU v7x, 32 devices: a whole 2x2x4 slice. The times are simulated.
32 devices in a mesh: dp: 4 (over y, core), rows: 8 (over z, x).
Axes of the slice: x: 2, y: 2, z: 4, core: 2. Of those that a mesh axis runs over, the one named last changes fastest.
Arguments:
- item_table: float32 [16384, 256], P('rows'), may hold values from -0.5 to 0.5
- row_accum: float32 [16384], P('rows'), may hold values from 0.1 to 10
- owner_map: int32 [4, 8, 512, 1], P('dp', 'rows'), may hold values from 0 to 7; in each aligned block of 512 rows (0 to 511, 512 to 1023, ..., all dimensions but the last counted through in order) at most 192 rows name the same one
- row_index: int32 [4, 8, 512], P('dp', 'rows'), may hold values from 0 to 2047
- bag_index: int32 [4, 8, 512], P('dp', 'rows'), may hold values from 0 to 3, never falling along the last dimension, each value on 1 to 256 neighbouring positions
- prev_owner: int32 [4, 8, 512, 1], P('dp', 'rows'), may hold values from 0 to 7; in each aligned block of 512 rows (0 to 511, 512 to 1023, ..., all dimensions but the last counted through in order) at most 192 rows name the same one
- prev_row: int32 [4, 8, 512], P('dp', 'rows'), may hold values from 0 to 2047
- prev_bag: int32 [4, 8, 512], P('dp', 'rows'), may hold values from 0 to 3, never falling along the last dimension, each value on 1 to 256 neighbouring positions
- grad_pooled: float32 [4, 8, 4, 256], P('dp', 'rows'), may hold values from -6 to 6
Outputs:
- pooled: float32 [4, 8, 4, 256], P('dp', 'rows')
- new_table: float32 [16384, 256], P('rows')
- new_accum: float32 [16384], P('rows')
Inputs may be any that keep to these rules, and one draw needn't show every extreme that they name: `owner_map`: among the positions of one device no owner is named more than 192 times, a bound that some block reaches. `prev_owner`: among the positions of one device no owner is named more than 192 times, a bound that some block reaches. `bag_index`: never falls along a device's positions; every bag has 1 to 256 positions, one exactly 256. `prev_bag`: never falls along a device's positions; every bag has 1 to 256 positions, one exactly 256.
All inputs are finite; a program needn't handle non-finite values.
Results may differ from a plain program's by a relative error of at most 0.0003.
Values sent between devices are 32-bit elements; how exact they have to be, the bound alone decides.
No kernel may reach another device: no remote copies, remote signals or barrier semaphores. Data moves between devices by JAX's collectives and lax.ppermute only.
A program may use at most 64 MiB of HBM per device.

v0:
```python
import jax
import jax.numpy as jnp
from jax import lax
from jax.sharding import PartitionSpec as P

learn_rate = 0.1


def slot_numbers(owner_column, owners, capacity):
    owned = owner_column[:, 0]
    onehot = (owned[:, None] == jnp.arange(owners)[None, :]).astype(jnp.int32)
    placed = jnp.sum((jnp.cumsum(onehot, axis=0) - 1) * onehot, axis=1)
    return owned * capacity + placed


def bucketed(entries, slot_of, owners, capacity):
    filled = jnp.full((owners * capacity,), -1, jnp.int32).at[slot_of].set(entries)
    return filled.reshape(owners, capacity)


def look_up_rows(item_table, received):
    present = received >= 0
    looked = item_table[jnp.clip(received, 0)]
    return jnp.where(present[..., None], looked, 0.0)


def local(
    item_table,
    row_accum,
    owner_map,
    row_index,
    bag_index,
    prev_owner,
    prev_row,
    prev_bag,
    grad_pooled,
):
    owners = lax.axis_size("rows")
    rows_dev, width = item_table.shape
    bag_count = grad_pooled.shape[2]
    positions = row_index.shape[2]
    capacity = max(2, 3 * positions // owners)
    bag_range = jnp.arange(bag_count)
    row_range = jnp.arange(rows_dev)
    highest = lax.Precision.HIGHEST
    slot_of = slot_numbers(owner_map[0, 0], owners, capacity)
    send_rows = bucketed(row_index[0, 0], slot_of, owners, capacity)
    send_bags = bucketed(bag_index[0, 0], slot_of, owners, capacity)
    got_rows = lax.all_to_all(send_rows, "rows", split_axis=0, concat_axis=0, tiled=True)
    looked = look_up_rows(item_table, got_rows)
    returned = lax.all_to_all(looked, "rows", split_axis=0, concat_axis=0, tiled=True)
    member = (send_bags[..., None] == bag_range).astype(jnp.float32)
    pooled = jnp.einsum("scb,sce->be", member, returned, precision=highest)
    prev_slots = slot_numbers(prev_owner[0, 0], owners, capacity)
    old_rows = bucketed(prev_row[0, 0], prev_slots, owners, capacity)
    old_bags = bucketed(prev_bag[0, 0], prev_slots, owners, capacity)
    grad_table = grad_pooled[0, 0]
    old_member = (old_bags[..., None] == bag_range).astype(jnp.float32)
    grad_each = jnp.einsum("scb,be->sce", old_member, grad_table, precision=highest)
    got_old_rows = lax.all_to_all(old_rows, "rows", split_axis=0, concat_axis=0, tiled=True)
    got_grads = lax.all_to_all(grad_each, "rows", split_axis=0, concat_axis=0, tiled=True)
    row_hits = (got_old_rows[..., None] == row_range).astype(jnp.float32)
    local_grad = jnp.einsum("scr,sce->re", row_hits, got_grads, precision=highest)
    grad_rows = lax.psum(local_grad, "dp")
    new_accum = row_accum + jnp.mean(grad_rows * grad_rows, axis=1)
    new_table = item_table - learn_rate * grad_rows / jnp.sqrt(new_accum)[:, None]
    return (pooled[None, None], new_table, new_accum)


def solution(mesh):
    placed = (
        P("rows", None),
        P("rows"),
        P("dp", "rows", None, None),
        P("dp", "rows", None),
        P("dp", "rows", None),
        P("dp", "rows", None, None),
        P("dp", "rows", None),
        P("dp", "rows", None),
        P("dp", "rows", None, None),
    )
    return jax.shard_map(
        local,
        mesh=mesh,
        in_specs=placed,
        out_specs=(P("dp", "rows", None, None), P("rows", None), P("rows")),
        check_vma=False,
    )
```

profile of v0, /device:TPU:0, one launch (start us, length us, event | category | flops | bytes accessed | tf_op | source)
XLA Modules:
  0.0 164.6 jit_solution(14198805828078078126)
XLA Ops:
  7.2 0.0 copy-start
  7.2 0.7 fusion.9
  7.9 1.1 reduce-window.16
  9.0 0.2 slice_reduce_fusion
  9.3 0.8 fusion.4
  10.0 0.7 compare_select_fusion
  10.7 2.6 %scatter_custom_fusion.2 = s32[1536]{0:T(1024)S(1)} fusion(s32[512]{0:T(512)S(1)} %bitcast.67, s32[512]{0:T(512)} %bitcast.69, s32[]{:T(128)} %constant.9.clone.1), kind=kCustom, calls=%fused_computation.40 | custom fusion | bytes 6656 | tf_op jit(solution)/shard_map/scatter | solution.py:17
  13.3 0.7 all_to_all.21
  14.0 7.3 %all-to-all-start.2 = ((s32[8,1,192]{2,1,0:T(1,128)}), s32[8,1,192]{2,1,0:T(1,128)S(1)}, u32[]{:S(2)}, u32[]{:S(2)}) async-start(s32[8,1,192]{2,1,0:T(1,128)} %all_to_all.21), calls=%async_computation.2 | async-start | bytes 16384 | tf_op jit(solution)/shard_map/all_to_all | solution.py:60
  21.3 0.7 fusion.8
  22.0 1.1 reduce-window.14
  23.1 0.2 slice_reduce_fusion.1
  23.3 0.8 fusion.5
  24.1 0.7 compare_select_fusion.1
  24.8 2.6 %scatter_custom_fusion.3 = s32[1536]{0:T(1024)S(1)} fusion(s32[512]{0:T(512)S(1)} %bitcast.68, s32[512]{0:T(512)} %bitcast.70, s32[]{:T(128)} %constant.9.clone.1), kind=kCustom, calls=%fused_computation.38 | custom fusion | bytes 6656 | tf_op jit(solution)/shard_map/scatter | solution.py:17
  27.4 0.1 eq.119
  27.5 2.6 %scatter_custom_fusion.1 = s32[1536]{0:T(1024)S(1)} fusion(s32[512]{0:T(512)S(1)} %bitcast.65, s32[512]{0:T(512)} %bitcast.71, s32[]{:T(128)} %constant.9.clone.1), kind=kCustom, calls=%fused_computation.42 | custom fusion | bytes 6656 | tf_op jit(solution)/shard_map/scatter | solution.py:17
  30.1 0.7 all_to_all.18
  30.8 0.0 all-to-all-done.2
  30.8 6.0 %all-to-all-start = ((s32[8,1,192]{2,1,0:T(1,128)}), s32[8,1,192]{2,1,0:T(1,128)S(1)}, u32[]{:S(2)}, u32[]{:S(2)}) async-start(s32[8,1,192]{2,1,0:T(1,128)} %all_to_all.18), calls=%async_computation | async-start | bytes 16384 | tf_op jit(solution)/shard_map/all_to_all | solution.py:49
  36.8 0.0 copy-done
  36.8 0.0 copy-start.1
  36.8 2.0 %fusion.3 = f32[8,192,256]{2,1,0:T(8,128)} fusion(s32[8,192]{1,0:T(8,128)S(1)} %eq.119, f32[1,1,4,256]{3,2,1,0:T(4,128)S(1)} %copy-done), kind=kOutput, calls=%fused_computation.15 | convolution fusion | flops 18880512 | bytes 1583104 | tf_op jit(solution)/shard_map/scb,be->sce/dot_general | solution.py:59
  38.8 4.5 %all-to-all-done = s32[8,1,192]{2,1,0:T(1,128)S(1)} async-done(((s32[8,1,192]{2,1,0:T(1,128)}), s32[8,1,192]{2,1,0:T(1,128)S(1)}, u32[]{:S(2)}, u32[]{:S(2)}) %all-to-all-start) | async-done | bytes 6176 | tf_op jit(solution)/shard_map/all_to_all | solution.py:49
  43.3 4.3 %all-to-all-start.3 = ((f32[8,192,256]{2,1,0:T(8,128)}), f32[8,192,256]{2,1,0:T(8,128)}, u32[]{:S(2)}, u32[]{:S(2)}) async-start(f32[8,192,256]{2,1,0:T(8,128)} %fusion.3), calls=%async_computation.3 | async-start | bytes 3145728 | tf_op jit(solution)/shard_map/all_to_all | solution.py:61
  47.6 0.1 reshape.136
  47.7 0.0 copy-done.1
  47.7 4.6 %gather_fusion = f32[1536,256]{1,0:T(8,128)} fusion(f32[2048,256]{1,0:T(8,128)S(1)} %copy-done.1, s32[2048]{0:T(1024)S(1)} %pad_clamp_fusion), kind=kCustom, calls=%fused_computation | custom fusion | bytes 3151872 | tf_op jit(solution)/shard_map/gather | solution.py:23
  52.3 2.8 %broadcast_select_fusion = f32[8,192,256]{2,1,0:T(8,128)} fusion(f32[8,192,256]{2,1,0:T(8,128)} %bitcast.57, pred[8,192]{1,0:T(8,128)(4,1)S(1)} %compare_bitcast_fusion), kind=kLoop, calls=%fused_computation.12 | loop fusion | flops 393216 | bytes 3147264 | tf_op jit(solution)/shard_map/jit(_where)/select_n | solution.py:24
  55.2 27.9 %all-to-all-done.3 = f32[8,192,256]{2,1,0:T(8,128)} async-done(((f32[8,192,256]{2,1,0:T(8,128)}), f32[8,192,256]{2,1,0:T(8,128)}, u32[]{:S(2)}, u32[]{:S(2)}) %all-to-all-start.3) | async-done | bytes 1572896 | tf_op jit(solution)/shard_map/all_to_all | solution.py:61
  83.1 4.3 %all-to-all-start.1 = ((f32[8,192,256]{2,1,0:T(8,128)}), f32[8,192,256]{2,1,0:T(8,128)}, u32[]{:S(2)}, u32[]{:S(2)}) async-start(f32[8,192,256]{2,1,0:T(8,128)} %broadcast_select_fusion), calls=%async_computation.1 | async-start | bytes 3145728 | tf_op jit(solution)/shard_map/all_to_all | solution.py:51
  87.4 0.2 all-reduce.2.cloned.1.call-start
  87.6 13.0 %fusion.2 = f32[2048,256]{1,0:T(8,128)} fusion(f32[8,192,256]{2,1,0:T(8,128)} %all-to-all-done.3, s32[8,192]{1,0:T(8,128)S(1)} %bitcast.62), kind=kOutput, calls=%fused_computation.8 | convolution fusion | flops 9666822144 | bytes 3676160 | tf_op jit(solution)/shard_map/scr,sce->re/dot_general | solution.py:63
  100.6 0.0 all-reduce.2.cloned.1.call-update
  100.6 0.0 copy-start.3
  100.6 2.6 %scatter_custom_fusion = s32[1536]{0:T(1024)S(1)} fusion(s32[512]{0:T(512)S(1)} %bitcast.66, s32[512]{0:T(512)} %bitcast.72, s32[]{:T(128)} %constant.9.clone.1), kind=kCustom, calls=%fused_computation.44 | custom fusion | bytes 6656 | tf_op jit(solution)/shard_map/scatter | solution.py:17
  103.3 0.1 eq.103
  103.3 20.5 %all-to-all-done.1 = f32[8,192,256]{2,1,0:T(8,128)} async-done(((f32[8,192,256]{2,1,0:T(8,128)}), f32[8,192,256]{2,1,0:T(8,128)}, u32[]{:S(2)}, u32[]{:S(2)}) %all-to-all-start.1) | async-done | bytes 1572896 | tf_op jit(solution)/shard_map/all_to_all | solution.py:51
  123.8 2.7 %convolution_bitcast_fusion = f32[1,1,4,256]{3,2,1,0:T(4,128)} fusion(f32[8,192,256]{2,1,0:T(8,128)} %all-to-all-done.1, s32[8,192]{1,0:T(8,128)S(1)} %eq.103), kind=kOutput, calls=%fused_computation.11 | convolution fusion | flops 18880512 | bytes 1583104 | tf_op jit(solution)/shard_map/scb,sce->be/dot_general | solution.py:53
  126.5 26.8 %all-reduce.2.cloned.1.call-done = f32[2048,256]{1,0:T(8,128)} async-done(((f32[2048,256]{1,0:T(8,128)}), f32[2048,256]{1,0:T(8,128)}) %all-reduce.2.cloned.1.call-update) | async-done | bytes 2097168 | tf_op jit(solution)/shard_map/psum | solution.py:64
  153.3 0.0 copy-start.2
  153.3 2.1 %multiply_reduce_fusion = f32[2048]{0:T(1024)S(1)} fusion(f32[2048,256]{1,0:T(8,128)} %all-reduce.2.cloned.1.call-done), kind=kLoop, calls=%fused_computation.10 | loop fusion | flops 1046528 | bytes 2105344 | tf_op jit(solution)/shard_map/reduce_sum | solution.py:65
  155.4 0.0 copy-done.3
  155.4 0.6 fusion.19
  156.0 0.0 copy-done.2
  156.0 1.8 %divide_subtract_fusion = f32[2048,256]{1,0:T(8,128)} fusion(f32[2048,256]{1,0:T(8,128)S(1)} %copy-done.1, f32[2048,256]{1,0:T(8,128)S(1)} %copy-done.2, f32[2048]{0:T(1024)S(1)} %get-tuple-element.3), kind=kLoop, calls=%fused_computation.9 | loop fusion | flops 1572864 | bytes 6299648 | tf_op jit(solution)/shard_map/sub | solution.py:66
  (8 shorter events, 0.1 us)
Async XLA Ops:
  7.2 29.6 %copy-start = (f32[1,1,4,256]{3,2,1,0:T(4,128)S(1)}, f32[1,1,4,256]{3,2,1,0:T(4,128)}, u32[]{:S(2)}) copy-start(f32[1,1,4,256]{3,2,1,0:T(4,128)} %param.17) | copy-start | bytes 12292
  14.0 16.8 %all-to-all-start.2 = ((s32[8,1,192]{2,1,0:T(1,128)}), s32[8,1,192]{2,1,0:T(1,128)S(1)}, u32[]{:S(2)}, u32[]{:S(2)}) async-start(s32[8,1,192]{2,1,0:T(1,128)} %all_to_all.21), calls=%async_computation.2 | async-start | bytes 16384 | tf_op jit(solution)/shard_map/all_to_all | solution.py:60
  30.8 12.5 %all-to-all-start = ((s32[8,1,192]{2,1,0:T(1,128)}), s32[8,1,192]{2,1,0:T(1,128)S(1)}, u32[]{:S(2)}, u32[]{:S(2)}) async-start(s32[8,1,192]{2,1,0:T(1,128)} %all_to_all.18), calls=%async_computation | async-start | bytes 16384 | tf_op jit(solution)/shard_map/all_to_all | solution.py:49
  36.8 10.9 %copy-start.1 = (f32[2048,256]{1,0:T(8,128)S(1)}, f32[2048,256]{1,0:T(8,128)}, u32[]{:S(2)}) copy-start(f32[2048,256]{1,0:T(8,128)} %param.9) | copy-start | bytes 6291460
  43.3 39.8 %all-to-all-start.3 = ((f32[8,192,256]{2,1,0:T(8,128)}), f32[8,192,256]{2,1,0:T(8,128)}, u32[]{:S(2)}, u32[]{:S(2)}) async-start(f32[8,192,256]{2,1,0:T(8,128)} %fusion.3), calls=%async_computation.3 | async-start | bytes 3145728 | tf_op jit(solution)/shard_map/all_to_all | solution.py:61
  83.1 40.7 %all-to-all-start.1 = ((f32[8,192,256]{2,1,0:T(8,128)}), f32[8,192,256]{2,1,0:T(8,128)}, u32[]{:S(2)}, u32[]{:S(2)}) async-start(f32[8,192,256]{2,1,0:T(8,128)} %broadcast_select_fusion), calls=%async_computation.1 | async-start | bytes 3145728 | tf_op jit(solution)/shard_map/all_to_all | solution.py:51
  87.4 65.9 %all-reduce.2.cloned.1.call-start = ((), (), s32[]{:S(2)}) async-start(), calls=%async_computation.4 | async-start | bytes 4194304 | tf_op jit(solution)/shard_map/psum | solution.py:64
  100.6 54.8 %copy-start.3 = (f32[2048]{0:T(1024)S(1)}, f32[2048]{0:T(1024)}, u32[]{:S(2)}) copy-start(f32[2048]{0:T(1024)} %param.10) | copy-start | bytes 24580
  153.3 2.7 %copy-start.2 = (f32[2048,256]{1,0:T(8,128)S(1)}, f32[2048,256]{1,0:T(8,128)}, u32[]{:S(2)}) copy-start(f32[2048,256]{1,0:T(8,128)} %all-reduce.2.cloned.1.call-done) | copy-start | bytes 6291460
Sparse Core Ops, SparseCore 0:
  100.8 52.4 all-reduce.1
where the time goes:
time: 165 us
  waiting for transfers between devices  79.7 us (48%)
  starting transfers between devices  22.1 us (13%)
  matrix products  17.7 us (11%)
  local copies, waits for them, and re-layouts  17.1 us (10%)
  between operations  14.2 us (9%)
  other arithmetic  13.9 us (8%)
    all_to_all x1, waiting for transfers between devices, local(): lax.all_to_all(grad_each, 'rows', split_axis=0, concat_axis=0, tiled=True)  27.9 us
    psum x1, waiting for transfers between devices, local(): grad_rows = lax.psum(local_grad, 'dp')  26.8 us
    all_to_all x1, waiting for transfers between devices, local(): lax.all_to_all(looked, 'rows', split_axis=0, concat_axis=0, tiled=True)  20.5 us
    dot_general x1, matrix products, local(): jnp.einsum('scr,sce->re', row_hits, got_grads, precision=highest)  13 us
    scatter x4, local copies, waits for them, and re-layouts, bucketed(): jnp.full((owners * capacity,), -1, jnp.int32).at[slot_of].set(entries)  10.4 us
    all_to_all x1, starting transfers between devices, local(): lax.all_to_all(old_rows, 'rows', split_axis=0, concat_axis=0, tiled=True)  7.25 us
    all_to_all x1, starting transfers between devices, local(): lax.all_to_all(send_rows, 'rows', split_axis=0, concat_axis=0, tiled=True)  6 us
    gather x1, local copies, waits for them, and re-layouts, look_up_rows(): looked = item_table[jnp.clip(received, 0)]  4.64 us
  transfers between devices with their start and end apart: 5, of which 4 were waited for; matrix products, arithmetic and copies ran while one was open for 22% of the time, Pallas kernels for 0%

commit v1 on v0

v1 whole, which is shorter than its diff:
```python
import functools

import jax
import jax.numpy as jnp
from jax import lax
from jax.experimental import pallas as pl
from jax.experimental.pallas import tpu as pltpu
from jax.sharding import PartitionSpec as P

learn_rate = 0.1
LANES = 128
PREV_BOUNDS = 64


def bound_block(bags, bag_count, first):
    lane = lax.broadcasted_iota(jnp.int32, (1, LANES), 1)
    block = jnp.zeros((1, LANES), jnp.float32)
    for j in range(1, bag_count):
        start = jnp.sum((bags < j).astype(jnp.float32), axis=1, keepdims=True)
        block = jnp.where(lane == first + j - 1, start, block)
    return block


def pack_kernel(rows_dev, owner, row, bag, prev_owner, prev_row, prev_bag, grad, out):
    copies = out.shape[0]
    positions = row.shape[1]
    bag_count, width = grad.shape

    def put(start, value):
        shape = (copies, 1, value.shape[1])
        out[:, :, start:start + value.shape[1]] = jnp.broadcast_to(value[None], shape)

    put(0, (owner[...] * rows_dev + row[...]).astype(jnp.float32))
    put(positions, (prev_owner[...] * rows_dev + prev_row[...]).astype(jnp.float32))
    put(
        2 * positions,
        bound_block(bag[...], bag_count, 0)
        + bound_block(prev_bag[...], bag_count, PREV_BOUNDS),
    )
    for j in range(bag_count):
        put(2 * positions + LANES + j * width, grad[j:j + 1, :])


def split_two(x):
    high = x.astype(jnp.bfloat16)
    return high, (x - high.astype(jnp.float32)).astype(jnp.bfloat16)


def codes(ids, bounds, first, bag_count, base):
    rel = ids.astype(jnp.int32) - base
    place = lax.broadcasted_iota(jnp.int32, ids.shape, 1).astype(jnp.float32)
    bag = jnp.zeros(ids.shape, jnp.int32)
    for j in range(1, bag_count):
        start = bounds[:, first + j - 1:first + j]
        bag = bag + (place >= start).astype(jnp.int32)
    code = lax.shift_right_arithmetic(rel, 7) * bag_count + bag
    return code.astype(jnp.float32), (rel & (LANES - 1)).astype(jnp.float32)


def count_into(counts, code_ref, lane_ref, devices, bag_count):
    blocks = counts.shape[0]
    positions = code_ref.shape[1]
    code_range = lax.broadcasted_iota(
        jnp.int32, (blocks * bag_count, positions), 0).astype(jnp.bfloat16)
    lane_range = lax.broadcasted_iota(
        jnp.int32, (LANES, positions), 0).astype(jnp.bfloat16)
    for d in range(devices):
        code = code_ref[d:d + 1, :].astype(jnp.bfloat16)
        lane = lane_ref[d:d + 1, :].astype(jnp.bfloat16)
        one, none = jnp.ones((), jnp.bfloat16), jnp.zeros((), jnp.bfloat16)
        left = jnp.where(code_range == code, one, none)
        right = jnp.where(lane_range == lane, one, none)
        hits = lax.dot_general(
            left, right, (((1,), (1,)), ((), ())), preferred_element_type=jnp.float32)
        counts[:, d * bag_count:(d + 1) * bag_count, :] = hits.reshape(
            blocks, bag_count, LANES)


def pool_kernel(bag_count, positions, msg, table, out, code_ref, lane_ref, counts):
    rows_dev = table.shape[0]
    devices = out.shape[0]
    group = lax.axis_index("dp") * devices
    base = lax.axis_index("rows") * rows_dev
    ids = msg[pl.ds(group, devices), 0, 0:positions]
    bounds = msg[pl.ds(group, devices), 0, 2 * positions:2 * positions + LANES]
    code_ref[...], lane_ref[...] = codes(ids, bounds, 0, bag_count, base)
    count_into(counts, code_ref, lane_ref, devices, bag_count)
    blocks = rows_dev // LANES
    total = jnp.zeros((devices * bag_count, table.shape[1]), jnp.float32)
    flat = jnp.concatenate(
        [counts[h].astype(jnp.bfloat16) for h in range(blocks)], axis=1)
    for part in split_two(table[...]):
        total += jnp.dot(flat, part, preferred_element_type=jnp.float32)
    out[...] = total.reshape(out.shape)


def update_kernel(
    bag_count, positions, chunk, msg, table, accum, new_table, new_accum,
    code_ref, lane_ref, counts, grads, sums,
):
    devices = msg.shape[0]
    step_rows, width = table.shape
    blocks = counts.shape[0]
    base = lax.axis_index("rows") * (blocks * LANES)
    step = pl.program_id(0)
    offset = 2 * positions + LANES

    def count_chunk(first):
        ids = msg[pl.ds(first, chunk), 0, positions:2 * positions]
        bounds = msg[pl.ds(first, chunk), 0, 2 * positions:2 * positions + LANES]
        code_ref[...], lane_ref[...] = codes(ids, bounds, PREV_BOUNDS, bag_count, base)
        count_into(counts, code_ref, lane_ref, chunk, bag_count)
        for d in range(chunk):
            for j in range(bag_count):
                grads[d * bag_count + j:d * bag_count + j + 1, :] = msg[
                    first + d, :, offset + j * width:offset + (j + 1) * width]

    def block_sum(h, parts):
        hits = counts[h].astype(jnp.bfloat16)
        total = jnp.zeros((LANES, width), jnp.float32)
        for part in parts:
            total += lax.dot_general(
                hits, part, (((0,), (0,)), ((), ())), preferred_element_type=jnp.float32)
        return total

    single = devices == chunk

    @pl.when(step == 0)
    def _():
        if single:
            count_chunk(0)
            return
        sums[...] = jnp.zeros_like(sums)

        @pl.loop(0, devices // chunk)
        def _(c):
            count_chunk(c * chunk)
            parts = split_two(grads[...])

            @pl.loop(0, blocks)
            def _(h):
                sums[h] += block_sum(h, parts)

    diagonal = (
        lax.broadcasted_iota(jnp.int32, (LANES, LANES), 0)
        == lax.broadcasted_iota(jnp.int32, (LANES, LANES), 1))
    if single:
        parts = split_two(grads[...])
    per_step = step_rows // LANES
    for i in range(per_step):
        h = step * per_step + i
        grad = block_sum(h, parts) if single else sums[h]
        here = slice(i * LANES, (i + 1) * LANES)
        squares = grad * grad
        folded = squares[:, 0:LANES]
        for k in range(1, width // LANES):
            folded += squares[:, k * LANES:(k + 1) * LANES]
        old = jnp.where(diagonal, accum[pl.ds(h, 1), :], 0.0)
        fresh = jnp.sum(folded * (1.0 / width) + old, axis=1, keepdims=True)
        new_table[here, :] = table[here, :] - grad * (learn_rate * lax.rsqrt(fresh))
        new_accum[pl.ds(h, 1), :] = jnp.sum(
            jnp.where(diagonal, fresh, 0.0), axis=0, keepdims=True)


def local(
    item_table, row_accum, owner_map, row_index, bag_index,
    prev_owner, prev_row, prev_bag, grad_pooled,
):
    owners = lax.axis_size("rows")
    devices = owners * lax.axis_size("dp")
    rows_dev, width = item_table.shape
    bag_count = grad_pooled.shape[2]
    positions = row_index.shape[2]
    blocks = rows_dev // LANES
    length = 2 * positions + LANES + bag_count * width
    vmem = pl.BlockSpec(memory_space=pltpu.VMEM)
    params = pltpu.CompilerParams(vmem_limit_bytes=48 * 1024 * 1024)

    def line(x):
        return x.reshape(1, positions)

    message = pl.pallas_call(
        functools.partial(pack_kernel, rows_dev),
        out_shape=jax.ShapeDtypeStruct((devices, 1, length), jnp.float32),
        in_specs=[vmem] * 7,
        out_specs=vmem,
        compiler_params=params,
        name="pack",
    )(
        line(owner_map), line(row_index), line(bag_index),
        line(prev_owner), line(prev_row), line(prev_bag), grad_pooled[0, 0],
    )
    gathered = lax.all_to_all(
        message, ("dp", "rows"), split_axis=0, concat_axis=0, tiled=True)

    partial_pooled = pl.pallas_call(
        functools.partial(pool_kernel, bag_count, positions),
        out_shape=jax.ShapeDtypeStruct((owners, bag_count, width), jnp.float32),
        in_specs=[vmem] * 2,
        out_specs=vmem,
        scratch_shapes=[
            pltpu.VMEM((owners, positions), jnp.float32),
            pltpu.VMEM((owners, positions), jnp.float32),
            pltpu.VMEM((blocks, owners * bag_count, LANES), jnp.float32),
        ],
        compiler_params=params,
        cost_estimate=pl.CostEstimate(
            flops=4 * owners * bag_count * rows_dev * width,
            bytes_accessed=rows_dev * width * 4, transcendentals=0),
        name="pool",
    )(gathered, item_table)
    returned = lax.all_to_all(
        partial_pooled, "rows", split_axis=0, concat_axis=0, tiled=True)

    chunk = min(devices, LANES // bag_count)
    steps = 4
    step_rows = rows_dev // steps
    segments = chunk * bag_count
    whole = lambda i: (0, 0)
    new_table, new_accum = pl.pallas_call(
        functools.partial(update_kernel, bag_count, positions, chunk),
        grid=(steps,),
        out_shape=(
            jax.ShapeDtypeStruct((rows_dev, width), jnp.float32),
            jax.ShapeDtypeStruct((blocks, LANES), jnp.float32),
        ),
        in_specs=[
            vmem,
            pl.BlockSpec((step_rows, width), lambda i: (i, 0)),
            pl.BlockSpec((blocks, LANES), whole),
        ],
        out_specs=(
            pl.BlockSpec((step_rows, width), lambda i: (i, 0)),
            pl.BlockSpec((blocks, LANES), whole),
        ),
        scratch_shapes=[
            pltpu.VMEM((chunk, positions), jnp.float32),
            pltpu.VMEM((chunk, positions), jnp.float32),
            pltpu.VMEM((blocks, segments, LANES), jnp.float32),
            pltpu.VMEM((segments, width), jnp.float32),
            pltpu.VMEM((blocks, LANES, width) if devices > chunk else (1, 8, LANES), jnp.float32),
        ],
        compiler_params=params,
        cost_estimate=pl.CostEstimate(
            flops=8 * devices * bag_count * rows_dev * width,
            bytes_accessed=3 * rows_dev * width * 4, transcendentals=0),
        name="update",
    )(gathered, item_table, row_accum.reshape(blocks, LANES))

    pooled = jnp.sum(returned, axis=0)
    return (pooled[None, None], new_table, new_accum.reshape(rows_dev))


def solution(mesh):
    placed = (
        P("rows", None),
        P("rows"),
        P("dp", "rows", None, None),
        P("dp", "rows", None),
        P("dp", "rows", None),
        P("dp", "rows", None, None),
        P("dp", "rows", None),
        P("dp", "rows", None),
        P("dp", "rows", None, None),
    )
    return jax.shard_map(
        local,
        mesh=mesh,
        in_specs=placed,
        out_specs=(P("dp", "rows", None, None), P("rows", None), P("rows")),
        check_vma=False,
    )
```

time: 165 us -> 38.3 us (0.23)
  waiting for transfers between devices: 79.7 us -> 1.99 us
  starting transfers between devices: 22.1 us -> 3.33 us
  blocking collectives: 0 us -> 18.2 us
  matrix products: 17.7 us -> 0 us
  between operations: 14.2 us -> 0.69 us
  other arithmetic: 13.9 us -> 0.61 us
  local copies, waits for them, and re-layouts: 17.1 us -> 6.37 us
  Pallas kernels: 0 us -> 6.66 us
    all_to_all x4 -> x1, waiting for transfers between devices: 52.8 us -> 1.99 us  [local(): lax.all_to_all(partial_pooled, 'rows', split_axis=0, concat_axis=0, tiled...]
    psum x1 -> x0, waiting for transfers between devices: 26.8 us -> none  [local(): grad_rows = lax.psum(local_grad, 'dp')]
    all_to_all x4 -> x1, starting transfers between devices: 21.8 us -> 3.33 us  [local(): lax.all_to_all(partial_pooled, 'rows', split_axis=0, concat_axis=0, tiled...]
    all_to_all x0 -> x1, blocking collectives: none -> 18.2 us  [local(): lax.all_to_all(message, ('dp', 'rows'), split_axis=0, concat_axis=0, tile...]
    dot_general x3 -> x0, matrix products: 17.7 us -> none  [the longest x1 13 us: local(): jnp.einsum('scr,sce->re', row_hits, got_grads, precision=highest)]
    scatter x4 -> x0, local copies, waits for them, and re-layouts: 10.4 us -> none  [bucketed(): jnp.full((owners * capacity,), -1, jnp.int32).at[slot_of].set(entries)]
    pallas_call x0 -> x3, Pallas kernels: none -> 6.66 us  [the longest x1 4.61 us: local(): pl.pallas_call(functools.partial(update_kernel, bag_count, positions, chu...]
    unnamed x9 -> x20, local copies, waits for them, and re-layouts: 0.03 us -> 6.37 us
  transfers between devices with their start and end apart: 5 -> 1, of which waited for: 4 -> 1; matrix products, arithmetic and copies ran while one was open for 22% -> 0% of each run, Pallas kernels for 0% -> 12%
where the time goes in v1:
time: 38.3 us; the launch traced here: 37.8 us
  blocking collectives  18.2 us (48%)
  Pallas kernels  6.66 us (17%)
  local copies, waits for them, and re-layouts  6.37 us (17%)
  starting transfers between devices  3.33 us (9%)
  waiting for transfers between devices  1.99 us (5%)
  between operations  0.69 us (2%)
  other arithmetic  0.61 us (2%)
    all_to_all x1, blocking collectives, local(): lax.all_to_all(message, ('dp', 'rows'), split_axis=0, concat_axis=0, tile...  18.2 us
    unnamed x20, local copies, waits for them, and re-layouts  6.37 us
    pallas_call x1, Pallas kernels, local(): pl.pallas_call(functools.partial(update_kernel, bag_count, positions, chu...  4.61 us
    all_to_all x1, starting transfers between devices, local(): lax.all_to_all(partial_pooled, 'rows', split_axis=0, concat_axis=0, tiled...  3.33 us
    all_to_all x1, waiting for transfers between devices, local(): lax.all_to_all(partial_pooled, 'rows', split_axis=0, concat_axis=0, tiled...  1.99 us
    pallas_call x1, Pallas kernels, local(): pl.pallas_call(functools.partial(pool_kernel, bag_count, positions), out_...  1.95 us
  transfers between devices with their start and end apart: 1, of which 1 were waited for; matrix products, arithmetic and copies ran while one was open for 0% of the time, Pallas kernels for 12%

profile of v1, /device:TPU:0, one launch (start us, length us, event | category | flops | bytes accessed | tf_op | source)
XLA Modules:
  0.0 37.8 jit_solution(9143724032012369392)
XLA Ops:
  0.6 0.0 copy-start.2
  0.6 0.0 copy-start.3
  0.7 0.7 %copy-done.3 = f32[1,1,4,256]{3,2,1,0:T(4,128)S(1)} copy-done((f32[1,1,4,256]{3,2,1,0:T(4,128)S(1)}, f32[1,1,4,256]{3,2,1,0:T(4,128)}, u32[]{:S(2)}) %copy-start.3) | copy-done | bytes 4120
  1.3 0.0 copy-start.4
  1.3 0.7 %copy-done.4 = s32[1,1,512,1]{2,3,1,0:T(1,128)S(1)} copy-done((s32[1,1,512,1]{2,3,1,0:T(1,128)S(1)}, s32[1,1,512,1]{2,3,1,0:T(1,128)}, u32[]{:S(2)}) %copy-start.4) | copy-done | bytes 2072
  2.0 0.0 copy-start.5
  2.0 0.7 %copy-done.5 = s32[1,1,512]{2,1,0:T(1,128)S(1)} copy-done((s32[1,1,512]{2,1,0:T(1,128)S(1)}, s32[1,1,512]{2,1,0:T(1,128)}, u32[]{:S(2)}) %copy-start.5) | copy-done | bytes 2072
  2.7 0.0 copy-start.6
  2.7 0.7 %copy-done.6 = s32[1,1,512]{2,1,0:T(1,128)S(1)} copy-done((s32[1,1,512]{2,1,0:T(1,128)S(1)}, s32[1,1,512]{2,1,0:T(1,128)}, u32[]{:S(2)}) %copy-start.6) | copy-done | bytes 2072
  3.4 0.0 copy-start.7
  3.4 0.7 %copy-done.7 = s32[1,1,512,1]{2,3,1,0:T(1,128)S(1)} copy-done((s32[1,1,512,1]{2,3,1,0:T(1,128)S(1)}, s32[1,1,512,1]{2,3,1,0:T(1,128)}, u32[]{:S(2)}) %copy-start.7) | copy-done | bytes 2072
  4.1 0.0 copy-start.8
  4.1 0.7 %copy-done.8 = s32[1,1,512]{2,1,0:T(1,128)S(1)} copy-done((s32[1,1,512]{2,1,0:T(1,128)S(1)}, s32[1,1,512]{2,1,0:T(1,128)}, u32[]{:S(2)}) %copy-start.8) | copy-done | bytes 2072
  4.7 0.0 copy-start.9
  4.8 0.7 %copy-done.9 = s32[1,1,512]{2,1,0:T(1,128)S(1)} copy-done((s32[1,1,512]{2,1,0:T(1,128)S(1)}, s32[1,1,512]{2,1,0:T(1,128)}, u32[]{:S(2)}) %copy-start.9) | copy-done | bytes 2072
  5.4 0.1 pack.1
  5.5 18.2 %all_to_all.10.msg = f32[32,1,2176]{2,1,0:T(1,128)S(1)} all-to-all(f32[32,1,2176]{2,1,0:T(1,128)S(1)} %pack.1), channel_id=1, replica_groups=mesh['dp'=4,'rows'=8] {'dp','rows'}, dimensions={0} | all-to-all | bytes 557056 | tf_op jit(solution)/shard_map/all_to_all | solution.py:193
  23.7 0.0 copy-start
  23.7 1.6 %copy-done = f32[2048,256]{1,0:T(8,128)S(1)} copy-done((f32[2048,256]{1,0:T(8,128)S(1)}, f32[2048,256]{1,0:T(8,128)}, u32[]{:S(2)}) %copy-start) | copy-done | bytes 2097176
  25.3 0.0 copy-start.1
  25.3 2.0 %pool.1 = f32[8,4,256]{2,1,0:T(4,128)} custom-call(f32[32,1,2176]{2,1,0:T(1,128)S(1)} %all_to_all.10.msg, f32[2048,256]{1,0:T(8,128)S(1)} %copy-done), custom_call_target="tpu_custom_call" | custom-call | flops 67108864 | bytes 2097152 | tf_op jit(solution)/shard_map/pool/pallas_call | solution.py:196
  27.3 3.3 %all-to-all-start.1 = ((f32[8,4,256]{2,1,0:T(4,128)}), f32[8,4,256]{2,1,0:T(4,128)S(1)}, u32[]{:S(2)}, u32[]{:S(2)}) async-start(f32[8,4,256]{2,1,0:T(4,128)} %pool.1), calls=%async_computation.1 | async-start | bytes 65536 | tf_op jit(solution)/shard_map/all_to_all | solution.py:212
  30.6 0.0 copy-done.2
  30.6 0.0 copy-done.1
  30.6 4.6 %update.1 = (f32[2048,256]{1,0:T(8,128)}, f32[16,128]{1,0:T(8,128)}) custom-call(f32[32,1,2176]{2,1,0:T(1,128)S(1)} %all_to_all.10.msg, f32[2048,256]{1,0:T(8,128)S(1)} %copy-done.1, f32[16,128]{1,0:T(8,128)S(1)} %bitcast.10), custom_call_target="tpu_custom_call" | custom-call | flops 536870912 | bytes 6291456 | tf_op jit(solution)/shard_map/update/pallas_call | solution.py:220
  35.2 2.0 %all-to-all-done.1 = f32[8,4,256]{2,1,0:T(4,128)S(1)} async-done(((f32[8,4,256]{2,1,0:T(4,128)}), f32[8,4,256]{2,1,0:T(4,128)S(1)}, u32[]{:S(2)}, u32[]{:S(2)}) %all-to-all-start.1) | async-done | bytes 32800 | tf_op jit(solution)/shard_map/all_to_all | solution.py:212
  37.2 0.6 %reduce_sum.9 = f32[4,256]{1,0:T(4,128)} reduce(f32[8,4,256]{2,1,0:T(4,128)S(1)} %all-to-all-done.1, f32[]{:T(128)} %constant.0.clone.1), dimensions={0}, to_apply=%region_0.0 | reduce | flops 7168 | bytes 36868 | tf_op jit(solution)/shard_map/reduce_sum | solution.py:250
Async XLA Ops:
  0.6 30.0 %copy-start.2 = (f32[2048]{0:T(1024)S(1)}, f32[2048]{0:T(1024)}, u32[]{:S(2)}) copy-start(f32[2048]{0:T(1024)} %param.10) | copy-start | bytes 24580
  0.6 0.7 %copy-start.3 = (f32[1,1,4,256]{3,2,1,0:T(4,128)S(1)}, f32[1,1,4,256]{3,2,1,0:T(4,128)}, u32[]{:S(2)}) copy-start(f32[1,1,4,256]{3,2,1,0:T(4,128)} %param.17) | copy-start | bytes 12292
  1.3 0.7 %copy-start.4 = (s32[1,1,512,1]{2,3,1,0:T(1,128)S(1)}, s32[1,1,512,1]{2,3,1,0:T(1,128)}, u32[]{:S(2)}) copy-start(s32[1,1,512,1]{2,3,1,0:T(1,128)} %param.11) | copy-start | bytes 6148
  2.0 0.7 %copy-start.5 = (s32[1,1,512]{2,1,0:T(1,128)S(1)}, s32[1,1,512]{2,1,0:T(1,128)}, u32[]{:S(2)}) copy-start(s32[1,1,512]{2,1,0:T(1,128)} %param.12) | copy-start | bytes 6148
  2.7 0.7 %copy-start.6 = (s32[1,1,512]{2,1,0:T(1,128)S(1)}, s32[1,1,512]{2,1,0:T(1,128)}, u32[]{:S(2)}) copy-start(s32[1,1,512]{2,1,0:T(1,128)} %param.13) | copy-start | bytes 6148
  3.4 0.7 %copy-start.7 = (s32[1,1,512,1]{2,3,1,0:T(1,128)S(1)}, s32[1,1,512,1]{2,3,1,0:T(1,128)}, u32[]{:S(2)}) copy-start(s32[1,1,512,1]{2,3,1,0:T(1,128)} %param.14) | copy-start | bytes 6148
  4.1 0.7 %copy-start.8 = (s32[1,1,512]{2,1,0:T(1,128)S(1)}, s32[1,1,512]{2,1,0:T(1,128)}, u32[]{:S(2)}) copy-start(s32[1,1,512]{2,1,0:T(1,128)} %param.15) | copy-start | bytes 6148
  4.7 0.7 %copy-start.9 = (s32[1,1,512]{2,1,0:T(1,128)S(1)}, s32[1,1,512]{2,1,0:T(1,128)}, u32[]{:S(2)}) copy-start(s32[1,1,512]{2,1,0:T(1,128)} %param.16) | copy-start | bytes 6148
  23.7 1.6 %copy-start = (f32[2048,256]{1,0:T(8,128)S(1)}, f32[2048,256]{1,0:T(8,128)}, u32[]{:S(2)}) copy-start(f32[2048,256]{1,0:T(8,128)} %table.3) | copy-start | bytes 6291460
  25.3 5.3 %copy-start.1 = (f32[2048,256]{1,0:T(8,128)S(1)}, f32[2048,256]{1,0:T(8,128)}, u32[]{:S(2)}) copy-start(f32[2048,256]{1,0:T(8,128)} %table.3) | copy-start | bytes 6291460
  27.3 10.0 %all-to-all-start.1 = ((f32[8,4,256]{2,1,0:T(4,128)}), f32[8,4,256]{2,1,0:T(4,128)S(1)}, u32[]{:S(2)}, u32[]{:S(2)}) async-start(f32[8,4,256]{2,1,0:T(4,128)} %pool.1), calls=%async_computation.1 | async-start | bytes 65536 | tf_op jit(solution)/shard_map/all_to_all | solution.py:212

commit v2 on v1

--- a/solution.py
+++ b/solution.py
@@ -9,36 +9,42 @@
 
 learn_rate = 0.1
 LANES = 128
-PREV_BOUNDS = 64
-
-
-def bound_block(bags, bag_count, first):
+
+
+def bound_block(bags, bag_count):
     lane = lax.broadcasted_iota(jnp.int32, (1, LANES), 1)
     block = jnp.zeros((1, LANES), jnp.float32)
     for j in range(1, bag_count):
         start = jnp.sum((bags < j).astype(jnp.float32), axis=1, keepdims=True)
-        block = jnp.where(lane == first + j - 1, start, block)
+        block = jnp.where(lane == j - 1, start, block)
     return block
 
 
-def pack_kernel(rows_dev, owner, row, bag, prev_owner, prev_row, prev_bag, grad, out):
-    copies = out.shape[0]
+def pack_kernel(rows_dev, *refs):
+    sources, out, held, sems = refs[:7], refs[7], refs[8:15], refs[15]
+    copies = [
+        pltpu.make_async_copy(source, place, sems.at[i])
+        for i, (source, place) in enumerate(zip(sources, held))
+    ]
+    for copy in copies:
+        copy.start()
+    for copy in copies:
+        copy.wait()
+    owner, row, bag, prev_owner, prev_row, prev_bag, grad = held
     positions = row.shape[1]
     bag_count, width = grad.shape
 
     def put(start, value):
-        shape = (copies, 1, value.shape[1])
-        out[:, :, start:start + value.shape[1]] = jnp.broadcast_to(value[None], shape)
+        out[:, start:start + value.shape[1]] = value
 
     put(0, (owner[...] * rows_dev + row[...]).astype(jnp.float32))
-    put(positions, (prev_owner[...] * rows_dev + prev_row[...]).astype(jnp.float32))
-    put(
-        2 * positions,
-        bound_block(bag[...], bag_count, 0)
-        + bound_block(prev_bag[...], bag_count, PREV_BOUNDS),
-    )
+    put(positions, bound_block(bag[...], bag_count))
+    start = positions + LANES
+    put(start, (prev_owner[...] * rows_dev + prev_row[...]).astype(jnp.float32))
+    put(start + positions, bound_block(prev_bag[...], bag_count))
+    start = start + positions + LANES
     for j in range(bag_count):
-        put(2 * positions + LANES + j * width, grad[j:j + 1, :])
+        put(start + j * width, grad[j:j + 1, :])
 
 
 def split_two(x):
@@ -46,12 +52,12 @@
     return high, (x - high.astype(jnp.float32)).astype(jnp.bfloat16)
 
 
-def codes(ids, bounds, first, bag_count, base):
+def codes(ids, bounds, bag_count, base):
     rel = ids.astype(jnp.int32) - base
     place = lax.broadcasted_iota(jnp.int32, ids.shape, 1).astype(jnp.float32)
     bag = jnp.zeros(ids.shape, jnp.int32)
     for j in range(1, bag_count):
-        start = bounds[:, first + j - 1:first + j]
+        start = bounds[:, j - 1:j]
         bag = bag + (place >= start).astype(jnp.int32)
     code = lax.shift_right_arithmetic(rel, 7) * bag_count + bag
     return code.astype(jnp.float32), (rel & (LANES - 1)).astype(jnp.float32)
@@ -76,39 +82,51 @@
             blocks, bag_count, LANES)
 
 
-def pool_kernel(bag_count, positions, msg, table, out, code_ref, lane_ref, counts):
-    rows_dev = table.shape[0]
-    devices = out.shape[0]
-    group = lax.axis_index("dp") * devices
+def join_kernel(start, *refs):
+    sources, out = refs[:-1], refs[-1]
+    for i, source in enumerate(sources):
+        out[i] = source[:, start:]
+
+
+def pool_kernel(bag_count, positions, owners, *refs):
+    sources, table = refs[:owners], refs[owners]
+    outs = refs[owners + 1:2 * owners + 1]
+    ids_ref, bounds_ref, code_ref, lane_ref, counts, held, sem = refs[2 * owners + 1:]
+    copy = pltpu.make_async_copy(table, held, sem)
+    copy.start()
+    rows_dev, width = table.shape
     base = lax.axis_index("rows") * rows_dev
-    ids = msg[pl.ds(group, devices), 0, 0:positions]
-    bounds = msg[pl.ds(group, devices), 0, 2 * positions:2 * positions + LANES]
-    code_ref[...], lane_ref[...] = codes(ids, bounds, 0, bag_count, base)
-    count_into(counts, code_ref, lane_ref, devices, bag_count)
+    for i, source in enumerate(sources):
+        ids_ref[i:i + 1, :] = source[:, 0:positions]
+        bounds_ref[i:i + 1, :] = source[:, positions:positions + LANES]
+    code_ref[...], lane_ref[...] = codes(ids_ref[...], bounds_ref[...], bag_count, base)
+    count_into(counts, code_ref, lane_ref, owners, bag_count)
     blocks = rows_dev // LANES
-    total = jnp.zeros((devices * bag_count, table.shape[1]), jnp.float32)
     flat = jnp.concatenate(
         [counts[h].astype(jnp.bfloat16) for h in range(blocks)], axis=1)
-    for part in split_two(table[...]):
+    copy.wait()
+    total = jnp.zeros((owners * bag_count, width), jnp.float32)
+    for part in split_two(held[...]):
         total += jnp.dot(flat, part, preferred_element_type=jnp.float32)
-    out[...] = total.reshape(out.shape)
-
-
-def update_kernel(
-    bag_count, positions, chunk, msg, table, accum, new_table, new_accum,
-    code_ref, lane_ref, counts, grads, sums,
-):
+    for i, out in enumerate(outs):
+        out[...] = total[i * bag_count:(i + 1) * bag_count, :]
+
+
+def update_kernel(bag_count, positions, groups, chunk, *refs):
+    sources, (table, accum, new_table, new_accum) = refs[:groups], refs[groups:groups + 4]
+    msg, code_ref, lane_ref, counts, grads, sums = refs[groups + 4:]
     devices = msg.shape[0]
+    owners = devices // groups
     step_rows, width = table.shape
     blocks = counts.shape[0]
     base = lax.axis_index("rows") * (blocks * LANES)
     step = pl.program_id(0)
-    offset = 2 * positions + LANES
+    offset = positions + LANES
 
     def count_chunk(first):
-        ids = msg[pl.ds(first, chunk), 0, positions:2 * positions]
-        bounds = msg[pl.ds(first, chunk), 0, 2 * positions:2 * positions + LANES]
-        code_ref[...], lane_ref[...] = codes(ids, bounds, PREV_BOUNDS, bag_count, base)
+        ids = msg[pl.ds(first, chunk), 0, 0:positions]
+        bounds = msg[pl.ds(first, chunk), 0, positions:positions + LANES]
+        code_ref[...], lane_ref[...] = codes(ids, bounds, bag_count, base)
         count_into(counts, code_ref, lane_ref, chunk, bag_count)
         for d in range(chunk):
             for j in range(bag_count):
@@ -127,6 +145,8 @@
 
     @pl.when(step == 0)
     def _():
+        for i, source in enumerate(sources):
+            msg[i * owners:(i + 1) * owners] = source[...]
         if single:
             count_chunk(0)
             return
@@ -162,55 +182,78 @@
             jnp.where(diagonal, fresh, 0.0), axis=0, keepdims=True)
 
 
+def shift(x, axis, step):
+    size = lax.axis_size(axis)
+    return lax.ppermute(x, axis, [(i, (i + step) % size) for i in range(size)])
+
+
 def local(
     item_table, row_accum, owner_map, row_index, bag_index,
     prev_owner, prev_row, prev_bag, grad_pooled,
 ):
-    owners = lax.axis_size("rows")
-    devices = owners * lax.axis_size("dp")
+    owners, groups = lax.axis_size("rows"), lax.axis_size("dp")
+    devices = owners * groups
     rows_dev, width = item_table.shape
     bag_count = grad_pooled.shape[2]
     positions = row_index.shape[2]
     blocks = rows_dev // LANES
-    length = 2 * positions + LANES + bag_count * width
+    now_length = positions + LANES
+    prev_length = now_length + bag_count * width
     vmem = pl.BlockSpec(memory_space=pltpu.VMEM)
+    hbm = pl.BlockSpec(memory_space=pltpu.HBM)
     params = pltpu.CompilerParams(vmem_limit_bytes=48 * 1024 * 1024)
+    greedy = pltpu.CompilerParams(vmem_limit_bytes=64 * 1024 * 1024)
 
     def line(x):
         return x.reshape(1, positions)
 
     message = pl.pallas_call(
         functools.partial(pack_kernel, rows_dev),
-        out_shape=jax.ShapeDtypeStruct((devices, 1, length), jnp.float32),
-        in_specs=[vmem] * 7,
+        out_shape=jax.ShapeDtypeStruct((1, now_length + prev_length), jnp.float32),
+        in_specs=[hbm] * 7,
         out_specs=vmem,
-        compiler_params=params,
+        scratch_shapes=[pltpu.VMEM((1, positions), jnp.int32)] * 6
+        + [pltpu.VMEM((bag_count, width), jnp.float32), pltpu.SemaphoreType.DMA((7,))],
+        compiler_params=greedy,
         name="pack",
     )(
         line(owner_map), line(row_index), line(bag_index),
         line(prev_owner), line(prev_row), line(prev_bag), grad_pooled[0, 0],
     )
-    gathered = lax.all_to_all(
-        message, ("dp", "rows"), split_axis=0, concat_axis=0, tiled=True)
-
-    partial_pooled = pl.pallas_call(
-        functools.partial(pool_kernel, bag_count, positions),
-        out_shape=jax.ShapeDtypeStruct((owners, bag_count, width), jnp.float32),
-        in_specs=[vmem] * 2,
+    messages = [message] + [shift(message, "rows", k) for k in range(1, owners)]
+
+    joined = pl.pallas_call(
+        functools.partial(join_kernel, now_length),
+        out_shape=jax.ShapeDtypeStruct((owners, 1, prev_length), jnp.float32),
+        in_specs=[vmem] * owners,
         out_specs=vmem,
+        compiler_params=params,
+        name="join",
+    )(*messages)
+    all_groups = [joined] + [shift(joined, "dp", k) for k in range(1, groups)]
+
+    partials = pl.pallas_call(
+        functools.partial(pool_kernel, bag_count, positions, owners),
+        out_shape=[jax.ShapeDtypeStruct((bag_count, width), jnp.float32)] * owners,
+        in_specs=[vmem] * owners + [hbm],
+        out_specs=[vmem] * owners,
         scratch_shapes=[
+            pltpu.VMEM((owners, positions), jnp.float32),
+            pltpu.VMEM((owners, LANES), jnp.float32),
             pltpu.VMEM((owners, positions), jnp.float32),
             pltpu.VMEM((owners, positions), jnp.float32),
             pltpu.VMEM((blocks, owners * bag_count, LANES), jnp.float32),
+            pltpu.VMEM((rows_dev, width), jnp.float32),
+            pltpu.SemaphoreType.DMA,
         ],
         compiler_params=params,
         cost_estimate=pl.CostEstimate(
             flops=4 * owners * bag_count * rows_dev * width,
             bytes_accessed=rows_dev * width * 4, transcendentals=0),
         name="pool",
-    )(gathered, item_table)
-    returned = lax.all_to_all(
-        partial_pooled, "rows", split_axis=0, concat_axis=0, tiled=True)
+    )(*messages, item_table)
+    answers = [partials[0]] + [
+        shift(partials[k], "rows", owners - k) for k in range(1, owners)]
 
     chunk = min(devices, LANES // bag_count)
     steps = 4
@@ -218,14 +261,13 @@
     segments = chunk * bag_count
     whole = lambda i: (0, 0)
     new_table, new_accum = pl.pallas_call(
-        functools.partial(update_kernel, bag_count, positions, chunk),
+        functools.partial(update_kernel, bag_count, positions, groups, chunk),
         grid=(steps,),
         out_shape=(
             jax.ShapeDtypeStruct((rows_dev, width), jnp.float32),
             jax.ShapeDtypeStruct((blocks, LANES), jnp.float32),
         ),
-        in_specs=[
-            vmem,
+        in_specs=[vmem] * groups + [
             pl.BlockSpec((step_rows, width), lambda i: (i, 0)),
             pl.BlockSpec((blocks, LANES), whole),
         ],
@@ -234,6 +276,7 @@
             pl.BlockSpec((blocks, LANES), whole),
         ),
         scratch_shapes=[
+            pltpu.VMEM((devices, 1, prev_length), jnp.float32),
             pltpu.VMEM((chunk, positions), jnp.float32),
             pltpu.VMEM((chunk, positions), jnp.float32),
             pltpu.VMEM((blocks, segments, LANES), jnp.float32),
@@ -245,9 +288,9 @@
             flops=8 * devices * bag_count * rows_dev * width,
             bytes_accessed=3 * rows_dev * width * 4, transcendentals=0),
         name="update",
-    )(gathered, item_table, row_accum.reshape(blocks, LANES))
-
-    pooled = jnp.sum(returned, axis=0)
+    )(*all_groups, item_table, row_accum.reshape(blocks, LANES))
+
+    pooled = functools.reduce(lambda x, y: x + y, answers)
     return (pooled[None, None], new_table, new_accum.reshape(rows_dev))
 
 

time: 38.3 us -> 43.8 us (1.14)
  starting transfers between devices: 3.33 us -> 23.9 us
  blocking collectives: 18.2 us -> 0 us
  waiting for transfers between devices: 1.99 us -> 8.42 us
  local copies, waits for them, and re-layouts: 6.37 us -> 2.3 us
  Pallas kernels: 6.66 us -> 7.68 us
    ppermute x0 -> x17, starting transfers between devices: none -> 23.9 us  [shift(): return lax.ppermute(x, axis, [(i, (i + step) % size) for i in range(size)])]
    all_to_all x1 -> x0, blocking collectives: 18.2 us -> none  [local(): lax.all_to_all(message, ('dp', 'rows'), split_axis=0, concat_axis=0, tile...]
    ppermute x0 -> x17, waiting for transfers between devices: none -> 8.42 us  [shift(): return lax.ppermute(x, axis, [(i, (i + step) % size) for i in range(size)])]
    unnamed x20 -> x8, local copies, waits for them, and re-layouts: 6.37 us -> 2.3 us
    all_to_all x1 -> x0, starting transfers between devices: 3.33 us -> none  [local(): lax.all_to_all(partial_pooled, 'rows', split_axis=0, concat_axis=0, tiled...]
    all_to_all x1 -> x0, waiting for transfers between devices: 1.99 us -> none  [local(): lax.all_to_all(partial_pooled, 'rows', split_axis=0, concat_axis=0, tiled...]
    pallas_call x1, Pallas kernels: 0.1 us -> 1.53 us  [local(): pl.pallas_call(functools.partial(pack_kernel, rows_dev), out_shape=jax.Sh...]
    reduce_sum x1 -> x0, other arithmetic: 0.61 us -> none  [local(): pooled = jnp.sum(returned, axis=0)]
  transfers between devices with their start and end apart: 1 -> 17, of which waited for: 1 -> 5; matrix products, arithmetic and copies ran while one was open for 0% -> 1% of each run, Pallas kernels for 12% -> 0%
where the time goes in v2:
time: 43.8 us; the launch traced here: 43.6 us
  starting transfers between devices  23.9 us (55%)
  waiting for transfers between devices  8.42 us (19%)
  Pallas kernels  7.68 us (18%)
  local copies, waits for them, and re-layouts  2.3 us (5%)
  between operations  0.69 us (2%)
  other arithmetic  0.6 us (1%)
    ppermute x17, starting transfers between devices, shift(): return lax.ppermute(x, axis, [(i, (i + step) % size) for i in range(size)])  23.9 us
    ppermute x17, waiting for transfers between devices, shift(): return lax.ppermute(x, axis, [(i, (i + step) % size) for i in range(size)])  8.42 us
    pallas_call x1, Pallas kernels, local(): pl.pallas_call(functools.partial(update_kernel, bag_count, positions, gro...  4.59 us
    unnamed x8, local copies, waits for them, and re-layouts  2.3 us
    pallas_call x1, Pallas kernels, local(): pl.pallas_call(functools.partial(pool_kernel, bag_count, positions, owner...  1.55 us
    pallas_call x1, Pallas kernels, local(): pl.pallas_call(functools.partial(pack_kernel, rows_dev), out_shape=jax.Sh...  1.53 us
  transfers between devices with their start and end apart: 17, of which 5 were waited for; matrix products, arithmetic and copies ran while one was open for 1% of the time, Pallas kernels for 0%

profile of v2, /device:TPU:0, one launch (start us, length us, event | category | flops | bytes accessed | tf_op | source)
XLA Modules:
  0.0 43.6 jit_solution(14572684332614897580)
XLA Ops:
  0.6 1.5 %pack.1.refs_0_ = f32[1,2304]{1,0:T(1,128)} custom-call(s32[1,512]{1,0:T(1,128)} %bitcast.13, s32[1,512]{1,0:T(1,128)} %bitcast.14, s32[1,512]{1,0:T(1,128)} %bitcast.15, s32[1,512]{1,0:T(1,128)} %bitcast.16, s32[1,512]{1,0:T(1,128)} %bitcast.17, s32[1,512]{1,0:T(1,128)} %bitcast.18, f32[4,256]{1,0:T(4,128)} %bitcast.12), custom_call_target="tpu_custom_call" | custom-call | tf_op jit(solution)/shard_map/pack/pallas_call | solution.py:210
  2.2 6.0 %collective-permute-start.6 = (f32[1,2304]{1,0:T(1,128)}, f32[1,2304]{1,0:T(1,128)S(1)}, u32[]{:S(2)}, u32[]{:S(2)}) collective-permute-start(f32[1,2304]{1,0:T(1,128)} %pack.1.refs_0_), channel_id=1, source_target_pairs={{0,7},{1,0},{2,1},{3,2},{4,3},{5,4},{6,5},{7,6},{8,15},{9,8},{10,9... | collective-permute-start | bytes 27656 | tf_op jit(solution)/shard_map/ppermute | solution.py:187
  8.2 0.4 %collective-permute-start.5 = (f32[1,2304]{1,0:T(1,128)}, f32[1,2304]{1,0:T(1,128)S(1)}, u32[]{:S(2)}, u32[]{:S(2)}) collective-permute-start(f32[1,2304]{1,0:T(1,128)} %pack.1.refs_0_), channel_id=1, source_target_pairs={{0,6},{1,7},{2,0},{3,1},{4,2},{5,3},{6,4},{7,5},{8,14},{9,15},{10,... | collective-permute-start | bytes 27656 | tf_op jit(solution)/shard_map/ppermute | solution.py:187
  8.7 0.0 collective-permute-start.4
  8.7 3.0 %collective-permute-start.3 = (f32[1,2304]{1,0:T(1,128)}, f32[1,2304]{1,0:T(1,128)S(1)}, u32[]{:S(2)}, u32[]{:S(2)}) collective-permute-start(f32[1,2304]{1,0:T(1,128)} %pack.1.refs_0_), channel_id=1, source_target_pairs={{0,4},{1,5},{2,6},{3,7},{4,0},{5,1},{6,2},{7,3},{8,12},{9,13},{10,... | collective-permute-start | bytes 27656 | tf_op jit(solution)/shard_map/ppermute | solution.py:187
  11.7 0.0 collective-permute-start.2
  11.7 0.0 collective-permute-done.6.refs_7_
  11.7 1.8 %collective-permute-start.1 = (f32[1,2304]{1,0:T(1,128)}, f32[1,2304]{1,0:T(1,128)S(1)}, u32[]{:S(2)}, u32[]{:S(2)}) collective-permute-start(f32[1,2304]{1,0:T(1,128)} %pack.1.refs_0_), channel_id=1, source_target_pairs={{0,2},{1,3},{2,4},{3,5},{4,6},{5,7},{6,0},{7,1},{8,10},{9,11},{10,... | collective-permute-start | bytes 27656 | tf_op jit(solution)/shard_map/ppermute | solution.py:187
  13.5 0.0 collective-permute-done.5.refs_6_
  13.5 1.1 %collective-permute-start = (f32[1,2304]{1,0:T(1,128)}, f32[1,2304]{1,0:T(1,128)S(1)}, u32[]{:S(2)}, u32[]{:S(2)}) collective-permute-start(f32[1,2304]{1,0:T(1,128)} %pack.1.refs_0_), channel_id=1, source_target_pairs={{0,1},{1,2},{2,3},{3,4},{4,5},{5,6},{6,7},{7,0},{8,9},{9,10},{10,1... | collective-permute-start | bytes 27656 | tf_op jit(solution)/shard_map/ppermute | solution.py:187
  14.6 0.0 collective-permute-done.4.refs_5_
  14.6 0.0 collective-permute-done.3.refs_4_
  14.6 2.7 %collective-permute-done.2.refs_3_ = f32[1,2304]{1,0:T(1,128)S(1)} collective-permute-done((f32[1,2304]{1,0:T(1,128)}, f32[1,2304]{1,0:T(1,128)S(1)}, u32[]{:S(2)}, u32[]{:S(2)}) %collective-permute-start.2) | collective-permute-done | bytes 9248 | tf_op jit(solution)/shard_map/ppermute | solution.py:187
  17.4 1.0 %collective-permute-done.1.refs_2_ = f32[1,2304]{1,0:T(1,128)S(1)} collective-permute-done((f32[1,2304]{1,0:T(1,128)}, f32[1,2304]{1,0:T(1,128)S(1)}, u32[]{:S(2)}, u32[]{:S(2)}) %collective-permute-start.1) | collective-permute-done | bytes 9248 | tf_op jit(solution)/shard_map/ppermute | solution.py:187
  18.4 1.7 %collective-permute-done.refs_1_ = f32[1,2304]{1,0:T(1,128)S(1)} collective-permute-done((f32[1,2304]{1,0:T(1,128)}, f32[1,2304]{1,0:T(1,128)S(1)}, u32[]{:S(2)}, u32[]{:S(2)}) %collective-permute-start) | collective-permute-done | bytes 9248 | tf_op jit(solution)/shard_map/ppermute | solution.py:187
  20.1 0.0 copy-start
  20.1 1.6 %copy-done = f32[2048,256]{1,0:T(8,128)S(1)} copy-done((f32[2048,256]{1,0:T(8,128)S(1)}, f32[2048,256]{1,0:T(8,128)}, u32[]{:S(2)}) %copy-start) | copy-done | bytes 2097176
  21.7 0.0 copy-start.2
  21.7 0.7 %copy-done.2 = f32[1,2304]{1,0:T(1,128)S(1)} copy-done((f32[1,2304]{1,0:T(1,128)S(1)}, f32[1,2304]{1,0:T(1,128)}, u32[]{:S(2)}) %copy-start.2) | copy-done | bytes 9240
  22.4 0.0 copy-start.1
  22.4 0.0 copy-start.3
  22.4 1.6 %pool.1 = (f32[4,256]{1,0:T(4,128)S(1)}, f32[4,256]{1,0:T(4,128)S(1)}, f32[4,256]{1,0:T(4,128)S(1)}, f32[4,256]{1,0:T(4,128)S(1)}, f32[4,256]{1,0:T(4,128)S(1)},...) custom-call(f32[1,2304]{1,0:T(1,128)S(1)} %copy-done.2, ...), custom_call_target="tpu_custom_call" | custom-call | flops 67108864 | bytes 2097152 | tf_op jit(solution)/shard_map/pool/pallas_call | solution.py:235
  23.9 0.3 collective-permute-start.7
  24.2 1.5 %collective-permute-start.8 = (f32[4,256]{1,0:T(4,128)S(1)}, f32[4,256]{1,0:T(4,128)S(1)}, u32[]{:S(2)}, u32[]{:S(2)}) collective-permute-start(f32[4,256]{1,0:T(4,128)S(1)} %get-tuple-element.15), channel_id=1, source_target_pairs={{0,6},{1,7},{2,0},{3,1},{4,2},{5,3},{6,4},{7,5},{8,14},{9,15},{10,... | collective-permute-start | bytes 12296 | tf_op jit(solution)/shard_map/ppermute | solution.py:187
  25.7 1.4 %collective-permute-start.9 = (f32[4,256]{1,0:T(4,128)S(1)}, f32[4,256]{1,0:T(4,128)S(1)}, u32[]{:S(2)}, u32[]{:S(2)}) collective-permute-start(f32[4,256]{1,0:T(4,128)S(1)} %get-tuple-element.16), channel_id=1, source_target_pairs={{0,5},{1,6},{2,7},{3,0},{4,1},{5,2},{6,3},{7,4},{8,13},{9,14},{10,... | collective-permute-start | bytes 12296 | tf_op jit(solution)/shard_map/ppermute | solution.py:187
  27.1 2.4 %collective-permute-start.10 = (f32[4,256]{1,0:T(4,128)S(1)}, f32[4,256]{1,0:T(4,128)S(1)}, u32[]{:S(2)}, u32[]{:S(2)}) collective-permute-start(f32[4,256]{1,0:T(4,128)S(1)} %get-tuple-element.17), channel_id=1, source_target_pairs={{0,4},{1,5},{2,6},{3,7},{4,0},{5,1},{6,2},{7,3},{8,12},{9,13},{10,... | collective-permute-start | bytes 12296 | tf_op jit(solution)/shard_map/ppermute | solution.py:187
  29.6 0.0 collective-permute-start.11
  29.6 0.0 collective-permute-done.7
  29.6 2.0 %collective-permute-start.12 = (f32[4,256]{1,0:T(4,128)S(1)}, f32[4,256]{1,0:T(4,128)S(1)}, u32[]{:S(2)}, u32[]{:S(2)}) collective-permute-start(f32[4,256]{1,0:T(4,128)S(1)} %get-tuple-element.19), channel_id=1, source_target_pairs={{0,2},{1,3},{2,4},{3,5},{4,6},{5,7},{6,0},{7,1},{8,10},{9,11},{10,... | collective-permute-start | bytes 12296 | tf_op jit(solution)/shard_map/ppermute | solution.py:187
  31.6 0.0 collective-permute-done.8
  31.6 2.0 %collective-permute-start.13 = (f32[4,256]{1,0:T(4,128)S(1)}, f32[4,256]{1,0:T(4,128)S(1)}, u32[]{:S(2)}, u32[]{:S(2)}) collective-permute-start(f32[4,256]{1,0:T(4,128)S(1)} %get-tuple-element.20), channel_id=1, source_target_pairs={{0,1},{1,2},{2,3},{3,4},{4,5},{5,6},{6,7},{7,0},{8,9},{9,10},{10,1... | collective-permute-start | bytes 12296 | tf_op jit(solution)/shard_map/ppermute | solution.py:187
  33.6 0.0 collective-permute-done.9
  33.6 0.1 collective-permute-start.16
  33.6 0.0 collective-permute-done.10
  33.6 1.6 %collective-permute-start.15 = (f32[8,1,1664]{2,1,0:T(1,128)S(1)}, f32[8,1,1664]{2,1,0:T(1,128)S(1)}, u32[]{:S(2)}, u32[]{:S(2)}) collective-permute-start(f32[8,1,1664]{2,1,0:T(1,128)S(1)} %join.1.refs_0_), channel_id=1, source_target_pairs={{0,16},{8,24},{16,0},{24,8},{1,17},{9,25},{17,1},{25,9},{2,18},{10... | collective-permute-start | bytes 159752 | tf_op jit(solution)/shard_map/ppermute | solution.py:187
  35.2 0.0 collective-permute-done.11
  35.2 0.2 collective-permute-start.14
  35.4 0.0 collective-permute-done.12
  35.4 2.5 %collective-permute-done.13 = f32[4,256]{1,0:T(4,128)S(1)} collective-permute-done((f32[4,256]{1,0:T(4,128)S(1)}, f32[4,256]{1,0:T(4,128)S(1)}, u32[]{:S(2)}, u32[]{:S(2)}) %collective-permute-start.13) | collective-permute-done | bytes 4128 | tf_op jit(solution)/shard_map/ppermute | solution.py:187
  37.9 0.6 %add_bitcast_fusion = f32[1,1,4,256]{3,2,1,0:T(4,128)} fusion(f32[4,256]{1,0:T(4,128)S(1)} %collective-permute-done.13, f32[4,256]{1,0:T(4,128)S(1)} %collective-permute-done.12, f32[4,256]{1,0:T(4,128)S(1)} %collective-permute-done.11, f32[4,256]{1,0:T(4,128)S(1)} %collective-permute-done.10, f32[4,256]{1,0:T(4,128)S(1)} %collective-permute-done.9, ...), kind=kLoop, calls=%fused_computation | loop fusion | flops 7168 | bytes 36864 | tf_op jit(solution)/shard_map/broadcast_in_dim | solution.py:294
  38.5 0.0 collective-permute-done.16.refs_3_
  38.5 0.0 collective-permute-done.15.refs_2_
  38.5 0.5 %collective-permute-done.14.refs_1_ = f32[8,1,1664]{2,1,0:T(1,128)S(1)} collective-permute-done((f32[8,1,1664]{2,1,0:T(1,128)S(1)}, f32[8,1,1664]{2,1,0:T(1,128)S(1)}, u32[]{:S(2)}, u32[]{:S(2)}) %collective-permute-start.14) | collective-permute-done | bytes 53280 | tf_op jit(solution)/shard_map/ppermute | solution.py:187
  39.0 0.0 copy-done.1
  39.0 0.0 copy-done.3
  39.0 4.6 %update.1 = (f32[2048,256]{1,0:T(8,128)}, f32[16,128]{1,0:T(8,128)}) custom-call(f32[8,1,1664]{2,1,0:T(1,128)S(1)} %join.1.refs_0_, f32[8,1,1664]{2,1,0:T(1,128)S(1)} %collective-permute-done.14.refs_1_, f32[8,1,1664]{2,1,0:T(1,128)S(1)} %collective-permute-done.15.refs_2_, f32[8,1,1664]{2,1,0:T(1,128)S(1)} %collective-permute-done.16.refs_3_, ...), custom_call_target="tpu_custom_call" | custom-call | flops 536870912 | bytes 6291456 | tf_op jit(solution)/shard_map/update/pallas_call | solution.py:263
  (1 shorter events, 0.0 us)
Async XLA Ops:
  2.2 9.5 %collective-permute-start.6 = (f32[1,2304]{1,0:T(1,128)}, f32[1,2304]{1,0:T(1,128)S(1)}, u32[]{:S(2)}, u32[]{:S(2)}) collective-permute-start(f32[1,2304]{1,0:T(1,128)} %pack.1.refs_0_), channel_id=1, source_target_pairs={{0,7},{1,0},{2,1},{3,2},{4,3},{5,4},{6,5},{7,6},{8,15},{9,8},{10,9... | collective-permute-start | bytes 27656 | tf_op jit(solution)/shard_map/ppermute | solution.py:187
  8.2 5.3 %collective-permute-start.5 = (f32[1,2304]{1,0:T(1,128)}, f32[1,2304]{1,0:T(1,128)S(1)}, u32[]{:S(2)}, u32[]{:S(2)}) collective-permute-start(f32[1,2304]{1,0:T(1,128)} %pack.1.refs_0_), channel_id=1, source_target_pairs={{0,6},{1,7},{2,0},{3,1},{4,2},{5,3},{6,4},{7,5},{8,14},{9,15},{10,... | collective-permute-start | bytes 27656 | tf_op jit(solution)/shard_map/ppermute | solution.py:187
  8.7 6.0 %collective-permute-start.4 = (f32[1,2304]{1,0:T(1,128)}, f32[1,2304]{1,0:T(1,128)S(1)}, u32[]{:S(2)}, u32[]{:S(2)}) collective-permute-start(f32[1,2304]{1,0:T(1,128)} %pack.1.refs_0_), channel_id=1, source_target_pairs={{0,5},{1,6},{2,7},{3,0},{4,1},{5,2},{6,3},{7,4},{8,13},{9,14},{10,... | collective-permute-start | bytes 27656 | tf_op jit(solution)/shard_map/ppermute | solution.py:187
  8.7 6.0 %collective-permute-start.3 = (f32[1,2304]{1,0:T(1,128)}, f32[1,2304]{1,0:T(1,128)S(1)}, u32[]{:S(2)}, u32[]{:S(2)}) collective-permute-start(f32[1,2304]{1,0:T(1,128)} %pack.1.refs_0_), channel_id=1, source_target_pairs={{0,4},{1,5},{2,6},{3,7},{4,0},{5,1},{6,2},{7,3},{8,12},{9,13},{10,... | collective-permute-start | bytes 27656 | tf_op jit(solution)/shard_map/ppermute | solution.py:187
  11.7 5.7 %collective-permute-start.2 = (f32[1,2304]{1,0:T(1,128)}, f32[1,2304]{1,0:T(1,128)S(1)}, u32[]{:S(2)}, u32[]{:S(2)}) collective-permute-start(f32[1,2304]{1,0:T(1,128)} %pack.1.refs_0_), channel_id=1, source_target_pairs={{0,3},{1,4},{2,5},{3,6},{4,7},{5,0},{6,1},{7,2},{8,11},{9,12},{10,... | collective-permute-start | bytes 27656 | tf_op jit(solution)/shard_map/ppermute | solution.py:187
  11.7 6.7 %collective-permute-start.1 = (f32[1,2304]{1,0:T(1,128)}, f32[1,2304]{1,0:T(1,128)S(1)}, u32[]{:S(2)}, u32[]{:S(2)}) collective-permute-start(f32[1,2304]{1,0:T(1,128)} %pack.1.refs_0_), channel_id=1, source_target_pairs={{0,2},{1,3},{2,4},{3,5},{4,6},{5,7},{6,0},{7,1},{8,10},{9,11},{10,... | collective-permute-start | bytes 27656 | tf_op jit(solution)/shard_map/ppermute | solution.py:187
  13.5 6.6 %collective-permute-start = (f32[1,2304]{1,0:T(1,128)}, f32[1,2304]{1,0:T(1,128)S(1)}, u32[]{:S(2)}, u32[]{:S(2)}) collective-permute-start(f32[1,2304]{1,0:T(1,128)} %pack.1.refs_0_), channel_id=1, source_target_pairs={{0,1},{1,2},{2,3},{3,4},{4,5},{5,6},{6,7},{7,0},{8,9},{9,10},{10,1... | collective-permute-start | bytes 27656 | tf_op jit(solution)/shard_map/ppermute | solution.py:187
  20.1 1.6 %copy-start = (f32[2048,256]{1,0:T(8,128)S(1)}, f32[2048,256]{1,0:T(8,128)}, u32[]{:S(2)}) copy-start(f32[2048,256]{1,0:T(8,128)} %refs_4_.1) | copy-start | bytes 6291460
  21.7 0.7 %copy-start.2 = (f32[1,2304]{1,0:T(1,128)S(1)}, f32[1,2304]{1,0:T(1,128)}, u32[]{:S(2)}) copy-start(f32[1,2304]{1,0:T(1,128)} %pack.1.refs_0_) | copy-start | bytes 27652
  22.4 16.6 %copy-start.1 = (f32[2048,256]{1,0:T(8,128)S(1)}, f32[2048,256]{1,0:T(8,128)}, u32[]{:S(2)}) copy-start(f32[2048,256]{1,0:T(8,128)} %refs_4_.1) | copy-start | bytes 6291460
  22.4 16.6 %copy-start.3 = (f32[2048]{0:T(1024)S(1)}, f32[2048]{0:T(1024)}, u32[]{:S(2)}) copy-start(f32[2048]{0:T(1024)} %param.10) | copy-start | bytes 24580
  23.9 5.6 %collective-permute-start.7 = (f32[4,256]{1,0:T(4,128)S(1)}, f32[4,256]{1,0:T(4,128)S(1)}, u32[]{:S(2)}, u32[]{:S(2)}) collective-permute-start(f32[4,256]{1,0:T(4,128)S(1)} %get-tuple-element.14), channel_id=1, source_target_pairs={{0,7},{1,0},{2,1},{3,2},{4,3},{5,4},{6,5},{7,6},{8,15},{9,8},{10,9... | collective-permute-start | bytes 12296 | tf_op jit(solution)/shard_map/ppermute | solution.py:187
  24.2 7.4 %collective-permute-start.8 = (f32[4,256]{1,0:T(4,128)S(1)}, f32[4,256]{1,0:T(4,128)S(1)}, u32[]{:S(2)}, u32[]{:S(2)}) collective-permute-start(f32[4,256]{1,0:T(4,128)S(1)} %get-tuple-element.15), channel_id=1, source_target_pairs={{0,6},{1,7},{2,0},{3,1},{4,2},{5,3},{6,4},{7,5},{8,14},{9,15},{10,... | collective-permute-start | bytes 12296 | tf_op jit(solution)/shard_map/ppermute | solution.py:187
  25.7 7.9 %collective-permute-start.9 = (f32[4,256]{1,0:T(4,128)S(1)}, f32[4,256]{1,0:T(4,128)S(1)}, u32[]{:S(2)}, u32[]{:S(2)}) collective-permute-start(f32[4,256]{1,0:T(4,128)S(1)} %get-tuple-element.16), channel_id=1, source_target_pairs={{0,5},{1,6},{2,7},{3,0},{4,1},{5,2},{6,3},{7,4},{8,13},{9,14},{10,... | collective-permute-start | bytes 12296 | tf_op jit(solution)/shard_map/ppermute | solution.py:187
  27.1 6.5 %collective-permute-start.10 = (f32[4,256]{1,0:T(4,128)S(1)}, f32[4,256]{1,0:T(4,128)S(1)}, u32[]{:S(2)}, u32[]{:S(2)}) collective-permute-start(f32[4,256]{1,0:T(4,128)S(1)} %get-tuple-element.17), channel_id=1, source_target_pairs={{0,4},{1,5},{2,6},{3,7},{4,0},{5,1},{6,2},{7,3},{8,12},{9,13},{10,... | collective-permute-start | bytes 12296 | tf_op jit(solution)/shard_map/ppermute | solution.py:187
  29.6 5.7 %collective-permute-start.11 = (f32[4,256]{1,0:T(4,128)S(1)}, f32[4,256]{1,0:T(4,128)S(1)}, u32[]{:S(2)}, u32[]{:S(2)}) collective-permute-start(f32[4,256]{1,0:T(4,128)S(1)} %get-tuple-element.18), channel_id=1, source_target_pairs={{0,3},{1,4},{2,5},{3,6},{4,7},{5,0},{6,1},{7,2},{8,11},{9,12},{10,... | collective-permute-start | bytes 12296 | tf_op jit(solution)/shard_map/ppermute | solution.py:187
  29.6 5.8 %collective-permute-start.12 = (f32[4,256]{1,0:T(4,128)S(1)}, f32[4,256]{1,0:T(4,128)S(1)}, u32[]{:S(2)}, u32[]{:S(2)}) collective-permute-start(f32[4,256]{1,0:T(4,128)S(1)} %get-tuple-element.19), channel_id=1, source_target_pairs={{0,2},{1,3},{2,4},{3,5},{4,6},{5,7},{6,0},{7,1},{8,10},{9,11},{10,... | collective-permute-start | bytes 12296 | tf_op jit(solution)/shard_map/ppermute | solution.py:187
  31.6 6.3 %collective-permute-start.13 = (f32[4,256]{1,0:T(4,128)S(1)}, f32[4,256]{1,0:T(4,128)S(1)}, u32[]{:S(2)}, u32[]{:S(2)}) collective-permute-start(f32[4,256]{1,0:T(4,128)S(1)} %get-tuple-element.20), channel_id=1, source_target_pairs={{0,1},{1,2},{2,3},{3,4},{4,5},{5,6},{6,7},{7,0},{8,9},{9,10},{10,1... | collective-permute-start | bytes 12296 | tf_op jit(solution)/shard_map/ppermute | solution.py:187
  33.6 4.9 %collective-permute-start.16 = (f32[8,1,1664]{2,1,0:T(1,128)S(1)}, f32[8,1,1664]{2,1,0:T(1,128)S(1)}, u32[]{:S(2)}, u32[]{:S(2)}) collective-permute-start(f32[8,1,1664]{2,1,0:T(1,128)S(1)} %join.1.refs_0_), channel_id=1, source_target_pairs={{0,24},{8,0},{16,8},{24,16},{1,25},{9,1},{17,9},{25,17},{2,26},{10... | collective-permute-start | bytes 159752 | tf_op jit(solution)/shard_map/ppermute | solution.py:187
  33.6 4.9 %collective-permute-start.15 = (f32[8,1,1664]{2,1,0:T(1,128)S(1)}, f32[8,1,1664]{2,1,0:T(1,128)S(1)}, u32[]{:S(2)}, u32[]{:S(2)}) collective-permute-start(f32[8,1,1664]{2,1,0:T(1,128)S(1)} %join.1.refs_0_), channel_id=1, source_target_pairs={{0,16},{8,24},{16,0},{24,8},{1,17},{9,25},{17,1},{25,9},{2,18},{10... | collective-permute-start | bytes 159752 | tf_op jit(solution)/shard_map/ppermute | solution.py:187
  35.2 3.7 %collective-permute-start.14 = (f32[8,1,1664]{2,1,0:T(1,128)S(1)}, f32[8,1,1664]{2,1,0:T(1,128)S(1)}, u32[]{:S(2)}, u32[]{:S(2)}) collective-permute-start(f32[8,1,1664]{2,1,0:T(1,128)S(1)} %join.1.refs_0_), channel_id=1, source_target_pairs={{0,8},{8,16},{16,24},{24,0},{1,9},{9,17},{17,25},{25,1},{2,10},{10... | collective-permute-start | bytes 159752 | tf_op jit(solution)/shard_map/ppermute | solution.py:187

commit v3 on v2

--- a/solution.py
+++ b/solution.py
@@ -35,7 +35,8 @@
     bag_count, width = grad.shape
 
     def put(start, value):
-        out[:, start:start + value.shape[1]] = value
+        shape = (out.shape[0], 1, value.shape[1])
+        out[:, :, start:start + value.shape[1]] = jnp.broadcast_to(value[None], shape)
 
     put(0, (owner[...] * rows_dev + row[...]).astype(jnp.float32))
     put(positions, bound_block(bag[...], bag_count))
@@ -82,34 +83,30 @@
             blocks, bag_count, LANES)
 
 
-def join_kernel(start, *refs):
-    sources, out = refs[:-1], refs[-1]
-    for i, source in enumerate(sources):
-        out[i] = source[:, start:]
-
-
-def pool_kernel(bag_count, positions, owners, *refs):
-    sources, table = refs[:owners], refs[owners]
-    outs = refs[owners + 1:2 * owners + 1]
-    ids_ref, bounds_ref, code_ref, lane_ref, counts, held, sem = refs[2 * owners + 1:]
-    copy = pltpu.make_async_copy(table, held, sem)
-    copy.start()
-    rows_dev, width = table.shape
+def prepare_kernel(table, high, low):
+    rows = table.shape[0]
+    here = pl.ds(pl.multiple_of(pl.program_id(0) * rows, rows), rows)
+    high[here, :], low[here, :] = split_two(table[...])
+
+
+def pool_kernel(
+    bag_count, positions, msg, high, low, out, joined, code_ref, lane_ref, counts,
+):
+    rows_dev, width = high.shape
+    owners = msg.shape[0]
     base = lax.axis_index("rows") * rows_dev
-    for i, source in enumerate(sources):
-        ids_ref[i:i + 1, :] = source[:, 0:positions]
-        bounds_ref[i:i + 1, :] = source[:, positions:positions + LANES]
-    code_ref[...], lane_ref[...] = codes(ids_ref[...], bounds_ref[...], bag_count, base)
+    ids = msg[:, 0, 0:positions]
+    bounds = msg[:, 0, positions:positions + LANES]
+    code_ref[...], lane_ref[...] = codes(ids, bounds, bag_count, base)
     count_into(counts, code_ref, lane_ref, owners, bag_count)
     blocks = rows_dev // LANES
     flat = jnp.concatenate(
         [counts[h].astype(jnp.bfloat16) for h in range(blocks)], axis=1)
-    copy.wait()
     total = jnp.zeros((owners * bag_count, width), jnp.float32)
-    for part in split_two(held[...]):
-        total += jnp.dot(flat, part, preferred_element_type=jnp.float32)
-    for i, out in enumerate(outs):
-        out[...] = total[i * bag_count:(i + 1) * bag_count, :]
+    for part in (high, low):
+        total += jnp.dot(flat, part[...], preferred_element_type=jnp.float32)
+    out[...] = total.reshape(out.shape)
+    joined[...] = msg[:, :, positions + LANES:]
 
 
 def update_kernel(bag_count, positions, groups, chunk, *refs):
@@ -202,62 +199,67 @@
     vmem = pl.BlockSpec(memory_space=pltpu.VMEM)
     hbm = pl.BlockSpec(memory_space=pltpu.HBM)
     params = pltpu.CompilerParams(vmem_limit_bytes=48 * 1024 * 1024)
-    greedy = pltpu.CompilerParams(vmem_limit_bytes=64 * 1024 * 1024)
 
     def line(x):
         return x.reshape(1, positions)
 
+    def stay(x):
+        return pltpu.with_memory_space_constraint(x, pltpu.HBM)
+
     message = pl.pallas_call(
         functools.partial(pack_kernel, rows_dev),
-        out_shape=jax.ShapeDtypeStruct((1, now_length + prev_length), jnp.float32),
+        out_shape=jax.ShapeDtypeStruct((owners, 1, now_length + prev_length), jnp.float32),
         in_specs=[hbm] * 7,
         out_specs=vmem,
         scratch_shapes=[pltpu.VMEM((1, positions), jnp.int32)] * 6
         + [pltpu.VMEM((bag_count, width), jnp.float32), pltpu.SemaphoreType.DMA((7,))],
-        compiler_params=greedy,
+        compiler_params=params,
         name="pack",
-    )(
+    )(*[stay(x) for x in (
         line(owner_map), line(row_index), line(bag_index),
         line(prev_owner), line(prev_row), line(prev_bag), grad_pooled[0, 0],
-    )
-    messages = [message] + [shift(message, "rows", k) for k in range(1, owners)]
-
-    joined = pl.pallas_call(
-        functools.partial(join_kernel, now_length),
-        out_shape=jax.ShapeDtypeStruct((owners, 1, prev_length), jnp.float32),
-        in_specs=[vmem] * owners,
-        out_specs=vmem,
+    )])
+    gathered = lax.all_to_all(message, "rows", split_axis=0, concat_axis=0, tiled=True)
+
+    steps = 4
+    step_rows = rows_dev // steps
+    high, low = pl.pallas_call(
+        prepare_kernel,
+        grid=(steps,),
+        out_shape=[jax.ShapeDtypeStruct((rows_dev, width), jnp.bfloat16)] * 2,
+        in_specs=[pl.BlockSpec((step_rows, width), lambda i: (i, 0))],
+        out_specs=[vmem] * 2,
         compiler_params=params,
-        name="join",
-    )(*messages)
-    all_groups = [joined] + [shift(joined, "dp", k) for k in range(1, groups)]
-
-    partials = pl.pallas_call(
-        functools.partial(pool_kernel, bag_count, positions, owners),
-        out_shape=[jax.ShapeDtypeStruct((bag_count, width), jnp.float32)] * owners,
-        in_specs=[vmem] * owners + [hbm],
-        out_specs=[vmem] * owners,
+        cost_estimate=pl.CostEstimate(
+            flops=4 * rows_dev * width, bytes_accessed=2 * rows_dev * width * 4,
+            transcendentals=0),
+        name="prepare",
+    )(stay(item_table))
+
+    partial_pooled, joined = pl.pallas_call(
+        functools.partial(pool_kernel, bag_count, positions),
+        out_shape=(
+            jax.ShapeDtypeStruct((owners, bag_count, width), jnp.float32),
+            jax.ShapeDtypeStruct((owners, 1, prev_length), jnp.float32),
+        ),
+        in_specs=[vmem] * 3,
+        out_specs=[vmem] * 2,
         scratch_shapes=[
-            pltpu.VMEM((owners, positions), jnp.float32),
-            pltpu.VMEM((owners, LANES), jnp.float32),
             pltpu.VMEM((owners, positions), jnp.float32),
             pltpu.VMEM((owners, positions), jnp.float32),
             pltpu.VMEM((blocks, owners * bag_count, LANES), jnp.float32),
-            pltpu.VMEM((rows_dev, width), jnp.float32),
-            pltpu.SemaphoreType.DMA,
         ],
         compiler_params=params,
         cost_estimate=pl.CostEstimate(
             flops=4 * owners * bag_count * rows_dev * width,
             bytes_accessed=rows_dev * width * 4, transcendentals=0),
         name="pool",
-    )(*messages, item_table)
-    answers = [partials[0]] + [
-        shift(partials[k], "rows", owners - k) for k in range(1, owners)]
+    )(gathered, high, low)
+    returned = lax.all_to_all(
+        partial_pooled, "rows", split_axis=0, concat_axis=0, tiled=True)
+    all_groups = [joined] + [shift(joined, "dp", k) for k in range(1, groups)]
 
     chunk = min(devices, LANES // bag_count)
-    steps = 4
-    step_rows = rows_dev // steps
     segments = chunk * bag_count
     whole = lambda i: (0, 0)
     new_table, new_accum = pl.pallas_call(
@@ -288,9 +290,9 @@
             flops=8 * devices * bag_count * rows_dev * width,
             bytes_accessed=3 * rows_dev * width * 4, transcendentals=0),
         name="update",
-    )(*all_groups, item_table, row_accum.reshape(blocks, LANES))
-
-    pooled = functools.reduce(lambda x, y: x + y, answers)
+    )(*all_groups, stay(item_table), row_accum.reshape(blocks, LANES))
+
+    pooled = jnp.sum(returned, axis=0)
     return (pooled[None, None], new_table, new_accum.reshape(rows_dev))
 
 

time: 43.8 us -> 31.1 us (0.71)
  starting transfers between devices: 23.9 us -> 12.4 us
  Pallas kernels: 7.68 us -> 12.3 us
  waiting for transfers between devices: 8.42 us -> 4.8 us
  local copies, waits for them, and re-layouts: 2.3 us -> 0.01 us
    ppermute x17 -> x3, starting transfers between devices: 23.9 us -> 1.75 us  [shift(): return lax.ppermute(x, axis, [(i, (i + step) % size) for i in range(size)])]
    all_to_all x0 -> x2, starting transfers between devices: none -> 10.6 us  [the longest x1 7.26 us: local(): lax.all_to_all(message, 'rows', split_axis=0, concat_axis=0, tiled=True)]
    ppermute x17 -> x3, waiting for transfers between devices: 8.42 us -> 0.23 us  [shift(): return lax.ppermute(x, axis, [(i, (i + step) % size) for i in range(size)])]
    all_to_all x0 -> x2, waiting for transfers between devices: none -> 4.57 us  [the longest x1 4.45 us: local(): lax.all_to_all(message, 'rows', split_axis=0, concat_axis=0, tiled=True)]
    pallas_call x2, Pallas kernels: 1.56 us -> 4.43 us  [the longest x1 2.49 us: local(): pl.pallas_call(prepare_kernel, grid=(steps,), out_shape=[jax.ShapeDtypeSt...]
    unnamed x8 -> x2, local copies, waits for them, and re-layouts: 2.3 us -> 0.01 us
    pallas_call x1, Pallas kernels: 4.59 us -> 6.26 us  [local(): pl.pallas_call(functools.partial(update_kernel, bag_count, positions, gro...]
    reduce_sum x0 -> x1, other arithmetic: none -> 0.61 us  [local(): pooled = jnp.sum(returned, axis=0)]
  transfers between devices with their start and end apart: 17 -> 5, of which waited for: 5 -> 3; matrix products, arithmetic and copies ran while one was open for 1% -> 0% of each run, Pallas kernels for 0% -> 29%
where the time goes in v3:
time: 31.1 us; the launch traced here: 30.7 us
  starting transfers between devices  12.4 us (40%)
  Pallas kernels  12.3 us (40%)
  waiting for transfers between devices  4.8 us (15%)
  between operations  0.68 us (2%)
  other arithmetic  0.61 us (2%)
    all_to_all x1, starting transfers between devices, local(): lax.all_to_all(message, 'rows', split_axis=0, concat_axis=0, tiled=True)  7.26 us
    pallas_call x1, Pallas kernels, local(): pl.pallas_call(functools.partial(update_kernel, bag_count, positions, gro...  6.26 us
    all_to_all x1, waiting for transfers between devices, local(): lax.all_to_all(message, 'rows', split_axis=0, concat_axis=0, tiled=True)  4.45 us
    all_to_all x1, starting transfers between devices, local(): lax.all_to_all(partial_pooled, 'rows', split_axis=0, concat_axis=0, tiled...  3.34 us
    pallas_call x1, Pallas kernels, local(): pl.pallas_call(prepare_kernel, grid=(steps,), out_shape=[jax.ShapeDtypeSt...  2.49 us
    pallas_call x1, Pallas kernels, local(): pl.pallas_call(functools.partial(pool_kernel, bag_count, positions), out_...  1.93 us
    ppermute x3, starting transfers between devices, shift(): return lax.ppermute(x, axis, [(i, (i + step) % size) for i in range(size)])  1.75 us
    pallas_call x1, Pallas kernels, local(): pl.pallas_call(functools.partial(pack_kernel, rows_dev), out_shape=jax.Sh...  1.57 us
  transfers between devices with their start and end apart: 5, of which 3 were waited for; matrix products, arithmetic and copies ran while one was open for 0% of the time, Pallas kernels for 29%

profile of v3, /device:TPU:0, one launch (start us, length us, event | category | flops | bytes accessed | tf_op | source)
XLA Modules:
  0.0 30.7 jit_solution(16273719183792519178)
XLA Ops:
  0.6 1.6 %pack.1 = f32[8,1,2304]{2,1,0:T(1,128)} custom-call(s32[1,512]{1,0:T(1,128)} %bitcast.13, s32[1,512]{1,0:T(1,128)} %bitcast.14, s32[1,512]{1,0:T(1,128)} %bitcast.15, s32[1,512]{1,0:T(1,128)} %bitcast.16, s32[1,512]{1,0:T(1,128)} %bitcast.17, s32[1,512]{1,0:T(1,128)} %bitcast.18, f32[4,256]{1,0:T(4,128)} %bitcast.11), custom_call_target="tpu_custom_call" | custom-call | tf_op jit(solution)/shard_map/pack/pallas_call | solution.py:209
  2.2 7.3 %all-to-all-start = ((f32[8,1,2304]{2,1,0:T(1,128)}), f32[8,1,2304]{2,1,0:T(1,128)S(1)}, u32[]{:S(2)}, u32[]{:S(2)}) async-start(f32[8,1,2304]{2,1,0:T(1,128)} %pack.1), calls=%async_computation | async-start | bytes 147456 | tf_op jit(solution)/shard_map/all_to_all | solution.py:222
  9.5 0.0 copy-start
  9.5 2.5 %prepare.1 = (bf16[2048,256]{1,0:T(8,128)(2,1)S(1)}, bf16[2048,256]{1,0:T(8,128)(2,1)S(1)}) custom-call(f32[2048,256]{1,0:T(8,128)} %refs_4_.1), custom_call_target="tpu_custom_call" | custom-call | flops 2097152 | bytes 4194304 | tf_op jit(solution)/shard_map/prepare/pallas_call | solution.py:226
  12.0 4.5 %all-to-all-done.msg = f32[8,1,2304]{2,1,0:T(1,128)S(1)} async-done(((f32[8,1,2304]{2,1,0:T(1,128)}), f32[8,1,2304]{2,1,0:T(1,128)S(1)}, u32[]{:S(2)}, u32[]{:S(2)}) %all-to-all-start) | async-done | bytes 73760 | tf_op jit(solution)/shard_map/all_to_all | solution.py:222
  16.4 1.9 %pool.1 = (f32[8,4,256]{2,1,0:T(4,128)}, f32[8,1,1664]{2,1,0:T(1,128)S(1)}) custom-call(f32[8,1,2304]{2,1,0:T(1,128)S(1)} %all-to-all-done.msg, bf16[2048,256]{1,0:T(8,128)(2,1)S(1)} %get-tuple-element.9.high, bf16[2048,256]{1,0:T(8,128)(2,1)S(1)} %get-tuple-element.10.low), custom_call_target="tpu_custom_call" | custom-call | flops 67108864 | bytes 2097152 | tf_op jit(solution)/shard_map/pool/pallas_call | solution.py:239
  18.4 0.0 collective-permute-start.2
  18.4 1.5 %collective-permute-start.1 = (f32[8,1,1664]{2,1,0:T(1,128)S(1)}, f32[8,1,1664]{2,1,0:T(1,128)S(1)}, u32[]{:S(2)}, u32[]{:S(2)}) collective-permute-start(f32[8,1,1664]{2,1,0:T(1,128)S(1)} %get-tuple-element.12.refs_0_), channel_id=1, source_target_pairs={{0,16},{8,24},{16,0},{24,8},{1,17},{9,25},{17,1},{25,9},{2,18},{10... | collective-permute-start | bytes 159752 | tf_op jit(solution)/shard_map/ppermute | solution.py:184
  19.9 0.2 collective-permute-start
  20.1 3.3 %all-to-all-start.1 = ((f32[8,4,256]{2,1,0:T(4,128)}), f32[8,4,256]{2,1,0:T(4,128)S(1)}, u32[]{:S(2)}, u32[]{:S(2)}) async-start(f32[8,4,256]{2,1,0:T(4,128)} %get-tuple-element.11), calls=%async_computation.1 | async-start | bytes 65536 | tf_op jit(solution)/shard_map/all_to_all | solution.py:258
  23.5 0.0 collective-permute-done.2.refs_3_
  23.5 0.0 collective-permute-done.1.refs_2_
  23.5 0.2 collective-permute-done.refs_1_
  23.7 0.0 copy-done
  23.7 6.3 %update.1 = (f32[2048,256]{1,0:T(8,128)}, f32[16,128]{1,0:T(8,128)}) custom-call(f32[8,1,1664]{2,1,0:T(1,128)S(1)} %get-tuple-element.12.refs_0_, f32[8,1,1664]{2,1,0:T(1,128)S(1)} %collective-permute-done.refs_1_, f32[8,1,1664]{2,1,0:T(1,128)S(1)} %collective-permute-done.1.refs_2_, f32[8,1,1664]{2,1,0:T(1,128)S(1)} %collective-permute-done.2.refs_3_, ...), custom_call_target="tpu_custom_call" | custom-call | flops 536870912 | bytes 6291456 | tf_op jit(solution)/shard_map/update/pallas_call | solution.py:265
  30.0 0.1 all-to-all-done.1
  30.1 0.6 %reduce_sum.9 = f32[4,256]{1,0:T(4,128)} reduce(f32[8,4,256]{2,1,0:T(4,128)S(1)} %all-to-all-done.1, f32[]{:T(128)} %constant.0.clone.1), dimensions={0}, to_apply=%region_0.0 | reduce | flops 7168 | bytes 36868 | tf_op jit(solution)/shard_map/reduce_sum | solution.py:295
Async XLA Ops:
  2.2 14.2 %all-to-all-start = ((f32[8,1,2304]{2,1,0:T(1,128)}), f32[8,1,2304]{2,1,0:T(1,128)S(1)}, u32[]{:S(2)}, u32[]{:S(2)}) async-start(f32[8,1,2304]{2,1,0:T(1,128)} %pack.1), calls=%async_computation | async-start | bytes 147456 | tf_op jit(solution)/shard_map/all_to_all | solution.py:222
  9.5 14.2 %copy-start = (f32[2048]{0:T(1024)S(1)}, f32[2048]{0:T(1024)}, u32[]{:S(2)}) copy-start(f32[2048]{0:T(1024)} %param.10) | copy-start | bytes 24580
  18.4 5.1 %collective-permute-start.2 = (f32[8,1,1664]{2,1,0:T(1,128)S(1)}, f32[8,1,1664]{2,1,0:T(1,128)S(1)}, u32[]{:S(2)}, u32[]{:S(2)}) collective-permute-start(f32[8,1,1664]{2,1,0:T(1,128)S(1)} %get-tuple-element.12.refs_0_), channel_id=1, source_target_pairs={{0,24},{8,0},{16,8},{24,16},{1,25},{9,1},{17,9},{25,17},{2,26},{10... | collective-permute-start | bytes 159752 | tf_op jit(solution)/shard_map/ppermute | solution.py:184
  18.4 5.1 %collective-permute-start.1 = (f32[8,1,1664]{2,1,0:T(1,128)S(1)}, f32[8,1,1664]{2,1,0:T(1,128)S(1)}, u32[]{:S(2)}, u32[]{:S(2)}) collective-permute-start(f32[8,1,1664]{2,1,0:T(1,128)S(1)} %get-tuple-element.12.refs_0_), channel_id=1, source_target_pairs={{0,16},{8,24},{16,0},{24,8},{1,17},{9,25},{17,1},{25,9},{2,18},{10... | collective-permute-start | bytes 159752 | tf_op jit(solution)/shard_map/ppermute | solution.py:184
  19.9 3.8 %collective-permute-start = (f32[8,1,1664]{2,1,0:T(1,128)S(1)}, f32[8,1,1664]{2,1,0:T(1,128)S(1)}, u32[]{:S(2)}, u32[]{:S(2)}) collective-permute-start(f32[8,1,1664]{2,1,0:T(1,128)S(1)} %get-tuple-element.12.refs_0_), channel_id=1, source_target_pairs={{0,8},{8,16},{16,24},{24,0},{1,9},{9,17},{17,25},{25,1},{2,10},{10... | collective-permute-start | bytes 159752 | tf_op jit(solution)/shard_map/ppermute | solution.py:184
  20.1 10.0 %all-to-all-start.1 = ((f32[8,4,256]{2,1,0:T(4,128)}), f32[8,4,256]{2,1,0:T(4,128)S(1)}, u32[]{:S(2)}, u32[]{:S(2)}) async-start(f32[8,4,256]{2,1,0:T(4,128)} %get-tuple-element.11), calls=%async_computation.1 | async-start | bytes 65536 | tf_op jit(solution)/shard_map/all_to_all | solution.py:258

commit v4 on v3

v4 whole, which is shorter than its diff:
```python
import functools

import jax
import jax.numpy as jnp
from jax import lax
from jax.experimental import pallas as pl
from jax.experimental.pallas import tpu as pltpu
from jax.sharding import PartitionSpec as P

learn_rate = 0.1
LANES = 128


def pack_kernel(rows_dev, *refs):
    sources, out, held, sems = refs[:7], refs[7], refs[8:15], refs[15]
    copies = [
        pltpu.make_async_copy(source, place, sems.at[i])
        for i, (source, place) in enumerate(zip(sources, held))
    ]
    for copy in copies:
        copy.start()
    for copy in copies:
        copy.wait()
    owner, row, bag, prev_owner, prev_row, prev_bag, grad = held
    lines = row.shape[0]
    bag_count, width = grad.shape

    def put(start, value):
        shape = (out.shape[0],) + value.shape
        out[:, start:start + value.shape[0], :] = jnp.broadcast_to(value[None], shape)

    put(0, (owner[...] * rows_dev + row[...]).astype(jnp.float32))
    put(lines, bag[...].astype(jnp.float32))
    put(2 * lines, (prev_owner[...] * rows_dev + prev_row[...]).astype(jnp.float32))
    put(3 * lines, prev_bag[...].astype(jnp.float32))
    for k in range(width // LANES):
        put(4 * lines + k * bag_count, grad[:, k * LANES:(k + 1) * LANES])


def split_two(x):
    high = x.astype(jnp.bfloat16)
    return high, (x - high.astype(jnp.float32)).astype(jnp.bfloat16)


def prepare_kernel(table, high, low, kept):
    rows = table.shape[0]
    here = pl.ds(pl.multiple_of(pl.program_id(0) * rows, rows), rows)
    values = table[...]
    kept[here, :] = values
    high[here, :], low[here, :] = split_two(values)


def codes(ids, bags, bag_count, base):
    rel = ids.astype(jnp.int32) - base
    code = lax.shift_right_arithmetic(rel, 7) * bag_count + bags.astype(jnp.int32)
    return code.astype(jnp.float32), (rel & (LANES - 1)).astype(jnp.float32)


def count_into(counts, code_ref, lane_ref, devices, bag_count):
    blocks = counts.shape[0]
    lines = code_ref.shape[1]
    one, none = jnp.ones((), jnp.bfloat16), jnp.zeros((), jnp.bfloat16)

    def one_hot(ref, d, size):
        numbers = lax.broadcasted_iota(jnp.int32, (size, LANES), 0).astype(jnp.bfloat16)
        parts = []
        for k in range(lines):
            row = jnp.broadcast_to(ref[d, k:k + 1, :], (size, LANES)).astype(jnp.bfloat16)
            parts.append(jnp.where(numbers == row, one, none))
        return jnp.concatenate(parts, axis=1)

    for d in range(devices):
        hits = lax.dot_general(
            one_hot(code_ref, d, blocks * bag_count), one_hot(lane_ref, d, LANES),
            (((1,), (1,)), ((), ())), preferred_element_type=jnp.float32)
        counts[:, d * bag_count:(d + 1) * bag_count, :] = hits.reshape(
            blocks, bag_count, LANES)


def pool_kernel(bag_count, lines, msg, high, low, out, joined, code_ref, lane_ref, counts):
    rows_dev, width = high.shape
    owners = msg.shape[0]
    base = lax.axis_index("rows") * rows_dev
    code_ref[...], lane_ref[...] = codes(
        msg[:, 0:lines, :], msg[:, lines:2 * lines, :], bag_count, base)
    joined[...] = msg[:, 2 * lines:, :]
    count_into(counts, code_ref, lane_ref, owners, bag_count)
    blocks = rows_dev // LANES
    flat = jnp.concatenate(
        [counts[h].astype(jnp.bfloat16) for h in range(blocks)], axis=1)
    total = jnp.zeros((owners * bag_count, width), jnp.float32)
    for part in (high, low):
        total += jnp.dot(flat, part[...], preferred_element_type=jnp.float32)
    out[...] = total.reshape(out.shape)


def update_kernel(bag_count, lines, groups, chunk, *refs):
    sources, (table, accum, new_table, new_accum) = refs[:groups], refs[groups:groups + 4]
    msg, code_ref, lane_ref, counts, grads, sums, fresh_table, sems = refs[groups + 4:]
    rows_dev, width = table.shape
    devices = msg.shape[0]
    owners = devices // groups
    blocks = counts.shape[0]
    base = lax.axis_index("rows") * rows_dev
    single = devices == chunk

    def count_chunk(first):
        here = pl.ds(first, chunk)
        code_ref[...], lane_ref[...] = codes(
            msg[here, 0:lines, :], msg[here, lines:2 * lines, :], bag_count, base)
        count_into(counts, code_ref, lane_ref, chunk, bag_count)
        for k in range(width // LANES):
            start = 2 * lines + k * bag_count
            grads[:, k * LANES:(k + 1) * LANES] = msg[
                here, start:start + bag_count, :].reshape(chunk * bag_count, LANES)
        return split_two(grads[...])

    def block_sum(h, parts):
        hits = counts[h].astype(jnp.bfloat16)
        total = jnp.zeros((LANES, width), jnp.float32)
        for part in parts:
            total += lax.dot_general(
                hits, part, (((0,), (0,)), ((), ())), preferred_element_type=jnp.float32)
        return total

    for i, source in enumerate(sources):
        msg[i * owners:(i + 1) * owners] = source[...]
    if single:
        parts = count_chunk(0)
    else:
        sums[...] = jnp.zeros_like(sums)

        @pl.loop(0, devices // chunk)
        def _(c):
            parts = count_chunk(c * chunk)

            @pl.loop(0, blocks)
            def _(h):
                sums[h] += block_sum(h, parts)

    diagonal = (
        lax.broadcasted_iota(jnp.int32, (LANES, LANES), 0)
        == lax.broadcasted_iota(jnp.int32, (LANES, LANES), 1))
    pieces = sems.shape[0]
    per_piece = blocks // pieces
    copies = []
    for h in range(blocks):
        grad = block_sum(h, parts) if single else sums[h]
        here = slice(h * LANES, (h + 1) * LANES)
        squares = grad * grad
        folded = squares[:, 0:LANES]
        for k in range(1, width // LANES):
            folded += squares[:, k * LANES:(k + 1) * LANES]
        old = jnp.where(diagonal, accum[h:h + 1, :], 0.0)
        fresh = jnp.sum(folded * (1.0 / width) + old, axis=1, keepdims=True)
        fresh_table[here, :] = table[here, :] - grad * (learn_rate * lax.rsqrt(fresh))
        new_accum[h:h + 1, :] = jnp.sum(
            jnp.where(diagonal, fresh, 0.0), axis=0, keepdims=True)
        if (h + 1) % per_piece == 0:
            i = h // per_piece
            piece = pl.ds(i * per_piece * LANES, per_piece * LANES)
            copies.append(pltpu.make_async_copy(
                fresh_table.at[piece, :], new_table.at[piece, :], sems.at[i]))
            copies[-1].start()
    for copy in copies:
        copy.wait()


def shift(x, axis, step):
    size = lax.axis_size(axis)
    return lax.ppermute(x, axis, [(i, (i + step) % size) for i in range(size)])


def local(
    item_table, row_accum, owner_map, row_index, bag_index,
    prev_owner, prev_row, prev_bag, grad_pooled,
):
    owners, groups = lax.axis_size("rows"), lax.axis_size("dp")
    devices = owners * groups
    rows_dev, width = item_table.shape
    bag_count = grad_pooled.shape[2]
    lines = row_index.shape[2] // LANES
    blocks = rows_dev // LANES
    prev_length = 2 * lines + bag_count * width // LANES
    vmem = pl.BlockSpec(memory_space=pltpu.VMEM)
    hbm = pl.BlockSpec(memory_space=pltpu.HBM)
    params = pltpu.CompilerParams(vmem_limit_bytes=48 * 1024 * 1024)

    def stay(x):
        return pltpu.with_memory_space_constraint(x, pltpu.HBM)

    def line(x):
        return x.reshape(lines, LANES)

    message = pl.pallas_call(
        functools.partial(pack_kernel, rows_dev),
        out_shape=jax.ShapeDtypeStruct((owners, 2 * lines + prev_length, LANES), jnp.float32),
        in_specs=[hbm] * 7,
        out_specs=vmem,
        scratch_shapes=[pltpu.VMEM((lines, LANES), jnp.int32)] * 6
        + [pltpu.VMEM((bag_count, width), jnp.float32), pltpu.SemaphoreType.DMA((7,))],
        compiler_params=params,
        name="pack",
    )(*[stay(x) for x in (
        line(owner_map), line(row_index), line(bag_index),
        line(prev_owner), line(prev_row), line(prev_bag), grad_pooled[0, 0],
    )])
    gathered = lax.all_to_all(message, "rows", split_axis=0, concat_axis=0, tiled=True)

    steps = 4
    step_rows = rows_dev // steps
    high, low, kept = pl.pallas_call(
        prepare_kernel,
        grid=(steps,),
        out_shape=[
            jax.ShapeDtypeStruct((rows_dev, width), jnp.bfloat16),
            jax.ShapeDtypeStruct((rows_dev, width), jnp.bfloat16),
            jax.ShapeDtypeStruct((rows_dev, width), jnp.float32),
        ],
        in_specs=[pl.BlockSpec((step_rows, width), lambda i: (i, 0))],
        out_specs=[vmem] * 3,
        compiler_params=params,
        cost_estimate=pl.CostEstimate(
            flops=4 * rows_dev * width, bytes_accessed=3 * rows_dev * width * 4,
            transcendentals=0),
        name="prepare",
    )(stay(item_table))

    partial_pooled, joined = pl.pallas_call(
        functools.partial(pool_kernel, bag_count, lines),
        out_shape=(
            jax.ShapeDtypeStruct((owners, bag_count, width), jnp.float32),
            jax.ShapeDtypeStruct((owners, prev_length, LANES), jnp.float32),
        ),
        in_specs=[vmem] * 3,
        out_specs=[vmem] * 2,
        scratch_shapes=[
            pltpu.VMEM((owners, lines, LANES), jnp.float32),
            pltpu.VMEM((owners, lines, LANES), jnp.float32),
            pltpu.VMEM((blocks, owners * bag_count, LANES), jnp.float32),
        ],
        compiler_params=params,
        cost_estimate=pl.CostEstimate(
            flops=4 * owners * bag_count * rows_dev * width,
            bytes_accessed=rows_dev * width * 4, transcendentals=0),
        name="pool",
    )(gathered, high, low)
    returned = lax.all_to_all(
        partial_pooled, "rows", split_axis=0, concat_axis=0, tiled=True)
    all_groups = [joined] + [shift(joined, "dp", k) for k in range(1, groups)]

    chunk = min(devices, LANES // bag_count)
    segments = chunk * bag_count
    pieces = 4
    new_table, new_accum = pl.pallas_call(
        functools.partial(update_kernel, bag_count, lines, groups, chunk),
        out_shape=(
            jax.ShapeDtypeStruct((rows_dev, width), jnp.float32),
            jax.ShapeDtypeStruct((blocks, LANES), jnp.float32),
        ),
        in_specs=[vmem] * (groups + 2),
        out_specs=(hbm, vmem),
        scratch_shapes=[
            pltpu.VMEM((devices, prev_length, LANES), jnp.float32),
            pltpu.VMEM((chunk, lines, LANES), jnp.float32),
            pltpu.VMEM((chunk, lines, LANES), jnp.float32),
            pltpu.VMEM((blocks, segments, LANES), jnp.float32),
            pltpu.VMEM((segments, width), jnp.float32),
            pltpu.VMEM((blocks, LANES, width) if devices > chunk else (1, 8, LANES), jnp.float32),
            pltpu.VMEM((rows_dev, width), jnp.float32),
            pltpu.SemaphoreType.DMA((pieces,)),
        ],
        compiler_params=params,
        cost_estimate=pl.CostEstimate(flops=1, bytes_accessed=1024, transcendentals=0),
        name="update",
    )(*all_groups, kept, row_accum.reshape(blocks, LANES))

    pooled = jnp.sum(returned, axis=0)
    return (pooled[None, None], new_table, new_accum.reshape(rows_dev))


def solution(mesh):
    placed = (
        P("rows", None),
        P("rows"),
        P("dp", "rows", None, None),
        P("dp", "rows", None),
        P("dp", "rows", None),
        P("dp", "rows", None, None),
        P("dp", "rows", None),
        P("dp", "rows", None),
        P("dp", "rows", None, None),
    )
    return jax.shard_map(
        local,
        mesh=mesh,
        in_specs=placed,
        out_specs=(P("dp", "rows", None, None), P("rows", None), P("rows")),
        check_vma=False,
    )
```

time: 31.1 us -> 34.8 us (1.12)
  blocking collectives: 0 us -> 9.05 us
  starting transfers between devices: 12.4 us -> 9.02 us
  Pallas kernels: 12.3 us -> 9.27 us
  local copies, waits for them, and re-layouts: 0.01 us -> 2.19 us
  waiting for transfers between devices: 4.8 us -> 3.59 us
    all_to_all x0 -> x1, blocking collectives: none -> 9.05 us  [local(): lax.all_to_all(partial_pooled, 'rows', split_axis=0, concat_axis=0, tiled...]
    all_to_all x1 -> x0, starting transfers between devices: 3.34 us -> none  [local(): lax.all_to_all(partial_pooled, 'rows', split_axis=0, concat_axis=0, tiled...]
    pallas_call x2, Pallas kernels: 8.19 us -> 5.22 us  [the longest x1 3.97 us: local(): pl.pallas_call(functools.partial(update_kernel, bag_count, lines, groups,...]
    unnamed x2 -> x6, local copies, waits for them, and re-layouts: 0.01 us -> 2.19 us
    all_to_all x1, waiting for transfers between devices: 4.45 us -> 3.58 us  [local(): lax.all_to_all(message, 'rows', split_axis=0, concat_axis=0, tiled=True)]
  transfers between devices with their start and end apart: 5 -> 4, of which waited for: 3 -> 1; matrix products, arithmetic and copies ran while one was open for 0% -> 2% of each run, Pallas kernels for 29% -> 7%
where the time goes in v4:
time: 34.8 us; the launch traced here: 34.4 us
  Pallas kernels  9.27 us (27%)
  blocking collectives  9.05 us (26%)
  starting transfers between devices  9.02 us (26%)
  waiting for transfers between devices  3.59 us (10%)
  local copies, waits for them, and re-layouts  2.19 us (6%)
  between operations  0.69 us (2%)
  other arithmetic  0.61 us (2%)
    all_to_all x1, blocking collectives, local(): lax.all_to_all(partial_pooled, 'rows', split_axis=0, concat_axis=0, tiled...  9.05 us
    all_to_all x1, starting transfers between devices, local(): lax.all_to_all(message, 'rows', split_axis=0, concat_axis=0, tiled=True)  7.26 us
    pallas_call x1, Pallas kernels, local(): pl.pallas_call(functools.partial(update_kernel, bag_count, lines, groups,...  3.97 us
    all_to_all x1, waiting for transfers between devices, local(): lax.all_to_all(message, 'rows', split_axis=0, concat_axis=0, tiled=True)  3.58 us
    pallas_call x1, Pallas kernels, local(): pl.pallas_call(prepare_kernel, grid=(steps,), out_shape=[jax.ShapeDtypeSt...  2.56 us
    unnamed x6, local copies, waits for them, and re-layouts  2.19 us
    ppermute x3, starting transfers between devices, shift(): return lax.ppermute(x, axis, [(i, (i + step) % size) for i in range(size)])  1.76 us
    pallas_call x1, Pallas kernels, local(): pl.pallas_call(functools.partial(pack_kernel, rows_dev), out_shape=jax.Sh...  1.49 us
  transfers between devices with their start and end apart: 4, of which 1 were waited for; matrix products, arithmetic and copies ran while one was open for 2% of the time, Pallas kernels for 7%

profile of v4, /device:TPU:0, one launch (start us, length us, event | category | flops | bytes accessed | tf_op | source)
XLA Modules:
  0.0 34.4 jit_solution(5350510893084172164)
XLA Ops:
  0.6 1.5 %pack.1 = f32[8,24,128]{2,1,0:T(8,128)} custom-call(s32[4,128]{1,0:T(4,128)} %bitcast.13, s32[4,128]{1,0:T(4,128)} %bitcast.14, s32[4,128]{1,0:T(4,128)} %bitcast.15, s32[4,128]{1,0:T(4,128)} %bitcast.16, s32[4,128]{1,0:T(4,128)} %bitcast.17, s32[4,128]{1,0:T(4,128)} %bitcast.18, f32[4,256]{1,0:T(4,128)} %bitcast.11), custom_call_target="tpu_custom_call" | custom-call | tf_op jit(solution)/shard_map/pack/pallas_call | solution.py:195
  2.1 7.3 %all-to-all-start = ((f32[8,24,128]{2,1,0:T(8,128)}), f32[8,24,128]{2,1,0:T(8,128)S(1)}, u32[]{:S(2)}, u32[]{:S(2)}) async-start(f32[8,24,128]{2,1,0:T(8,128)} %pack.1), calls=%async_computation | async-start | bytes 196608 | tf_op jit(solution)/shard_map/all_to_all | solution.py:208
  9.4 0.0 copy-start.2
  9.4 2.6 %prepare.1 = (bf16[2048,256]{1,0:T(8,128)(2,1)S(1)}, bf16[2048,256]{1,0:T(8,128)(2,1)S(1)}, f32[2048,256]{1,0:T(8,128)S(1)}) custom-call(f32[2048,256]{1,0:T(8,128)} %table.1), custom_call_target="tpu_custom_call" | custom-call | flops 2097152 | bytes 6291456 | tf_op jit(solution)/shard_map/prepare/pallas_call | solution.py:212
  12.0 0.0 copy-start
  12.0 1.0 %copy-done = bf16[2048,256]{1,0:T(8,128)(2,1)} copy-done((bf16[2048,256]{1,0:T(8,128)(2,1)}, bf16[2048,256]{1,0:T(8,128)(2,1)S(1)}, u32[]{:S(2)}) %copy-start) | copy-done | bytes 1048600
  12.9 3.6 %all-to-all-done.msg = f32[8,24,128]{2,1,0:T(8,128)S(1)} async-done(((f32[8,24,128]{2,1,0:T(8,128)}), f32[8,24,128]{2,1,0:T(8,128)S(1)}, u32[]{:S(2)}, u32[]{:S(2)}) %all-to-all-start) | async-done | bytes 98336 | tf_op jit(solution)/shard_map/all_to_all | solution.py:208
  16.5 0.0 copy-start.1
  16.5 1.2 %copy-done.1 = bf16[2048,256]{1,0:T(8,128)(2,1)S(1)} copy-done((bf16[2048,256]{1,0:T(8,128)(2,1)S(1)}, bf16[2048,256]{1,0:T(8,128)(2,1)}, u32[]{:S(2)}) %copy-start.1) | copy-done | bytes 1048600
  17.7 1.2 %pool.1 = (f32[8,4,256]{2,1,0:T(4,128)S(1)}, f32[8,16,128]{2,1,0:T(8,128)S(1)}) custom-call(f32[8,24,128]{2,1,0:T(8,128)S(1)} %all-to-all-done.msg, bf16[2048,256]{1,0:T(8,128)(2,1)S(1)} %get-tuple-element.10.high, bf16[2048,256]{1,0:T(8,128)(2,1)S(1)} %copy-done.1), custom_call_target="tpu_custom_call" | custom-call | flops 67108864 | bytes 2097152 | tf_op jit(solution)/shard_map/pool/pallas_call | solution.py:229
  19.0 0.0 collective-permute-start.2
  19.0 1.6 %collective-permute-start.1 = (f32[8,16,128]{2,1,0:T(8,128)S(1)}, f32[8,16,128]{2,1,0:T(8,128)S(1)}, u32[]{:S(2)}, u32[]{:S(2)}) collective-permute-start(f32[8,16,128]{2,1,0:T(8,128)S(1)} %get-tuple-element.13.refs_0_), channel_id=1, source_target_pairs={{0,16},{8,24},{16,0},{24,8},{1,17},{9,25},{17,1},{25,9},{2,18},{10... | collective-permute-start | bytes 196616 | tf_op jit(solution)/shard_map/ppermute | solution.py:171
  20.6 0.2 collective-permute-start
  20.8 9.0 %all_to_all.10 = f32[8,4,256]{2,1,0:T(4,128)S(1)} all-to-all(f32[8,4,256]{2,1,0:T(4,128)S(1)} %get-tuple-element.12), channel_id=1, replica_groups=mesh['dp'=4,'rows'=8] {'rows'}, dimensions={0} | all-to-all | bytes 65536 | tf_op jit(solution)/shard_map/all_to_all | solution.py:248
  29.8 0.6 %reduce_sum.9 = f32[4,256]{1,0:T(4,128)} reduce(f32[8,4,256]{2,1,0:T(4,128)S(1)} %all_to_all.10, f32[]{:T(128)} %constant.0.clone.1), dimensions={0}, to_apply=%region_0.0 | reduce | flops 7168 | bytes 36868 | tf_op jit(solution)/shard_map/reduce_sum | solution.py:278
  30.4 0.0 collective-permute-done.2.refs_3_
  30.4 0.0 collective-permute-done.1.refs_2_
  30.4 0.0 collective-permute-done.refs_1_
  30.4 0.0 copy-done.2
  30.4 4.0 %update.1 = (f32[2048,256]{1,0:T(8,128)}, f32[16,128]{1,0:T(8,128)}) custom-call(f32[8,16,128]{2,1,0:T(8,128)S(1)} %get-tuple-element.13.refs_0_, f32[8,16,128]{2,1,0:T(8,128)S(1)} %collective-permute-done.refs_1_, f32[8,16,128]{2,1,0:T(8,128)S(1)} %collective-permute-done.1.refs_2_, f32[8,16,128]{2,1,0:T(8,128)S(1)} %collective-permute-done.2.refs_3_, ...), custom_call_target="tpu_custom_call" | custom-call | flops 1 | bytes 1024 | tf_op jit(solution)/shard_map/update/pallas_call | solution.py:255
Async XLA Ops:
  2.1 14.4 %all-to-all-start = ((f32[8,24,128]{2,1,0:T(8,128)}), f32[8,24,128]{2,1,0:T(8,128)S(1)}, u32[]{:S(2)}, u32[]{:S(2)}) async-start(f32[8,24,128]{2,1,0:T(8,128)} %pack.1), calls=%async_computation | async-start | bytes 196608 | tf_op jit(solution)/shard_map/all_to_all | solution.py:208
  9.4 21.0 %copy-start.2 = (f32[2048]{0:T(1024)S(1)}, f32[2048]{0:T(1024)}, u32[]{:S(2)}) copy-start(f32[2048]{0:T(1024)} %param.10) | copy-start | bytes 24580
  12.0 1.0 %copy-start = (bf16[2048,256]{1,0:T(8,128)(2,1)}, bf16[2048,256]{1,0:T(8,128)(2,1)S(1)}, u32[]{:S(2)}) copy-start(bf16[2048,256]{1,0:T(8,128)(2,1)S(1)} %get-tuple-element.11.low) | copy-start | bytes 3145732
  16.5 1.2 %copy-start.1 = (bf16[2048,256]{1,0:T(8,128)(2,1)S(1)}, bf16[2048,256]{1,0:T(8,128)(2,1)}, u32[]{:S(2)}) copy-start(bf16[2048,256]{1,0:T(8,128)(2,1)} %copy-done) | copy-start | bytes 3145732
  19.0 11.4 %collective-permute-start.2 = (f32[8,16,128]{2,1,0:T(8,128)S(1)}, f32[8,16,128]{2,1,0:T(8,128)S(1)}, u32[]{:S(2)}, u32[]{:S(2)}) collective-permute-start(f32[8,16,128]{2,1,0:T(8,128)S(1)} %get-tuple-element.13.refs_0_), channel_id=1, source_target_pairs={{0,24},{8,0},{16,8},{24,16},{1,25},{9,1},{17,9},{25,17},{2,26},{10... | collective-permute-start | bytes 196616 | tf_op jit(solution)/shard_map/ppermute | solution.py:171
  19.0 11.4 %collective-permute-start.1 = (f32[8,16,128]{2,1,0:T(8,128)S(1)}, f32[8,16,128]{2,1,0:T(8,128)S(1)}, u32[]{:S(2)}, u32[]{:S(2)}) collective-permute-start(f32[8,16,128]{2,1,0:T(8,128)S(1)} %get-tuple-element.13.refs_0_), channel_id=1, source_target_pairs={{0,16},{8,24},{16,0},{24,8},{1,17},{9,25},{17,1},{25,9},{2,18},{10... | collective-permute-start | bytes 196616 | tf_op jit(solution)/shard_map/ppermute | solution.py:171
  20.6 9.8 %collective-permute-start = (f32[8,16,128]{2,1,0:T(8,128)S(1)}, f32[8,16,128]{2,1,0:T(8,128)S(1)}, u32[]{:S(2)}, u32[]{:S(2)}) collective-permute-start(f32[8,16,128]{2,1,0:T(8,128)S(1)} %get-tuple-element.13.refs_0_), channel_id=1, source_target_pairs={{0,8},{8,16},{16,24},{24,0},{1,9},{9,17},{17,25},{25,1},{2,10},{10... | collective-permute-start | bytes 196616 | tf_op jit(solution)/shard_map/ppermute | solution.py:171

commit v5 on v4

--- a/solution.py
+++ b/solution.py
@@ -166,6 +166,14 @@
         copy.wait()
 
 
+def finish_kernel(returned, accum, pooled, new_accum):
+    total = returned[0]
+    for i in range(1, returned.shape[0]):
+        total += returned[i]
+    pooled[...] = total
+    new_accum[...] = accum[...]
+
+
 def shift(x, axis, step):
     size = lax.axis_size(axis)
     return lax.ppermute(x, axis, [(i, (i + step) % size) for i in range(size)])
@@ -184,7 +192,8 @@
     prev_length = 2 * lines + bag_count * width // LANES
     vmem = pl.BlockSpec(memory_space=pltpu.VMEM)
     hbm = pl.BlockSpec(memory_space=pltpu.HBM)
-    params = pltpu.CompilerParams(vmem_limit_bytes=48 * 1024 * 1024)
+    params = pltpu.CompilerParams(vmem_limit_bytes=16 * 1024 * 1024)
+    chunk = min(devices, LANES // bag_count)
 
     def stay(x):
         return pltpu.with_memory_space_constraint(x, pltpu.HBM)
@@ -213,9 +222,9 @@
         prepare_kernel,
         grid=(steps,),
         out_shape=[
-            jax.ShapeDtypeStruct((rows_dev, width), jnp.bfloat16),
-            jax.ShapeDtypeStruct((rows_dev, width), jnp.bfloat16),
-            jax.ShapeDtypeStruct((rows_dev, width), jnp.float32),
+            pltpu.VMEM((rows_dev, width), jnp.bfloat16),
+            pltpu.VMEM((rows_dev, width), jnp.bfloat16),
+            pltpu.VMEM((rows_dev, width), jnp.float32),
         ],
         in_specs=[pl.BlockSpec((step_rows, width), lambda i: (i, 0))],
         out_specs=[vmem] * 3,
@@ -249,14 +258,13 @@
         partial_pooled, "rows", split_axis=0, concat_axis=0, tiled=True)
     all_groups = [joined] + [shift(joined, "dp", k) for k in range(1, groups)]
 
-    chunk = min(devices, LANES // bag_count)
     segments = chunk * bag_count
     pieces = 4
     new_table, new_accum = pl.pallas_call(
         functools.partial(update_kernel, bag_count, lines, groups, chunk),
         out_shape=(
             jax.ShapeDtypeStruct((rows_dev, width), jnp.float32),
-            jax.ShapeDtypeStruct((blocks, LANES), jnp.float32),
+            pltpu.VMEM((blocks, LANES), jnp.float32),
         ),
         in_specs=[vmem] * (groups + 2),
         out_specs=(hbm, vmem),
@@ -270,12 +278,23 @@
             pltpu.VMEM((rows_dev, width), jnp.float32),
             pltpu.SemaphoreType.DMA((pieces,)),
         ],
-        compiler_params=params,
-        cost_estimate=pl.CostEstimate(flops=1, bytes_accessed=1024, transcendentals=0),
+        compiler_params=params if devices == chunk else pltpu.CompilerParams(
+            vmem_limit_bytes=40 * 1024 * 1024),
+        cost_estimate=pl.CostEstimate(flops=1, bytes_accessed=1 << 20, transcendentals=0),
         name="update",
     )(*all_groups, kept, row_accum.reshape(blocks, LANES))
 
-    pooled = jnp.sum(returned, axis=0)
+    pooled, new_accum = pl.pallas_call(
+        finish_kernel,
+        out_shape=(
+            jax.ShapeDtypeStruct((bag_count, width), jnp.float32),
+            jax.ShapeDtypeStruct((blocks, LANES), jnp.float32),
+        ),
+        in_specs=[vmem] * 2,
+        out_specs=[vmem] * 2,
+        compiler_params=params,
+        name="finish",
+    )(returned, new_accum)
     return (pooled[None, None], new_table, new_accum.reshape(rows_dev))
 
 

time: 34.8 us -> 32.3 us (0.928)
  blocking collectives: 9.05 us -> 0 us
  starting transfers between devices: 9.02 us -> 12.3 us
  waiting for transfers between devices: 3.59 us -> 6.84 us
  Pallas kernels: 9.27 us -> 9.89 us
  other arithmetic: 0.61 us -> 0 us
    all_to_all x1 -> x0, blocking collectives: 9.05 us -> none  [local(): lax.all_to_all(partial_pooled, 'rows', split_axis=0, concat_axis=0, tiled...]
    all_to_all x0 -> x1, starting transfers between devices: none -> 3.33 us  [local(): lax.all_to_all(partial_pooled, 'rows', split_axis=0, concat_axis=0, tiled...]
    all_to_all x0 -> x1, waiting for transfers between devices: none -> 2.49 us  [local(): lax.all_to_all(partial_pooled, 'rows', split_axis=0, concat_axis=0, tiled...]
    ppermute x3, waiting for transfers between devices: 0.01 us -> 0.77 us  [shift(): return lax.ppermute(x, axis, [(i, (i + step) % size) for i in range(size)])]
    pallas_call x1, Pallas kernels: 1.25 us -> 1.87 us  [local(): pl.pallas_call(functools.partial(pool_kernel, bag_count, lines), out_shap...]
    reduce_sum x1 -> x0, other arithmetic: 0.61 us -> none  [local(): pooled = jnp.sum(returned, axis=0)]
    pallas_call x1 -> x2, Pallas kernels: 2.56 us -> 3.16 us  [the longest x1 2.56 us: local(): pl.pallas_call(prepare_kernel, grid=(steps,), out_shape=[pltpu.VMEM((rows...]
    pallas_call x1, Pallas kernels: 3.97 us -> 3.37 us  [local(): pl.pallas_call(functools.partial(update_kernel, bag_count, lines, groups,...]
  transfers between devices with their start and end apart: 4 -> 5, of which waited for: 1 -> 4; matrix products, arithmetic and copies ran while one was open for 2% -> 0% of each run, Pallas kernels for 7% -> 19%
where the time goes in v5:
time: 32.3 us; the launch traced here: 32 us
  starting transfers between devices  12.3 us (38%)
  Pallas kernels  9.89 us (31%)
  waiting for transfers between devices  6.84 us (21%)
  local copies, waits for them, and re-layouts  2.19 us (7%)
  between operations  0.69 us (2%)
    all_to_all x1, starting transfers between devices, local(): lax.all_to_all(message, 'rows', split_axis=0, concat_axis=0, tiled=True)  7.26 us
    all_to_all x1, waiting for transfers between devices, local(): lax.all_to_all(message, 'rows', split_axis=0, concat_axis=0, tiled=True)  3.58 us
    pallas_call x1, Pallas kernels, local(): pl.pallas_call(functools.partial(update_kernel, bag_count, lines, groups,...  3.37 us
    all_to_all x1, starting transfers between devices, local(): lax.all_to_all(partial_pooled, 'rows', split_axis=0, concat_axis=0, tiled...  3.33 us
    pallas_call x1, Pallas kernels, local(): pl.pallas_call(prepare_kernel, grid=(steps,), out_shape=[pltpu.VMEM((rows...  2.56 us
    all_to_all x1, waiting for transfers between devices, local(): lax.all_to_all(partial_pooled, 'rows', split_axis=0, concat_axis=0, tiled...  2.49 us
    unnamed x6, local copies, waits for them, and re-layouts  2.19 us
    pallas_call x1, Pallas kernels, local(): pl.pallas_call(functools.partial(pool_kernel, bag_count, lines), out_shap...  1.87 us
  transfers between devices with their start and end apart: 5, of which 4 were waited for; matrix products, arithmetic and copies ran while one was open for 0% of the time, Pallas kernels for 19%

profile of v5, /device:TPU:0, one launch (start us, length us, event | category | flops | bytes accessed | tf_op | source)
XLA Modules:
  0.0 32.0 jit_solution(6173982054228465456)
XLA Ops:
  0.6 1.5 %pack.1 = f32[8,24,128]{2,1,0:T(8,128)} custom-call(s32[4,128]{1,0:T(4,128)} %bitcast.12, s32[4,128]{1,0:T(4,128)} %bitcast.13, s32[4,128]{1,0:T(4,128)} %bitcast.14, s32[4,128]{1,0:T(4,128)} %bitcast.15, s32[4,128]{1,0:T(4,128)} %bitcast.16, s32[4,128]{1,0:T(4,128)} %bitcast.17, f32[4,256]{1,0:T(4,128)} %bitcast.11), custom_call_target="tpu_custom_call" | custom-call | tf_op jit(solution)/shard_map/pack/pallas_call | solution.py:204
  2.1 7.3 %all-to-all-start = ((f32[8,24,128]{2,1,0:T(8,128)}), f32[8,24,128]{2,1,0:T(8,128)S(1)}, u32[]{:S(2)}, u32[]{:S(2)}) async-start(f32[8,24,128]{2,1,0:T(8,128)} %pack.1), calls=%async_computation | async-start | bytes 196608 | tf_op jit(solution)/shard_map/all_to_all | solution.py:217
  9.4 0.0 copy-start.2
  9.4 2.6 %prepare.1 = (bf16[2048,256]{1,0:T(8,128)(2,1)S(1)}, bf16[2048,256]{1,0:T(8,128)(2,1)S(1)}, f32[2048,256]{1,0:T(8,128)S(1)}) custom-call(f32[2048,256]{1,0:T(8,128)} %table.1), custom_call_target="tpu_custom_call" | custom-call | flops 2097152 | bytes 6291456 | tf_op jit(solution)/shard_map/prepare/pallas_call | solution.py:221
  12.0 0.0 copy-start
  12.0 1.0 %copy-done = bf16[2048,256]{1,0:T(8,128)(2,1)} copy-done((bf16[2048,256]{1,0:T(8,128)(2,1)}, bf16[2048,256]{1,0:T(8,128)(2,1)S(1)}, u32[]{:S(2)}) %copy-start) | copy-done | bytes 1048600
  12.9 3.6 %all-to-all-done.msg = f32[8,24,128]{2,1,0:T(8,128)S(1)} async-done(((f32[8,24,128]{2,1,0:T(8,128)}), f32[8,24,128]{2,1,0:T(8,128)S(1)}, u32[]{:S(2)}, u32[]{:S(2)}) %all-to-all-start) | async-done | bytes 98336 | tf_op jit(solution)/shard_map/all_to_all | solution.py:217
  16.5 0.0 copy-start.1
  16.5 1.2 %copy-done.1 = bf16[2048,256]{1,0:T(8,128)(2,1)S(1)} copy-done((bf16[2048,256]{1,0:T(8,128)(2,1)S(1)}, bf16[2048,256]{1,0:T(8,128)(2,1)}, u32[]{:S(2)}) %copy-start.1) | copy-done | bytes 1048600
  17.7 1.9 %pool.1 = (f32[8,4,256]{2,1,0:T(4,128)}, f32[8,16,128]{2,1,0:T(8,128)S(1)}) custom-call(f32[8,24,128]{2,1,0:T(8,128)S(1)} %all-to-all-done.msg, bf16[2048,256]{1,0:T(8,128)(2,1)S(1)} %get-tuple-element.12.high, bf16[2048,256]{1,0:T(8,128)(2,1)S(1)} %copy-done.1), custom_call_target="tpu_custom_call" | custom-call | flops 67108864 | bytes 2097152 | tf_op jit(solution)/shard_map/pool/pallas_call | solution.py:238
  19.6 0.0 collective-permute-start.2
  19.6 1.5 %collective-permute-start.1 = (f32[8,16,128]{2,1,0:T(8,128)S(1)}, f32[8,16,128]{2,1,0:T(8,128)S(1)}, u32[]{:S(2)}, u32[]{:S(2)}) collective-permute-start(f32[8,16,128]{2,1,0:T(8,128)S(1)} %get-tuple-element.15.refs_0_), channel_id=1, source_target_pairs={{0,16},{8,24},{16,0},{24,8},{1,17},{9,25},{17,1},{25,9},{2,18},{10... | collective-permute-start | bytes 196616 | tf_op jit(solution)/shard_map/ppermute | solution.py:179
  21.1 0.2 collective-permute-start
  21.4 3.3 %all-to-all-start.1 = ((f32[8,4,256]{2,1,0:T(4,128)}), f32[8,4,256]{2,1,0:T(4,128)S(1)}, u32[]{:S(2)}, u32[]{:S(2)}) async-start(f32[8,4,256]{2,1,0:T(4,128)} %get-tuple-element.14), calls=%async_computation.1 | async-start | bytes 65536 | tf_op jit(solution)/shard_map/all_to_all | solution.py:257
  24.7 0.0 collective-permute-done.2.refs_3_
  24.7 0.7 %collective-permute-done.1.refs_2_ = f32[8,16,128]{2,1,0:T(8,128)S(1)} collective-permute-done((f32[8,16,128]{2,1,0:T(8,128)S(1)}, f32[8,16,128]{2,1,0:T(8,128)S(1)}, u32[]{:S(2)}, u32[]{:S(2)}) %collective-permute-start.1) | collective-permute-done | bytes 65568 | tf_op jit(solution)/shard_map/ppermute | solution.py:179
  25.4 0.1 collective-permute-done.refs_1_
  25.5 0.0 copy-done.2
  25.5 3.4 %update.1 = (f32[2048,256]{1,0:T(8,128)}, f32[16,128]{1,0:T(8,128)S(1)}) custom-call(f32[8,16,128]{2,1,0:T(8,128)S(1)} %get-tuple-element.15.refs_0_, f32[8,16,128]{2,1,0:T(8,128)S(1)} %collective-permute-done.refs_1_, f32[8,16,128]{2,1,0:T(8,128)S(1)} %collective-permute-done.1.refs_2_, f32[8,16,128]{2,1,0:T(8,128)S(1)} %collective-permute-done.2.refs_3_, ...), custom_call_target="tpu_custom_call" | custom-call | flops 1 | bytes 1048576 | tf_op jit(solution)/shard_map/update/pallas_call | solution.py:263
  28.9 2.5 %all-to-all-done.1.returned = f32[8,4,256]{2,1,0:T(4,128)S(1)} async-done(((f32[8,4,256]{2,1,0:T(4,128)}), f32[8,4,256]{2,1,0:T(4,128)S(1)}, u32[]{:S(2)}, u32[]{:S(2)}) %all-to-all-start.1) | async-done | bytes 32800 | tf_op jit(solution)/shard_map/all_to_all | solution.py:257
  31.3 0.6 %finish.1 = (f32[4,256]{1,0:T(4,128)}, f32[16,128]{1,0:T(8,128)}) custom-call(f32[8,4,256]{2,1,0:T(4,128)S(1)} %all-to-all-done.1.returned, f32[16,128]{1,0:T(8,128)S(1)} %get-tuple-element.17.accum), custom_call_target="tpu_custom_call" | custom-call | tf_op jit(solution)/shard_map/finish/pallas_call | solution.py:287
Async XLA Ops:
  2.1 14.4 %all-to-all-start = ((f32[8,24,128]{2,1,0:T(8,128)}), f32[8,24,128]{2,1,0:T(8,128)S(1)}, u32[]{:S(2)}, u32[]{:S(2)}) async-start(f32[8,24,128]{2,1,0:T(8,128)} %pack.1), calls=%async_computation | async-start | bytes 196608 | tf_op jit(solution)/shard_map/all_to_all | solution.py:217
  9.4 16.1 %copy-start.2 = (f32[2048]{0:T(1024)S(1)}, f32[2048]{0:T(1024)}, u32[]{:S(2)}) copy-start(f32[2048]{0:T(1024)} %param.10) | copy-start | bytes 24580
  12.0 1.0 %copy-start = (bf16[2048,256]{1,0:T(8,128)(2,1)}, bf16[2048,256]{1,0:T(8,128)(2,1)S(1)}, u32[]{:S(2)}) copy-start(bf16[2048,256]{1,0:T(8,128)(2,1)S(1)} %get-tuple-element.13.low) | copy-start | bytes 3145732
  16.5 1.2 %copy-start.1 = (bf16[2048,256]{1,0:T(8,128)(2,1)S(1)}, bf16[2048,256]{1,0:T(8,128)(2,1)}, u32[]{:S(2)}) copy-start(bf16[2048,256]{1,0:T(8,128)(2,1)} %copy-done) | copy-start | bytes 3145732
  19.6 5.1 %collective-permute-start.2 = (f32[8,16,128]{2,1,0:T(8,128)S(1)}, f32[8,16,128]{2,1,0:T(8,128)S(1)}, u32[]{:S(2)}, u32[]{:S(2)}) collective-permute-start(f32[8,16,128]{2,1,0:T(8,128)S(1)} %get-tuple-element.15.refs_0_), channel_id=1, source_target_pairs={{0,24},{8,0},{16,8},{24,16},{1,25},{9,1},{17,9},{25,17},{2,26},{10... | collective-permute-start | bytes 196616 | tf_op jit(solution)/shard_map/ppermute | solution.py:179
  19.6 5.8 %collective-permute-start.1 = (f32[8,16,128]{2,1,0:T(8,128)S(1)}, f32[8,16,128]{2,1,0:T(8,128)S(1)}, u32[]{:S(2)}, u32[]{:S(2)}) collective-permute-start(f32[8,16,128]{2,1,0:T(8,128)S(1)} %get-tuple-element.15.refs_0_), channel_id=1, source_target_pairs={{0,16},{8,24},{16,0},{24,8},{1,17},{9,25},{17,1},{25,9},{2,18},{10... | collective-permute-start | bytes 196616 | tf_op jit(solution)/shard_map/ppermute | solution.py:179
  21.1 4.3 %collective-permute-start = (f32[8,16,128]{2,1,0:T(8,128)S(1)}, f32[8,16,128]{2,1,0:T(8,128)S(1)}, u32[]{:S(2)}, u32[]{:S(2)}) collective-permute-start(f32[8,16,128]{2,1,0:T(8,128)S(1)} %get-tuple-element.15.refs_0_), channel_id=1, source_target_pairs={{0,8},{8,16},{16,24},{24,0},{1,9},{9,17},{17,25},{25,1},{2,10},{10... | collective-permute-start | bytes 196616 | tf_op jit(solution)/shard_map/ppermute | solution.py:179
  21.4 10.0 %all-to-all-start.1 = ((f32[8,4,256]{2,1,0:T(4,128)}), f32[8,4,256]{2,1,0:T(4,128)S(1)}, u32[]{:S(2)}, u32[]{:S(2)}) async-start(f32[8,4,256]{2,1,0:T(4,128)} %get-tuple-element.14), calls=%async_computation.1 | async-start | bytes 65536 | tf_op jit(solution)/shard_map/all_to_all | solution.py:257

commit v6 on v5

--- a/solution.py
+++ b/solution.py
@@ -42,12 +42,10 @@
     return high, (x - high.astype(jnp.float32)).astype(jnp.bfloat16)
 
 
-def prepare_kernel(table, high, low, kept):
+def prepare_kernel(table, high, low):
     rows = table.shape[0]
     here = pl.ds(pl.multiple_of(pl.program_id(0) * rows, rows), rows)
-    values = table[...]
-    kept[here, :] = values
-    high[here, :], low[here, :] = split_two(values)
+    high[here, :], low[here, :] = split_two(table[...])
 
 
 def codes(ids, bags, bag_count, base):
@@ -96,8 +94,19 @@
 
 def update_kernel(bag_count, lines, groups, chunk, *refs):
     sources, (table, accum, new_table, new_accum) = refs[:groups], refs[groups:groups + 4]
-    msg, code_ref, lane_ref, counts, grads, sums, fresh_table, sems = refs[groups + 4:]
+    msg, code_ref, lane_ref, counts, grads, sums, held, sems = refs[groups + 4:]
     rows_dev, width = table.shape
+    pieces = sems.shape[1]
+
+    def piece(i):
+        return pl.ds(i * (rows_dev // pieces), rows_dev // pieces)
+
+    fetches = [
+        pltpu.make_async_copy(table.at[piece(i), :], held.at[piece(i), :], sems.at[0, i])
+        for i in range(pieces)
+    ]
+    for fetch in fetches:
+        fetch.start()
     devices = msg.shape[0]
     owners = devices // groups
     blocks = counts.shape[0]
@@ -141,10 +150,12 @@
     diagonal = (
         lax.broadcasted_iota(jnp.int32, (LANES, LANES), 0)
         == lax.broadcasted_iota(jnp.int32, (LANES, LANES), 1))
-    pieces = sems.shape[0]
     per_piece = blocks // pieces
     copies = []
     for h in range(blocks):
+        i = h // per_piece
+        if h % per_piece == 0:
+            fetches[i].wait()
         grad = block_sum(h, parts) if single else sums[h]
         here = slice(h * LANES, (h + 1) * LANES)
         squares = grad * grad
@@ -153,14 +164,12 @@
             folded += squares[:, k * LANES:(k + 1) * LANES]
         old = jnp.where(diagonal, accum[h:h + 1, :], 0.0)
         fresh = jnp.sum(folded * (1.0 / width) + old, axis=1, keepdims=True)
-        fresh_table[here, :] = table[here, :] - grad * (learn_rate * lax.rsqrt(fresh))
+        held[here, :] = held[here, :] - grad * (learn_rate * lax.rsqrt(fresh))
         new_accum[h:h + 1, :] = jnp.sum(
             jnp.where(diagonal, fresh, 0.0), axis=0, keepdims=True)
         if (h + 1) % per_piece == 0:
-            i = h // per_piece
-            piece = pl.ds(i * per_piece * LANES, per_piece * LANES)
             copies.append(pltpu.make_async_copy(
-                fresh_table.at[piece, :], new_table.at[piece, :], sems.at[i]))
+                held.at[piece(i), :], new_table.at[piece(i), :], sems.at[1, i]))
             copies[-1].start()
     for copy in copies:
         copy.wait()
@@ -203,7 +212,7 @@
 
     message = pl.pallas_call(
         functools.partial(pack_kernel, rows_dev),
-        out_shape=jax.ShapeDtypeStruct((owners, 2 * lines + prev_length, LANES), jnp.float32),
+        out_shape=pltpu.VMEM((owners, 2 * lines + prev_length, LANES), jnp.float32),
         in_specs=[hbm] * 7,
         out_specs=vmem,
         scratch_shapes=[pltpu.VMEM((lines, LANES), jnp.int32)] * 6
@@ -218,19 +227,18 @@
 
     steps = 4
     step_rows = rows_dev // steps
-    high, low, kept = pl.pallas_call(
+    high, low = pl.pallas_call(
         prepare_kernel,
         grid=(steps,),
         out_shape=[
             pltpu.VMEM((rows_dev, width), jnp.bfloat16),
             pltpu.VMEM((rows_dev, width), jnp.bfloat16),
-            pltpu.VMEM((rows_dev, width), jnp.float32),
         ],
         in_specs=[pl.BlockSpec((step_rows, width), lambda i: (i, 0))],
-        out_specs=[vmem] * 3,
+        out_specs=[vmem] * 2,
         compiler_params=params,
         cost_estimate=pl.CostEstimate(
-            flops=4 * rows_dev * width, bytes_accessed=3 * rows_dev * width * 4,
+            flops=4 * rows_dev * width, bytes_accessed=2 * rows_dev * width * 4,
             transcendentals=0),
         name="prepare",
     )(stay(item_table))
@@ -238,8 +246,8 @@
     partial_pooled, joined = pl.pallas_call(
         functools.partial(pool_kernel, bag_count, lines),
         out_shape=(
-            jax.ShapeDtypeStruct((owners, bag_count, width), jnp.float32),
-            jax.ShapeDtypeStruct((owners, prev_length, LANES), jnp.float32),
+            pltpu.VMEM((owners, bag_count, width), jnp.float32),
+            pltpu.VMEM((owners, prev_length, LANES), jnp.float32),
         ),
         in_specs=[vmem] * 3,
         out_specs=[vmem] * 2,
@@ -266,7 +274,7 @@
             jax.ShapeDtypeStruct((rows_dev, width), jnp.float32),
             pltpu.VMEM((blocks, LANES), jnp.float32),
         ),
-        in_specs=[vmem] * (groups + 2),
+        in_specs=[vmem] * groups + [hbm, vmem],
         out_specs=(hbm, vmem),
         scratch_shapes=[
             pltpu.VMEM((devices, prev_length, LANES), jnp.float32),
@@ -276,13 +284,13 @@
             pltpu.VMEM((segments, width), jnp.float32),
             pltpu.VMEM((blocks, LANES, width) if devices > chunk else (1, 8, LANES), jnp.float32),
             pltpu.VMEM((rows_dev, width), jnp.float32),
-            pltpu.SemaphoreType.DMA((pieces,)),
+            pltpu.SemaphoreType.DMA((2, pieces)),
         ],
         compiler_params=params if devices == chunk else pltpu.CompilerParams(
             vmem_limit_bytes=40 * 1024 * 1024),
         cost_estimate=pl.CostEstimate(flops=1, bytes_accessed=1 << 20, transcendentals=0),
         name="update",
-    )(*all_groups, kept, row_accum.reshape(blocks, LANES))
+    )(*all_groups, stay(item_table), row_accum.reshape(blocks, LANES))
 
     pooled, new_accum = pl.pallas_call(
         finish_kernel,

time: 32.3 us -> 31.1 us (0.963)
  local copies, waits for them, and re-layouts: 2.19 us -> 0.01 us
  Pallas kernels: 9.89 us -> 11.4 us
  waiting for transfers between devices: 6.84 us -> 6.32 us
    unnamed x6 -> x2, local copies, waits for them, and re-layouts: 2.19 us -> 0.01 us
    all_to_all x1, waiting for transfers between devices: 2.49 us -> 0.93 us  [local(): lax.all_to_all(partial_pooled, 'rows', split_axis=0, concat_axis=0, tiled...]
    pallas_call x1, Pallas kernels: 3.37 us -> 4.9 us  [local(): pl.pallas_call(functools.partial(update_kernel, bag_count, lines, groups,...]
    all_to_all x1, waiting for transfers between devices: 3.58 us -> 4.62 us  [local(): lax.all_to_all(message, 'rows', split_axis=0, concat_axis=0, tiled=True)]
  transfers between devices with their start and end apart: 5 -> 5, of which waited for: 4 -> 4; matrix products, arithmetic and copies ran while one was open for 0% -> 0% of each run, Pallas kernels for 19% -> 24%
where the time goes in v6:
time: 31.1 us; the launch traced here: 30.7 us
  starting transfers between devices  12.3 us (40%)
  Pallas kernels  11.4 us (37%)
  waiting for transfers between devices  6.32 us (20%)
  between operations  0.68 us (2%)
    all_to_all x1, starting transfers between devices, local(): lax.all_to_all(message, 'rows', split_axis=0, concat_axis=0, tiled=True)  7.26 us
    pallas_call x1, Pallas kernels, local(): pl.pallas_call(functools.partial(update_kernel, bag_count, lines, groups,...  4.9 us
    all_to_all x1, waiting for transfers between devices, local(): lax.all_to_all(message, 'rows', split_axis=0, concat_axis=0, tiled=True)  4.62 us
    all_to_all x1, starting transfers between devices, local(): lax.all_to_all(partial_pooled, 'rows', split_axis=0, concat_axis=0, tiled...  3.33 us
    pallas_call x1, Pallas kernels, local(): pl.pallas_call(prepare_kernel, grid=(steps,), out_shape=[pltpu.VMEM((rows...  2.49 us
    pallas_call x1, Pallas kernels, local(): pl.pallas_call(functools.partial(pool_kernel, bag_count, lines), out_shap...  1.87 us
    ppermute x3, starting transfers between devices, shift(): return lax.ppermute(x, axis, [(i, (i + step) % size) for i in range(size)])  1.75 us
    pallas_call x1, Pallas kernels, local(): pl.pallas_call(functools.partial(pack_kernel, rows_dev), out_shape=pltpu....  1.5 us
  transfers between devices with their start and end apart: 5, of which 4 were waited for; matrix products, arithmetic and copies ran while one was open for 0% of the time, Pallas kernels for 24%

profile of v6, /device:TPU:0, one launch (start us, length us, event | category | flops | bytes accessed | tf_op | source)
XLA Modules:
  0.0 30.7 jit_solution(8681360160165757280)
XLA Ops:
  0.6 1.5 %pack.1 = f32[8,24,128]{2,1,0:T(8,128)} custom-call(s32[4,128]{1,0:T(4,128)} %bitcast.12, s32[4,128]{1,0:T(4,128)} %bitcast.13, s32[4,128]{1,0:T(4,128)} %bitcast.14, s32[4,128]{1,0:T(4,128)} %bitcast.15, s32[4,128]{1,0:T(4,128)} %bitcast.16, s32[4,128]{1,0:T(4,128)} %bitcast.17, f32[4,256]{1,0:T(4,128)} %bitcast.11), custom_call_target="tpu_custom_call" | custom-call | tf_op jit(solution)/shard_map/pack/pallas_call | solution.py:213
  2.1 7.3 %all-to-all-start = ((f32[8,24,128]{2,1,0:T(8,128)}), f32[8,24,128]{2,1,0:T(8,128)S(1)}, u32[]{:S(2)}, u32[]{:S(2)}) async-start(f32[8,24,128]{2,1,0:T(8,128)} %pack.1), calls=%async_computation | async-start | bytes 196608 | tf_op jit(solution)/shard_map/all_to_all | solution.py:226
  9.4 0.0 copy-start
  9.4 2.5 %prepare.1 = (bf16[2048,256]{1,0:T(8,128)(2,1)S(1)}, bf16[2048,256]{1,0:T(8,128)(2,1)S(1)}) custom-call(f32[2048,256]{1,0:T(8,128)} %refs_4_.1), custom_call_target="tpu_custom_call" | custom-call | flops 2097152 | bytes 4194304 | tf_op jit(solution)/shard_map/prepare/pallas_call | solution.py:230
  11.9 4.6 %all-to-all-done.msg = f32[8,24,128]{2,1,0:T(8,128)S(1)} async-done(((f32[8,24,128]{2,1,0:T(8,128)}), f32[8,24,128]{2,1,0:T(8,128)S(1)}, u32[]{:S(2)}, u32[]{:S(2)}) %all-to-all-start) | async-done | bytes 98336 | tf_op jit(solution)/shard_map/all_to_all | solution.py:226
  16.5 1.9 %pool.1 = (f32[8,4,256]{2,1,0:T(4,128)}, f32[8,16,128]{2,1,0:T(8,128)S(1)}) custom-call(f32[8,24,128]{2,1,0:T(8,128)S(1)} %all-to-all-done.msg, bf16[2048,256]{1,0:T(8,128)(2,1)S(1)} %get-tuple-element.11.high, bf16[2048,256]{1,0:T(8,128)(2,1)S(1)} %get-tuple-element.12.low), custom_call_target="tpu_custom_call" | custom-call | flops 67108864 | bytes 2097152 | tf_op jit(solution)/shard_map/pool/pallas_call | solution.py:246
  18.4 0.0 collective-permute-start.2
  18.4 1.5 %collective-permute-start.1 = (f32[8,16,128]{2,1,0:T(8,128)S(1)}, f32[8,16,128]{2,1,0:T(8,128)S(1)}, u32[]{:S(2)}, u32[]{:S(2)}) collective-permute-start(f32[8,16,128]{2,1,0:T(8,128)S(1)} %get-tuple-element.14.refs_0_), channel_id=1, source_target_pairs={{0,16},{8,24},{16,0},{24,8},{1,17},{9,25},{17,1},{25,9},{2,18},{10... | collective-permute-start | bytes 196616 | tf_op jit(solution)/shard_map/ppermute | solution.py:188
  19.9 0.2 collective-permute-start
  20.1 3.3 %all-to-all-start.1 = ((f32[8,4,256]{2,1,0:T(4,128)}), f32[8,4,256]{2,1,0:T(4,128)S(1)}, u32[]{:S(2)}, u32[]{:S(2)}) async-start(f32[8,4,256]{2,1,0:T(4,128)} %get-tuple-element.13), calls=%async_computation.1 | async-start | bytes 65536 | tf_op jit(solution)/shard_map/all_to_all | solution.py:265
  23.5 0.0 collective-permute-done.2.refs_3_
  23.5 0.7 %collective-permute-done.1.refs_2_ = f32[8,16,128]{2,1,0:T(8,128)S(1)} collective-permute-done((f32[8,16,128]{2,1,0:T(8,128)S(1)}, f32[8,16,128]{2,1,0:T(8,128)S(1)}, u32[]{:S(2)}, u32[]{:S(2)}) %collective-permute-start.1) | collective-permute-done | bytes 65568 | tf_op jit(solution)/shard_map/ppermute | solution.py:188
  24.2 0.1 collective-permute-done.refs_1_
  24.3 0.0 copy-done
  24.3 4.9 %update.1 = (f32[2048,256]{1,0:T(8,128)}, f32[16,128]{1,0:T(8,128)S(1)}) custom-call(f32[8,16,128]{2,1,0:T(8,128)S(1)} %get-tuple-element.14.refs_0_, f32[8,16,128]{2,1,0:T(8,128)S(1)} %collective-permute-done.refs_1_, f32[8,16,128]{2,1,0:T(8,128)S(1)} %collective-permute-done.1.refs_2_, f32[8,16,128]{2,1,0:T(8,128)S(1)} %collective-permute-done.2.refs_3_, ...), custom_call_target="tpu_custom_call" | custom-call | flops 1 | bytes 1048576 | tf_op jit(solution)/shard_map/update/pallas_call | solution.py:271
  29.2 0.9 %all-to-all-done.1.returned = f32[8,4,256]{2,1,0:T(4,128)S(1)} async-done(((f32[8,4,256]{2,1,0:T(4,128)}), f32[8,4,256]{2,1,0:T(4,128)S(1)}, u32[]{:S(2)}, u32[]{:S(2)}) %all-to-all-start.1) | async-done | bytes 32800 | tf_op jit(solution)/shard_map/all_to_all | solution.py:265
  30.1 0.6 %finish.1 = (f32[4,256]{1,0:T(4,128)}, f32[16,128]{1,0:T(8,128)}) custom-call(f32[8,4,256]{2,1,0:T(4,128)S(1)} %all-to-all-done.1.returned, f32[16,128]{1,0:T(8,128)S(1)} %get-tuple-element.15.accum), custom_call_target="tpu_custom_call" | custom-call | tf_op jit(solution)/shard_map/finish/pallas_call | solution.py:295
Async XLA Ops:
  2.1 14.4 %all-to-all-start = ((f32[8,24,128]{2,1,0:T(8,128)}), f32[8,24,128]{2,1,0:T(8,128)S(1)}, u32[]{:S(2)}, u32[]{:S(2)}) async-start(f32[8,24,128]{2,1,0:T(8,128)} %pack.1), calls=%async_computation | async-start | bytes 196608 | tf_op jit(solution)/shard_map/all_to_all | solution.py:226
  9.4 14.9 %copy-start = (f32[2048]{0:T(1024)S(1)}, f32[2048]{0:T(1024)}, u32[]{:S(2)}) copy-start(f32[2048]{0:T(1024)} %param.10) | copy-start | bytes 24580
  18.4 5.1 %collective-permute-start.2 = (f32[8,16,128]{2,1,0:T(8,128)S(1)}, f32[8,16,128]{2,1,0:T(8,128)S(1)}, u32[]{:S(2)}, u32[]{:S(2)}) collective-permute-start(f32[8,16,128]{2,1,0:T(8,128)S(1)} %get-tuple-element.14.refs_0_), channel_id=1, source_target_pairs={{0,24},{8,0},{16,8},{24,16},{1,25},{9,1},{17,9},{25,17},{2,26},{10... | collective-permute-start | bytes 196616 | tf_op jit(solution)/shard_map/ppermute | solution.py:188
  18.4 5.8 %collective-permute-start.1 = (f32[8,16,128]{2,1,0:T(8,128)S(1)}, f32[8,16,128]{2,1,0:T(8,128)S(1)}, u32[]{:S(2)}, u32[]{:S(2)}) collective-permute-start(f32[8,16,128]{2,1,0:T(8,128)S(1)} %get-tuple-element.14.refs_0_), channel_id=1, source_target_pairs={{0,16},{8,24},{16,0},{24,8},{1,17},{9,25},{17,1},{25,9},{2,18},{10... | collective-permute-start | bytes 196616 | tf_op jit(solution)/shard_map/ppermute | solution.py:188
  19.9 4.3 %collective-permute-start = (f32[8,16,128]{2,1,0:T(8,128)S(1)}, f32[8,16,128]{2,1,0:T(8,128)S(1)}, u32[]{:S(2)}, u32[]{:S(2)}) collective-permute-start(f32[8,16,128]{2,1,0:T(8,128)S(1)} %get-tuple-element.14.refs_0_), channel_id=1, source_target_pairs={{0,8},{8,16},{16,24},{24,0},{1,9},{9,17},{17,25},{25,1},{2,10},{10... | collective-permute-start | bytes 196616 | tf_op jit(solution)/shard_map/ppermute | solution.py:188
  20.1 10.0 %all-to-all-start.1 = ((f32[8,4,256]{2,1,0:T(4,128)}), f32[8,4,256]{2,1,0:T(4,128)S(1)}, u32[]{:S(2)}, u32[]{:S(2)}) async-start(f32[8,4,256]{2,1,0:T(4,128)} %get-tuple-element.13), calls=%async_computation.1 | async-start | bytes 65536 | tf_op jit(solution)/shard_map/all_to_all | solution.py:265

commit v7 on v5

--- a/solution.py
+++ b/solution.py
@@ -42,12 +42,10 @@
     return high, (x - high.astype(jnp.float32)).astype(jnp.bfloat16)
 
 
-def prepare_kernel(table, high, low, kept):
+def prepare_kernel(table, high, low):
     rows = table.shape[0]
     here = pl.ds(pl.multiple_of(pl.program_id(0) * rows, rows), rows)
-    values = table[...]
-    kept[here, :] = values
-    high[here, :], low[here, :] = split_two(values)
+    high[here, :], low[here, :] = split_two(table[...])
 
 
 def codes(ids, bags, bag_count, base):
@@ -77,7 +75,12 @@
             blocks, bag_count, LANES)
 
 
-def pool_kernel(bag_count, lines, msg, high, low, out, joined, code_ref, lane_ref, counts):
+def pool_kernel(
+    bag_count, lines, msg, high, low, table, out, joined, kept,
+    code_ref, lane_ref, counts, sem,
+):
+    fetch = pltpu.make_async_copy(table, kept, sem)
+    fetch.start()
     rows_dev, width = high.shape
     owners = msg.shape[0]
     base = lax.axis_index("rows") * rows_dev
@@ -92,12 +95,14 @@
     for part in (high, low):
         total += jnp.dot(flat, part[...], preferred_element_type=jnp.float32)
     out[...] = total.reshape(out.shape)
+    fetch.wait()
 
 
 def update_kernel(bag_count, lines, groups, chunk, *refs):
     sources, (table, accum, new_table, new_accum) = refs[:groups], refs[groups:groups + 4]
     msg, code_ref, lane_ref, counts, grads, sums, fresh_table, sems = refs[groups + 4:]
     rows_dev, width = table.shape
+    pieces = sems.shape[0]
     devices = msg.shape[0]
     owners = devices // groups
     blocks = counts.shape[0]
@@ -141,10 +146,10 @@
     diagonal = (
         lax.broadcasted_iota(jnp.int32, (LANES, LANES), 0)
         == lax.broadcasted_iota(jnp.int32, (LANES, LANES), 1))
-    pieces = sems.shape[0]
     per_piece = blocks // pieces
     copies = []
     for h in range(blocks):
+        i = h // per_piece
         grad = block_sum(h, parts) if single else sums[h]
         here = slice(h * LANES, (h + 1) * LANES)
         squares = grad * grad
@@ -157,7 +162,6 @@
         new_accum[h:h + 1, :] = jnp.sum(
             jnp.where(diagonal, fresh, 0.0), axis=0, keepdims=True)
         if (h + 1) % per_piece == 0:
-            i = h // per_piece
             piece = pl.ds(i * per_piece * LANES, per_piece * LANES)
             copies.append(pltpu.make_async_copy(
                 fresh_table.at[piece, :], new_table.at[piece, :], sems.at[i]))
@@ -203,7 +207,7 @@
 
     message = pl.pallas_call(
         functools.partial(pack_kernel, rows_dev),
-        out_shape=jax.ShapeDtypeStruct((owners, 2 * lines + prev_length, LANES), jnp.float32),
+        out_shape=pltpu.VMEM((owners, 2 * lines + prev_length, LANES), jnp.float32),
         in_specs=[hbm] * 7,
         out_specs=vmem,
         scratch_shapes=[pltpu.VMEM((lines, LANES), jnp.int32)] * 6
@@ -218,42 +222,43 @@
 
     steps = 4
     step_rows = rows_dev // steps
-    high, low, kept = pl.pallas_call(
+    high, low = pl.pallas_call(
         prepare_kernel,
         grid=(steps,),
         out_shape=[
             pltpu.VMEM((rows_dev, width), jnp.bfloat16),
             pltpu.VMEM((rows_dev, width), jnp.bfloat16),
-            pltpu.VMEM((rows_dev, width), jnp.float32),
         ],
         in_specs=[pl.BlockSpec((step_rows, width), lambda i: (i, 0))],
-        out_specs=[vmem] * 3,
+        out_specs=[vmem] * 2,
         compiler_params=params,
         cost_estimate=pl.CostEstimate(
-            flops=4 * rows_dev * width, bytes_accessed=3 * rows_dev * width * 4,
+            flops=4 * rows_dev * width, bytes_accessed=2 * rows_dev * width * 4,
             transcendentals=0),
         name="prepare",
     )(stay(item_table))
 
-    partial_pooled, joined = pl.pallas_call(
+    partial_pooled, joined, kept = pl.pallas_call(
         functools.partial(pool_kernel, bag_count, lines),
         out_shape=(
-            jax.ShapeDtypeStruct((owners, bag_count, width), jnp.float32),
-            jax.ShapeDtypeStruct((owners, prev_length, LANES), jnp.float32),
+            pltpu.VMEM((owners, bag_count, width), jnp.float32),
+            pltpu.VMEM((owners, prev_length, LANES), jnp.float32),
+            pltpu.VMEM((rows_dev, width), jnp.float32),
         ),
-        in_specs=[vmem] * 3,
-        out_specs=[vmem] * 2,
+        in_specs=[vmem] * 3 + [hbm],
+        out_specs=[vmem] * 3,
         scratch_shapes=[
             pltpu.VMEM((owners, lines, LANES), jnp.float32),
             pltpu.VMEM((owners, lines, LANES), jnp.float32),
             pltpu.VMEM((blocks, owners * bag_count, LANES), jnp.float32),
+            pltpu.SemaphoreType.DMA,
         ],
         compiler_params=params,
         cost_estimate=pl.CostEstimate(
             flops=4 * owners * bag_count * rows_dev * width,
             bytes_accessed=rows_dev * width * 4, transcendentals=0),
         name="pool",
-    )(gathered, high, low)
+    )(gathered, high, low, stay(item_table))
     returned = lax.all_to_all(
         partial_pooled, "rows", split_axis=0, concat_axis=0, tiled=True)
     all_groups = [joined] + [shift(joined, "dp", k) for k in range(1, groups)]

time: 32.3 us -> 32.9 us (1.019)
  Pallas kernels: 9.89 us -> 10.3 us
    pallas_call x1, Pallas kernels: 1.87 us -> 2.32 us  [local(): pl.pallas_call(functools.partial(pool_kernel, bag_count, lines), out_shap...]
  transfers between devices with their start and end apart: 5 -> 5, of which waited for: 4 -> 4; matrix products, arithmetic and copies ran while one was open for 0% -> 0% of each run, Pallas kernels for 19% -> 18%
where the time goes in v7:
time: 32.9 us; the launch traced here: 32.5 us
  starting transfers between devices  12.4 us (38%)
  Pallas kernels  10.3 us (31%)
  waiting for transfers between devices  6.89 us (21%)
  local copies, waits for them, and re-layouts  2.19 us (7%)
  between operations  0.7 us (2%)
    all_to_all x1, starting transfers between devices, local(): lax.all_to_all(message, 'rows', split_axis=0, concat_axis=0, tiled=True)  7.26 us
    all_to_all x1, waiting for transfers between devices, local(): lax.all_to_all(message, 'rows', split_axis=0, concat_axis=0, tiled=True)  3.66 us
    pallas_call x1, Pallas kernels, local(): pl.pallas_call(functools.partial(update_kernel, bag_count, lines, groups,...  3.37 us
    all_to_all x1, starting transfers between devices, local(): lax.all_to_all(partial_pooled, 'rows', split_axis=0, concat_axis=0, tiled...  3.33 us
    pallas_call x1, Pallas kernels, local(): pl.pallas_call(prepare_kernel, grid=(steps,), out_shape=[pltpu.VMEM((rows...  2.49 us
    all_to_all x1, waiting for transfers between devices, local(): lax.all_to_all(partial_pooled, 'rows', split_axis=0, concat_axis=0, tiled...  2.47 us
    pallas_call x1, Pallas kernels, local(): pl.pallas_call(functools.partial(pool_kernel, bag_count, lines), out_shap...  2.32 us
    unnamed x6, local copies, waits for them, and re-layouts  2.19 us
  transfers between devices with their start and end apart: 5, of which 4 were waited for; matrix products, arithmetic and copies ran while one was open for 0% of the time, Pallas kernels for 18%

profile of v7, /device:TPU:0, one launch (start us, length us, event | category | flops | bytes accessed | tf_op | source)
XLA Modules:
  0.0 32.5 jit_solution(10376806579632150652)
XLA Ops:
  0.6 1.5 %pack.1 = f32[8,24,128]{2,1,0:T(8,128)} custom-call(s32[4,128]{1,0:T(4,128)} %bitcast.12, s32[4,128]{1,0:T(4,128)} %bitcast.13, s32[4,128]{1,0:T(4,128)} %bitcast.14, s32[4,128]{1,0:T(4,128)} %bitcast.15, s32[4,128]{1,0:T(4,128)} %bitcast.16, s32[4,128]{1,0:T(4,128)} %bitcast.17, f32[4,256]{1,0:T(4,128)} %bitcast.11), custom_call_target="tpu_custom_call" | custom-call | tf_op jit(solution)/shard_map/pack/pallas_call | solution.py:208
  2.1 7.3 %all-to-all-start = ((f32[8,24,128]{2,1,0:T(8,128)}), f32[8,24,128]{2,1,0:T(8,128)S(1)}, u32[]{:S(2)}, u32[]{:S(2)}) async-start(f32[8,24,128]{2,1,0:T(8,128)} %pack.1), calls=%async_computation | async-start | bytes 196608 | tf_op jit(solution)/shard_map/all_to_all | solution.py:221
  9.4 2.5 %prepare.1 = (bf16[2048,256]{1,0:T(8,128)(2,1)S(1)}, bf16[2048,256]{1,0:T(8,128)(2,1)S(1)}) custom-call(f32[2048,256]{1,0:T(8,128)} %table.3), custom_call_target="tpu_custom_call" | custom-call | flops 2097152 | bytes 4194304 | tf_op jit(solution)/shard_map/prepare/pallas_call | solution.py:225
  11.9 0.0 copy-start
  11.9 1.0 %copy-done = bf16[2048,256]{1,0:T(8,128)(2,1)} copy-done((bf16[2048,256]{1,0:T(8,128)(2,1)}, bf16[2048,256]{1,0:T(8,128)(2,1)S(1)}, u32[]{:S(2)}) %copy-start) | copy-done | bytes 1048600
  12.9 3.7 %all-to-all-done.msg = f32[8,24,128]{2,1,0:T(8,128)S(1)} async-done(((f32[8,24,128]{2,1,0:T(8,128)}), f32[8,24,128]{2,1,0:T(8,128)S(1)}, u32[]{:S(2)}, u32[]{:S(2)}) %all-to-all-start) | async-done | bytes 98336 | tf_op jit(solution)/shard_map/all_to_all | solution.py:221
  16.5 0.0 copy-start.1
  16.5 1.2 %copy-done.1 = bf16[2048,256]{1,0:T(8,128)(2,1)S(1)} copy-done((bf16[2048,256]{1,0:T(8,128)(2,1)S(1)}, bf16[2048,256]{1,0:T(8,128)(2,1)}, u32[]{:S(2)}) %copy-start.1) | copy-done | bytes 1048600
  17.7 0.0 copy-start.2
  17.7 2.3 %pool.1 = (f32[8,4,256]{2,1,0:T(4,128)}, f32[8,16,128]{2,1,0:T(8,128)S(1)}, f32[2048,256]{1,0:T(8,128)S(1)}) custom-call(f32[8,24,128]{2,1,0:T(8,128)S(1)} %all-to-all-done.msg, bf16[2048,256]{1,0:T(8,128)(2,1)S(1)} %get-tuple-element.12.high, bf16[2048,256]{1,0:T(8,128)(2,1)S(1)} %copy-done.1, f32[2048,256]{1,0:T(8,128)} %table.3), custom_call_target="tpu_custom_call" | custom-call | flops 67108864 | bytes 2097152 | tf_op jit(solution)/shard_map/pool/pallas_call | solution.py:241
  20.1 0.1 collective-permute-start.2
  20.1 1.6 %collective-permute-start.1 = (f32[8,16,128]{2,1,0:T(8,128)S(1)}, f32[8,16,128]{2,1,0:T(8,128)S(1)}, u32[]{:S(2)}, u32[]{:S(2)}) collective-permute-start(f32[8,16,128]{2,1,0:T(8,128)S(1)} %get-tuple-element.15.refs_0_), channel_id=1, source_target_pairs={{0,16},{8,24},{16,0},{24,8},{1,17},{9,25},{17,1},{25,9},{2,18},{10... | collective-permute-start | bytes 196616 | tf_op jit(solution)/shard_map/ppermute | solution.py:183
  21.7 0.2 collective-permute-start
  21.9 3.3 %all-to-all-start.1 = ((f32[8,4,256]{2,1,0:T(4,128)}), f32[8,4,256]{2,1,0:T(4,128)S(1)}, u32[]{:S(2)}, u32[]{:S(2)}) async-start(f32[8,4,256]{2,1,0:T(4,128)} %get-tuple-element.14), calls=%async_computation.1 | async-start | bytes 65536 | tf_op jit(solution)/shard_map/all_to_all | solution.py:262
  25.2 0.0 collective-permute-done.2.refs_3_
  25.2 0.6 %collective-permute-done.1.refs_2_ = f32[8,16,128]{2,1,0:T(8,128)S(1)} collective-permute-done((f32[8,16,128]{2,1,0:T(8,128)S(1)}, f32[8,16,128]{2,1,0:T(8,128)S(1)}, u32[]{:S(2)}, u32[]{:S(2)}) %collective-permute-start.1) | collective-permute-done | bytes 65568 | tf_op jit(solution)/shard_map/ppermute | solution.py:183
  25.8 0.2 collective-permute-done.refs_1_
  26.0 0.0 copy-done.2
  26.0 3.4 %update.1 = (f32[2048,256]{1,0:T(8,128)}, f32[16,128]{1,0:T(8,128)S(1)}) custom-call(f32[8,16,128]{2,1,0:T(8,128)S(1)} %get-tuple-element.15.refs_0_, f32[8,16,128]{2,1,0:T(8,128)S(1)} %collective-permute-done.refs_1_, f32[8,16,128]{2,1,0:T(8,128)S(1)} %collective-permute-done.1.refs_2_, f32[8,16,128]{2,1,0:T(8,128)S(1)} %collective-permute-done.2.refs_3_, ...), custom_call_target="tpu_custom_call" | custom-call | flops 1 | bytes 1048576 | tf_op jit(solution)/shard_map/update/pallas_call | solution.py:268
  29.4 2.5 %all-to-all-done.1.returned = f32[8,4,256]{2,1,0:T(4,128)S(1)} async-done(((f32[8,4,256]{2,1,0:T(4,128)}), f32[8,4,256]{2,1,0:T(4,128)S(1)}, u32[]{:S(2)}, u32[]{:S(2)}) %all-to-all-start.1) | async-done | bytes 32800 | tf_op jit(solution)/shard_map/all_to_all | solution.py:262
  31.8 0.6 %finish.1 = (f32[4,256]{1,0:T(4,128)}, f32[16,128]{1,0:T(8,128)}) custom-call(f32[8,4,256]{2,1,0:T(4,128)S(1)} %all-to-all-done.1.returned, f32[16,128]{1,0:T(8,128)S(1)} %get-tuple-element.17.accum), custom_call_target="tpu_custom_call" | custom-call | tf_op jit(solution)/shard_map/finish/pallas_call | solution.py:292
Async XLA Ops:
  2.1 14.4 %all-to-all-start = ((f32[8,24,128]{2,1,0:T(8,128)}), f32[8,24,128]{2,1,0:T(8,128)S(1)}, u32[]{:S(2)}, u32[]{:S(2)}) async-start(f32[8,24,128]{2,1,0:T(8,128)} %pack.1), calls=%async_computation | async-start | bytes 196608 | tf_op jit(solution)/shard_map/all_to_all | solution.py:221
  11.9 1.0 %copy-start = (bf16[2048,256]{1,0:T(8,128)(2,1)}, bf16[2048,256]{1,0:T(8,128)(2,1)S(1)}, u32[]{:S(2)}) copy-start(bf16[2048,256]{1,0:T(8,128)(2,1)S(1)} %get-tuple-element.13.low) | copy-start | bytes 3145732
  16.5 1.2 %copy-start.1 = (bf16[2048,256]{1,0:T(8,128)(2,1)S(1)}, bf16[2048,256]{1,0:T(8,128)(2,1)}, u32[]{:S(2)}) copy-start(bf16[2048,256]{1,0:T(8,128)(2,1)} %copy-done) | copy-start | bytes 3145732
  17.7 8.3 %copy-start.2 = (f32[2048]{0:T(1024)S(1)}, f32[2048]{0:T(1024)}, u32[]{:S(2)}) copy-start(f32[2048]{0:T(1024)} %param.10) | copy-start | bytes 24580
  20.1 5.2 %collective-permute-start.2 = (f32[8,16,128]{2,1,0:T(8,128)S(1)}, f32[8,16,128]{2,1,0:T(8,128)S(1)}, u32[]{:S(2)}, u32[]{:S(2)}) collective-permute-start(f32[8,16,128]{2,1,0:T(8,128)S(1)} %get-tuple-element.15.refs_0_), channel_id=1, source_target_pairs={{0,24},{8,0},{16,8},{24,16},{1,25},{9,1},{17,9},{25,17},{2,26},{10... | collective-permute-start | bytes 196616 | tf_op jit(solution)/shard_map/ppermute | solution.py:183
  20.1 5.7 %collective-permute-start.1 = (f32[8,16,128]{2,1,0:T(8,128)S(1)}, f32[8,16,128]{2,1,0:T(8,128)S(1)}, u32[]{:S(2)}, u32[]{:S(2)}) collective-permute-start(f32[8,16,128]{2,1,0:T(8,128)S(1)} %get-tuple-element.15.refs_0_), channel_id=1, source_target_pairs={{0,16},{8,24},{16,0},{24,8},{1,17},{9,25},{17,1},{25,9},{2,18},{10... | collective-permute-start | bytes 196616 | tf_op jit(solution)/shard_map/ppermute | solution.py:183
  21.7 4.3 %collective-permute-start = (f32[8,16,128]{2,1,0:T(8,128)S(1)}, f32[8,16,128]{2,1,0:T(8,128)S(1)}, u32[]{:S(2)}, u32[]{:S(2)}) collective-permute-start(f32[8,16,128]{2,1,0:T(8,128)S(1)} %get-tuple-element.15.refs_0_), channel_id=1, source_target_pairs={{0,8},{8,16},{16,24},{24,0},{1,9},{9,17},{17,25},{25,1},{2,10},{10... | collective-permute-start | bytes 196616 | tf_op jit(solution)/shard_map/ppermute | solution.py:183
  21.9 10.0 %all-to-all-start.1 = ((f32[8,4,256]{2,1,0:T(4,128)}), f32[8,4,256]{2,1,0:T(4,128)S(1)}, u32[]{:S(2)}, u32[]{:S(2)}) async-start(f32[8,4,256]{2,1,0:T(4,128)} %get-tuple-element.14), calls=%async_computation.1 | async-start | bytes 65536 | tf_op jit(solution)/shard_map/all_to_all | solution.py:262

commit v8 on v7

--- a/solution.py
+++ b/solution.py
@@ -42,10 +42,18 @@
     return high, (x - high.astype(jnp.float32)).astype(jnp.bfloat16)
 
 
-def prepare_kernel(table, high, low):
-    rows = table.shape[0]
-    here = pl.ds(pl.multiple_of(pl.program_id(0) * rows, rows), rows)
-    high[here, :], low[here, :] = split_two(table[...])
+def prepare_kernel(table, kept, sems):
+    pieces = sems.shape[0]
+    rows = table.shape[0] // pieces
+    copies = [
+        pltpu.make_async_copy(
+            table.at[pl.ds(i * rows, rows), :], kept.at[pl.ds(i * rows, rows), :], sems.at[i])
+        for i in range(pieces)
+    ]
+    for copy in copies:
+        copy.start()
+    for copy in copies:
+        copy.wait()
 
 
 def codes(ids, bags, bag_count, base):
@@ -75,13 +83,8 @@
             blocks, bag_count, LANES)
 
 
-def pool_kernel(
-    bag_count, lines, msg, high, low, table, out, joined, kept,
-    code_ref, lane_ref, counts, sem,
-):
-    fetch = pltpu.make_async_copy(table, kept, sem)
-    fetch.start()
-    rows_dev, width = high.shape
+def pool_kernel(bag_count, lines, msg, table, out, joined, code_ref, lane_ref, counts):
+    rows_dev, width = table.shape
     owners = msg.shape[0]
     base = lax.axis_index("rows") * rows_dev
     code_ref[...], lane_ref[...] = codes(
@@ -92,10 +95,9 @@
     flat = jnp.concatenate(
         [counts[h].astype(jnp.bfloat16) for h in range(blocks)], axis=1)
     total = jnp.zeros((owners * bag_count, width), jnp.float32)
-    for part in (high, low):
-        total += jnp.dot(flat, part[...], preferred_element_type=jnp.float32)
+    for part in split_two(table[...]):
+        total += jnp.dot(flat, part, preferred_element_type=jnp.float32)
     out[...] = total.reshape(out.shape)
-    fetch.wait()
 
 
 def update_kernel(bag_count, lines, groups, chunk, *refs):
@@ -220,51 +222,43 @@
     )])
     gathered = lax.all_to_all(message, "rows", split_axis=0, concat_axis=0, tiled=True)
 
-    steps = 4
-    step_rows = rows_dev // steps
-    high, low = pl.pallas_call(
+    pieces = 4
+    kept = pl.pallas_call(
         prepare_kernel,
-        grid=(steps,),
-        out_shape=[
-            pltpu.VMEM((rows_dev, width), jnp.bfloat16),
-            pltpu.VMEM((rows_dev, width), jnp.bfloat16),
-        ],
-        in_specs=[pl.BlockSpec((step_rows, width), lambda i: (i, 0))],
-        out_specs=[vmem] * 2,
+        out_shape=pltpu.VMEM((rows_dev, width), jnp.float32),
+        in_specs=[hbm],
+        out_specs=vmem,
+        scratch_shapes=[pltpu.SemaphoreType.DMA((pieces,))],
         compiler_params=params,
         cost_estimate=pl.CostEstimate(
-            flops=4 * rows_dev * width, bytes_accessed=2 * rows_dev * width * 4,
-            transcendentals=0),
+            flops=0, bytes_accessed=2 * rows_dev * width * 4, transcendentals=0),
         name="prepare",
     )(stay(item_table))
 
-    partial_pooled, joined, kept = pl.pallas_call(
+    partial_pooled, joined = pl.pallas_call(
         functools.partial(pool_kernel, bag_count, lines),
         out_shape=(
             pltpu.VMEM((owners, bag_count, width), jnp.float32),
             pltpu.VMEM((owners, prev_length, LANES), jnp.float32),
-            pltpu.VMEM((rows_dev, width), jnp.float32),
         ),
-        in_specs=[vmem] * 3 + [hbm],
-        out_specs=[vmem] * 3,
+        in_specs=[vmem] * 2,
+        out_specs=[vmem] * 2,
         scratch_shapes=[
             pltpu.VMEM((owners, lines, LANES), jnp.float32),
             pltpu.VMEM((owners, lines, LANES), jnp.float32),
             pltpu.VMEM((blocks, owners * bag_count, LANES), jnp.float32),
-            pltpu.SemaphoreType.DMA,
         ],
         compiler_params=params,
         cost_estimate=pl.CostEstimate(
             flops=4 * owners * bag_count * rows_dev * width,
             bytes_accessed=rows_dev * width * 4, transcendentals=0),
         name="pool",
-    )(gathered, high, low, stay(item_table))
+    )(gathered, kept)
     returned = lax.all_to_all(
         partial_pooled, "rows", split_axis=0, concat_axis=0, tiled=True)
     all_groups = [joined] + [shift(joined, "dp", k) for k in range(1, groups)]
 
     segments = chunk * bag_count
-    pieces = 4
     new_table, new_accum = pl.pallas_call(
         functools.partial(update_kernel, bag_count, lines, groups, chunk),
         out_shape=(

time: 32.9 us -> 31.1 us (0.945)
  local copies, waits for them, and re-layouts: 2.19 us -> 0.01 us
  waiting for transfers between devices: 6.89 us -> 8.78 us
  Pallas kernels: 10.3 us -> 8.92 us
    unnamed x6 -> x2, local copies, waits for them, and re-layouts: 2.19 us -> 0.01 us
    all_to_all x1, waiting for transfers between devices: 3.66 us -> 5.56 us  [local(): lax.all_to_all(message, 'rows', split_axis=0, concat_axis=0, tiled=True)]
    pallas_call x1, Pallas kernels: 2.49 us -> 1.55 us  [local(): pl.pallas_call(prepare_kernel, out_shape=pltpu.VMEM((rows_dev, width), jn...]
    pallas_call x1, Pallas kernels: 2.32 us -> 1.89 us  [local(): pl.pallas_call(functools.partial(pool_kernel, bag_count, lines), out_shap...]
  transfers between devices with their start and end apart: 5 -> 5, of which waited for: 4 -> 4; matrix products, arithmetic and copies ran while one was open for 0% -> 0% of each run, Pallas kernels for 18% -> 16%
where the time goes in v8:
time: 31.1 us; the launch traced here: 30.7 us
  starting transfers between devices  12.3 us (40%)
  Pallas kernels  8.92 us (29%)
  waiting for transfers between devices  8.78 us (28%)
  between operations  0.69 us (2%)
    all_to_all x1, starting transfers between devices, local(): lax.all_to_all(message, 'rows', split_axis=0, concat_axis=0, tiled=True)  7.26 us
    all_to_all x1, waiting for transfers between devices, local(): lax.all_to_all(message, 'rows', split_axis=0, concat_axis=0, tiled=True)  5.56 us
    pallas_call x1, Pallas kernels, local(): pl.pallas_call(functools.partial(update_kernel, bag_count, lines, groups,...  3.37 us
    all_to_all x1, starting transfers between devices, local(): lax.all_to_all(partial_pooled, 'rows', split_axis=0, concat_axis=0, tiled...  3.33 us
    all_to_all x1, waiting for transfers between devices, local(): lax.all_to_all(partial_pooled, 'rows', split_axis=0, concat_axis=0, tiled...  2.46 us
    pallas_call x1, Pallas kernels, local(): pl.pallas_call(functools.partial(pool_kernel, bag_count, lines), out_shap...  1.89 us
    ppermute x3, starting transfers between devices, shift(): return lax.ppermute(x, axis, [(i, (i + step) % size) for i in range(size)])  1.75 us
    pallas_call x1, Pallas kernels, local(): pl.pallas_call(prepare_kernel, out_shape=pltpu.VMEM((rows_dev, width), jn...  1.55 us
  transfers between devices with their start and end apart: 5, of which 4 were waited for; matrix products, arithmetic and copies ran while one was open for 0% of the time, Pallas kernels for 16%

profile of v8, /device:TPU:0, one launch (start us, length us, event | category | flops | bytes accessed | tf_op | source)
XLA Modules:
  0.0 30.7 jit_solution(17854035408585994946)
XLA Ops:
  0.6 1.5 %pack.1 = f32[8,24,128]{2,1,0:T(8,128)} custom-call(s32[4,128]{1,0:T(4,128)} %bitcast.12, s32[4,128]{1,0:T(4,128)} %bitcast.13, s32[4,128]{1,0:T(4,128)} %bitcast.14, s32[4,128]{1,0:T(4,128)} %bitcast.15, s32[4,128]{1,0:T(4,128)} %bitcast.16, s32[4,128]{1,0:T(4,128)} %bitcast.17, f32[4,256]{1,0:T(4,128)} %bitcast.11), custom_call_target="tpu_custom_call" | custom-call | tf_op jit(solution)/shard_map/pack/pallas_call | solution.py:210
  2.1 7.3 %all-to-all-start = ((f32[8,24,128]{2,1,0:T(8,128)}), f32[8,24,128]{2,1,0:T(8,128)S(1)}, u32[]{:S(2)}, u32[]{:S(2)}) async-start(f32[8,24,128]{2,1,0:T(8,128)} %pack.1), calls=%async_computation | async-start | bytes 196608 | tf_op jit(solution)/shard_map/all_to_all | solution.py:223
  9.4 1.5 %prepare.1.table.refs_4_ = f32[2048,256]{1,0:T(8,128)S(1)} custom-call(f32[2048,256]{1,0:T(8,128)} %table.1), custom_call_target="tpu_custom_call" | custom-call | bytes 4194304 | tf_op jit(solution)/shard_map/prepare/pallas_call | solution.py:226
  11.0 0.0 copy-start
  11.0 5.6 %all-to-all-done.msg = f32[8,24,128]{2,1,0:T(8,128)S(1)} async-done(((f32[8,24,128]{2,1,0:T(8,128)}), f32[8,24,128]{2,1,0:T(8,128)S(1)}, u32[]{:S(2)}, u32[]{:S(2)}) %all-to-all-start) | async-done | bytes 98336 | tf_op jit(solution)/shard_map/all_to_all | solution.py:223
  16.5 1.9 %pool.1 = (f32[8,4,256]{2,1,0:T(4,128)}, f32[8,16,128]{2,1,0:T(8,128)S(1)}) custom-call(f32[8,24,128]{2,1,0:T(8,128)S(1)} %all-to-all-done.msg, f32[2048,256]{1,0:T(8,128)S(1)} %prepare.1.table.refs_4_), custom_call_target="tpu_custom_call" | custom-call | flops 67108864 | bytes 2097152 | tf_op jit(solution)/shard_map/pool/pallas_call | solution.py:238
  18.4 0.0 collective-permute-start.2
  18.4 1.5 %collective-permute-start.1 = (f32[8,16,128]{2,1,0:T(8,128)S(1)}, f32[8,16,128]{2,1,0:T(8,128)S(1)}, u32[]{:S(2)}, u32[]{:S(2)}) collective-permute-start(f32[8,16,128]{2,1,0:T(8,128)S(1)} %get-tuple-element.10.refs_0_), channel_id=1, source_target_pairs={{0,16},{8,24},{16,0},{24,8},{1,17},{9,25},{17,1},{25,9},{2,18},{10... | collective-permute-start | bytes 196616 | tf_op jit(solution)/shard_map/ppermute | solution.py:185
  19.9 0.2 collective-permute-start
  20.2 3.3 %all-to-all-start.1 = ((f32[8,4,256]{2,1,0:T(4,128)}), f32[8,4,256]{2,1,0:T(4,128)S(1)}, u32[]{:S(2)}, u32[]{:S(2)}) async-start(f32[8,4,256]{2,1,0:T(4,128)} %get-tuple-element.9), calls=%async_computation.1 | async-start | bytes 65536 | tf_op jit(solution)/shard_map/all_to_all | solution.py:257
  23.5 0.0 collective-permute-done.2.refs_3_
  23.5 0.7 %collective-permute-done.1.refs_2_ = f32[8,16,128]{2,1,0:T(8,128)S(1)} collective-permute-done((f32[8,16,128]{2,1,0:T(8,128)S(1)}, f32[8,16,128]{2,1,0:T(8,128)S(1)}, u32[]{:S(2)}, u32[]{:S(2)}) %collective-permute-start.1) | collective-permute-done | bytes 65568 | tf_op jit(solution)/shard_map/ppermute | solution.py:185
  24.2 0.1 collective-permute-done.refs_1_
  24.3 0.0 copy-done
  24.3 3.4 %update.1 = (f32[2048,256]{1,0:T(8,128)}, f32[16,128]{1,0:T(8,128)S(1)}) custom-call(f32[8,16,128]{2,1,0:T(8,128)S(1)} %get-tuple-element.10.refs_0_, f32[8,16,128]{2,1,0:T(8,128)S(1)} %collective-permute-done.refs_1_, f32[8,16,128]{2,1,0:T(8,128)S(1)} %collective-permute-done.1.refs_2_, f32[8,16,128]{2,1,0:T(8,128)S(1)} %collective-permute-done.2.refs_3_, ...), custom_call_target="tpu_custom_call" | custom-call | flops 1 | bytes 1048576 | tf_op jit(solution)/shard_map/update/pallas_call | solution.py:262
  27.7 2.5 %all-to-all-done.1.returned = f32[8,4,256]{2,1,0:T(4,128)S(1)} async-done(((f32[8,4,256]{2,1,0:T(4,128)}), f32[8,4,256]{2,1,0:T(4,128)S(1)}, u32[]{:S(2)}, u32[]{:S(2)}) %all-to-all-start.1) | async-done | bytes 32800 | tf_op jit(solution)/shard_map/all_to_all | solution.py:257
  30.1 0.6 %finish.1 = (f32[4,256]{1,0:T(4,128)}, f32[16,128]{1,0:T(8,128)}) custom-call(f32[8,4,256]{2,1,0:T(4,128)S(1)} %all-to-all-done.1.returned, f32[16,128]{1,0:T(8,128)S(1)} %get-tuple-element.11.accum), custom_call_target="tpu_custom_call" | custom-call | tf_op jit(solution)/shard_map/finish/pallas_call | solution.py:286
Async XLA Ops:
  2.1 14.4 %all-to-all-start = ((f32[8,24,128]{2,1,0:T(8,128)}), f32[8,24,128]{2,1,0:T(8,128)S(1)}, u32[]{:S(2)}, u32[]{:S(2)}) async-start(f32[8,24,128]{2,1,0:T(8,128)} %pack.1), calls=%async_computation | async-start | bytes 196608 | tf_op jit(solution)/shard_map/all_to_all | solution.py:223
  11.0 13.3 %copy-start = (f32[2048]{0:T(1024)S(1)}, f32[2048]{0:T(1024)}, u32[]{:S(2)}) copy-start(f32[2048]{0:T(1024)} %param.10) | copy-start | bytes 24580
  18.4 5.1 %collective-permute-start.2 = (f32[8,16,128]{2,1,0:T(8,128)S(1)}, f32[8,16,128]{2,1,0:T(8,128)S(1)}, u32[]{:S(2)}, u32[]{:S(2)}) collective-permute-start(f32[8,16,128]{2,1,0:T(8,128)S(1)} %get-tuple-element.10.refs_0_), channel_id=1, source_target_pairs={{0,24},{8,0},{16,8},{24,16},{1,25},{9,1},{17,9},{25,17},{2,26},{10... | collective-permute-start | bytes 196616 | tf_op jit(solution)/shard_map/ppermute | solution.py:185
  18.4 5.8 %collective-permute-start.1 = (f32[8,16,128]{2,1,0:T(8,128)S(1)}, f32[8,16,128]{2,1,0:T(8,128)S(1)}, u32[]{:S(2)}, u32[]{:S(2)}) collective-permute-start(f32[8,16,128]{2,1,0:T(8,128)S(1)} %get-tuple-element.10.refs_0_), channel_id=1, source_target_pairs={{0,16},{8,24},{16,0},{24,8},{1,17},{9,25},{17,1},{25,9},{2,18},{10... | collective-permute-start | bytes 196616 | tf_op jit(solution)/shard_map/ppermute | solution.py:185
  19.9 4.3 %collective-permute-start = (f32[8,16,128]{2,1,0:T(8,128)S(1)}, f32[8,16,128]{2,1,0:T(8,128)S(1)}, u32[]{:S(2)}, u32[]{:S(2)}) collective-permute-start(f32[8,16,128]{2,1,0:T(8,128)S(1)} %get-tuple-element.10.refs_0_), channel_id=1, source_target_pairs={{0,8},{8,16},{16,24},{24,0},{1,9},{9,17},{17,25},{25,1},{2,10},{10... | collective-permute-start | bytes 196616 | tf_op jit(solution)/shard_map/ppermute | solution.py:185
  20.2 10.0 %all-to-all-start.1 = ((f32[8,4,256]{2,1,0:T(4,128)}), f32[8,4,256]{2,1,0:T(4,128)S(1)}, u32[]{:S(2)}, u32[]{:S(2)}) async-start(f32[8,4,256]{2,1,0:T(4,128)} %get-tuple-element.9), calls=%async_computation.1 | async-start | bytes 65536 | tf_op jit(solution)/shard_map/all_to_all | solution.py:257

commit v9 on v8

--- a/solution.py
+++ b/solution.py
@@ -83,7 +83,10 @@
             blocks, bag_count, LANES)
 
 
-def pool_kernel(bag_count, lines, msg, table, out, joined, code_ref, lane_ref, counts):
+def pool_kernel(
+    bag_count, lines, msg, table, out, joined, go, code_ref, lane_ref, counts,
+):
+    go[0, 0] = 1
     rows_dev, width = table.shape
     owners = msg.shape[0]
     base = lax.axis_index("rows") * rows_dev
@@ -172,6 +175,13 @@
         copy.wait()
 
 
+def pass_kernel(table, accum, new_table, new_accum, sem):
+    copy = pltpu.make_async_copy(table, new_table, sem)
+    copy.start()
+    new_accum[...] = accum[...]
+    copy.wait()
+
+
 def finish_kernel(returned, accum, pooled, new_accum):
     total = returned[0]
     for i in range(1, returned.shape[0]):
@@ -235,14 +245,15 @@
         name="prepare",
     )(stay(item_table))
 
-    partial_pooled, joined = pl.pallas_call(
+    partial_pooled, joined, go = pl.pallas_call(
         functools.partial(pool_kernel, bag_count, lines),
         out_shape=(
             pltpu.VMEM((owners, bag_count, width), jnp.float32),
             pltpu.VMEM((owners, prev_length, LANES), jnp.float32),
+            jax.ShapeDtypeStruct((1, 1), jnp.int32),
         ),
         in_specs=[vmem] * 2,
-        out_specs=[vmem] * 2,
+        out_specs=[vmem] * 2 + [pl.BlockSpec(memory_space=pltpu.SMEM)],
         scratch_shapes=[
             pltpu.VMEM((owners, lines, LANES), jnp.float32),
             pltpu.VMEM((owners, lines, LANES), jnp.float32),
@@ -256,32 +267,52 @@
     )(gathered, kept)
     returned = lax.all_to_all(
         partial_pooled, "rows", split_axis=0, concat_axis=0, tiled=True)
-    all_groups = [joined] + [shift(joined, "dp", k) for k in range(1, groups)]
-
     segments = chunk * bag_count
-    new_table, new_accum = pl.pallas_call(
-        functools.partial(update_kernel, bag_count, lines, groups, chunk),
-        out_shape=(
-            jax.ShapeDtypeStruct((rows_dev, width), jnp.float32),
-            pltpu.VMEM((blocks, LANES), jnp.float32),
-        ),
-        in_specs=[vmem] * (groups + 2),
-        out_specs=(hbm, vmem),
-        scratch_shapes=[
-            pltpu.VMEM((devices, prev_length, LANES), jnp.float32),
-            pltpu.VMEM((chunk, lines, LANES), jnp.float32),
-            pltpu.VMEM((chunk, lines, LANES), jnp.float32),
-            pltpu.VMEM((blocks, segments, LANES), jnp.float32),
-            pltpu.VMEM((segments, width), jnp.float32),
-            pltpu.VMEM((blocks, LANES, width) if devices > chunk else (1, 8, LANES), jnp.float32),
-            pltpu.VMEM((rows_dev, width), jnp.float32),
-            pltpu.SemaphoreType.DMA((pieces,)),
-        ],
-        compiler_params=params if devices == chunk else pltpu.CompilerParams(
-            vmem_limit_bytes=40 * 1024 * 1024),
-        cost_estimate=pl.CostEstimate(flops=1, bytes_accessed=1 << 20, transcendentals=0),
-        name="update",
-    )(*all_groups, kept, row_accum.reshape(blocks, LANES))
+
+    def forward_and_update(joined, kept, row_accum):
+        all_groups = [joined] + [shift(joined, "dp", k) for k in range(1, groups)]
+
+        return pl.pallas_call(
+            functools.partial(update_kernel, bag_count, lines, groups, chunk),
+            out_shape=(
+                pltpu.HBM((rows_dev, width), jnp.float32),
+                pltpu.VMEM((blocks, LANES), jnp.float32),
+            ),
+            in_specs=[vmem] * (groups + 2),
+            out_specs=(hbm, vmem),
+            scratch_shapes=[
+                pltpu.VMEM((devices, prev_length, LANES), jnp.float32),
+                pltpu.VMEM((chunk, lines, LANES), jnp.float32),
+                pltpu.VMEM((chunk, lines, LANES), jnp.float32),
+                pltpu.VMEM((blocks, segments, LANES), jnp.float32),
+                pltpu.VMEM((segments, width), jnp.float32),
+                pltpu.VMEM((blocks, LANES, width) if devices > chunk else (1, 8, LANES), jnp.float32),
+                pltpu.VMEM((rows_dev, width), jnp.float32),
+                pltpu.SemaphoreType.DMA((pieces,)),
+            ],
+            compiler_params=params if devices == chunk else pltpu.CompilerParams(
+                vmem_limit_bytes=40 * 1024 * 1024),
+            cost_estimate=pl.CostEstimate(flops=1, bytes_accessed=1 << 20, transcendentals=0),
+            name="update",
+        )(*all_groups, kept, row_accum)
+
+    def skip(joined, kept, row_accum):
+        return pl.pallas_call(
+            pass_kernel,
+            out_shape=(
+                pltpu.HBM((rows_dev, width), jnp.float32),
+                pltpu.VMEM((blocks, LANES), jnp.float32),
+            ),
+            in_specs=[vmem] * 2,
+            out_specs=(hbm, vmem),
+            scratch_shapes=[pltpu.SemaphoreType.DMA],
+            compiler_params=params,
+            name="pass",
+        )(kept, row_accum)
+
+    new_table, new_accum = lax.cond(
+        go[0, 0] > 0, forward_and_update, skip,
+        joined, kept, row_accum.reshape(blocks, LANES))
 
     pooled, new_accum = pl.pallas_call(
         finish_kernel,

time: 31.1 us -> 32.7 us (1.051)
  waiting for transfers between devices: 8.78 us -> 9.66 us
  between operations: 0.69 us -> 1.35 us
    ppermute x3, waiting for transfers between devices: 0.77 us -> 4.11 us  [shift(): return lax.ppermute(x, axis, [(i, (i + step) % size) for i in range(size)])]
    all_to_all x1, waiting for transfers between devices: 2.46 us -> 0.01 us  [local(): lax.all_to_all(partial_pooled, 'rows', split_axis=0, concat_axis=0, tiled...]
  transfers between devices with their start and end apart: 5 -> 5, of which waited for: 4 -> 4; matrix products, arithmetic and copies ran while one was open for 0% -> 0% of each run, Pallas kernels for 16% -> 15%
where the time goes in v9:
time: 32.7 us; the launch traced here: 32.4 us
  starting transfers between devices  12.4 us (38%)
  waiting for transfers between devices  9.66 us (30%)
  Pallas kernels  8.91 us (27%)
  between operations  1.35 us (4%)
    all_to_all x1, starting transfers between devices, local(): lax.all_to_all(message, 'rows', split_axis=0, concat_axis=0, tiled=True)  7.26 us
    all_to_all x1, waiting for transfers between devices, local(): lax.all_to_all(message, 'rows', split_axis=0, concat_axis=0, tiled=True)  5.56 us
    ppermute x3, waiting for transfers between devices, shift(): return lax.ppermute(x, axis, [(i, (i + step) % size) for i in range(size)])  4.11 us
    pallas_call x1, Pallas kernels, forward_and_update(): pl.pallas_call(functools.partial(update_kernel, bag_count, lines, groups,...  3.37 us
    all_to_all x1, starting transfers between devices, local(): lax.all_to_all(partial_pooled, 'rows', split_axis=0, concat_axis=0, tiled...  3.34 us
    pallas_call x1, Pallas kernels, local(): pl.pallas_call(functools.partial(pool_kernel, bag_count, lines), out_shap...  1.89 us
    ppermute x3, starting transfers between devices, shift(): return lax.ppermute(x, axis, [(i, (i + step) % size) for i in range(size)])  1.81 us
    pallas_call x1, Pallas kernels, local(): pl.pallas_call(prepare_kernel, out_shape=pltpu.VMEM((rows_dev, width), jn...  1.55 us
  transfers between devices with their start and end apart: 5, of which 4 were waited for; matrix products, arithmetic and copies ran while one was open for 0% of the time, Pallas kernels for 15%

profile of v9, /device:TPU:0, one launch (start us, length us, event | category | flops | bytes accessed | tf_op | source)
XLA Modules:
  0.0 32.4 jit_solution(1609064397593205546)
XLA Ops:
  0.6 1.5 %pack.1 = f32[8,24,128]{2,1,0:T(8,128)} custom-call(s32[4,128]{1,0:T(4,128)} %bitcast.14, s32[4,128]{1,0:T(4,128)} %bitcast.15, s32[4,128]{1,0:T(4,128)} %bitcast.16, s32[4,128]{1,0:T(4,128)} %bitcast.17, s32[4,128]{1,0:T(4,128)} %bitcast.18, s32[4,128]{1,0:T(4,128)} %bitcast.19, f32[4,256]{1,0:T(4,128)} %bitcast.13), custom_call_target="tpu_custom_call" | custom-call | tf_op jit(solution)/shard_map/pack/pallas_call | solution.py:220
  2.1 7.3 %all-to-all-start = ((f32[8,24,128]{2,1,0:T(8,128)}), f32[8,24,128]{2,1,0:T(8,128)S(1)}, u32[]{:S(2)}, u32[]{:S(2)}) async-start(f32[8,24,128]{2,1,0:T(8,128)} %pack.1), calls=%async_computation | async-start | bytes 196608 | tf_op jit(solution)/shard_map/all_to_all | solution.py:233
  9.4 1.5 %prepare.1.table = f32[2048,256]{1,0:T(8,128)S(1)} custom-call(f32[2048,256]{1,0:T(8,128)} %table.1), custom_call_target="tpu_custom_call" | custom-call | bytes 4194304 | tf_op jit(solution)/shard_map/prepare/pallas_call | solution.py:236
  11.0 0.0 copy-start
  11.0 5.6 %all-to-all-done.msg = f32[8,24,128]{2,1,0:T(8,128)S(1)} async-done(((f32[8,24,128]{2,1,0:T(8,128)}), f32[8,24,128]{2,1,0:T(8,128)S(1)}, u32[]{:S(2)}, u32[]{:S(2)}) %all-to-all-start) | async-done | bytes 98336 | tf_op jit(solution)/shard_map/all_to_all | solution.py:233
  16.5 1.9 %pool.1 = (f32[8,4,256]{2,1,0:T(4,128)}, f32[8,16,128]{2,1,0:T(8,128)S(1)}, s32[1,1]{1,0:T(1,128)}) custom-call(f32[8,24,128]{2,1,0:T(8,128)S(1)} %all-to-all-done.msg, f32[2048,256]{1,0:T(8,128)S(1)} %prepare.1.table), custom_call_target="tpu_custom_call" | custom-call | flops 67108864 | bytes 2097152 | tf_op jit(solution)/shard_map/pool/pallas_call | solution.py:248
  18.4 3.3 %all-to-all-start.1 = ((f32[8,4,256]{2,1,0:T(4,128)}), f32[8,4,256]{2,1,0:T(4,128)S(1)}, u32[]{:S(2)}, u32[]{:S(2)}) async-start(f32[8,4,256]{2,1,0:T(4,128)} %get-tuple-element.25), calls=%async_computation.1 | async-start | bytes 65536 | tf_op jit(solution)/shard_map/all_to_all | solution.py:268
  22.4 0.0 copy-done
  22.4 9.3 %conditional.1 = ((f32[2048,256]{1,0:T(8,128)}, f32[16,128]{1,0:T(8,128)S(1)})) conditional(s32[]{:T(128)} %bitcast.7, (f32[2048,256]{1,0:T(8,128)S(1)}, f32[16,128]{1,0:T(8,128)S(1)}) %tuple.21, (f32[8,16,128]{2,1,0:T(8,128)S(1)}, f32[2048,256]{1,0:T(8,128)S(1)}, f32[16,128]{1,0:T(8,128)S(1)}) %tuple.22), branch_computations={%region_0.0_spmd, %region_1.0_spmd} | conditional | flops 1 | bytes 1835136 | solution.py:313
  22.5 0.1 collective-permute-start.2
  22.5 1.6 %collective-permute-start.1 = (f32[8,16,128]{2,1,0:T(8,128)S(1)}, f32[8,16,128]{2,1,0:T(8,128)S(1)}, u32[]{:S(2)}, u32[]{:S(2)}) collective-permute-start(f32[8,16,128]{2,1,0:T(8,128)S(1)} %get-tuple-element.12.refs_0_), channel_id=1, source_target_pairs={{0,16},{8,24},{16,0},{24,8},{1,17},{9,25},{17,1},{25,9},{2,18},{10... | collective-permute-start | bytes 196616 | tf_op jit(solution)/shard_map/cond/branch_1_fun/ppermute | solution.py:195
  24.1 0.2 collective-permute-start
  24.3 0.1 collective-permute-done.2.refs_3_
  24.4 3.8 %collective-permute-done.1.refs_2_ = f32[8,16,128]{2,1,0:T(8,128)S(1)} collective-permute-done((f32[8,16,128]{2,1,0:T(8,128)S(1)}, f32[8,16,128]{2,1,0:T(8,128)S(1)}, u32[]{:S(2)}, u32[]{:S(2)}) %collective-permute-start.1) | collective-permute-done | bytes 65568 | tf_op jit(solution)/shard_map/cond/branch_1_fun/ppermute | solution.py:195
  28.2 0.2 collective-permute-done.refs_1_
  28.4 3.4 %update.1 = (f32[2048,256]{1,0:T(8,128)}, f32[16,128]{1,0:T(8,128)S(1)}) custom-call(f32[8,16,128]{2,1,0:T(8,128)S(1)} %get-tuple-element.12.refs_0_, f32[8,16,128]{2,1,0:T(8,128)S(1)} %collective-permute-done.refs_1_, f32[8,16,128]{2,1,0:T(8,128)S(1)} %collective-permute-done.1.refs_2_, f32[8,16,128]{2,1,0:T(8,128)S(1)} %collective-permute-done.2.refs_3_, ...), custom_call_target="tpu_custom_call" | custom-call | flops 1 | bytes 1048576 | tf_op jit(solution)/shard_map/cond/branch_1_fun/update/pallas_call | solution.py:275
  31.8 0.0 all-to-all-done.1.returned
  31.8 0.6 %finish.1 = (f32[4,256]{1,0:T(4,128)}, f32[16,128]{1,0:T(8,128)}) custom-call(f32[8,4,256]{2,1,0:T(4,128)S(1)} %all-to-all-done.1.returned, f32[16,128]{1,0:T(8,128)S(1)} %get-tuple-element.28.accum), custom_call_target="tpu_custom_call" | custom-call | tf_op jit(solution)/shard_map/finish/pallas_call | solution.py:317
Async XLA Ops:
  2.1 14.4 %all-to-all-start = ((f32[8,24,128]{2,1,0:T(8,128)}), f32[8,24,128]{2,1,0:T(8,128)S(1)}, u32[]{:S(2)}, u32[]{:S(2)}) async-start(f32[8,24,128]{2,1,0:T(8,128)} %pack.1), calls=%async_computation | async-start | bytes 196608 | tf_op jit(solution)/shard_map/all_to_all | solution.py:233
  11.0 11.5 %copy-start = (f32[2048]{0:T(1024)S(1)}, f32[2048]{0:T(1024)}, u32[]{:S(2)}) copy-start(f32[2048]{0:T(1024)} %param.12) | copy-start | bytes 24580
  18.4 13.3 %all-to-all-start.1 = ((f32[8,4,256]{2,1,0:T(4,128)}), f32[8,4,256]{2,1,0:T(4,128)S(1)}, u32[]{:S(2)}, u32[]{:S(2)}) async-start(f32[8,4,256]{2,1,0:T(4,128)} %get-tuple-element.25), calls=%async_computation.1 | async-start | bytes 65536 | tf_op jit(solution)/shard_map/all_to_all | solution.py:268
  22.5 2.0 %collective-permute-start.2 = (f32[8,16,128]{2,1,0:T(8,128)S(1)}, f32[8,16,128]{2,1,0:T(8,128)S(1)}, u32[]{:S(2)}, u32[]{:S(2)}) collective-permute-start(f32[8,16,128]{2,1,0:T(8,128)S(1)} %get-tuple-element.12.refs_0_), channel_id=1, source_target_pairs={{0,24},{8,0},{16,8},{24,16},{1,25},{9,1},{17,9},{25,17},{2,26},{10... | collective-permute-start | bytes 196616 | tf_op jit(solution)/shard_map/cond/branch_1_fun/ppermute | solution.py:195
  22.5 5.7 %collective-permute-start.1 = (f32[8,16,128]{2,1,0:T(8,128)S(1)}, f32[8,16,128]{2,1,0:T(8,128)S(1)}, u32[]{:S(2)}, u32[]{:S(2)}) collective-permute-start(f32[8,16,128]{2,1,0:T(8,128)S(1)} %get-tuple-element.12.refs_0_), channel_id=1, source_target_pairs={{0,16},{8,24},{16,0},{24,8},{1,17},{9,25},{17,1},{25,9},{2,18},{10... | collective-permute-start | bytes 196616 | tf_op jit(solution)/shard_map/cond/branch_1_fun/ppermute | solution.py:195
  24.1 4.3 %collective-permute-start = (f32[8,16,128]{2,1,0:T(8,128)S(1)}, f32[8,16,128]{2,1,0:T(8,128)S(1)}, u32[]{:S(2)}, u32[]{:S(2)}) collective-permute-start(f32[8,16,128]{2,1,0:T(8,128)S(1)} %get-tuple-element.12.refs_0_), channel_id=1, source_target_pairs={{0,8},{8,16},{16,24},{24,0},{1,9},{9,17},{17,25},{25,1},{2,10},{10... | collective-permute-start | bytes 196616 | tf_op jit(solution)/shard_map/cond/branch_1_fun/ppermute | solution.py:195

commit v10 on v8

--- a/solution.py
+++ b/solution.py
@@ -180,6 +180,13 @@
     new_accum[...] = accum[...]
 
 
+def exchange(x, axis):
+    size = lax.axis_size(axis)
+    order = [(i + size // 2) % size for i in range(size)]
+    return lax.all_to_all(
+        x, axis, split_axis=0, concat_axis=0, axis_index_groups=[order], tiled=True)
+
+
 def shift(x, axis, step):
     size = lax.axis_size(axis)
     return lax.ppermute(x, axis, [(i, (i + step) % size) for i in range(size)])
@@ -220,7 +227,7 @@
         line(owner_map), line(row_index), line(bag_index),
         line(prev_owner), line(prev_row), line(prev_bag), grad_pooled[0, 0],
     )])
-    gathered = lax.all_to_all(message, "rows", split_axis=0, concat_axis=0, tiled=True)
+    gathered = exchange(message, "rows")
 
     pieces = 4
     kept = pl.pallas_call(
@@ -254,8 +261,7 @@
             bytes_accessed=rows_dev * width * 4, transcendentals=0),
         name="pool",
     )(gathered, kept)
-    returned = lax.all_to_all(
-        partial_pooled, "rows", split_axis=0, concat_axis=0, tiled=True)
+    returned = exchange(partial_pooled, "rows")
     all_groups = [joined] + [shift(joined, "dp", k) for k in range(1, groups)]
 
     segments = chunk * bag_count

time: 31.1 us -> 27.9 us (0.90)
  waiting for transfers between devices: 8.78 us -> 4.11 us
  starting transfers between devices: 12.3 us -> 13.8 us
    all_to_all x2, waiting for transfers between devices: 8.02 us -> 4.1 us  [exchange(): lax.all_to_all(x, axis, split_axis=0, concat_axis=0, axis_index_groups=[o...]
    all_to_all x2, starting transfers between devices: 10.6 us -> 12.1 us  [exchange(): lax.all_to_all(x, axis, split_axis=0, concat_axis=0, axis_index_groups=[o...]
    ppermute x3, waiting for transfers between devices: 0.77 us -> 0.01 us  [shift(): return lax.ppermute(x, axis, [(i, (i + step) % size) for i in range(size)])]
  transfers between devices with their start and end apart: 5 -> 5, of which waited for: 4 -> 2; matrix products, arithmetic and copies ran while one was open for 0% -> 0% of each run, Pallas kernels for 16% -> 18%
where the time goes in v10:
time: 27.9 us; the launch traced here: 27.5 us
  starting transfers between devices  13.8 us (49%)
  Pallas kernels  8.91 us (32%)
  waiting for transfers between devices  4.11 us (15%)
  between operations  0.69 us (2%)
    all_to_all x2, starting transfers between devices, exchange(): lax.all_to_all(x, axis, split_axis=0, concat_axis=0, axis_index_groups=[o...  12.1 us
    all_to_all x2, waiting for transfers between devices, exchange(): lax.all_to_all(x, axis, split_axis=0, concat_axis=0, axis_index_groups=[o...  4.1 us
    pallas_call x1, Pallas kernels, local(): pl.pallas_call(functools.partial(update_kernel, bag_count, lines, groups,...  3.37 us
    pallas_call x1, Pallas kernels, local(): pl.pallas_call(functools.partial(pool_kernel, bag_count, lines), out_shap...  1.89 us
    ppermute x3, starting transfers between devices, shift(): return lax.ppermute(x, axis, [(i, (i + step) % size) for i in range(size)])  1.75 us
    pallas_call x1, Pallas kernels, local(): pl.pallas_call(prepare_kernel, out_shape=pltpu.VMEM((rows_dev, width), jn...  1.55 us
    pallas_call x1, Pallas kernels, local(): pl.pallas_call(functools.partial(pack_kernel, rows_dev), out_shape=pltpu....  1.5 us
    pallas_call x1, Pallas kernels, local(): pl.pallas_call(finish_kernel, out_shape=(jax.ShapeDtypeStruct((bag_count,...  0.6 us
  transfers between devices with their start and end apart: 5, of which 2 were waited for; matrix products, arithmetic and copies ran while one was open for 0% of the time, Pallas kernels for 18%

profile of v10, /device:TPU:0, one launch (start us, length us, event | category | flops | bytes accessed | tf_op | source)
XLA Modules:
  0.0 27.5 jit_solution(17273260154420005954)
XLA Ops:
  0.6 1.5 %pack.1 = f32[8,24,128]{2,1,0:T(8,128)} custom-call(s32[4,128]{1,0:T(4,128)} %bitcast.12, s32[4,128]{1,0:T(4,128)} %bitcast.13, s32[4,128]{1,0:T(4,128)} %bitcast.14, s32[4,128]{1,0:T(4,128)} %bitcast.15, s32[4,128]{1,0:T(4,128)} %bitcast.16, s32[4,128]{1,0:T(4,128)} %bitcast.17, f32[4,256]{1,0:T(4,128)} %bitcast.11), custom_call_target="tpu_custom_call" | custom-call | tf_op jit(solution)/shard_map/pack/pallas_call | solution.py:217
  2.1 7.8 %all-to-all-start = ((f32[8,24,128]{2,1,0:T(8,128)}), f32[8,24,128]{2,1,0:T(8,128)S(1)}, u32[]{:S(2)}, u32[]{:S(2)}) async-start(f32[8,24,128]{2,1,0:T(8,128)} %pack.1), calls=%async_computation | async-start | bytes 196608 | tf_op jit(solution)/shard_map/all_to_all | solution.py:186
  10.0 1.5 %prepare.1.table.refs_4_ = f32[2048,256]{1,0:T(8,128)S(1)} custom-call(f32[2048,256]{1,0:T(8,128)} %table.1), custom_call_target="tpu_custom_call" | custom-call | bytes 4194304 | tf_op jit(solution)/shard_map/prepare/pallas_call | solution.py:233
  11.5 0.0 copy-start
  11.5 3.2 %all-to-all-done.msg = f32[8,24,128]{2,1,0:T(8,128)S(1)} async-done(((f32[8,24,128]{2,1,0:T(8,128)}), f32[8,24,128]{2,1,0:T(8,128)S(1)}, u32[]{:S(2)}, u32[]{:S(2)}) %all-to-all-start) | async-done | bytes 98336 | tf_op jit(solution)/shard_map/all_to_all | solution.py:186
  14.7 1.9 %pool.1 = (f32[8,4,256]{2,1,0:T(4,128)}, f32[8,16,128]{2,1,0:T(8,128)S(1)}) custom-call(f32[8,24,128]{2,1,0:T(8,128)S(1)} %all-to-all-done.msg, f32[2048,256]{1,0:T(8,128)S(1)} %prepare.1.table.refs_4_), custom_call_target="tpu_custom_call" | custom-call | flops 67108864 | bytes 2097152 | tf_op jit(solution)/shard_map/pool/pallas_call | solution.py:245
  16.6 0.0 collective-permute-start.2
  16.6 1.5 %collective-permute-start.1 = (f32[8,16,128]{2,1,0:T(8,128)S(1)}, f32[8,16,128]{2,1,0:T(8,128)S(1)}, u32[]{:S(2)}, u32[]{:S(2)}) collective-permute-start(f32[8,16,128]{2,1,0:T(8,128)S(1)} %get-tuple-element.10.refs_0_), channel_id=1, source_target_pairs={{0,16},{8,24},{16,0},{24,8},{1,17},{9,25},{17,1},{25,9},{2,18},{10... | collective-permute-start | bytes 196616 | tf_op jit(solution)/shard_map/ppermute | solution.py:192
  18.1 0.2 collective-permute-start
  18.4 4.2 %all-to-all-start.1 = ((f32[8,4,256]{2,1,0:T(4,128)}), f32[8,4,256]{2,1,0:T(4,128)S(1)}, u32[]{:S(2)}, u32[]{:S(2)}) async-start(f32[8,4,256]{2,1,0:T(4,128)} %get-tuple-element.9), calls=%async_computation.1 | async-start | bytes 65536 | tf_op jit(solution)/shard_map/all_to_all | solution.py:186
  22.6 0.0 collective-permute-done.2.refs_3_
  22.6 0.0 collective-permute-done.1.refs_2_
  22.6 0.0 collective-permute-done.refs_1_
  22.6 0.0 copy-done
  22.6 3.4 %update.1 = (f32[2048,256]{1,0:T(8,128)}, f32[16,128]{1,0:T(8,128)S(1)}) custom-call(f32[8,16,128]{2,1,0:T(8,128)S(1)} %get-tuple-element.10.refs_0_, f32[8,16,128]{2,1,0:T(8,128)S(1)} %collective-permute-done.refs_1_, f32[8,16,128]{2,1,0:T(8,128)S(1)} %collective-permute-done.1.refs_2_, f32[8,16,128]{2,1,0:T(8,128)S(1)} %collective-permute-done.2.refs_3_, ...), custom_call_target="tpu_custom_call" | custom-call | flops 1 | bytes 1048576 | tf_op jit(solution)/shard_map/update/pallas_call | solution.py:268
  26.0 0.9 %all-to-all-done.1.returned = f32[8,4,256]{2,1,0:T(4,128)S(1)} async-done(((f32[8,4,256]{2,1,0:T(4,128)}), f32[8,4,256]{2,1,0:T(4,128)S(1)}, u32[]{:S(2)}, u32[]{:S(2)}) %all-to-all-start.1) | async-done | bytes 32800 | tf_op jit(solution)/shard_map/all_to_all | solution.py:186
  26.9 0.6 %finish.1 = (f32[4,256]{1,0:T(4,128)}, f32[16,128]{1,0:T(8,128)}) custom-call(f32[8,4,256]{2,1,0:T(4,128)S(1)} %all-to-all-done.1.returned, f32[16,128]{1,0:T(8,128)S(1)} %get-tuple-element.11.accum), custom_call_target="tpu_custom_call" | custom-call | tf_op jit(solution)/shard_map/finish/pallas_call | solution.py:292
Async XLA Ops:
  2.1 12.6 %all-to-all-start = ((f32[8,24,128]{2,1,0:T(8,128)}), f32[8,24,128]{2,1,0:T(8,128)S(1)}, u32[]{:S(2)}, u32[]{:S(2)}) async-start(f32[8,24,128]{2,1,0:T(8,128)} %pack.1), calls=%async_computation | async-start | bytes 196608 | tf_op jit(solution)/shard_map/all_to_all | solution.py:186
  11.5 11.1 %copy-start = (f32[2048]{0:T(1024)S(1)}, f32[2048]{0:T(1024)}, u32[]{:S(2)}) copy-start(f32[2048]{0:T(1024)} %param.10) | copy-start | bytes 24580
  16.6 6.0 %collective-permute-start.2 = (f32[8,16,128]{2,1,0:T(8,128)S(1)}, f32[8,16,128]{2,1,0:T(8,128)S(1)}, u32[]{:S(2)}, u32[]{:S(2)}) collective-permute-start(f32[8,16,128]{2,1,0:T(8,128)S(1)} %get-tuple-element.10.refs_0_), channel_id=1, source_target_pairs={{0,24},{8,0},{16,8},{24,16},{1,25},{9,1},{17,9},{25,17},{2,26},{10... | collective-permute-start | bytes 196616 | tf_op jit(solution)/shard_map/ppermute | solution.py:192
  16.6 6.0 %collective-permute-start.1 = (f32[8,16,128]{2,1,0:T(8,128)S(1)}, f32[8,16,128]{2,1,0:T(8,128)S(1)}, u32[]{:S(2)}, u32[]{:S(2)}) collective-permute-start(f32[8,16,128]{2,1,0:T(8,128)S(1)} %get-tuple-element.10.refs_0_), channel_id=1, source_target_pairs={{0,16},{8,24},{16,0},{24,8},{1,17},{9,25},{17,1},{25,9},{2,18},{10... | collective-permute-start | bytes 196616 | tf_op jit(solution)/shard_map/ppermute | solution.py:192
  18.1 4.5 %collective-permute-start = (f32[8,16,128]{2,1,0:T(8,128)S(1)}, f32[8,16,128]{2,1,0:T(8,128)S(1)}, u32[]{:S(2)}, u32[]{:S(2)}) collective-permute-start(f32[8,16,128]{2,1,0:T(8,128)S(1)} %get-tuple-element.10.refs_0_), channel_id=1, source_target_pairs={{0,8},{8,16},{16,24},{24,0},{1,9},{9,17},{17,25},{25,1},{2,10},{10... | collective-permute-start | bytes 196616 | tf_op jit(solution)/shard_map/ppermute | solution.py:192
  18.4 8.6 %all-to-all-start.1 = ((f32[8,4,256]{2,1,0:T(4,128)}), f32[8,4,256]{2,1,0:T(4,128)S(1)}, u32[]{:S(2)}, u32[]{:S(2)}) async-start(f32[8,4,256]{2,1,0:T(4,128)} %get-tuple-element.9), calls=%async_computation.1 | async-start | bytes 65536 | tf_op jit(solution)/shard_map/all_to_all | solution.py:186

commit v11 on v10

--- a/solution.py
+++ b/solution.py
@@ -182,7 +182,7 @@
 
 def exchange(x, axis):
     size = lax.axis_size(axis)
-    order = [(i + size // 2) % size for i in range(size)]
+    order = [(i + size // 2 - 1) % size for i in range(size)]
     return lax.all_to_all(
         x, axis, split_axis=0, concat_axis=0, axis_index_groups=[order], tiled=True)
 

time: 27.9 us -> 28.4 us (1.018)
  starting transfers between devices: 13.8 us -> 14.3 us
    all_to_all x2, starting transfers between devices: 12.1 us -> 12.6 us  [exchange(): lax.all_to_all(x, axis, split_axis=0, concat_axis=0, axis_index_groups=[o...]
where the time goes in v11:
time: 28.4 us; the launch traced here: 28 us
  starting transfers between devices  14.3 us (50%)
  Pallas kernels  8.92 us (31%)
  waiting for transfers between devices  4.11 us (14%)
  between operations  0.69 us (2%)
    all_to_all x2, starting transfers between devices, exchange(): lax.all_to_all(x, axis, split_axis=0, concat_axis=0, axis_index_groups=[o...  12.6 us
    all_to_all x2, waiting for transfers between devices, exchange(): lax.all_to_all(x, axis, split_axis=0, concat_axis=0, axis_index_groups=[o...  4.1 us
    pallas_call x1, Pallas kernels, local(): pl.pallas_call(functools.partial(update_kernel, bag_count, lines, groups,...  3.38 us
    pallas_call x1, Pallas kernels, local(): pl.pallas_call(functools.partial(pool_kernel, bag_count, lines), out_shap...  1.89 us
    ppermute x3, starting transfers between devices, shift(): return lax.ppermute(x, axis, [(i, (i + step) % size) for i in range(size)])  1.75 us
    pallas_call x1, Pallas kernels, local(): pl.pallas_call(prepare_kernel, out_shape=pltpu.VMEM((rows_dev, width), jn...  1.55 us
    pallas_call x1, Pallas kernels, local(): pl.pallas_call(functools.partial(pack_kernel, rows_dev), out_shape=pltpu....  1.5 us
    pallas_call x1, Pallas kernels, local(): pl.pallas_call(finish_kernel, out_shape=(jax.ShapeDtypeStruct((bag_count,...  0.6 us
  transfers between devices with their start and end apart: 5, of which 2 were waited for; matrix products, arithmetic and copies ran while one was open for 0% of the time, Pallas kernels for 18%

profile of v11, /device:TPU:0, one launch (start us, length us, event | category | flops | bytes accessed | tf_op | source)
XLA Modules:
  0.0 28.0 jit_solution(12086939575151309558)
XLA Ops:
  0.6 1.5 %pack.1 = f32[8,24,128]{2,1,0:T(8,128)} custom-call(s32[4,128]{1,0:T(4,128)} %bitcast.12, s32[4,128]{1,0:T(4,128)} %bitcast.13, s32[4,128]{1,0:T(4,128)} %bitcast.14, s32[4,128]{1,0:T(4,128)} %bitcast.15, s32[4,128]{1,0:T(4,128)} %bitcast.16, s32[4,128]{1,0:T(4,128)} %bitcast.17, f32[4,256]{1,0:T(4,128)} %bitcast.11), custom_call_target="tpu_custom_call" | custom-call | tf_op jit(solution)/shard_map/pack/pallas_call | solution.py:217
  2.1 7.8 %all-to-all-start = ((f32[8,24,128]{2,1,0:T(8,128)}), f32[8,24,128]{2,1,0:T(8,128)S(1)}, u32[]{:S(2)}, u32[]{:S(2)}) async-start(f32[8,24,128]{2,1,0:T(8,128)} %pack.1), calls=%async_computation | async-start | bytes 196608 | tf_op jit(solution)/shard_map/all_to_all | solution.py:186
  10.0 1.5 %prepare.1.table.refs_4_ = f32[2048,256]{1,0:T(8,128)S(1)} custom-call(f32[2048,256]{1,0:T(8,128)} %table.1), custom_call_target="tpu_custom_call" | custom-call | bytes 4194304 | tf_op jit(solution)/shard_map/prepare/pallas_call | solution.py:233
  11.5 0.0 copy-start
  11.5 3.2 %all-to-all-done.msg = f32[8,24,128]{2,1,0:T(8,128)S(1)} async-done(((f32[8,24,128]{2,1,0:T(8,128)}), f32[8,24,128]{2,1,0:T(8,128)S(1)}, u32[]{:S(2)}, u32[]{:S(2)}) %all-to-all-start) | async-done | bytes 98336 | tf_op jit(solution)/shard_map/all_to_all | solution.py:186
  14.7 1.9 %pool.1 = (f32[8,4,256]{2,1,0:T(4,128)}, f32[8,16,128]{2,1,0:T(8,128)S(1)}) custom-call(f32[8,24,128]{2,1,0:T(8,128)S(1)} %all-to-all-done.msg, f32[2048,256]{1,0:T(8,128)S(1)} %prepare.1.table.refs_4_), custom_call_target="tpu_custom_call" | custom-call | flops 67108864 | bytes 2097152 | tf_op jit(solution)/shard_map/pool/pallas_call | solution.py:245
  16.6 0.0 collective-permute-start.2
  16.6 1.5 %collective-permute-start.1 = (f32[8,16,128]{2,1,0:T(8,128)S(1)}, f32[8,16,128]{2,1,0:T(8,128)S(1)}, u32[]{:S(2)}, u32[]{:S(2)}) collective-permute-start(f32[8,16,128]{2,1,0:T(8,128)S(1)} %get-tuple-element.10.refs_0_), channel_id=1, source_target_pairs={{0,16},{8,24},{16,0},{24,8},{1,17},{9,25},{17,1},{25,9},{2,18},{10... | collective-permute-start | bytes 196616 | tf_op jit(solution)/shard_map/ppermute | solution.py:192
  18.1 0.2 collective-permute-start
  18.4 4.8 %all-to-all-start.1 = ((f32[8,4,256]{2,1,0:T(4,128)}), f32[8,4,256]{2,1,0:T(4,128)S(1)}, u32[]{:S(2)}, u32[]{:S(2)}) async-start(f32[8,4,256]{2,1,0:T(4,128)} %get-tuple-element.9), calls=%async_computation.1 | async-start | bytes 65536 | tf_op jit(solution)/shard_map/all_to_all | solution.py:186
  23.1 0.0 collective-permute-done.2.refs_3_
  23.1 0.0 collective-permute-done.1.refs_2_
  23.1 0.0 collective-permute-done.refs_1_
  23.1 0.0 copy-done
  23.2 3.4 %update.1 = (f32[2048,256]{1,0:T(8,128)}, f32[16,128]{1,0:T(8,128)S(1)}) custom-call(f32[8,16,128]{2,1,0:T(8,128)S(1)} %get-tuple-element.10.refs_0_, f32[8,16,128]{2,1,0:T(8,128)S(1)} %collective-permute-done.refs_1_, f32[8,16,128]{2,1,0:T(8,128)S(1)} %collective-permute-done.1.refs_2_, f32[8,16,128]{2,1,0:T(8,128)S(1)} %collective-permute-done.2.refs_3_, ...), custom_call_target="tpu_custom_call" | custom-call | flops 1 | bytes 1048576 | tf_op jit(solution)/shard_map/update/pallas_call | solution.py:268
  26.5 0.9 %all-to-all-done.1.returned = f32[8,4,256]{2,1,0:T(4,128)S(1)} async-done(((f32[8,4,256]{2,1,0:T(4,128)}), f32[8,4,256]{2,1,0:T(4,128)S(1)}, u32[]{:S(2)}, u32[]{:S(2)}) %all-to-all-start.1) | async-done | bytes 32800 | tf_op jit(solution)/shard_map/all_to_all | solution.py:186
  27.4 0.6 %finish.1 = (f32[4,256]{1,0:T(4,128)}, f32[16,128]{1,0:T(8,128)}) custom-call(f32[8,4,256]{2,1,0:T(4,128)S(1)} %all-to-all-done.1.returned, f32[16,128]{1,0:T(8,128)S(1)} %get-tuple-element.11.accum), custom_call_target="tpu_custom_call" | custom-call | tf_op jit(solution)/shard_map/finish/pallas_call | solution.py:292
Async XLA Ops:
  2.1 12.6 %all-to-all-start = ((f32[8,24,128]{2,1,0:T(8,128)}), f32[8,24,128]{2,1,0:T(8,128)S(1)}, u32[]{:S(2)}, u32[]{:S(2)}) async-start(f32[8,24,128]{2,1,0:T(8,128)} %pack.1), calls=%async_computation | async-start | bytes 196608 | tf_op jit(solution)/shard_map/all_to_all | solution.py:186
  11.5 11.6 %copy-start = (f32[2048]{0:T(1024)S(1)}, f32[2048]{0:T(1024)}, u32[]{:S(2)}) copy-start(f32[2048]{0:T(1024)} %param.10) | copy-start | bytes 24580
  16.6 6.5 %collective-permute-start.2 = (f32[8,16,128]{2,1,0:T(8,128)S(1)}, f32[8,16,128]{2,1,0:T(8,128)S(1)}, u32[]{:S(2)}, u32[]{:S(2)}) collective-permute-start(f32[8,16,128]{2,1,0:T(8,128)S(1)} %get-tuple-element.10.refs_0_), channel_id=1, source_target_pairs={{0,24},{8,0},{16,8},{24,16},{1,25},{9,1},{17,9},{25,17},{2,26},{10... | collective-permute-start | bytes 196616 | tf_op jit(solution)/shard_map/ppermute | solution.py:192
  16.6 6.5 %collective-permute-start.1 = (f32[8,16,128]{2,1,0:T(8,128)S(1)}, f32[8,16,128]{2,1,0:T(8,128)S(1)}, u32[]{:S(2)}, u32[]{:S(2)}) collective-permute-start(f32[8,16,128]{2,1,0:T(8,128)S(1)} %get-tuple-element.10.refs_0_), channel_id=1, source_target_pairs={{0,16},{8,24},{16,0},{24,8},{1,17},{9,25},{17,1},{25,9},{2,18},{10... | collective-permute-start | bytes 196616 | tf_op jit(solution)/shard_map/ppermute | solution.py:192
  18.1 5.0 %collective-permute-start = (f32[8,16,128]{2,1,0:T(8,128)S(1)}, f32[8,16,128]{2,1,0:T(8,128)S(1)}, u32[]{:S(2)}, u32[]{:S(2)}) collective-permute-start(f32[8,16,128]{2,1,0:T(8,128)S(1)} %get-tuple-element.10.refs_0_), channel_id=1, source_target_pairs={{0,8},{8,16},{16,24},{24,0},{1,9},{9,17},{17,25},{25,1},{2,10},{10... | collective-permute-start | bytes 196616 | tf_op jit(solution)/shard_map/ppermute | solution.py:192
  18.4 9.1 %all-to-all-start.1 = ((f32[8,4,256]{2,1,0:T(4,128)}), f32[8,4,256]{2,1,0:T(4,128)S(1)}, u32[]{:S(2)}, u32[]{:S(2)}) async-start(f32[8,4,256]{2,1,0:T(4,128)} %get-tuple-element.9), calls=%async_computation.1 | async-start | bytes 65536 | tf_op jit(solution)/shard_map/all_to_all | solution.py:186

commit v12 on v11

--- a/solution.py
+++ b/solution.py
@@ -83,7 +83,7 @@
             blocks, bag_count, LANES)
 
 
-def pool_kernel(bag_count, lines, msg, table, out, joined, code_ref, lane_ref, counts):
+def pool_kernel(bag_count, lines, turn, msg, table, out, joined, code_ref, lane_ref, counts):
     rows_dev, width = table.shape
     owners = msg.shape[0]
     base = lax.axis_index("rows") * rows_dev
@@ -97,7 +97,9 @@
     total = jnp.zeros((owners * bag_count, width), jnp.float32)
     for part in split_two(table[...]):
         total += jnp.dot(flat, part, preferred_element_type=jnp.float32)
-    out[...] = total.reshape(out.shape)
+    for i in range(owners):
+        seen = (i + turn) % owners
+        out[i] = total[seen * bag_count:(seen + 1) * bag_count, :]
 
 
 def update_kernel(bag_count, lines, groups, chunk, *refs):
@@ -180,9 +182,12 @@
     new_accum[...] = accum[...]
 
 
-def exchange(x, axis):
-    size = lax.axis_size(axis)
-    order = [(i + size // 2 - 1) % size for i in range(size)]
+def listing(size, leader):
+    return [(i + leader) % size for i in range(size)]
+
+
+def exchange(x, axis, leader):
+    order = listing(lax.axis_size(axis), leader)
     return lax.all_to_all(
         x, axis, split_axis=0, concat_axis=0, axis_index_groups=[order], tiled=True)
 
@@ -198,6 +203,7 @@
 ):
     owners, groups = lax.axis_size("rows"), lax.axis_size("dp")
     devices = owners * groups
+    out_leader, back_leader = owners // 2 - 1, owners // 2
     rows_dev, width = item_table.shape
     bag_count = grad_pooled.shape[2]
     lines = row_index.shape[2] // LANES
@@ -227,7 +233,7 @@
         line(owner_map), line(row_index), line(bag_index),
         line(prev_owner), line(prev_row), line(prev_bag), grad_pooled[0, 0],
     )])
-    gathered = exchange(message, "rows")
+    gathered = exchange(message, "rows", out_leader)
 
     pieces = 4
     kept = pl.pallas_call(
@@ -243,7 +249,7 @@
     )(stay(item_table))
 
     partial_pooled, joined = pl.pallas_call(
-        functools.partial(pool_kernel, bag_count, lines),
+        functools.partial(pool_kernel, bag_count, lines, back_leader - out_leader),
         out_shape=(
             pltpu.VMEM((owners, bag_count, width), jnp.float32),
             pltpu.VMEM((owners, prev_length, LANES), jnp.float32),
@@ -261,7 +267,7 @@
             bytes_accessed=rows_dev * width * 4, transcendentals=0),
         name="pool",
     )(gathered, kept)
-    returned = exchange(partial_pooled, "rows")
+    returned = exchange(partial_pooled, "rows", back_leader)
     all_groups = [joined] + [shift(joined, "dp", k) for k in range(1, groups)]
 
     segments = chunk * bag_count

time: 28.4 us -> 28.4 us (level)
  no operation moved by 1% of the time
where the time goes in v12:
time: 28.4 us; the launch traced here: 28 us
  starting transfers between devices  14.3 us (50%)
  Pallas kernels  8.91 us (31%)
  waiting for transfers between devices  4.12 us (15%)
  between operations  0.69 us (2%)
    all_to_all x2, starting transfers between devices, exchange(): lax.all_to_all(x, axis, split_axis=0, concat_axis=0, axis_index_groups=[o...  12.6 us
    all_to_all x2, waiting for transfers between devices, exchange(): lax.all_to_all(x, axis, split_axis=0, concat_axis=0, axis_index_groups=[o...  4.11 us
    pallas_call x1, Pallas kernels, local(): pl.pallas_call(functools.partial(update_kernel, bag_count, lines, groups,...  3.37 us
    pallas_call x1, Pallas kernels, local(): pl.pallas_call(functools.partial(pool_kernel, bag_count, lines, back_lead...  1.89 us
    ppermute x3, starting transfers between devices, shift(): return lax.ppermute(x, axis, [(i, (i + step) % size) for i in range(size)])  1.75 us
    pallas_call x1, Pallas kernels, local(): pl.pallas_call(prepare_kernel, out_shape=pltpu.VMEM((rows_dev, width), jn...  1.55 us
    pallas_call x1, Pallas kernels, local(): pl.pallas_call(functools.partial(pack_kernel, rows_dev), out_shape=pltpu....  1.5 us
    pallas_call x1, Pallas kernels, local(): pl.pallas_call(finish_kernel, out_shape=(jax.ShapeDtypeStruct((bag_count,...  0.6 us
  transfers between devices with their start and end apart: 5, of which 2 were waited for; matrix products, arithmetic and copies ran while one was open for 0% of the time, Pallas kernels for 18%

profile of v12, /device:TPU:0, one launch (start us, length us, event | category | flops | bytes accessed | tf_op | source)
XLA Modules:
  0.0 28.0 jit_solution(17094978655945175901)
XLA Ops:
  0.6 1.5 %pack.1 = f32[8,24,128]{2,1,0:T(8,128)} custom-call(s32[4,128]{1,0:T(4,128)} %bitcast.12, s32[4,128]{1,0:T(4,128)} %bitcast.13, s32[4,128]{1,0:T(4,128)} %bitcast.14, s32[4,128]{1,0:T(4,128)} %bitcast.15, s32[4,128]{1,0:T(4,128)} %bitcast.16, s32[4,128]{1,0:T(4,128)} %bitcast.17, f32[4,256]{1,0:T(4,128)} %bitcast.11), custom_call_target="tpu_custom_call" | custom-call | tf_op jit(solution)/shard_map/pack/pallas_call | solution.py:223
  2.1 7.8 %all-to-all-start = ((f32[8,24,128]{2,1,0:T(8,128)}), f32[8,24,128]{2,1,0:T(8,128)S(1)}, u32[]{:S(2)}, u32[]{:S(2)}) async-start(f32[8,24,128]{2,1,0:T(8,128)} %pack.1), calls=%async_computation | async-start | bytes 196608 | tf_op jit(solution)/shard_map/all_to_all | solution.py:191
  10.0 1.5 %prepare.1.table.refs_4_ = f32[2048,256]{1,0:T(8,128)S(1)} custom-call(f32[2048,256]{1,0:T(8,128)} %table.1), custom_call_target="tpu_custom_call" | custom-call | bytes 4194304 | tf_op jit(solution)/shard_map/prepare/pallas_call | solution.py:239
  11.5 0.0 copy-start
  11.5 3.2 %all-to-all-done.msg = f32[8,24,128]{2,1,0:T(8,128)S(1)} async-done(((f32[8,24,128]{2,1,0:T(8,128)}), f32[8,24,128]{2,1,0:T(8,128)S(1)}, u32[]{:S(2)}, u32[]{:S(2)}) %all-to-all-start) | async-done | bytes 98336 | tf_op jit(solution)/shard_map/all_to_all | solution.py:191
  14.7 1.9 %pool.1 = (f32[8,4,256]{2,1,0:T(4,128)}, f32[8,16,128]{2,1,0:T(8,128)S(1)}) custom-call(f32[8,24,128]{2,1,0:T(8,128)S(1)} %all-to-all-done.msg, f32[2048,256]{1,0:T(8,128)S(1)} %prepare.1.table.refs_4_), custom_call_target="tpu_custom_call" | custom-call | flops 67108864 | bytes 2097152 | tf_op jit(solution)/shard_map/pool/pallas_call | solution.py:251
  16.6 0.0 collective-permute-start.2
  16.6 1.5 %collective-permute-start.1 = (f32[8,16,128]{2,1,0:T(8,128)S(1)}, f32[8,16,128]{2,1,0:T(8,128)S(1)}, u32[]{:S(2)}, u32[]{:S(2)}) collective-permute-start(f32[8,16,128]{2,1,0:T(8,128)S(1)} %get-tuple-element.10.refs_0_), channel_id=1, source_target_pairs={{0,16},{8,24},{16,0},{24,8},{1,17},{9,25},{17,1},{25,9},{2,18},{10... | collective-permute-start | bytes 196616 | tf_op jit(solution)/shard_map/ppermute | solution.py:197
  18.1 0.2 collective-permute-start
  18.4 4.7 %all-to-all-start.1 = ((f32[8,4,256]{2,1,0:T(4,128)}), f32[8,4,256]{2,1,0:T(4,128)S(1)}, u32[]{:S(2)}, u32[]{:S(2)}) async-start(f32[8,4,256]{2,1,0:T(4,128)} %get-tuple-element.9), calls=%async_computation.1 | async-start | bytes 65536 | tf_op jit(solution)/shard_map/all_to_all | solution.py:191
  23.1 0.0 collective-permute-done.2.refs_3_
  23.1 0.0 collective-permute-done.1.refs_2_
  23.1 0.0 collective-permute-done.refs_1_
  23.1 0.0 copy-done
  23.1 3.4 %update.1 = (f32[2048,256]{1,0:T(8,128)}, f32[16,128]{1,0:T(8,128)S(1)}) custom-call(f32[8,16,128]{2,1,0:T(8,128)S(1)} %get-tuple-element.10.refs_0_, f32[8,16,128]{2,1,0:T(8,128)S(1)} %collective-permute-done.refs_1_, f32[8,16,128]{2,1,0:T(8,128)S(1)} %collective-permute-done.1.refs_2_, f32[8,16,128]{2,1,0:T(8,128)S(1)} %collective-permute-done.2.refs_3_, ...), custom_call_target="tpu_custom_call" | custom-call | flops 1 | bytes 1048576 | tf_op jit(solution)/shard_map/update/pallas_call | solution.py:274
  26.5 0.9 %all-to-all-done.1.returned = f32[8,4,256]{2,1,0:T(4,128)S(1)} async-done(((f32[8,4,256]{2,1,0:T(4,128)}), f32[8,4,256]{2,1,0:T(4,128)S(1)}, u32[]{:S(2)}, u32[]{:S(2)}) %all-to-all-start.1) | async-done | bytes 32800 | tf_op jit(solution)/shard_map/all_to_all | solution.py:191
  27.4 0.6 %finish.1 = (f32[4,256]{1,0:T(4,128)}, f32[16,128]{1,0:T(8,128)}) custom-call(f32[8,4,256]{2,1,0:T(4,128)S(1)} %all-to-all-done.1.returned, f32[16,128]{1,0:T(8,128)S(1)} %get-tuple-element.11.accum), custom_call_target="tpu_custom_call" | custom-call | tf_op jit(solution)/shard_map/finish/pallas_call | solution.py:298
Async XLA Ops:
  2.1 12.6 %all-to-all-start = ((f32[8,24,128]{2,1,0:T(8,128)}), f32[8,24,128]{2,1,0:T(8,128)S(1)}, u32[]{:S(2)}, u32[]{:S(2)}) async-start(f32[8,24,128]{2,1,0:T(8,128)} %pack.1), calls=%async_computation | async-start | bytes 196608 | tf_op jit(solution)/shard_map/all_to_all | solution.py:191
  11.5 11.6 %copy-start = (f32[2048]{0:T(1024)S(1)}, f32[2048]{0:T(1024)}, u32[]{:S(2)}) copy-start(f32[2048]{0:T(1024)} %param.10) | copy-start | bytes 24580
  16.6 6.5 %collective-permute-start.2 = (f32[8,16,128]{2,1,0:T(8,128)S(1)}, f32[8,16,128]{2,1,0:T(8,128)S(1)}, u32[]{:S(2)}, u32[]{:S(2)}) collective-permute-start(f32[8,16,128]{2,1,0:T(8,128)S(1)} %get-tuple-element.10.refs_0_), channel_id=1, source_target_pairs={{0,24},{8,0},{16,8},{24,16},{1,25},{9,1},{17,9},{25,17},{2,26},{10... | collective-permute-start | bytes 196616 | tf_op jit(solution)/shard_map/ppermute | solution.py:197
  16.6 6.5 %collective-permute-start.1 = (f32[8,16,128]{2,1,0:T(8,128)S(1)}, f32[8,16,128]{2,1,0:T(8,128)S(1)}, u32[]{:S(2)}, u32[]{:S(2)}) collective-permute-start(f32[8,16,128]{2,1,0:T(8,128)S(1)} %get-tuple-element.10.refs_0_), channel_id=1, source_target_pairs={{0,16},{8,24},{16,0},{24,8},{1,17},{9,25},{17,1},{25,9},{2,18},{10... | collective-permute-start | bytes 196616 | tf_op jit(solution)/shard_map/ppermute | solution.py:197
  18.1 5.0 %collective-permute-start = (f32[8,16,128]{2,1,0:T(8,128)S(1)}, f32[8,16,128]{2,1,0:T(8,128)S(1)}, u32[]{:S(2)}, u32[]{:S(2)}) collective-permute-start(f32[8,16,128]{2,1,0:T(8,128)S(1)} %get-tuple-element.10.refs_0_), channel_id=1, source_target_pairs={{0,8},{8,16},{16,24},{24,0},{1,9},{9,17},{17,25},{25,1},{2,10},{10... | collective-permute-start | bytes 196616 | tf_op jit(solution)/shard_map/ppermute | solution.py:197
  18.4 9.1 %all-to-all-start.1 = ((f32[8,4,256]{2,1,0:T(4,128)}), f32[8,4,256]{2,1,0:T(4,128)S(1)}, u32[]{:S(2)}, u32[]{:S(2)}) async-start(f32[8,4,256]{2,1,0:T(4,128)} %get-tuple-element.9), calls=%async_computation.1 | async-start | bytes 65536 | tf_op jit(solution)/shard_map/all_to_all | solution.py:191

commit v13 on v9

--- a/solution.py
+++ b/solution.py
@@ -84,7 +84,7 @@
 
 
 def pool_kernel(
-    bag_count, lines, msg, table, out, joined, go, code_ref, lane_ref, counts,
+    bag_count, lines, turn, msg, table, out, joined, go, code_ref, lane_ref, counts,
 ):
     go[0, 0] = 1
     rows_dev, width = table.shape
@@ -100,62 +100,39 @@
     total = jnp.zeros((owners * bag_count, width), jnp.float32)
     for part in split_two(table[...]):
         total += jnp.dot(flat, part, preferred_element_type=jnp.float32)
-    out[...] = total.reshape(out.shape)
-
-
-def update_kernel(bag_count, lines, groups, chunk, *refs):
-    sources, (table, accum, new_table, new_accum) = refs[:groups], refs[groups:groups + 4]
-    msg, code_ref, lane_ref, counts, grads, sums, fresh_table, sems = refs[groups + 4:]
-    rows_dev, width = table.shape
-    pieces = sems.shape[0]
-    devices = msg.shape[0]
-    owners = devices // groups
-    blocks = counts.shape[0]
-    base = lax.axis_index("rows") * rows_dev
-    single = devices == chunk
-
-    def count_chunk(first):
-        here = pl.ds(first, chunk)
-        code_ref[...], lane_ref[...] = codes(
-            msg[here, 0:lines, :], msg[here, lines:2 * lines, :], bag_count, base)
-        count_into(counts, code_ref, lane_ref, chunk, bag_count)
-        for k in range(width // LANES):
-            start = 2 * lines + k * bag_count
-            grads[:, k * LANES:(k + 1) * LANES] = msg[
-                here, start:start + bag_count, :].reshape(chunk * bag_count, LANES)
-        return split_two(grads[...])
-
-    def block_sum(h, parts):
-        hits = counts[h].astype(jnp.bfloat16)
-        total = jnp.zeros((LANES, width), jnp.float32)
-        for part in parts:
-            total += lax.dot_general(
-                hits, part, (((0,), (0,)), ((), ())), preferred_element_type=jnp.float32)
-        return total
-
-    for i, source in enumerate(sources):
-        msg[i * owners:(i + 1) * owners] = source[...]
-    if single:
-        parts = count_chunk(0)
-    else:
-        sums[...] = jnp.zeros_like(sums)
-
-        @pl.loop(0, devices // chunk)
-        def _(c):
-            parts = count_chunk(c * chunk)
-
-            @pl.loop(0, blocks)
-            def _(h):
-                sums[h] += block_sum(h, parts)
-
+    for i in range(owners):
+        seen = (i + turn) % owners
+        out[i] = total[seen * bag_count:(seen + 1) * bag_count, :]
+
+
+def read_chunk(msg, here, chunk, lines, bag_count, base, code_ref, lane_ref, counts, grads):
+    width = grads.shape[1]
+    code_ref[...], lane_ref[...] = codes(
+        msg[here, 0:lines, :], msg[here, lines:2 * lines, :], bag_count, base)
+    count_into(counts, code_ref, lane_ref, chunk, bag_count)
+    for k in range(width // LANES):
+        start = 2 * lines + k * bag_count
+        grads[:, k * LANES:(k + 1) * LANES] = msg[
+            here, start:start + bag_count, :].reshape(chunk * bag_count, LANES)
+
+
+def block_sum(hits, parts):
+    total = jnp.zeros((hits.shape[1], parts[0].shape[1]), jnp.float32)
+    for part in parts:
+        total += lax.dot_general(
+            hits, part, (((0,), (0,)), ((), ())), preferred_element_type=jnp.float32)
+    return total
+
+
+def apply_rows(grad_of, table, accum, new_table, new_accum, fresh_table, sems):
+    blocks, width = accum.shape[0], table.shape[1]
     diagonal = (
         lax.broadcasted_iota(jnp.int32, (LANES, LANES), 0)
         == lax.broadcasted_iota(jnp.int32, (LANES, LANES), 1))
-    per_piece = blocks // pieces
+    per_piece = blocks // sems.shape[0]
     copies = []
     for h in range(blocks):
-        i = h // per_piece
-        grad = block_sum(h, parts) if single else sums[h]
+        grad = grad_of(h)
         here = slice(h * LANES, (h + 1) * LANES)
         squares = grad * grad
         folded = squares[:, 0:LANES]
@@ -167,6 +144,7 @@
         new_accum[h:h + 1, :] = jnp.sum(
             jnp.where(diagonal, fresh, 0.0), axis=0, keepdims=True)
         if (h + 1) % per_piece == 0:
+            i = h // per_piece
             piece = pl.ds(i * per_piece * LANES, per_piece * LANES)
             copies.append(pltpu.make_async_copy(
                 fresh_table.at[piece, :], new_table.at[piece, :], sems.at[i]))
@@ -175,6 +153,65 @@
         copy.wait()
 
 
+def count_kernel(bag_count, lines, *refs):
+    sources, (counts_out, high, low) = refs[:-8], refs[-8:-5]
+    msg, code_ref, lane_ref, counts, grads = refs[-5:]
+    owners = sources[0].shape[0]
+    devices, blocks = msg.shape[0], counts.shape[0]
+    base = lax.axis_index("rows") * (blocks * LANES)
+    for i, source in enumerate(sources):
+        msg[i * owners:(i + 1) * owners] = source[...]
+    read_chunk(
+        msg, slice(0, devices), devices, lines, bag_count, base,
+        code_ref, lane_ref, counts, grads)
+    counts_out[...] = counts[...].astype(jnp.bfloat16)
+    high[...], low[...] = split_two(grads[...])
+
+
+def apply_kernel(bag_count, lines, *refs):
+    msg, counted, high, low, table, accum, new_table, new_accum = refs[:8]
+    code_ref, lane_ref, counts, grads, fresh_table, sems = refs[8:]
+    devices, blocks = msg.shape[0], counts.shape[0]
+    base = lax.axis_index("rows") * (blocks * LANES)
+    read_chunk(
+        msg, slice(0, devices), devices, lines, bag_count, base,
+        code_ref, lane_ref, counts, grads)
+    parts = [
+        jnp.concatenate([early[...], late], axis=0)
+        for early, late in zip((high, low), split_two(grads[...]))
+    ]
+
+    def grad_of(h):
+        hits = jnp.concatenate([counted[h], counts[h].astype(jnp.bfloat16)], axis=0)
+        return block_sum(hits, parts)
+
+    apply_rows(grad_of, table, accum, new_table, new_accum, fresh_table, sems)
+
+
+def update_kernel(bag_count, lines, groups, chunk, *refs):
+    sources, (table, accum, new_table, new_accum) = refs[:groups], refs[groups:groups + 4]
+    msg, code_ref, lane_ref, counts, grads, sums, fresh_table, sems = refs[groups + 4:]
+    devices, blocks = msg.shape[0], counts.shape[0]
+    owners = devices // groups
+    base = lax.axis_index("rows") * (blocks * LANES)
+    for i, source in enumerate(sources):
+        msg[i * owners:(i + 1) * owners] = source[...]
+    sums[...] = jnp.zeros_like(sums)
+
+    @pl.loop(0, devices // chunk)
+    def _(c):
+        read_chunk(
+            msg, pl.ds(c * chunk, chunk), chunk, lines, bag_count, base,
+            code_ref, lane_ref, counts, grads)
+        parts = split_two(grads[...])
+
+        @pl.loop(0, blocks)
+        def _(h):
+            sums[h] += block_sum(counts[h].astype(jnp.bfloat16), parts)
+
+    apply_rows(lambda h: sums[h], table, accum, new_table, new_accum, fresh_table, sems)
+
+
 def pass_kernel(table, accum, new_table, new_accum, sem):
     copy = pltpu.make_async_copy(table, new_table, sem)
     copy.start()
@@ -190,9 +227,20 @@
     new_accum[...] = accum[...]
 
 
-def shift(x, axis, step):
+def listing(size, leader):
+    return [(i + leader) % size for i in range(size)]
+
+
+def exchange(x, axis, leader):
+    order = listing(lax.axis_size(axis), leader)
+    return lax.all_to_all(
+        x, axis, split_axis=0, concat_axis=0, axis_index_groups=[order], tiled=True)
+
+
+def forward(x, axis, step):
     size = lax.axis_size(axis)
-    return lax.ppermute(x, axis, [(i, (i + step) % size) for i in range(size)])
+    return lax.ppermute(
+        x, axis, [(i, ((i // 2 + step) * 2 + 1 - i % 2) % size) for i in range(size)])
 
 
 def local(
@@ -201,6 +249,7 @@
 ):
     owners, groups = lax.axis_size("rows"), lax.axis_size("dp")
     devices = owners * groups
+    out_leader, back_leader = owners // 2 - 1, owners // 2
     rows_dev, width = item_table.shape
     bag_count = grad_pooled.shape[2]
     lines = row_index.shape[2] // LANES
@@ -230,7 +279,7 @@
         line(owner_map), line(row_index), line(bag_index),
         line(prev_owner), line(prev_row), line(prev_bag), grad_pooled[0, 0],
     )])
-    gathered = lax.all_to_all(message, "rows", split_axis=0, concat_axis=0, tiled=True)
+    gathered = exchange(message, "rows", out_leader)
 
     pieces = 4
     kept = pl.pallas_call(
@@ -246,7 +295,7 @@
     )(stay(item_table))
 
     partial_pooled, joined, go = pl.pallas_call(
-        functools.partial(pool_kernel, bag_count, lines),
+        functools.partial(pool_kernel, bag_count, lines, back_leader - out_leader),
         out_shape=(
             pltpu.VMEM((owners, bag_count, width), jnp.float32),
             pltpu.VMEM((owners, prev_length, LANES), jnp.float32),
@@ -265,44 +314,78 @@
             bytes_accessed=rows_dev * width * 4, transcendentals=0),
         name="pool",
     )(gathered, kept)
-    returned = lax.all_to_all(
-        partial_pooled, "rows", split_axis=0, concat_axis=0, tiled=True)
+    returned = exchange(partial_pooled, "rows", back_leader)
+    own = [joined, forward(joined, "dp", 0)]
+    across = [forward(joined, "dp", step) for step in range(1, groups // 2)]
+
     segments = chunk * bag_count
-
-    def forward_and_update(joined, kept, row_accum):
-        all_groups = [joined] + [shift(joined, "dp", k) for k in range(1, groups)]
-
+    updated = (
+        pltpu.HBM((rows_dev, width), jnp.float32),
+        pltpu.VMEM((blocks, LANES), jnp.float32),
+    )
+
+    def room(count):
+        return [
+            pltpu.VMEM((count, lines, LANES), jnp.float32),
+            pltpu.VMEM((count, lines, LANES), jnp.float32),
+            pltpu.VMEM((blocks, count * bag_count, LANES), jnp.float32),
+            pltpu.VMEM((count * bag_count, width), jnp.float32),
+        ]
+
+    fresh_room = [
+        pltpu.VMEM((rows_dev, width), jnp.float32),
+        pltpu.SemaphoreType.DMA((pieces,)),
+    ]
+
+    def split_update(early, late, kept, row_accum):
+        count = len(early) * owners
+        counted = pl.pallas_call(
+            functools.partial(count_kernel, bag_count, lines),
+            out_shape=(
+                pltpu.VMEM((blocks, count * bag_count, LANES), jnp.bfloat16),
+                pltpu.VMEM((count * bag_count, width), jnp.bfloat16),
+                pltpu.VMEM((count * bag_count, width), jnp.bfloat16),
+            ),
+            in_specs=[vmem] * len(early),
+            out_specs=[vmem] * 3,
+            scratch_shapes=[pltpu.VMEM((count, prev_length, LANES), jnp.float32)] + room(count),
+            compiler_params=params,
+            cost_estimate=pl.CostEstimate(
+                flops=1 << 28, bytes_accessed=1 << 22, transcendentals=0),
+            name="count",
+        )(*early)
+        return pl.pallas_call(
+            functools.partial(apply_kernel, bag_count, lines),
+            out_shape=updated,
+            in_specs=[vmem] * 6,
+            out_specs=(hbm, vmem),
+            scratch_shapes=room(owners) + fresh_room,
+            compiler_params=params,
+            name="apply",
+        )(late, *counted, kept, row_accum)
+
+    def whole_update(sources, kept, row_accum):
         return pl.pallas_call(
             functools.partial(update_kernel, bag_count, lines, groups, chunk),
-            out_shape=(
-                pltpu.HBM((rows_dev, width), jnp.float32),
-                pltpu.VMEM((blocks, LANES), jnp.float32),
-            ),
+            out_shape=updated,
             in_specs=[vmem] * (groups + 2),
             out_specs=(hbm, vmem),
-            scratch_shapes=[
-                pltpu.VMEM((devices, prev_length, LANES), jnp.float32),
-                pltpu.VMEM((chunk, lines, LANES), jnp.float32),
-                pltpu.VMEM((chunk, lines, LANES), jnp.float32),
-                pltpu.VMEM((blocks, segments, LANES), jnp.float32),
-                pltpu.VMEM((segments, width), jnp.float32),
-                pltpu.VMEM((blocks, LANES, width) if devices > chunk else (1, 8, LANES), jnp.float32),
-                pltpu.VMEM((rows_dev, width), jnp.float32),
-                pltpu.SemaphoreType.DMA((pieces,)),
-            ],
-            compiler_params=params if devices == chunk else pltpu.CompilerParams(
-                vmem_limit_bytes=40 * 1024 * 1024),
-            cost_estimate=pl.CostEstimate(flops=1, bytes_accessed=1 << 20, transcendentals=0),
+            scratch_shapes=[pltpu.VMEM((devices, prev_length, LANES), jnp.float32)]
+            + room(chunk) + [pltpu.VMEM((blocks, LANES, width), jnp.float32)] + fresh_room,
+            compiler_params=pltpu.CompilerParams(vmem_limit_bytes=40 * 1024 * 1024),
             name="update",
-        )(*all_groups, kept, row_accum)
-
-    def skip(joined, kept, row_accum):
+        )(*sources, kept, row_accum)
+
+    def hand_over(own, across, kept, row_accum):
+        handed = [forward(x, "dp", 0) for x in across]
+        if devices == chunk and len(handed) == 1:
+            return split_update([*own, *across], handed[0], kept, row_accum)
+        return whole_update([*own, *across, *handed], kept, row_accum)
+
+    def skip(own, across, kept, row_accum):
         return pl.pallas_call(
             pass_kernel,
-            out_shape=(
-                pltpu.HBM((rows_dev, width), jnp.float32),
-                pltpu.VMEM((blocks, LANES), jnp.float32),
-            ),
+            out_shape=updated,
             in_specs=[vmem] * 2,
             out_specs=(hbm, vmem),
             scratch_shapes=[pltpu.SemaphoreType.DMA],
@@ -311,8 +394,7 @@
         )(kept, row_accum)
 
     new_table, new_accum = lax.cond(
-        go[0, 0] > 0, forward_and_update, skip,
-        joined, kept, row_accum.reshape(blocks, LANES))
+        go[0, 0] > 0, hand_over, skip, own, across, kept, row_accum.reshape(blocks, LANES))
 
     pooled, new_accum = pl.pallas_call(
         finish_kernel,

time: 32.7 us -> 28.5 us (0.87)
  waiting for transfers between devices: 9.66 us -> 3.21 us
  starting transfers between devices: 12.4 us -> 14.3 us
    ppermute x3, waiting for transfers between devices: 4.11 us -> 0.01 us  [forward(): lax.ppermute(x, axis, [(i, ((i // 2 + step) * 2 + 1 - i % 2) % size) for...]
    all_to_all x2, waiting for transfers between devices: 5.56 us -> 3.2 us  [exchange(): lax.all_to_all(x, axis, split_axis=0, concat_axis=0, axis_index_groups=[o...]
    all_to_all x2, starting transfers between devices: 10.6 us -> 12.5 us  [exchange(): lax.all_to_all(x, axis, split_axis=0, concat_axis=0, axis_index_groups=[o...]
    pallas_call x2 -> x3, Pallas kernels: 5.26 us -> 5.41 us  [the longest x1 2.27 us: split_update(): pl.pallas_call(functools.partial(apply_kernel, bag_count, lines), out_sha...]
  transfers between devices with their start and end apart: 5 -> 5, of which waited for: 4 -> 1; matrix products, arithmetic and copies ran while one was open for 0% -> 0% of each run, Pallas kernels for 15% -> 18%
where the time goes in v13:
time: 28.5 us; the launch traced here: 28 us
  starting transfers between devices  14.3 us (50%)
  Pallas kernels  9.06 us (32%)
  waiting for transfers between devices  3.21 us (11%)
  between operations  1.37 us (5%)
    all_to_all x2, starting transfers between devices, exchange(): lax.all_to_all(x, axis, split_axis=0, concat_axis=0, axis_index_groups=[o...  12.5 us
    all_to_all x2, waiting for transfers between devices, exchange(): lax.all_to_all(x, axis, split_axis=0, concat_axis=0, axis_index_groups=[o...  3.2 us
    pallas_call x1, Pallas kernels, split_update(): pl.pallas_call(functools.partial(apply_kernel, bag_count, lines), out_sha...  2.27 us
    pallas_call x1, Pallas kernels, local(): pl.pallas_call(functools.partial(pool_kernel, bag_count, lines, back_lead...  1.89 us
    ppermute x3, starting transfers between devices, forward(): lax.ppermute(x, axis, [(i, ((i // 2 + step) * 2 + 1 - i % 2) % size) for...  1.78 us
    pallas_call x1, Pallas kernels, local(): pl.pallas_call(prepare_kernel, out_shape=pltpu.VMEM((rows_dev, width), jn...  1.55 us
    pallas_call x1, Pallas kernels, local(): pl.pallas_call(functools.partial(pack_kernel, rows_dev), out_shape=pltpu....  1.5 us
    pallas_call x1, Pallas kernels, split_update(): pl.pallas_call(functools.partial(count_kernel, bag_count, lines), out_sha...  1.25 us
  transfers between devices with their start and end apart: 5, of which 1 were waited for; matrix products, arithmetic and copies ran while one was open for 0% of the time, Pallas kernels for 18%

profile of v13, /device:TPU:0, one launch (start us, length us, event | category | flops | bytes accessed | tf_op | source)
XLA Modules:
  0.0 28.0 jit_solution(10143770052787707025)
XLA Ops:
  0.6 1.5 %pack.1 = f32[8,24,128]{2,1,0:T(8,128)} custom-call(s32[4,128]{1,0:T(4,128)} %bitcast.14, s32[4,128]{1,0:T(4,128)} %bitcast.15, s32[4,128]{1,0:T(4,128)} %bitcast.16, s32[4,128]{1,0:T(4,128)} %bitcast.17, s32[4,128]{1,0:T(4,128)} %bitcast.18, s32[4,128]{1,0:T(4,128)} %bitcast.19, f32[4,256]{1,0:T(4,128)} %bitcast.13), custom_call_target="tpu_custom_call" | custom-call | tf_op jit(solution)/shard_map/pack/pallas_call | solution.py:269
  2.1 7.8 %all-to-all-start = ((f32[8,24,128]{2,1,0:T(8,128)}), f32[8,24,128]{2,1,0:T(8,128)S(1)}, u32[]{:S(2)}, u32[]{:S(2)}) async-start(f32[8,24,128]{2,1,0:T(8,128)} %pack.1), calls=%async_computation | async-start | bytes 196608 | tf_op jit(solution)/shard_map/all_to_all | solution.py:236
  10.0 1.5 %prepare.1.table = f32[2048,256]{1,0:T(8,128)S(1)} custom-call(f32[2048,256]{1,0:T(8,128)} %table.1), custom_call_target="tpu_custom_call" | custom-call | bytes 4194304 | tf_op jit(solution)/shard_map/prepare/pallas_call | solution.py:285
  11.5 0.0 copy-start
  11.5 3.2 %all-to-all-done.msg = f32[8,24,128]{2,1,0:T(8,128)S(1)} async-done(((f32[8,24,128]{2,1,0:T(8,128)}), f32[8,24,128]{2,1,0:T(8,128)S(1)}, u32[]{:S(2)}, u32[]{:S(2)}) %all-to-all-start) | async-done | bytes 98336 | tf_op jit(solution)/shard_map/all_to_all | solution.py:236
  14.7 1.9 %pool.1 = (f32[8,4,256]{2,1,0:T(4,128)}, f32[8,16,128]{2,1,0:T(8,128)S(1)}, s32[1,1]{1,0:T(1,128)}) custom-call(f32[8,24,128]{2,1,0:T(8,128)S(1)} %all-to-all-done.msg, f32[2048,256]{1,0:T(8,128)S(1)} %prepare.1.table), custom_call_target="tpu_custom_call" | custom-call | flops 67108864 | bytes 2097152 | tf_op jit(solution)/shard_map/pool/pallas_call | solution.py:297
  16.6 0.1 collective-permute-start.2
  16.7 1.6 %collective-permute-start.1 = (f32[8,16,128]{2,1,0:T(8,128)S(1)}, f32[8,16,128]{2,1,0:T(8,128)S(1)}, u32[]{:S(2)}, u32[]{:S(2)}) collective-permute-start(f32[8,16,128]{2,1,0:T(8,128)S(1)} %get-tuple-element.36), channel_id=1, source_target_pairs={{0,24},{8,16},{16,8},{24,0},{1,25},{9,17},{17,9},{25,1},{2,26},{10... | collective-permute-start | bytes 196616 | tf_op jit(solution)/shard_map/ppermute | solution.py:242
  18.3 4.7 %all-to-all-start.1 = ((f32[8,4,256]{2,1,0:T(4,128)}), f32[8,4,256]{2,1,0:T(4,128)S(1)}, u32[]{:S(2)}, u32[]{:S(2)}) async-start(f32[8,4,256]{2,1,0:T(4,128)} %get-tuple-element.34), calls=%async_computation.1 | async-start | bytes 65536 | tf_op jit(solution)/shard_map/all_to_all | solution.py:236
  23.7 0.0 collective-permute-done.2
  23.7 0.0 collective-permute-done.1
  23.7 0.0 copy-done
  23.7 3.6 %conditional.1 = ((f32[2048,256]{1,0:T(8,128)}, f32[16,128]{1,0:T(8,128)S(1)})) conditional(s32[]{:T(128)} %bitcast.7, (f32[2048,256]{1,0:T(8,128)S(1)}, f32[16,128]{1,0:T(8,128)S(1)}) %tuple.21, (f32[8,16,128]{2,1,0:T(8,128)S(1)}, f32[8,16,128]{2,1,0:T(8,128)S(1)}, f32[8,16,128]{2,1,0:T(8,128)S(1)}, f32[2048,256]{1,0:T(8,128)S(1)}, ...), branch_computations={%region_0.0_spmd, %region_1.0_spmd} | conditional | flops 268435456 | bytes 4456496 | solution.py:396
  23.8 0.1 collective-permute-start
  23.8 1.2 %count.1 = (bf16[16,96,128]{2,1,0:T(8,128)(2,1)S(1)}, bf16[96,256]{1,0:T(8,128)(2,1)S(1)}, bf16[96,256]{1,0:T(8,128)(2,1)S(1)}) custom-call(f32[8,16,128]{2,1,0:T(8,128)S(1)} %get-tuple-element.17.refs_0_, f32[8,16,128]{2,1,0:T(8,128)S(1)} %get-tuple-element.18.refs_1_, f32[8,16,128]{2,1,0:T(8,128)S(1)} %get-tuple-element.16.refs_2_), custom_call_target="tpu_custom_call" | custom-call | flops 268435456 | bytes 4194304 | tf_op jit(solution)/shard_map/cond/branch_1_fun/count/pallas_call | solution.py:342
  25.1 0.0 collective-permute-done.refs_0_
  25.1 2.3 %apply.1 = (f32[2048,256]{1,0:T(8,128)}, f32[16,128]{1,0:T(8,128)S(1)}) custom-call(f32[8,16,128]{2,1,0:T(8,128)S(1)} %collective-permute-done.refs_0_, bf16[16,96,128]{2,1,0:T(8,128)(2,1)S(1)} %get-tuple-element.19.refs_1_, bf16[96,256]{1,0:T(8,128)(2,1)S(1)} %get-tuple-element.20.refs_2_, bf16[96,256]{1,0:T(8,128)(2,1)S(1)} %get-tuple-element.21.refs_3_, ...), custom_call_target="tpu_custom_call" | custom-call | tf_op jit(solution)/shard_map/cond/branch_1_fun/apply/pallas_call | solution.py:357
  27.4 0.0 all-to-all-done.1.returned
  27.4 0.6 %finish.1 = (f32[4,256]{1,0:T(4,128)}, f32[16,128]{1,0:T(8,128)}) custom-call(f32[8,4,256]{2,1,0:T(4,128)S(1)} %all-to-all-done.1.returned, f32[16,128]{1,0:T(8,128)S(1)} %get-tuple-element.37.accum), custom_call_target="tpu_custom_call" | custom-call | tf_op jit(solution)/shard_map/finish/pallas_call | solution.py:399
Async XLA Ops:
  2.1 12.6 %all-to-all-start = ((f32[8,24,128]{2,1,0:T(8,128)}), f32[8,24,128]{2,1,0:T(8,128)S(1)}, u32[]{:S(2)}, u32[]{:S(2)}) async-start(f32[8,24,128]{2,1,0:T(8,128)} %pack.1), calls=%async_computation | async-start | bytes 196608 | tf_op jit(solution)/shard_map/all_to_all | solution.py:236
  11.5 12.2 %copy-start = (f32[2048]{0:T(1024)S(1)}, f32[2048]{0:T(1024)}, u32[]{:S(2)}) copy-start(f32[2048]{0:T(1024)} %param.12) | copy-start | bytes 24580
  16.6 7.1 %collective-permute-start.2 = (f32[8,16,128]{2,1,0:T(8,128)S(1)}, f32[8,16,128]{2,1,0:T(8,128)S(1)}, u32[]{:S(2)}, u32[]{:S(2)}) collective-permute-start(f32[8,16,128]{2,1,0:T(8,128)S(1)} %get-tuple-element.36), channel_id=1, source_target_pairs={{0,8},{8,0},{16,24},{24,16},{1,9},{9,1},{17,25},{25,17},{2,10},{10... | collective-permute-start | bytes 196616 | tf_op jit(solution)/shard_map/ppermute | solution.py:242
  16.7 7.0 %collective-permute-start.1 = (f32[8,16,128]{2,1,0:T(8,128)S(1)}, f32[8,16,128]{2,1,0:T(8,128)S(1)}, u32[]{:S(2)}, u32[]{:S(2)}) collective-permute-start(f32[8,16,128]{2,1,0:T(8,128)S(1)} %get-tuple-element.36), channel_id=1, source_target_pairs={{0,24},{8,16},{16,8},{24,0},{1,25},{9,17},{17,9},{25,1},{2,26},{10... | collective-permute-start | bytes 196616 | tf_op jit(solution)/shard_map/ppermute | solution.py:242
  18.3 9.0 %all-to-all-start.1 = ((f32[8,4,256]{2,1,0:T(4,128)}), f32[8,4,256]{2,1,0:T(4,128)S(1)}, u32[]{:S(2)}, u32[]{:S(2)}) async-start(f32[8,4,256]{2,1,0:T(4,128)} %get-tuple-element.34), calls=%async_computation.1 | async-start | bytes 65536 | tf_op jit(solution)/shard_map/all_to_all | solution.py:236
  23.8 1.3 %collective-permute-start = (f32[8,16,128]{2,1,0:T(8,128)S(1)}, f32[8,16,128]{2,1,0:T(8,128)S(1)}, u32[]{:S(2)}, u32[]{:S(2)}) collective-permute-start(f32[8,16,128]{2,1,0:T(8,128)S(1)} %get-tuple-element.16.refs_2_), channel_id=1, source_target_pairs={{0,8},{8,0},{16,24},{24,16},{1,9},{9,1},{17,25},{25,17},{2,10},{10... | collective-permute-start | bytes 196616 | tf_op jit(solution)/shard_map/cond/branch_1_fun/ppermute | solution.py:242

commit v14 on v13

--- a/solution.py
+++ b/solution.py
@@ -168,11 +168,14 @@
     high[...], low[...] = split_two(grads[...])
 
 
-def apply_kernel(bag_count, lines, *refs):
-    msg, counted, high, low, table, accum, new_table, new_accum = refs[:8]
-    code_ref, lane_ref, counts, grads, fresh_table, sems = refs[8:]
+def apply_kernel(bag_count, lines, late, *refs):
+    sources, (counted, high, low, table, accum) = refs[:late], refs[late:late + 5]
+    new_table, new_accum, msg, code_ref, lane_ref, counts, grads, fresh_table, sems = refs[late + 5:]
+    owners = sources[0].shape[0]
     devices, blocks = msg.shape[0], counts.shape[0]
     base = lax.axis_index("rows") * (blocks * LANES)
+    for i, source in enumerate(sources):
+        msg[i * owners:(i + 1) * owners] = source[...]
     read_chunk(
         msg, slice(0, devices), devices, lines, bag_count, base,
         code_ref, lane_ref, counts, grads)
@@ -315,10 +318,10 @@
         name="pool",
     )(gathered, kept)
     returned = exchange(partial_pooled, "rows", back_leader)
-    own = [joined, forward(joined, "dp", 0)]
-    across = [forward(joined, "dp", step) for step in range(1, groups // 2)]
+    there = [joined] + [forward(joined, "dp", step) for step in range(1, groups // 2)]
 
     segments = chunk * bag_count
+    results = 8 if blocks % 8 == 0 else 1
     updated = (
         pltpu.HBM((rows_dev, width), jnp.float32),
         pltpu.VMEM((blocks, LANES), jnp.float32),
@@ -334,7 +337,7 @@
 
     fresh_room = [
         pltpu.VMEM((rows_dev, width), jnp.float32),
-        pltpu.SemaphoreType.DMA((pieces,)),
+        pltpu.SemaphoreType.DMA((results,)),
     ]
 
     def split_update(early, late, kept, row_accum):
@@ -355,14 +358,15 @@
             name="count",
         )(*early)
         return pl.pallas_call(
-            functools.partial(apply_kernel, bag_count, lines),
+            functools.partial(apply_kernel, bag_count, lines, len(late)),
             out_shape=updated,
-            in_specs=[vmem] * 6,
+            in_specs=[vmem] * (len(late) + 5),
             out_specs=(hbm, vmem),
-            scratch_shapes=room(owners) + fresh_room,
+            scratch_shapes=[pltpu.VMEM((count, prev_length, LANES), jnp.float32)]
+            + room(count) + fresh_room,
             compiler_params=params,
             name="apply",
-        )(late, *counted, kept, row_accum)
+        )(*late, *counted, kept, row_accum)
 
     def whole_update(sources, kept, row_accum):
         return pl.pallas_call(
@@ -376,13 +380,13 @@
             name="update",
         )(*sources, kept, row_accum)
 
-    def hand_over(own, across, kept, row_accum):
-        handed = [forward(x, "dp", 0) for x in across]
-        if devices == chunk and len(handed) == 1:
-            return split_update([*own, *across], handed[0], kept, row_accum)
-        return whole_update([*own, *across, *handed], kept, row_accum)
-
-    def skip(own, across, kept, row_accum):
+    def hand_over(there, kept, row_accum):
+        handed = [forward(x, "dp", 0) for x in there]
+        if devices == chunk:
+            return split_update(there, handed, kept, row_accum)
+        return whole_update([*there, *handed], kept, row_accum)
+
+    def skip(there, kept, row_accum):
         return pl.pallas_call(
             pass_kernel,
             out_shape=updated,
@@ -394,7 +398,7 @@
         )(kept, row_accum)
 
     new_table, new_accum = lax.cond(
-        go[0, 0] > 0, hand_over, skip, own, across, kept, row_accum.reshape(blocks, LANES))
+        go[0, 0] > 0, hand_over, skip, there, kept, row_accum.reshape(blocks, LANES))
 
     pooled, new_accum = pl.pallas_call(
         finish_kernel,

time: 28.5 us -> 28.1 us (0.986)
  starting transfers between devices: 14.3 us -> 13.8 us
    ppermute x3, starting transfers between devices: 1.78 us -> 1.27 us  [forward(): lax.ppermute(x, axis, [(i, ((i // 2 + step) * 2 + 1 - i % 2) % size) for...]
    pallas_call x1, Pallas kernels: 1.25 us -> 0.88 us  [split_update(): pl.pallas_call(functools.partial(count_kernel, bag_count, lines), out_sha...]
    pallas_call x1, Pallas kernels: 2.27 us -> 2.6 us  [split_update(): pl.pallas_call(functools.partial(apply_kernel, bag_count, lines, len(late...]
  transfers between devices with their start and end apart: 5 -> 5, of which waited for: 1 -> 2; matrix products, arithmetic and copies ran while one was open for 0% -> 0% of each run, Pallas kernels for 18% -> 18%
where the time goes in v14:
time: 28.1 us; the launch traced here: 27.7 us
  starting transfers between devices  13.8 us (49%)
  Pallas kernels  9.02 us (32%)
  waiting for transfers between devices  3.48 us (12%)
  between operations  1.36 us (5%)
    all_to_all x2, starting transfers between devices, exchange(): lax.all_to_all(x, axis, split_axis=0, concat_axis=0, axis_index_groups=[o...  12.5 us
    all_to_all x2, waiting for transfers between devices, exchange(): lax.all_to_all(x, axis, split_axis=0, concat_axis=0, axis_index_groups=[o...  3.2 us
    pallas_call x1, Pallas kernels, split_update(): pl.pallas_call(functools.partial(apply_kernel, bag_count, lines, len(late...  2.6 us
    pallas_call x1, Pallas kernels, local(): pl.pallas_call(functools.partial(pool_kernel, bag_count, lines, back_lead...  1.89 us
    pallas_call x1, Pallas kernels, local(): pl.pallas_call(prepare_kernel, out_shape=pltpu.VMEM((rows_dev, width), jn...  1.55 us
    pallas_call x1, Pallas kernels, local(): pl.pallas_call(functools.partial(pack_kernel, rows_dev), out_shape=pltpu....  1.5 us
    ppermute x3, starting transfers between devices, forward(): lax.ppermute(x, axis, [(i, ((i // 2 + step) * 2 + 1 - i % 2) % size) for...  1.27 us
    pallas_call x1, Pallas kernels, split_update(): pl.pallas_call(functools.partial(count_kernel, bag_count, lines), out_sha...  0.88 us
  transfers between devices with their start and end apart: 5, of which 2 were waited for; matrix products, arithmetic and copies ran while one was open for 0% of the time, Pallas kernels for 18%

profile of v14, /device:TPU:0, one launch (start us, length us, event | category | flops | bytes accessed | tf_op | source)
XLA Modules:
  0.0 27.7 jit_solution(9051896552066236419)
XLA Ops:
  0.6 1.5 %pack.1 = f32[8,24,128]{2,1,0:T(8,128)} custom-call(s32[4,128]{1,0:T(4,128)} %bitcast.14, s32[4,128]{1,0:T(4,128)} %bitcast.15, s32[4,128]{1,0:T(4,128)} %bitcast.16, s32[4,128]{1,0:T(4,128)} %bitcast.17, s32[4,128]{1,0:T(4,128)} %bitcast.18, s32[4,128]{1,0:T(4,128)} %bitcast.19, f32[4,256]{1,0:T(4,128)} %bitcast.13), custom_call_target="tpu_custom_call" | custom-call | tf_op jit(solution)/shard_map/pack/pallas_call | solution.py:272
  2.1 7.8 %all-to-all-start = ((f32[8,24,128]{2,1,0:T(8,128)}), f32[8,24,128]{2,1,0:T(8,128)S(1)}, u32[]{:S(2)}, u32[]{:S(2)}) async-start(f32[8,24,128]{2,1,0:T(8,128)} %pack.1), calls=%async_computation | async-start | bytes 196608 | tf_op jit(solution)/shard_map/all_to_all | solution.py:239
  10.0 1.5 %prepare.1.table = f32[2048,256]{1,0:T(8,128)S(1)} custom-call(f32[2048,256]{1,0:T(8,128)} %table.1), custom_call_target="tpu_custom_call" | custom-call | bytes 4194304 | tf_op jit(solution)/shard_map/prepare/pallas_call | solution.py:288
  11.5 0.0 copy-start
  11.5 3.2 %all-to-all-done.msg = f32[8,24,128]{2,1,0:T(8,128)S(1)} async-done(((f32[8,24,128]{2,1,0:T(8,128)}), f32[8,24,128]{2,1,0:T(8,128)S(1)}, u32[]{:S(2)}, u32[]{:S(2)}) %all-to-all-start) | async-done | bytes 98336 | tf_op jit(solution)/shard_map/all_to_all | solution.py:239
  14.7 1.9 %pool.1 = (f32[8,4,256]{2,1,0:T(4,128)}, f32[8,16,128]{2,1,0:T(8,128)S(1)}, s32[1,1]{1,0:T(1,128)}) custom-call(f32[8,24,128]{2,1,0:T(8,128)S(1)} %all-to-all-done.msg, f32[2048,256]{1,0:T(8,128)S(1)} %prepare.1.table), custom_call_target="tpu_custom_call" | custom-call | flops 67108864 | bytes 2097152 | tf_op jit(solution)/shard_map/pool/pallas_call | solution.py:300
  16.6 0.1 collective-permute-start.2
  16.7 4.7 %all-to-all-start.1 = ((f32[8,4,256]{2,1,0:T(4,128)}), f32[8,4,256]{2,1,0:T(4,128)S(1)}, u32[]{:S(2)}, u32[]{:S(2)}) async-start(f32[8,4,256]{2,1,0:T(4,128)} %get-tuple-element.31), calls=%async_computation.1 | async-start | bytes 65536 | tf_op jit(solution)/shard_map/all_to_all | solution.py:239
  22.1 0.0 collective-permute-done.2
  22.1 0.0 copy-done
  22.1 5.0 %conditional.1 = ((f32[2048,256]{1,0:T(8,128)}, f32[16,128]{1,0:T(8,128)S(1)})) conditional(s32[]{:T(128)} %bitcast.7, (f32[2048,256]{1,0:T(8,128)S(1)}, f32[16,128]{1,0:T(8,128)S(1)}) %tuple.21, (f32[8,16,128]{2,1,0:T(8,128)S(1)}, f32[8,16,128]{2,1,0:T(8,128)S(1)}, f32[2048,256]{1,0:T(8,128)S(1)}, f32[16,128]{1,0:T(8,128)S(1)}) %tuple.22), branch_computations={%region_0.0_spmd, %region_1.0_spmd} | conditional | flops 268435456 | bytes 4718680 | solution.py:400
  22.1 1.1 %collective-permute-start = (f32[8,16,128]{2,1,0:T(8,128)S(1)}, f32[8,16,128]{2,1,0:T(8,128)S(1)}, u32[]{:S(2)}, u32[]{:S(2)}) collective-permute-start(f32[8,16,128]{2,1,0:T(8,128)S(1)} %get-tuple-element.14.refs_0_), channel_id=1, source_target_pairs={{0,8},{8,0},{16,24},{24,16},{1,9},{9,1},{17,25},{25,17},{2,10},{10... | collective-permute-start | bytes 196616 | tf_op jit(solution)/shard_map/cond/branch_1_fun/ppermute | solution.py:245
  23.2 0.1 collective-permute-start.1
  23.3 0.9 %count.1 = (bf16[16,64,128]{2,1,0:T(8,128)(2,1)S(1)}, bf16[64,256]{1,0:T(8,128)(2,1)S(1)}, bf16[64,256]{1,0:T(8,128)(2,1)S(1)}) custom-call(f32[8,16,128]{2,1,0:T(8,128)S(1)} %get-tuple-element.14.refs_0_, f32[8,16,128]{2,1,0:T(8,128)S(1)} %get-tuple-element.15.refs_1_), custom_call_target="tpu_custom_call" | custom-call | flops 268435456 | bytes 4194304 | tf_op jit(solution)/shard_map/cond/branch_1_fun/count/pallas_call | solution.py:345
  24.2 0.0 collective-permute-done.refs_0_
  24.2 0.3 %collective-permute-done.1.refs_1_ = f32[8,16,128]{2,1,0:T(8,128)S(1)} collective-permute-done((f32[8,16,128]{2,1,0:T(8,128)S(1)}, f32[8,16,128]{2,1,0:T(8,128)S(1)}, u32[]{:S(2)}, u32[]{:S(2)}) %collective-permute-start.1) | collective-permute-done | bytes 65568 | tf_op jit(solution)/shard_map/cond/branch_1_fun/ppermute | solution.py:245
  24.5 2.6 %apply.1 = (f32[2048,256]{1,0:T(8,128)}, f32[16,128]{1,0:T(8,128)S(1)}) custom-call(f32[8,16,128]{2,1,0:T(8,128)S(1)} %collective-permute-done.refs_0_, f32[8,16,128]{2,1,0:T(8,128)S(1)} %collective-permute-done.1.refs_1_, bf16[16,64,128]{2,1,0:T(8,128)(2,1)S(1)} %get-tuple-element.16.refs_2_, bf16[64,256]{1,0:T(8,128)(2,1)S(1)} %get-tuple-element.17.refs_3_, ...), custom_call_target="tpu_custom_call" | custom-call | tf_op jit(solution)/shard_map/cond/branch_1_fun/apply/pallas_call | solution.py:360
  27.1 0.0 all-to-all-done.1.returned
  27.1 0.6 %finish.1 = (f32[4,256]{1,0:T(4,128)}, f32[16,128]{1,0:T(8,128)}) custom-call(f32[8,4,256]{2,1,0:T(4,128)S(1)} %all-to-all-done.1.returned, f32[16,128]{1,0:T(8,128)S(1)} %get-tuple-element.34.accum), custom_call_target="tpu_custom_call" | custom-call | tf_op jit(solution)/shard_map/finish/pallas_call | solution.py:403
Async XLA Ops:
  2.1 12.6 %all-to-all-start = ((f32[8,24,128]{2,1,0:T(8,128)}), f32[8,24,128]{2,1,0:T(8,128)S(1)}, u32[]{:S(2)}, u32[]{:S(2)}) async-start(f32[8,24,128]{2,1,0:T(8,128)} %pack.1), calls=%async_computation | async-start | bytes 196608 | tf_op jit(solution)/shard_map/all_to_all | solution.py:239
  11.5 10.6 %copy-start = (f32[2048]{0:T(1024)S(1)}, f32[2048]{0:T(1024)}, u32[]{:S(2)}) copy-start(f32[2048]{0:T(1024)} %param.12) | copy-start | bytes 24580
  16.6 5.4 %collective-permute-start.2 = (f32[8,16,128]{2,1,0:T(8,128)S(1)}, f32[8,16,128]{2,1,0:T(8,128)S(1)}, u32[]{:S(2)}, u32[]{:S(2)}) collective-permute-start(f32[8,16,128]{2,1,0:T(8,128)S(1)} %get-tuple-element.33), channel_id=1, source_target_pairs={{0,24},{8,16},{16,8},{24,0},{1,25},{9,17},{17,9},{25,1},{2,26},{10... | collective-permute-start | bytes 196616 | tf_op jit(solution)/shard_map/ppermute | solution.py:245
  16.7 10.4 %all-to-all-start.1 = ((f32[8,4,256]{2,1,0:T(4,128)}), f32[8,4,256]{2,1,0:T(4,128)S(1)}, u32[]{:S(2)}, u32[]{:S(2)}) async-start(f32[8,4,256]{2,1,0:T(4,128)} %get-tuple-element.31), calls=%async_computation.1 | async-start | bytes 65536 | tf_op jit(solution)/shard_map/all_to_all | solution.py:239
  22.1 2.1 %collective-permute-start = (f32[8,16,128]{2,1,0:T(8,128)S(1)}, f32[8,16,128]{2,1,0:T(8,128)S(1)}, u32[]{:S(2)}, u32[]{:S(2)}) collective-permute-start(f32[8,16,128]{2,1,0:T(8,128)S(1)} %get-tuple-element.14.refs_0_), channel_id=1, source_target_pairs={{0,8},{8,0},{16,24},{24,16},{1,9},{9,1},{17,25},{25,17},{2,10},{10... | collective-permute-start | bytes 196616 | tf_op jit(solution)/shard_map/cond/branch_1_fun/ppermute | solution.py:245
  23.2 1.3 %collective-permute-start.1 = (f32[8,16,128]{2,1,0:T(8,128)S(1)}, f32[8,16,128]{2,1,0:T(8,128)S(1)}, u32[]{:S(2)}, u32[]{:S(2)}) collective-permute-start(f32[8,16,128]{2,1,0:T(8,128)S(1)} %get-tuple-element.15.refs_1_), channel_id=1, source_target_pairs={{0,8},{8,0},{16,24},{24,16},{1,9},{9,1},{17,25},{25,17},{2,10},{10... | collective-permute-start | bytes 196616 | tf_op jit(solution)/shard_map/cond/branch_1_fun/ppermute | solution.py:245

commit v15 on v12

--- a/solution.py
+++ b/solution.py
@@ -102,13 +102,19 @@
         out[i] = total[seen * bag_count:(seen + 1) * bag_count, :]
 
 
-def update_kernel(bag_count, lines, groups, chunk, *refs):
-    sources, (table, accum, new_table, new_accum) = refs[:groups], refs[groups:groups + 4]
-    msg, code_ref, lane_ref, counts, grads, sums, fresh_table, sems = refs[groups + 4:]
+def join_kernel(joined, swapped, both):
+    devices, length, _ = joined.shape
+    both[0:devices] = joined[...]
+    both[devices:] = swapped[:, swapped.shape[1] - length:, :]
+
+
+def update_kernel(bag_count, lines, pairs, chunk, *refs):
+    sources, (table, accum, new_table, new_accum) = refs[:pairs], refs[pairs:pairs + 4]
+    msg, code_ref, lane_ref, counts, grads, sums, fresh_table, sems = refs[pairs + 4:]
     rows_dev, width = table.shape
     pieces = sems.shape[0]
     devices = msg.shape[0]
-    owners = devices // groups
+    per_source = devices // pairs
     blocks = counts.shape[0]
     base = lax.axis_index("rows") * rows_dev
     single = devices == chunk
@@ -133,7 +139,7 @@
         return total
 
     for i, source in enumerate(sources):
-        msg[i * owners:(i + 1) * owners] = source[...]
+        msg[i * per_source:(i + 1) * per_source] = source[...]
     if single:
         parts = count_chunk(0)
     else:
@@ -192,9 +198,10 @@
         x, axis, split_axis=0, concat_axis=0, axis_index_groups=[order], tiled=True)
 
 
-def shift(x, axis, step):
+def forward(x, axis, step):
     size = lax.axis_size(axis)
-    return lax.ppermute(x, axis, [(i, (i + step) % size) for i in range(size)])
+    return lax.ppermute(
+        x, axis, [(i, ((i // 2 + step) * 2 + 1 - i % 2) % size) for i in range(size)])
 
 
 def local(
@@ -235,6 +242,8 @@
     )])
     gathered = exchange(message, "rows", out_leader)
 
+    swapped = forward(gathered, "dp", 0)
+
     pieces = 4
     kept = pl.pallas_call(
         prepare_kernel,
@@ -268,16 +277,25 @@
         name="pool",
     )(gathered, kept)
     returned = exchange(partial_pooled, "rows", back_leader)
-    all_groups = [joined] + [shift(joined, "dp", k) for k in range(1, groups)]
+    both = pl.pallas_call(
+        join_kernel,
+        out_shape=pltpu.VMEM((2 * owners, prev_length, LANES), jnp.float32),
+        in_specs=[vmem] * 2,
+        out_specs=vmem,
+        compiler_params=params,
+        name="join",
+    )(joined, swapped)
+    pairs = groups // 2
+    sources = [both] + [forward(both, "dp", step) for step in range(1, pairs)]
 
     segments = chunk * bag_count
     new_table, new_accum = pl.pallas_call(
-        functools.partial(update_kernel, bag_count, lines, groups, chunk),
+        functools.partial(update_kernel, bag_count, lines, pairs, chunk),
         out_shape=(
             jax.ShapeDtypeStruct((rows_dev, width), jnp.float32),
             pltpu.VMEM((blocks, LANES), jnp.float32),
         ),
-        in_specs=[vmem] * (groups + 2),
+        in_specs=[vmem] * (pairs + 2),
         out_specs=(hbm, vmem),
         scratch_shapes=[
             pltpu.VMEM((devices, prev_length, LANES), jnp.float32),
@@ -293,7 +311,7 @@
             vmem_limit_bytes=40 * 1024 * 1024),
         cost_estimate=pl.CostEstimate(flops=1, bytes_accessed=1 << 20, transcendentals=0),
         name="update",
-    )(*all_groups, kept, row_accum.reshape(blocks, LANES))
+    )(*sources, kept, row_accum.reshape(blocks, LANES))
 
     pooled, new_accum = pl.pallas_call(
         finish_kernel,

time: 28.4 us -> 29 us (1.021)
  blocking collectives: 0 us -> 12.4 us
  starting transfers between devices: 14.3 us -> 6.4 us
  waiting for transfers between devices: 4.12 us -> 0.94 us
  Pallas kernels: 8.91 us -> 8.27 us
    all_to_all x0 -> x1, blocking collectives: none -> 12.4 us  [exchange(): lax.all_to_all(x, axis, split_axis=0, concat_axis=0, axis_index_groups=[o...]
    all_to_all x2 -> x1, starting transfers between devices: 12.6 us -> 4.7 us  [exchange(): lax.all_to_all(x, axis, split_axis=0, concat_axis=0, axis_index_groups=[o...]
    all_to_all x2 -> x1, waiting for transfers between devices: 4.11 us -> 0.93 us  [exchange(): lax.all_to_all(x, axis, split_axis=0, concat_axis=0, axis_index_groups=[o...]
    pallas_call x1, Pallas kernels: 1.5 us -> 0.86 us  [local(): pl.pallas_call(functools.partial(pack_kernel, rows_dev), out_shape=pltpu....]
    ppermute x3 -> x2, starting transfers between devices: 1.75 us -> 1.7 us  [forward(): lax.ppermute(x, axis, [(i, ((i // 2 + step) * 2 + 1 - i % 2) % size) for...]
    pallas_call x1 -> x2, Pallas kernels: 3.37 us -> 3.38 us  [the longest x1 3.37 us: local(): pl.pallas_call(functools.partial(update_kernel, bag_count, lines, pairs,...]
  transfers between devices with their start and end apart: 5 -> 3, of which waited for: 2 -> 1; matrix products, arithmetic and copies ran while one was open for 0% -> 0% of each run, Pallas kernels for 18% -> 24%
where the time goes in v15:
time: 29 us; the launch traced here: 28.7 us
  blocking collectives  12.4 us (43%)
  Pallas kernels  8.27 us (29%)
  starting transfers between devices  6.4 us (22%)
  waiting for transfers between devices  0.94 us (3%)
  between operations  0.68 us (2%)
    all_to_all x1, blocking collectives, exchange(): lax.all_to_all(x, axis, split_axis=0, concat_axis=0, axis_index_groups=[o...  12.4 us
    all_to_all x1, starting transfers between devices, exchange(): lax.all_to_all(x, axis, split_axis=0, concat_axis=0, axis_index_groups=[o...  4.7 us
    pallas_call x1, Pallas kernels, local(): pl.pallas_call(functools.partial(update_kernel, bag_count, lines, pairs,...  3.37 us
    pallas_call x1, Pallas kernels, local(): pl.pallas_call(functools.partial(pool_kernel, bag_count, lines, back_lead...  1.87 us
    ppermute x2, starting transfers between devices, forward(): lax.ppermute(x, axis, [(i, ((i // 2 + step) * 2 + 1 - i % 2) % size) for...  1.7 us
    pallas_call x1, Pallas kernels, local(): pl.pallas_call(prepare_kernel, out_shape=pltpu.VMEM((rows_dev, width), jn...  1.55 us
    all_to_all x1, waiting for transfers between devices, exchange(): lax.all_to_all(x, axis, split_axis=0, concat_axis=0, axis_index_groups=[o...  0.93 us
    pallas_call x1, Pallas kernels, local(): pl.pallas_call(functools.partial(pack_kernel, rows_dev), out_shape=pltpu....  0.86 us
  transfers between devices with their start and end apart: 3, of which 1 were waited for; matrix products, arithmetic and copies ran while one was open for 0% of the time, Pallas kernels for 24%

profile of v15, /device:TPU:0, one launch (start us, length us, event | category | flops | bytes accessed | tf_op | source)
XLA Modules:
  0.0 28.7 jit_solution(11398779276761388776)
XLA Ops:
  0.6 0.9 %pack.1 = f32[8,24,128]{2,1,0:T(8,128)S(1)} custom-call(s32[4,128]{1,0:T(4,128)} %bitcast.12, s32[4,128]{1,0:T(4,128)} %bitcast.13, s32[4,128]{1,0:T(4,128)} %bitcast.14, s32[4,128]{1,0:T(4,128)} %bitcast.15, s32[4,128]{1,0:T(4,128)} %bitcast.16, s32[4,128]{1,0:T(4,128)} %bitcast.17, f32[4,256]{1,0:T(4,128)} %bitcast.11), custom_call_target="tpu_custom_call" | custom-call | tf_op jit(solution)/shard_map/pack/pallas_call | solution.py:230
  1.5 12.4 %all_to_all.10.msg = f32[8,24,128]{2,1,0:T(8,128)S(1)} all-to-all(f32[8,24,128]{2,1,0:T(8,128)S(1)} %pack.1), channel_id=1, replica_groups={{3,4,5,6,7,0,1,2},{11,12,13,14,15,8,9,10},{19,20,21,22,23,16,17,18},{27..., dimensions={0} | all-to-all | bytes 196608 | tf_op jit(solution)/shard_map/all_to_all | solution.py:197
  13.9 0.0 collective-permute-start
  13.9 1.5 %prepare.1.table.refs_2_ = f32[2048,256]{1,0:T(8,128)S(1)} custom-call(f32[2048,256]{1,0:T(8,128)} %table.1), custom_call_target="tpu_custom_call" | custom-call | bytes 4194304 | tf_op jit(solution)/shard_map/prepare/pallas_call | solution.py:248
  15.4 0.0 copy-start
  15.4 1.9 %pool.1 = (f32[8,4,256]{2,1,0:T(4,128)}, f32[8,16,128]{2,1,0:T(8,128)S(1)}) custom-call(f32[8,24,128]{2,1,0:T(8,128)S(1)} %all_to_all.10.msg, f32[2048,256]{1,0:T(8,128)S(1)} %prepare.1.table.refs_2_), custom_call_target="tpu_custom_call" | custom-call | flops 67108864 | bytes 2097152 | tf_op jit(solution)/shard_map/pool/pallas_call | solution.py:260
  17.3 0.0 collective-permute-done.swapped
  17.3 1.7 %collective-permute-start.1 = (f32[16,16,128]{2,1,0:T(8,128)S(1)}, f32[16,16,128]{2,1,0:T(8,128)S(1)}, u32[]{:S(2)}, u32[]{:S(2)}) collective-permute-start(f32[16,16,128]{2,1,0:T(8,128)S(1)} %join.1.refs_0_), channel_id=1, source_target_pairs={{0,24},{8,16},{16,8},{24,0},{1,25},{9,17},{17,9},{25,1},{2,26},{10... | collective-permute-start | bytes 393224 | tf_op jit(solution)/shard_map/ppermute | solution.py:203
  19.0 4.7 %all-to-all-start.1 = ((f32[8,4,256]{2,1,0:T(4,128)}), f32[8,4,256]{2,1,0:T(4,128)S(1)}, u32[]{:S(2)}, u32[]{:S(2)}) async-start(f32[8,4,256]{2,1,0:T(4,128)} %get-tuple-element.9), calls=%async_computation.1 | async-start | bytes 65536 | tf_op jit(solution)/shard_map/all_to_all | solution.py:197
  23.7 0.0 collective-permute-done.1.refs_1_
  23.7 0.0 copy-done
  23.7 3.4 %update.1 = (f32[2048,256]{1,0:T(8,128)}, f32[16,128]{1,0:T(8,128)S(1)}) custom-call(f32[16,16,128]{2,1,0:T(8,128)S(1)} %join.1.refs_0_, f32[16,16,128]{2,1,0:T(8,128)S(1)} %collective-permute-done.1.refs_1_, f32[2048,256]{1,0:T(8,128)S(1)} %prepare.1.table.refs_2_, f32[16,128]{1,0:T(8,128)S(1)} %bitcast.10), custom_call_target="tpu_custom_call" | custom-call | flops 1 | bytes 1048576 | tf_op jit(solution)/shard_map/update/pallas_call | solution.py:292
  27.1 0.9 %all-to-all-done.1.returned = f32[8,4,256]{2,1,0:T(4,128)S(1)} async-done(((f32[8,4,256]{2,1,0:T(4,128)}), f32[8,4,256]{2,1,0:T(4,128)S(1)}, u32[]{:S(2)}, u32[]{:S(2)}) %all-to-all-start.1) | async-done | bytes 32800 | tf_op jit(solution)/shard_map/all_to_all | solution.py:197
  28.1 0.6 %finish.1 = (f32[4,256]{1,0:T(4,128)}, f32[16,128]{1,0:T(8,128)}) custom-call(f32[8,4,256]{2,1,0:T(4,128)S(1)} %all-to-all-done.1.returned, f32[16,128]{1,0:T(8,128)S(1)} %get-tuple-element.11.accum), custom_call_target="tpu_custom_call" | custom-call | tf_op jit(solution)/shard_map/finish/pallas_call | solution.py:316
  (1 shorter events, 0.0 us)
Async XLA Ops:
  13.9 3.4 %collective-permute-start = (f32[8,24,128]{2,1,0:T(8,128)S(1)}, f32[8,24,128]{2,1,0:T(8,128)S(1)}, u32[]{:S(2)}, u32[]{:S(2)}) collective-permute-start(f32[8,24,128]{2,1,0:T(8,128)S(1)} %all_to_all.10.msg), channel_id=1, source_target_pairs={{0,8},{8,0},{16,24},{24,16},{1,9},{9,1},{17,25},{25,17},{2,10},{10... | collective-permute-start | bytes 294920 | tf_op jit(solution)/shard_map/ppermute | solution.py:203
  15.4 8.3 %copy-start = (f32[2048]{0:T(1024)S(1)}, f32[2048]{0:T(1024)}, u32[]{:S(2)}) copy-start(f32[2048]{0:T(1024)} %param.10) | copy-start | bytes 24580
  17.3 6.4 %collective-permute-start.1 = (f32[16,16,128]{2,1,0:T(8,128)S(1)}, f32[16,16,128]{2,1,0:T(8,128)S(1)}, u32[]{:S(2)}, u32[]{:S(2)}) collective-permute-start(f32[16,16,128]{2,1,0:T(8,128)S(1)} %join.1.refs_0_), channel_id=1, source_target_pairs={{0,24},{8,16},{16,8},{24,0},{1,25},{9,17},{17,9},{25,1},{2,26},{10... | collective-permute-start | bytes 393224 | tf_op jit(solution)/shard_map/ppermute | solution.py:203
  19.0 9.0 %all-to-all-start.1 = ((f32[8,4,256]{2,1,0:T(4,128)}), f32[8,4,256]{2,1,0:T(4,128)S(1)}, u32[]{:S(2)}, u32[]{:S(2)}) async-start(f32[8,4,256]{2,1,0:T(4,128)} %get-tuple-element.9), calls=%async_computation.1 | async-start | bytes 65536 | tf_op jit(solution)/shard_map/all_to_all | solution.py:197

commit v16 on v12

--- a/solution.py
+++ b/solution.py
@@ -42,20 +42,6 @@
     return high, (x - high.astype(jnp.float32)).astype(jnp.bfloat16)
 
 
-def prepare_kernel(table, kept, sems):
-    pieces = sems.shape[0]
-    rows = table.shape[0] // pieces
-    copies = [
-        pltpu.make_async_copy(
-            table.at[pl.ds(i * rows, rows), :], kept.at[pl.ds(i * rows, rows), :], sems.at[i])
-        for i in range(pieces)
-    ]
-    for copy in copies:
-        copy.start()
-    for copy in copies:
-        copy.wait()
-
-
 def codes(ids, bags, bag_count, base):
     rel = ids.astype(jnp.int32) - base
     code = lax.shift_right_arithmetic(rel, 7) * bag_count + bags.astype(jnp.int32)
@@ -83,8 +69,18 @@
             blocks, bag_count, LANES)
 
 
-def pool_kernel(bag_count, lines, turn, msg, table, out, joined, code_ref, lane_ref, counts):
+def pool_kernel(
+    bag_count, lines, turn, msg, table, out, joined, kept, code_ref, lane_ref, counts, sems,
+):
     rows_dev, width = table.shape
+    rows = rows_dev // sems.shape[0]
+    fetches = [
+        pltpu.make_async_copy(
+            table.at[pl.ds(i * rows, rows), :], kept.at[pl.ds(i * rows, rows), :], sems.at[i])
+        for i in range(sems.shape[0])
+    ]
+    for fetch in fetches:
+        fetch.start()
     owners = msg.shape[0]
     base = lax.axis_index("rows") * rows_dev
     code_ref[...], lane_ref[...] = codes(
@@ -95,8 +91,11 @@
     flat = jnp.concatenate(
         [counts[h].astype(jnp.bfloat16) for h in range(blocks)], axis=1)
     total = jnp.zeros((owners * bag_count, width), jnp.float32)
-    for part in split_two(table[...]):
-        total += jnp.dot(flat, part, preferred_element_type=jnp.float32)
+    for i, fetch in enumerate(fetches):
+        fetch.wait()
+        here = slice(i * rows, (i + 1) * rows)
+        for part in split_two(kept[here, :]):
+            total += jnp.dot(flat[:, here], part, preferred_element_type=jnp.float32)
     for i in range(owners):
         seen = (i + turn) % owners
         out[i] = total[seen * bag_count:(seen + 1) * bag_count, :]
@@ -236,37 +235,27 @@
     gathered = exchange(message, "rows", out_leader)
 
     pieces = 4
-    kept = pl.pallas_call(
-        prepare_kernel,
-        out_shape=pltpu.VMEM((rows_dev, width), jnp.float32),
-        in_specs=[hbm],
-        out_specs=vmem,
-        scratch_shapes=[pltpu.SemaphoreType.DMA((pieces,))],
-        compiler_params=params,
-        cost_estimate=pl.CostEstimate(
-            flops=0, bytes_accessed=2 * rows_dev * width * 4, transcendentals=0),
-        name="prepare",
-    )(stay(item_table))
-
-    partial_pooled, joined = pl.pallas_call(
+    partial_pooled, joined, kept = pl.pallas_call(
         functools.partial(pool_kernel, bag_count, lines, back_leader - out_leader),
         out_shape=(
             pltpu.VMEM((owners, bag_count, width), jnp.float32),
             pltpu.VMEM((owners, prev_length, LANES), jnp.float32),
+            pltpu.VMEM((rows_dev, width), jnp.float32),
         ),
-        in_specs=[vmem] * 2,
-        out_specs=[vmem] * 2,
+        in_specs=[vmem, hbm],
+        out_specs=[vmem] * 3,
         scratch_shapes=[
             pltpu.VMEM((owners, lines, LANES), jnp.float32),
             pltpu.VMEM((owners, lines, LANES), jnp.float32),
             pltpu.VMEM((blocks, owners * bag_count, LANES), jnp.float32),
+            pltpu.SemaphoreType.DMA((pieces,)),
         ],
         compiler_params=params,
         cost_estimate=pl.CostEstimate(
             flops=4 * owners * bag_count * rows_dev * width,
             bytes_accessed=rows_dev * width * 4, transcendentals=0),
         name="pool",
-    )(gathered, kept)
+    )(gathered, stay(item_table))
     returned = exchange(partial_pooled, "rows", back_leader)
     all_groups = [joined] + [shift(joined, "dp", k) for k in range(1, groups)]
 

time: 28.4 us -> 28.1 us (0.989)
  blocking collectives: 0 us -> 12.4 us
  starting transfers between devices: 14.3 us -> 6.51 us
  waiting for transfers between devices: 4.12 us -> 0.92 us
  Pallas kernels: 8.91 us -> 7.26 us
    all_to_all x0 -> x1, blocking collectives: none -> 12.4 us  [exchange(): lax.all_to_all(x, axis, split_axis=0, concat_axis=0, axis_index_groups=[o...]
    all_to_all x2 -> x1, starting transfers between devices: 12.6 us -> 4.7 us  [exchange(): lax.all_to_all(x, axis, split_axis=0, concat_axis=0, axis_index_groups=[o...]
    all_to_all x2 -> x1, waiting for transfers between devices: 4.11 us -> 0.91 us  [exchange(): lax.all_to_all(x, axis, split_axis=0, concat_axis=0, axis_index_groups=[o...]
    pallas_call x1 -> x0, Pallas kernels: 1.55 us -> none  [local(): pl.pallas_call(prepare_kernel, out_shape=pltpu.VMEM((rows_dev, width), jn...]
    pallas_call x1, Pallas kernels: 1.5 us -> 0.86 us  [local(): pl.pallas_call(functools.partial(pack_kernel, rows_dev), out_shape=pltpu....]
    pallas_call x1, Pallas kernels: 1.89 us -> 2.42 us  [local(): pl.pallas_call(functools.partial(pool_kernel, bag_count, lines, back_lead...]
  transfers between devices with their start and end apart: 5 -> 4, of which waited for: 2 -> 1; matrix products, arithmetic and copies ran while one was open for 0% -> 0% of each run, Pallas kernels for 18% -> 12%
where the time goes in v16:
time: 28.1 us; the launch traced here: 27.8 us
  blocking collectives  12.4 us (44%)
  Pallas kernels  7.26 us (26%)
  starting transfers between devices  6.51 us (23%)
  waiting for transfers between devices  0.92 us (3%)
  between operations  0.7 us (2%)
    all_to_all x1, blocking collectives, exchange(): lax.all_to_all(x, axis, split_axis=0, concat_axis=0, axis_index_groups=[o...  12.4 us
    all_to_all x1, starting transfers between devices, exchange(): lax.all_to_all(x, axis, split_axis=0, concat_axis=0, axis_index_groups=[o...  4.7 us
    pallas_call x1, Pallas kernels, local(): pl.pallas_call(functools.partial(update_kernel, bag_count, lines, groups,...  3.38 us
    pallas_call x1, Pallas kernels, local(): pl.pallas_call(functools.partial(pool_kernel, bag_count, lines, back_lead...  2.42 us
    ppermute x3, starting transfers between devices, shift(): return lax.ppermute(x, axis, [(i, (i + step) % size) for i in range(size)])  1.81 us
    all_to_all x1, waiting for transfers between devices, exchange(): lax.all_to_all(x, axis, split_axis=0, concat_axis=0, axis_index_groups=[o...  0.91 us
    pallas_call x1, Pallas kernels, local(): pl.pallas_call(functools.partial(pack_kernel, rows_dev), out_shape=pltpu....  0.86 us
    pallas_call x1, Pallas kernels, local(): pl.pallas_call(finish_kernel, out_shape=(jax.ShapeDtypeStruct((bag_count,...  0.6 us
  transfers between devices with their start and end apart: 4, of which 1 were waited for; matrix products, arithmetic and copies ran while one was open for 0% of the time, Pallas kernels for 12%

profile of v16, /device:TPU:0, one launch (start us, length us, event | category | flops | bytes accessed | tf_op | source)
XLA Modules:
  0.0 27.8 jit_solution(13849415565707258479)
XLA Ops:
  0.6 0.0 copy-start
  0.6 0.9 %pack.1 = f32[8,24,128]{2,1,0:T(8,128)S(1)} custom-call(s32[4,128]{1,0:T(4,128)} %bitcast.12, s32[4,128]{1,0:T(4,128)} %bitcast.13, s32[4,128]{1,0:T(4,128)} %bitcast.14, s32[4,128]{1,0:T(4,128)} %bitcast.15, s32[4,128]{1,0:T(4,128)} %bitcast.16, s32[4,128]{1,0:T(4,128)} %bitcast.17, f32[4,256]{1,0:T(4,128)} %bitcast.11), custom_call_target="tpu_custom_call" | custom-call | tf_op jit(solution)/shard_map/pack/pallas_call | solution.py:222
  1.5 12.4 %all_to_all.10.msg = f32[8,24,128]{2,1,0:T(8,128)S(1)} all-to-all(f32[8,24,128]{2,1,0:T(8,128)S(1)} %pack.1), channel_id=1, replica_groups={{3,4,5,6,7,0,1,2},{11,12,13,14,15,8,9,10},{19,20,21,22,23,16,17,18},{27..., dimensions={0} | all-to-all | bytes 196608 | tf_op jit(solution)/shard_map/all_to_all | solution.py:190
  13.9 2.4 %pool.1 = (f32[8,4,256]{2,1,0:T(4,128)}, f32[8,16,128]{2,1,0:T(8,128)S(1)}, f32[2048,256]{1,0:T(8,128)S(1)}) custom-call(f32[8,24,128]{2,1,0:T(8,128)S(1)} %all_to_all.10.msg, f32[2048,256]{1,0:T(8,128)} %table.1), custom_call_target="tpu_custom_call" | custom-call | flops 67108864 | bytes 2097152 | tf_op jit(solution)/shard_map/pool/pallas_call | solution.py:238
  16.3 0.1 collective-permute-start.2
  16.4 1.6 %collective-permute-start.1 = (f32[8,16,128]{2,1,0:T(8,128)S(1)}, f32[8,16,128]{2,1,0:T(8,128)S(1)}, u32[]{:S(2)}, u32[]{:S(2)}) collective-permute-start(f32[8,16,128]{2,1,0:T(8,128)S(1)} %get-tuple-element.11.refs_0_), channel_id=1, source_target_pairs={{0,16},{8,24},{16,0},{24,8},{1,17},{9,25},{17,1},{25,9},{2,18},{10... | collective-permute-start | bytes 196616 | tf_op jit(solution)/shard_map/ppermute | solution.py:196
  18.0 0.2 collective-permute-start
  18.1 4.7 %all-to-all-start.1 = ((f32[8,4,256]{2,1,0:T(4,128)}), f32[8,4,256]{2,1,0:T(4,128)S(1)}, u32[]{:S(2)}, u32[]{:S(2)}) async-start(f32[8,4,256]{2,1,0:T(4,128)} %get-tuple-element.10), calls=%async_computation.1 | async-start | bytes 65536 | tf_op jit(solution)/shard_map/all_to_all | solution.py:190
  22.8 0.0 collective-permute-done.2.refs_3_
  22.8 0.0 collective-permute-done.1.refs_2_
  22.8 0.0 collective-permute-done.refs_1_
  22.9 0.0 copy-done
  22.9 3.4 %update.1 = (f32[2048,256]{1,0:T(8,128)}, f32[16,128]{1,0:T(8,128)S(1)}) custom-call(f32[8,16,128]{2,1,0:T(8,128)S(1)} %get-tuple-element.11.refs_0_, f32[8,16,128]{2,1,0:T(8,128)S(1)} %collective-permute-done.refs_1_, f32[8,16,128]{2,1,0:T(8,128)S(1)} %collective-permute-done.1.refs_2_, f32[8,16,128]{2,1,0:T(8,128)S(1)} %collective-permute-done.2.refs_3_, ...), custom_call_target="tpu_custom_call" | custom-call | flops 1 | bytes 1048576 | tf_op jit(solution)/shard_map/update/pallas_call | solution.py:263
  26.3 0.9 %all-to-all-done.1.returned = f32[8,4,256]{2,1,0:T(4,128)S(1)} async-done(((f32[8,4,256]{2,1,0:T(4,128)}), f32[8,4,256]{2,1,0:T(4,128)S(1)}, u32[]{:S(2)}, u32[]{:S(2)}) %all-to-all-start.1) | async-done | bytes 32800 | tf_op jit(solution)/shard_map/all_to_all | solution.py:190
  27.2 0.6 %finish.1 = (f32[4,256]{1,0:T(4,128)}, f32[16,128]{1,0:T(8,128)}) custom-call(f32[8,4,256]{2,1,0:T(4,128)S(1)} %all-to-all-done.1.returned, f32[16,128]{1,0:T(8,128)S(1)} %get-tuple-element.13.accum), custom_call_target="tpu_custom_call" | custom-call | tf_op jit(solution)/shard_map/finish/pallas_call | solution.py:287
Async XLA Ops:
  0.6 22.2 %copy-start = (f32[2048]{0:T(1024)S(1)}, f32[2048]{0:T(1024)}, u32[]{:S(2)}) copy-start(f32[2048]{0:T(1024)} %param.10) | copy-start | bytes 24580
  16.3 6.5 %collective-permute-start.2 = (f32[8,16,128]{2,1,0:T(8,128)S(1)}, f32[8,16,128]{2,1,0:T(8,128)S(1)}, u32[]{:S(2)}, u32[]{:S(2)}) collective-permute-start(f32[8,16,128]{2,1,0:T(8,128)S(1)} %get-tuple-element.11.refs_0_), channel_id=1, source_target_pairs={{0,24},{8,0},{16,8},{24,16},{1,25},{9,1},{17,9},{25,17},{2,26},{10... | collective-permute-start | bytes 196616 | tf_op jit(solution)/shard_map/ppermute | solution.py:196
  16.4 6.5 %collective-permute-start.1 = (f32[8,16,128]{2,1,0:T(8,128)S(1)}, f32[8,16,128]{2,1,0:T(8,128)S(1)}, u32[]{:S(2)}, u32[]{:S(2)}) collective-permute-start(f32[8,16,128]{2,1,0:T(8,128)S(1)} %get-tuple-element.11.refs_0_), channel_id=1, source_target_pairs={{0,16},{8,24},{16,0},{24,8},{1,17},{9,25},{17,1},{25,9},{2,18},{10... | collective-permute-start | bytes 196616 | tf_op jit(solution)/shard_map/ppermute | solution.py:196
  18.0 4.9 %collective-permute-start = (f32[8,16,128]{2,1,0:T(8,128)S(1)}, f32[8,16,128]{2,1,0:T(8,128)S(1)}, u32[]{:S(2)}, u32[]{:S(2)}) collective-permute-start(f32[8,16,128]{2,1,0:T(8,128)S(1)} %get-tuple-element.11.refs_0_), channel_id=1, source_target_pairs={{0,8},{8,16},{16,24},{24,0},{1,9},{9,17},{17,25},{25,1},{2,10},{10... | collective-permute-start | bytes 196616 | tf_op jit(solution)/shard_map/ppermute | solution.py:196
  18.1 9.0 %all-to-all-start.1 = ((f32[8,4,256]{2,1,0:T(4,128)}), f32[8,4,256]{2,1,0:T(4,128)S(1)}, u32[]{:S(2)}, u32[]{:S(2)}) async-start(f32[8,4,256]{2,1,0:T(4,128)} %get-tuple-element.10), calls=%async_computation.1 | async-start | bytes 65536 | tf_op jit(solution)/shard_map/all_to_all | solution.py:190

commit v17 on v14

--- a/solution.py
+++ b/solution.py
@@ -11,14 +11,17 @@
 LANES = 128
 
 
-def pack_kernel(rows_dev, *refs):
-    sources, out, held, sems = refs[:7], refs[7], refs[8:15], refs[15]
+def pack_kernel(*refs):
+    sources, table, out, part, held, sems = refs[:7], refs[7], refs[8], refs[9], refs[10:17], refs[17]
+    rows_dev = table.shape[0]
     copies = [
         pltpu.make_async_copy(source, place, sems.at[i])
         for i, (source, place) in enumerate(zip(sources, held))
     ]
     for copy in copies:
         copy.start()
+    fetch = pltpu.make_async_copy(table.at[pl.ds(0, part.shape[0]), :], part, sems.at[7])
+    fetch.start()
     for copy in copies:
         copy.wait()
     owner, row, bag, prev_owner, prev_row, prev_bag, grad = held
@@ -35,25 +38,12 @@
     put(3 * lines, prev_bag[...].astype(jnp.float32))
     for k in range(width // LANES):
         put(4 * lines + k * bag_count, grad[:, k * LANES:(k + 1) * LANES])
+    fetch.wait()
 
 
 def split_two(x):
     high = x.astype(jnp.bfloat16)
     return high, (x - high.astype(jnp.float32)).astype(jnp.bfloat16)
-
-
-def prepare_kernel(table, kept, sems):
-    pieces = sems.shape[0]
-    rows = table.shape[0] // pieces
-    copies = [
-        pltpu.make_async_copy(
-            table.at[pl.ds(i * rows, rows), :], kept.at[pl.ds(i * rows, rows), :], sems.at[i])
-        for i in range(pieces)
-    ]
-    for copy in copies:
-        copy.start()
-    for copy in copies:
-        copy.wait()
 
 
 def codes(ids, bags, bag_count, base):
@@ -84,10 +74,13 @@
 
 
 def pool_kernel(
-    bag_count, lines, turn, msg, table, out, joined, go, code_ref, lane_ref, counts,
+    bag_count, lines, turn, msg, first, table, out, joined, second,
+    code_ref, lane_ref, counts, sem,
 ):
-    go[0, 0] = 1
     rows_dev, width = table.shape
+    half = first.shape[0]
+    fetch = pltpu.make_async_copy(table.at[pl.ds(half, rows_dev - half), :], second, sem)
+    fetch.start()
     owners = msg.shape[0]
     base = lax.axis_index("rows") * rows_dev
     code_ref[...], lane_ref[...] = codes(
@@ -98,8 +91,11 @@
     flat = jnp.concatenate(
         [counts[h].astype(jnp.bfloat16) for h in range(blocks)], axis=1)
     total = jnp.zeros((owners * bag_count, width), jnp.float32)
-    for part in split_two(table[...]):
-        total += jnp.dot(flat, part, preferred_element_type=jnp.float32)
+    for part in split_two(first[...]):
+        total += jnp.dot(flat[:, :half], part, preferred_element_type=jnp.float32)
+    fetch.wait()
+    for part in split_two(second[...]):
+        total += jnp.dot(flat[:, half:], part, preferred_element_type=jnp.float32)
     for i in range(owners):
         seen = (i + turn) % owners
         out[i] = total[seen * bag_count:(seen + 1) * bag_count, :]
@@ -124,8 +120,9 @@
     return total
 
 
-def apply_rows(grad_of, table, accum, new_table, new_accum, fresh_table, sems):
-    blocks, width = accum.shape[0], table.shape[1]
+def apply_rows(grad_of, tables, accum, new_table, new_accum, fresh_table, sems):
+    blocks, width = accum.shape[0], fresh_table.shape[1]
+    per_table = blocks // len(tables)
     diagonal = (
         lax.broadcasted_iota(jnp.int32, (LANES, LANES), 0)
         == lax.broadcasted_iota(jnp.int32, (LANES, LANES), 1))
@@ -140,7 +137,9 @@
             folded += squares[:, k * LANES:(k + 1) * LANES]
         old = jnp.where(diagonal, accum[h:h + 1, :], 0.0)
         fresh = jnp.sum(folded * (1.0 / width) + old, axis=1, keepdims=True)
-        fresh_table[here, :] = table[here, :] - grad * (learn_rate * lax.rsqrt(fresh))
+        start = h % per_table * LANES
+        old_rows = tables[h // per_table][start:start + LANES, :]
+        fresh_table[here, :] = old_rows - grad * (learn_rate * lax.rsqrt(fresh))
         new_accum[h:h + 1, :] = jnp.sum(
             jnp.where(diagonal, fresh, 0.0), axis=0, keepdims=True)
         if (h + 1) % per_piece == 0:
@@ -154,13 +153,15 @@
 
 
 def count_kernel(bag_count, lines, *refs):
-    sources, (counts_out, high, low) = refs[:-8], refs[-8:-5]
+    number = (len(refs) - 8) // 2
+    sources, passed, (counts_out, high, low) = refs[:number], refs[number:-8], refs[-8:-5]
     msg, code_ref, lane_ref, counts, grads = refs[-5:]
     owners = sources[0].shape[0]
     devices, blocks = msg.shape[0], counts.shape[0]
     base = lax.axis_index("rows") * (blocks * LANES)
     for i, source in enumerate(sources):
         msg[i * owners:(i + 1) * owners] = source[...]
+        passed[i][...] = source[...]
     read_chunk(
         msg, slice(0, devices), devices, lines, bag_count, base,
         code_ref, lane_ref, counts, grads)
@@ -169,8 +170,8 @@
 
 
 def apply_kernel(bag_count, lines, late, *refs):
-    sources, (counted, high, low, table, accum) = refs[:late], refs[late:late + 5]
-    new_table, new_accum, msg, code_ref, lane_ref, counts, grads, fresh_table, sems = refs[late + 5:]
+    sources, (counted, high, low, *tables, accum) = refs[:late], refs[late:late + 6]
+    new_table, new_accum, msg, code_ref, lane_ref, counts, grads, fresh_table, sems = refs[late + 6:]
     owners = sources[0].shape[0]
     devices, blocks = msg.shape[0], counts.shape[0]
     base = lax.axis_index("rows") * (blocks * LANES)
@@ -188,12 +189,12 @@
         hits = jnp.concatenate([counted[h], counts[h].astype(jnp.bfloat16)], axis=0)
         return block_sum(hits, parts)
 
-    apply_rows(grad_of, table, accum, new_table, new_accum, fresh_table, sems)
+    apply_rows(grad_of, tables, accum, new_table, new_accum, fresh_table, sems)
 
 
 def update_kernel(bag_count, lines, groups, chunk, *refs):
-    sources, (table, accum, new_table, new_accum) = refs[:groups], refs[groups:groups + 4]
-    msg, code_ref, lane_ref, counts, grads, sums, fresh_table, sems = refs[groups + 4:]
+    sources, (*tables, accum, new_table, new_accum) = refs[:groups], refs[groups:groups + 5]
+    msg, code_ref, lane_ref, counts, grads, sums, fresh_table, sems = refs[groups + 5:]
     devices, blocks = msg.shape[0], counts.shape[0]
     owners = devices // groups
     base = lax.axis_index("rows") * (blocks * LANES)
@@ -212,14 +213,20 @@
         def _(h):
             sums[h] += block_sum(counts[h].astype(jnp.bfloat16), parts)
 
-    apply_rows(lambda h: sums[h], table, accum, new_table, new_accum, fresh_table, sems)
-
-
-def pass_kernel(table, accum, new_table, new_accum, sem):
-    copy = pltpu.make_async_copy(table, new_table, sem)
-    copy.start()
+    apply_rows(lambda h: sums[h], tables, accum, new_table, new_accum, fresh_table, sems)
+
+
+def pass_kernel(first, second, accum, new_table, new_accum, sems):
+    half = first.shape[0]
+    copies = [
+        pltpu.make_async_copy(part, new_table.at[pl.ds(i * half, half), :], sems.at[i])
+        for i, part in enumerate((first, second))
+    ]
+    for copy in copies:
+        copy.start()
     new_accum[...] = accum[...]
-    copy.wait()
+    for copy in copies:
+        copy.wait()
 
 
 def finish_kernel(returned, accum, pooled, new_accum):
@@ -269,54 +276,46 @@
     def line(x):
         return x.reshape(lines, LANES)
 
-    message = pl.pallas_call(
-        functools.partial(pack_kernel, rows_dev),
-        out_shape=pltpu.VMEM((owners, 2 * lines + prev_length, LANES), jnp.float32),
-        in_specs=[hbm] * 7,
-        out_specs=vmem,
+    half = rows_dev // 2
+    message, first = pl.pallas_call(
+        pack_kernel,
+        out_shape=(
+            pltpu.VMEM((owners, 2 * lines + prev_length, LANES), jnp.float32),
+            pltpu.VMEM((half, width), jnp.float32),
+        ),
+        in_specs=[hbm] * 8,
+        out_specs=[vmem] * 2,
         scratch_shapes=[pltpu.VMEM((lines, LANES), jnp.int32)] * 6
-        + [pltpu.VMEM((bag_count, width), jnp.float32), pltpu.SemaphoreType.DMA((7,))],
+        + [pltpu.VMEM((bag_count, width), jnp.float32), pltpu.SemaphoreType.DMA((8,))],
         compiler_params=params,
         name="pack",
     )(*[stay(x) for x in (
         line(owner_map), line(row_index), line(bag_index),
-        line(prev_owner), line(prev_row), line(prev_bag), grad_pooled[0, 0],
+        line(prev_owner), line(prev_row), line(prev_bag), grad_pooled[0, 0], item_table,
     )])
     gathered = exchange(message, "rows", out_leader)
 
-    pieces = 4
-    kept = pl.pallas_call(
-        prepare_kernel,
-        out_shape=pltpu.VMEM((rows_dev, width), jnp.float32),
-        in_specs=[hbm],
-        out_specs=vmem,
-        scratch_shapes=[pltpu.SemaphoreType.DMA((pieces,))],
-        compiler_params=params,
-        cost_estimate=pl.CostEstimate(
-            flops=0, bytes_accessed=2 * rows_dev * width * 4, transcendentals=0),
-        name="prepare",
-    )(stay(item_table))
-
-    partial_pooled, joined, go = pl.pallas_call(
+    partial_pooled, joined, second = pl.pallas_call(
         functools.partial(pool_kernel, bag_count, lines, back_leader - out_leader),
         out_shape=(
             pltpu.VMEM((owners, bag_count, width), jnp.float32),
             pltpu.VMEM((owners, prev_length, LANES), jnp.float32),
-            jax.ShapeDtypeStruct((1, 1), jnp.int32),
+            pltpu.VMEM((rows_dev - half, width), jnp.float32),
         ),
-        in_specs=[vmem] * 2,
-        out_specs=[vmem] * 2 + [pl.BlockSpec(memory_space=pltpu.SMEM)],
+        in_specs=[vmem, vmem, hbm],
+        out_specs=[vmem] * 3,
         scratch_shapes=[
             pltpu.VMEM((owners, lines, LANES), jnp.float32),
             pltpu.VMEM((owners, lines, LANES), jnp.float32),
             pltpu.VMEM((blocks, owners * bag_count, LANES), jnp.float32),
+            pltpu.SemaphoreType.DMA,
         ],
         compiler_params=params,
         cost_estimate=pl.CostEstimate(
             flops=4 * owners * bag_count * rows_dev * width,
             bytes_accessed=rows_dev * width * 4, transcendentals=0),
         name="pool",
-    )(gathered, kept)
+    )(gathered, first, stay(item_table))
     returned = exchange(partial_pooled, "rows", back_leader)
     there = [joined] + [forward(joined, "dp", step) for step in range(1, groups // 2)]
 
@@ -340,65 +339,60 @@
         pltpu.SemaphoreType.DMA((results,)),
     ]
 
-    def split_update(early, late, kept, row_accum):
-        count = len(early) * owners
-        counted = pl.pallas_call(
+    def hand_over(there, tables, row_accum):
+        if devices > chunk:
+            handed = [forward(x, "dp", 0) for x in there]
+            return pl.pallas_call(
+                functools.partial(update_kernel, bag_count, lines, groups, chunk),
+                out_shape=updated,
+                in_specs=[vmem] * (groups + 3),
+                out_specs=(hbm, vmem),
+                scratch_shapes=[pltpu.VMEM((devices, prev_length, LANES), jnp.float32)]
+                + room(chunk) + [pltpu.VMEM((blocks, LANES, width), jnp.float32)] + fresh_room,
+                compiler_params=pltpu.CompilerParams(vmem_limit_bytes=40 * 1024 * 1024),
+                name="update",
+            )(*there, *handed, *tables, row_accum)
+        number = len(there)
+        count = number * owners
+        *passed, counted, high, low = pl.pallas_call(
             functools.partial(count_kernel, bag_count, lines),
-            out_shape=(
+            out_shape=[pltpu.VMEM((owners, prev_length, LANES), jnp.float32)] * number + [
                 pltpu.VMEM((blocks, count * bag_count, LANES), jnp.bfloat16),
                 pltpu.VMEM((count * bag_count, width), jnp.bfloat16),
                 pltpu.VMEM((count * bag_count, width), jnp.bfloat16),
-            ),
-            in_specs=[vmem] * len(early),
-            out_specs=[vmem] * 3,
+            ],
+            in_specs=[vmem] * number,
+            out_specs=[vmem] * (number + 3),
             scratch_shapes=[pltpu.VMEM((count, prev_length, LANES), jnp.float32)] + room(count),
             compiler_params=params,
-            cost_estimate=pl.CostEstimate(
-                flops=1 << 28, bytes_accessed=1 << 22, transcendentals=0),
             name="count",
-        )(*early)
+        )(*there)
+        handed = [forward(x, "dp", 0) for x in passed]
         return pl.pallas_call(
-            functools.partial(apply_kernel, bag_count, lines, len(late)),
+            functools.partial(apply_kernel, bag_count, lines, number),
             out_shape=updated,
-            in_specs=[vmem] * (len(late) + 5),
+            in_specs=[vmem] * (number + 6),
             out_specs=(hbm, vmem),
             scratch_shapes=[pltpu.VMEM((count, prev_length, LANES), jnp.float32)]
             + room(count) + fresh_room,
             compiler_params=params,
             name="apply",
-        )(*late, *counted, kept, row_accum)
-
-    def whole_update(sources, kept, row_accum):
-        return pl.pallas_call(
-            functools.partial(update_kernel, bag_count, lines, groups, chunk),
-            out_shape=updated,
-            in_specs=[vmem] * (groups + 2),
-            out_specs=(hbm, vmem),
-            scratch_shapes=[pltpu.VMEM((devices, prev_length, LANES), jnp.float32)]
-            + room(chunk) + [pltpu.VMEM((blocks, LANES, width), jnp.float32)] + fresh_room,
-            compiler_params=pltpu.CompilerParams(vmem_limit_bytes=40 * 1024 * 1024),
-            name="update",
-        )(*sources, kept, row_accum)
-
-    def hand_over(there, kept, row_accum):
-        handed = [forward(x, "dp", 0) for x in there]
-        if devices == chunk:
-            return split_update(there, handed, kept, row_accum)
-        return whole_update([*there, *handed], kept, row_accum)
-
-    def skip(there, kept, row_accum):
+        )(*handed, counted, high, low, *tables, row_accum)
+
+    def skip(there, tables, row_accum):
         return pl.pallas_call(
             pass_kernel,
             out_shape=updated,
-            in_specs=[vmem] * 2,
+            in_specs=[vmem] * 3,
             out_specs=(hbm, vmem),
-            scratch_shapes=[pltpu.SemaphoreType.DMA],
+            scratch_shapes=[pltpu.SemaphoreType.DMA((2,))],
             compiler_params=params,
             name="pass",
-        )(kept, row_accum)
-
+        )(*tables, row_accum)
+
+    inside = lax.axis_index("dp") < groups
     new_table, new_accum = lax.cond(
-        go[0, 0] > 0, hand_over, skip, there, kept, row_accum.reshape(blocks, LANES))
+        inside, hand_over, skip, there, (first, second), row_accum.reshape(blocks, LANES))
 
     pooled, new_accum = pl.pallas_call(
         finish_kernel,

time: 28.1 us -> 28.3 us (level)
  blocking collectives: 0 us -> 12.4 us
  starting transfers between devices: 13.8 us -> 5.98 us
  waiting for transfers between devices: 3.48 us -> 1.18 us
  Pallas kernels: 9.02 us -> 7.73 us
  between operations: 1.36 us -> 0.69 us
    all_to_all x0 -> x1, blocking collectives: none -> 12.4 us  [exchange(): lax.all_to_all(x, axis, split_axis=0, concat_axis=0, axis_index_groups=[o...]
    all_to_all x2 -> x1, starting transfers between devices: 12.5 us -> 4.71 us  [exchange(): lax.all_to_all(x, axis, split_axis=0, concat_axis=0, axis_index_groups=[o...]
    all_to_all x2 -> x1, waiting for transfers between devices: 3.2 us -> 0.01 us  [exchange(): lax.all_to_all(x, axis, split_axis=0, concat_axis=0, axis_index_groups=[o...]
    pallas_call x4 -> x3, Pallas kernels: 6.52 us -> 4.88 us  [the longest x1 2.59 us: hand_over(): pl.pallas_call(functools.partial(apply_kernel, bag_count, lines, number),...]
    ppermute x3, waiting for transfers between devices: 0.28 us -> 1.18 us  [forward(): lax.ppermute(x, axis, [(i, ((i // 2 + step) * 2 + 1 - i % 2) % size) for...]
    pallas_call x1, Pallas kernels: 1.89 us -> 2.25 us  [local(): pl.pallas_call(functools.partial(pool_kernel, bag_count, lines, back_lead...]
  transfers between devices with their start and end apart: 5 -> 4, of which waited for: 2 -> 2; matrix products, arithmetic and copies ran while one was open for 0% -> 0% of each run, Pallas kernels for 18% -> 12%
where the time goes in v17:
time: 28.3 us; the launch traced here: 28 us
  blocking collectives  12.4 us (44%)
  Pallas kernels  7.73 us (27%)
  starting transfers between devices  5.98 us (21%)
  waiting for transfers between devices  1.18 us (4%)
  between operations  0.69 us (2%)
    all_to_all x1, blocking collectives, exchange(): lax.all_to_all(x, axis, split_axis=0, concat_axis=0, axis_index_groups=[o...  12.4 us
    all_to_all x1, starting transfers between devices, exchange(): lax.all_to_all(x, axis, split_axis=0, concat_axis=0, axis_index_groups=[o...  4.71 us
    pallas_call x1, Pallas kernels, hand_over(): pl.pallas_call(functools.partial(apply_kernel, bag_count, lines, number),...  2.59 us
    pallas_call x1, Pallas kernels, local(): pl.pallas_call(functools.partial(pool_kernel, bag_count, lines, back_lead...  2.25 us
    pallas_call x1, Pallas kernels, local(): pl.pallas_call(pack_kernel, out_shape=(pltpu.VMEM((owners, 2 * lines + pr...  1.41 us
    ppermute x3, starting transfers between devices, forward(): lax.ppermute(x, axis, [(i, ((i // 2 + step) * 2 + 1 - i % 2) % size) for...  1.26 us
    ppermute x3, waiting for transfers between devices, forward(): lax.ppermute(x, axis, [(i, ((i // 2 + step) * 2 + 1 - i % 2) % size) for...  1.18 us
    pallas_call x1, Pallas kernels, hand_over(): pl.pallas_call(functools.partial(count_kernel, bag_count, lines), out_sha...  0.88 us
  transfers between devices with their start and end apart: 4, of which 2 were waited for; matrix products, arithmetic and copies ran while one was open for 0% of the time, Pallas kernels for 12%

profile of v17, /device:TPU:0, one launch (start us, length us, event | category | flops | bytes accessed | tf_op | source)
XLA Modules:
  0.0 28.0 jit_solution(6043570650657526942)
XLA Ops:
  0.6 1.4 %pack.1 = (f32[8,24,128]{2,1,0:T(8,128)S(1)}, f32[1024,256]{1,0:T(8,128)S(1)}) custom-call(s32[4,128]{1,0:T(4,128)} %bitcast.13, s32[4,128]{1,0:T(4,128)} %bitcast.14, s32[4,128]{1,0:T(4,128)} %bitcast.15, s32[4,128]{1,0:T(4,128)} %bitcast.16, s32[4,128]{1,0:T(4,128)} %bitcast.17, s32[4,128]{1,0:T(4,128)} %bitcast.18, f32[4,256]{1,0:T(4,128)} %bitcast.12, ...), custom_call_target="tpu_custom_call" | custom-call | tf_op jit(solution)/shard_map/pack/pallas_call | solution.py:280
  2.0 0.0 copy-start
  2.1 12.4 %all_to_all.10.msg = f32[8,24,128]{2,1,0:T(8,128)S(1)} all-to-all(f32[8,24,128]{2,1,0:T(8,128)S(1)} %get-tuple-element.41), channel_id=1, replica_groups={{3,4,5,6,7,0,1,2},{11,12,13,14,15,8,9,10},{19,20,21,22,23,16,17,18},{27..., dimensions={0} | all-to-all | bytes 196608 | tf_op jit(solution)/shard_map/all_to_all | solution.py:246
  14.4 2.3 %pool.1 = (f32[8,4,256]{2,1,0:T(4,128)}, f32[8,16,128]{2,1,0:T(8,128)S(1)}, f32[1024,256]{1,0:T(8,128)S(1)}) custom-call(f32[8,24,128]{2,1,0:T(8,128)S(1)} %all_to_all.10.msg, f32[1024,256]{1,0:T(8,128)S(1)} %get-tuple-element.42.first, f32[2048,256]{1,0:T(8,128)} %table.1), custom_call_target="tpu_custom_call" | custom-call | flops 67108864 | bytes 2097152 | tf_op jit(solution)/shard_map/pool/pallas_call | solution.py:298
  16.7 0.1 collective-permute-start.2
  16.8 4.7 %all-to-all-start.1 = ((f32[8,4,256]{2,1,0:T(4,128)}), f32[8,4,256]{2,1,0:T(4,128)S(1)}, u32[]{:S(2)}, u32[]{:S(2)}) async-start(f32[8,4,256]{2,1,0:T(4,128)} %get-tuple-element.43), calls=%async_computation.1 | async-start | bytes 65536 | tf_op jit(solution)/shard_map/all_to_all | solution.py:246
  21.5 0.0 collective-permute-done.2
  21.5 0.0 copy-done
  21.5 5.9 %conditional.1 = ((f32[2048,256]{1,0:T(8,128)}, f32[16,128]{1,0:T(8,128)S(1)})) conditional(s32[]{:T(128)} %convert_element_type.3, (f32[1024,256]{1,0:T(8,128)S(1)}, f32[1024,256]{1,0:T(8,128)S(1)}, f32[16,128]{1,0:T(8,128)S(1)}) %tuple.21, (f32[8,16,128]{2,1,0:T(8,128)S(1)}, f32[8,16,128]{2,1,0:T(8,128)S(1)}, f32[1024,256]{1,0:T(8,128)S(1)}, ...), branch_computations={%region_0.0_spmd, %region_1.0_spmd} | conditional | bytes 524376 | solution.py:394
  21.5 0.9 %count.1 = (f32[8,16,128]{2,1,0:T(8,128)S(1)}, f32[8,16,128]{2,1,0:T(8,128)S(1)}, bf16[16,64,128]{2,1,0:T(8,128)(2,1)S(1)}, bf16[64,256]{1,0:T(8,128)(2,1)S(1)}, bf16[64,256]{1,0:T(8,128)(2,1)S(1)}) custom-call(f32[8,16,128]{2,1,0:T(8,128)S(1)} %get-tuple-element.19.refs_0_, f32[8,16,128]{2,1,0:T(8,128)S(1)} %get-tuple-element.20.refs_1_), custom_call_target="tpu_custom_call" | custom-call | tf_op jit(solution)/shard_map/cond/branch_1_fun/count/pallas_call | solution.py:357
  22.4 1.1 %collective-permute-start = (f32[8,16,128]{2,1,0:T(8,128)S(1)}, f32[8,16,128]{2,1,0:T(8,128)S(1)}, u32[]{:S(2)}, u32[]{:S(2)}) collective-permute-start(f32[8,16,128]{2,1,0:T(8,128)S(1)} %get-tuple-element.21), channel_id=1, source_target_pairs={{0,8},{8,0},{16,24},{24,16},{1,9},{9,1},{17,25},{25,17},{2,10},{10... | collective-permute-start | bytes 196616 | tf_op jit(solution)/shard_map/cond/branch_1_fun/ppermute | solution.py:252
  23.5 0.1 collective-permute-start.1
  23.6 0.8 %collective-permute-done.refs_0_ = f32[8,16,128]{2,1,0:T(8,128)S(1)} collective-permute-done((f32[8,16,128]{2,1,0:T(8,128)S(1)}, f32[8,16,128]{2,1,0:T(8,128)S(1)}, u32[]{:S(2)}, u32[]{:S(2)}) %collective-permute-start) | collective-permute-done | bytes 65568 | tf_op jit(solution)/shard_map/cond/branch_1_fun/ppermute | solution.py:252
  24.4 0.4 %collective-permute-done.1.refs_1_ = f32[8,16,128]{2,1,0:T(8,128)S(1)} collective-permute-done((f32[8,16,128]{2,1,0:T(8,128)S(1)}, f32[8,16,128]{2,1,0:T(8,128)S(1)}, u32[]{:S(2)}, u32[]{:S(2)}) %collective-permute-start.1) | collective-permute-done | bytes 65568 | tf_op jit(solution)/shard_map/cond/branch_1_fun/ppermute | solution.py:252
  24.8 2.6 %apply.1 = (f32[2048,256]{1,0:T(8,128)}, f32[16,128]{1,0:T(8,128)S(1)}) custom-call(f32[8,16,128]{2,1,0:T(8,128)S(1)} %collective-permute-done.refs_0_, f32[8,16,128]{2,1,0:T(8,128)S(1)} %collective-permute-done.1.refs_1_, bf16[16,64,128]{2,1,0:T(8,128)(2,1)S(1)} %get-tuple-element.23.refs_2_, bf16[64,256]{1,0:T(8,128)(2,1)S(1)} %get-tuple-element.24.refs_3_, ...), custom_call_target="tpu_custom_call" | custom-call | tf_op jit(solution)/shard_map/cond/branch_1_fun/apply/pallas_call | solution.py:371
  27.4 0.0 all-to-all-done.1.returned
  27.4 0.6 %finish.1 = (f32[4,256]{1,0:T(4,128)}, f32[16,128]{1,0:T(8,128)}) custom-call(f32[8,4,256]{2,1,0:T(4,128)S(1)} %all-to-all-done.1.returned, f32[16,128]{1,0:T(8,128)S(1)} %get-tuple-element.46.accum), custom_call_target="tpu_custom_call" | custom-call | tf_op jit(solution)/shard_map/finish/pallas_call | solution.py:397
Async XLA Ops:
  2.0 19.4 %copy-start = (f32[2048]{0:T(1024)S(1)}, f32[2048]{0:T(1024)}, u32[]{:S(2)}) copy-start(f32[2048]{0:T(1024)} %param.12) | copy-start | bytes 24580
  16.7 4.8 %collective-permute-start.2 = (f32[8,16,128]{2,1,0:T(8,128)S(1)}, f32[8,16,128]{2,1,0:T(8,128)S(1)}, u32[]{:S(2)}, u32[]{:S(2)}) collective-permute-start(f32[8,16,128]{2,1,0:T(8,128)S(1)} %get-tuple-element.45), channel_id=1, source_target_pairs={{0,24},{8,16},{16,8},{24,0},{1,25},{9,17},{17,9},{25,1},{2,26},{10... | collective-permute-start | bytes 196616 | tf_op jit(solution)/shard_map/ppermute | solution.py:252
  16.8 10.6 %all-to-all-start.1 = ((f32[8,4,256]{2,1,0:T(4,128)}), f32[8,4,256]{2,1,0:T(4,128)S(1)}, u32[]{:S(2)}, u32[]{:S(2)}) async-start(f32[8,4,256]{2,1,0:T(4,128)} %get-tuple-element.43), calls=%async_computation.1 | async-start | bytes 65536 | tf_op jit(solution)/shard_map/all_to_all | solution.py:246
  22.4 2.0 %collective-permute-start = (f32[8,16,128]{2,1,0:T(8,128)S(1)}, f32[8,16,128]{2,1,0:T(8,128)S(1)}, u32[]{:S(2)}, u32[]{:S(2)}) collective-permute-start(f32[8,16,128]{2,1,0:T(8,128)S(1)} %get-tuple-element.21), channel_id=1, source_target_pairs={{0,8},{8,0},{16,24},{24,16},{1,9},{9,1},{17,25},{25,17},{2,10},{10... | collective-permute-start | bytes 196616 | tf_op jit(solution)/shard_map/cond/branch_1_fun/ppermute | solution.py:252
  23.5 1.3 %collective-permute-start.1 = (f32[8,16,128]{2,1,0:T(8,128)S(1)}, f32[8,16,128]{2,1,0:T(8,128)S(1)}, u32[]{:S(2)}, u32[]{:S(2)}) collective-permute-start(f32[8,16,128]{2,1,0:T(8,128)S(1)} %get-tuple-element.22), channel_id=1, source_target_pairs={{0,8},{8,0},{16,24},{24,16},{1,9},{9,1},{17,25},{25,17},{2,10},{10... | collective-permute-start | bytes 196616 | tf_op jit(solution)/shard_map/cond/branch_1_fun/ppermute | solution.py:252

commit v18 on v14

--- a/solution.py
+++ b/solution.py
@@ -42,20 +42,6 @@
     return high, (x - high.astype(jnp.float32)).astype(jnp.bfloat16)
 
 
-def prepare_kernel(table, kept, sems):
-    pieces = sems.shape[0]
-    rows = table.shape[0] // pieces
-    copies = [
-        pltpu.make_async_copy(
-            table.at[pl.ds(i * rows, rows), :], kept.at[pl.ds(i * rows, rows), :], sems.at[i])
-        for i in range(pieces)
-    ]
-    for copy in copies:
-        copy.start()
-    for copy in copies:
-        copy.wait()
-
-
 def codes(ids, bags, bag_count, base):
     rel = ids.astype(jnp.int32) - base
     code = lax.shift_right_arithmetic(rel, 7) * bag_count + bags.astype(jnp.int32)
@@ -84,10 +70,18 @@
 
 
 def pool_kernel(
-    bag_count, lines, turn, msg, table, out, joined, go, code_ref, lane_ref, counts,
+    bag_count, lines, turn, msg, table, out, joined, kept, code_ref, lane_ref, counts, sems,
 ):
-    go[0, 0] = 1
     rows_dev, width = table.shape
+    pieces = sems.shape[0]
+    rows = rows_dev // pieces
+    fetches = [
+        pltpu.make_async_copy(
+            table.at[pl.ds(i * rows, rows), :], kept.at[pl.ds(i * rows, rows), :], sems.at[i])
+        for i in range(pieces)
+    ]
+    for fetch in fetches:
+        fetch.start()
     owners = msg.shape[0]
     base = lax.axis_index("rows") * rows_dev
     code_ref[...], lane_ref[...] = codes(
@@ -98,8 +92,11 @@
     flat = jnp.concatenate(
         [counts[h].astype(jnp.bfloat16) for h in range(blocks)], axis=1)
     total = jnp.zeros((owners * bag_count, width), jnp.float32)
-    for part in split_two(table[...]):
-        total += jnp.dot(flat, part, preferred_element_type=jnp.float32)
+    for i, fetch in enumerate(fetches):
+        fetch.wait()
+        here = slice(i * rows, (i + 1) * rows)
+        for part in split_two(kept[here, :]):
+            total += jnp.dot(flat[:, here], part, preferred_element_type=jnp.float32)
     for i in range(owners):
         seen = (i + turn) % owners
         out[i] = total[seen * bag_count:(seen + 1) * bag_count, :]
@@ -125,7 +122,7 @@
 
 
 def apply_rows(grad_of, table, accum, new_table, new_accum, fresh_table, sems):
-    blocks, width = accum.shape[0], table.shape[1]
+    blocks, width = accum.shape[0], fresh_table.shape[1]
     diagonal = (
         lax.broadcasted_iota(jnp.int32, (LANES, LANES), 0)
         == lax.broadcasted_iota(jnp.int32, (LANES, LANES), 1))
@@ -284,44 +281,32 @@
     )])
     gathered = exchange(message, "rows", out_leader)
 
-    pieces = 4
-    kept = pl.pallas_call(
-        prepare_kernel,
-        out_shape=pltpu.VMEM((rows_dev, width), jnp.float32),
-        in_specs=[hbm],
-        out_specs=vmem,
-        scratch_shapes=[pltpu.SemaphoreType.DMA((pieces,))],
-        compiler_params=params,
-        cost_estimate=pl.CostEstimate(
-            flops=0, bytes_accessed=2 * rows_dev * width * 4, transcendentals=0),
-        name="prepare",
-    )(stay(item_table))
-
-    partial_pooled, joined, go = pl.pallas_call(
+    pieces = 8 if blocks % 8 == 0 else 1
+    partial_pooled, joined, kept = pl.pallas_call(
         functools.partial(pool_kernel, bag_count, lines, back_leader - out_leader),
         out_shape=(
             pltpu.VMEM((owners, bag_count, width), jnp.float32),
             pltpu.VMEM((owners, prev_length, LANES), jnp.float32),
-            jax.ShapeDtypeStruct((1, 1), jnp.int32),
+            pltpu.VMEM((rows_dev, width), jnp.float32),
         ),
-        in_specs=[vmem] * 2,
-        out_specs=[vmem] * 2 + [pl.BlockSpec(memory_space=pltpu.SMEM)],
+        in_specs=[vmem, hbm],
+        out_specs=[vmem] * 3,
         scratch_shapes=[
             pltpu.VMEM((owners, lines, LANES), jnp.float32),
             pltpu.VMEM((owners, lines, LANES), jnp.float32),
             pltpu.VMEM((blocks, owners * bag_count, LANES), jnp.float32),
+            pltpu.SemaphoreType.DMA((pieces,)),
         ],
         compiler_params=params,
         cost_estimate=pl.CostEstimate(
             flops=4 * owners * bag_count * rows_dev * width,
             bytes_accessed=rows_dev * width * 4, transcendentals=0),
         name="pool",
-    )(gathered, kept)
+    )(gathered, stay(item_table))
     returned = exchange(partial_pooled, "rows", back_leader)
     there = [joined] + [forward(joined, "dp", step) for step in range(1, groups // 2)]
 
     segments = chunk * bag_count
-    results = 8 if blocks % 8 == 0 else 1
     updated = (
         pltpu.HBM((rows_dev, width), jnp.float32),
         pltpu.VMEM((blocks, LANES), jnp.float32),
@@ -337,54 +322,49 @@
 
     fresh_room = [
         pltpu.VMEM((rows_dev, width), jnp.float32),
-        pltpu.SemaphoreType.DMA((results,)),
+        pltpu.SemaphoreType.DMA((pieces,)),
     ]
 
-    def split_update(early, late, kept, row_accum):
-        count = len(early) * owners
-        counted = pl.pallas_call(
+    def hand_over(there, kept, row_accum):
+        handed = [forward(x, "dp", 0) for x in there]
+        if devices > chunk:
+            return pl.pallas_call(
+                functools.partial(update_kernel, bag_count, lines, groups, chunk),
+                out_shape=updated,
+                in_specs=[vmem] * (groups + 2),
+                out_specs=(hbm, vmem),
+                scratch_shapes=[pltpu.VMEM((devices, prev_length, LANES), jnp.float32)]
+                + room(chunk) + [pltpu.VMEM((blocks, LANES, width), jnp.float32)] + fresh_room,
+                compiler_params=pltpu.CompilerParams(vmem_limit_bytes=40 * 1024 * 1024),
+                name="update",
+            )(*there, *handed, kept, row_accum)
+        number = len(there)
+        count = number * owners
+        counted, high, low = pl.pallas_call(
             functools.partial(count_kernel, bag_count, lines),
-            out_shape=(
+            out_shape=[
                 pltpu.VMEM((blocks, count * bag_count, LANES), jnp.bfloat16),
                 pltpu.VMEM((count * bag_count, width), jnp.bfloat16),
                 pltpu.VMEM((count * bag_count, width), jnp.bfloat16),
-            ),
-            in_specs=[vmem] * len(early),
+            ],
+            in_specs=[vmem] * number,
             out_specs=[vmem] * 3,
             scratch_shapes=[pltpu.VMEM((count, prev_length, LANES), jnp.float32)] + room(count),
             compiler_params=params,
             cost_estimate=pl.CostEstimate(
                 flops=1 << 28, bytes_accessed=1 << 22, transcendentals=0),
             name="count",
-        )(*early)
+        )(*there)
         return pl.pallas_call(
-            functools.partial(apply_kernel, bag_count, lines, len(late)),
+            functools.partial(apply_kernel, bag_count, lines, number),
             out_shape=updated,
-            in_specs=[vmem] * (len(late) + 5),
+            in_specs=[vmem] * (number + 5),
             out_specs=(hbm, vmem),
             scratch_shapes=[pltpu.VMEM((count, prev_length, LANES), jnp.float32)]
             + room(count) + fresh_room,
             compiler_params=params,
             name="apply",
-        )(*late, *counted, kept, row_accum)
-
-    def whole_update(sources, kept, row_accum):
-        return pl.pallas_call(
-            functools.partial(update_kernel, bag_count, lines, groups, chunk),
-            out_shape=updated,
-            in_specs=[vmem] * (groups + 2),
-            out_specs=(hbm, vmem),
-            scratch_shapes=[pltpu.VMEM((devices, prev_length, LANES), jnp.float32)]
-            + room(chunk) + [pltpu.VMEM((blocks, LANES, width), jnp.float32)] + fresh_room,
-            compiler_params=pltpu.CompilerParams(vmem_limit_bytes=40 * 1024 * 1024),
-            name="update",
-        )(*sources, kept, row_accum)
-
-    def hand_over(there, kept, row_accum):
-        handed = [forward(x, "dp", 0) for x in there]
-        if devices == chunk:
-            return split_update(there, handed, kept, row_accum)
-        return whole_update([*there, *handed], kept, row_accum)
+        )(*handed, counted, high, low, kept, row_accum)
 
     def skip(there, kept, row_accum):
         return pl.pallas_call(
@@ -397,8 +377,9 @@
             name="pass",
         )(kept, row_accum)
 
+    inside = lax.axis_index("dp") < groups
     new_table, new_accum = lax.cond(
-        go[0, 0] > 0, hand_over, skip, there, kept, row_accum.reshape(blocks, LANES))
+        inside, hand_over, skip, there, kept, row_accum.reshape(blocks, LANES))
 
     pooled, new_accum = pl.pallas_call(
         finish_kernel,

time: 28.1 us -> 27.2 us (0.968)
  blocking collectives: 0 us -> 12.4 us
  starting transfers between devices: 13.8 us -> 5.98 us
  waiting for transfers between devices: 3.48 us -> 0.29 us
  Pallas kernels: 9.02 us -> 7.53 us
  between operations: 1.36 us -> 0.69 us
    all_to_all x0 -> x1, blocking collectives: none -> 12.4 us  [exchange(): lax.all_to_all(x, axis, split_axis=0, concat_axis=0, axis_index_groups=[o...]
    all_to_all x2 -> x1, starting transfers between devices: 12.5 us -> 4.71 us  [exchange(): lax.all_to_all(x, axis, split_axis=0, concat_axis=0, axis_index_groups=[o...]
    all_to_all x2 -> x1, waiting for transfers between devices: 3.2 us -> 0.01 us  [exchange(): lax.all_to_all(x, axis, split_axis=0, concat_axis=0, axis_index_groups=[o...]
    pallas_call x3 -> x2, Pallas kernels: 5.03 us -> 3.48 us  [the longest x1 2.6 us: hand_over(): pl.pallas_call(functools.partial(apply_kernel, bag_count, lines, number),...]
    pallas_call x1, Pallas kernels: 1.89 us -> 2.58 us  [local(): pl.pallas_call(functools.partial(pool_kernel, bag_count, lines, back_lead...]
    pallas_call x1, Pallas kernels: 1.5 us -> 0.86 us  [local(): pl.pallas_call(functools.partial(pack_kernel, rows_dev), out_shape=pltpu....]
  transfers between devices with their start and end apart: 5 -> 4, of which waited for: 2 -> 1; matrix products, arithmetic and copies ran while one was open for 0% -> 0% of each run, Pallas kernels for 18% -> 13%
where the time goes in v18:
time: 27.2 us; the launch traced here: 26.9 us
  blocking collectives  12.4 us (46%)
  Pallas kernels  7.53 us (28%)
  starting transfers between devices  5.98 us (22%)
  between operations  0.69 us (3%)
  waiting for transfers between devices  0.29 us (1%)
    all_to_all x1, blocking collectives, exchange(): lax.all_to_all(x, axis, split_axis=0, concat_axis=0, axis_index_groups=[o...  12.4 us
    all_to_all x1, starting transfers between devices, exchange(): lax.all_to_all(x, axis, split_axis=0, concat_axis=0, axis_index_groups=[o...  4.71 us
    pallas_call x1, Pallas kernels, hand_over(): pl.pallas_call(functools.partial(apply_kernel, bag_count, lines, number),...  2.6 us
    pallas_call x1, Pallas kernels, local(): pl.pallas_call(functools.partial(pool_kernel, bag_count, lines, back_lead...  2.58 us
    ppermute x3, starting transfers between devices, forward(): lax.ppermute(x, axis, [(i, ((i // 2 + step) * 2 + 1 - i % 2) % size) for...  1.26 us
    pallas_call x1, Pallas kernels, hand_over(): pl.pallas_call(functools.partial(count_kernel, bag_count, lines), out_sha...  0.88 us
    pallas_call x1, Pallas kernels, local(): pl.pallas_call(functools.partial(pack_kernel, rows_dev), out_shape=pltpu....  0.86 us
    pallas_call x1, Pallas kernels, local(): pl.pallas_call(finish_kernel, out_shape=(jax.ShapeDtypeStruct((bag_count,...  0.6 us
  transfers between devices with their start and end apart: 4, of which 1 were waited for; matrix products, arithmetic and copies ran while one was open for 0% of the time, Pallas kernels for 13%

profile of v18, /device:TPU:0, one launch (start us, length us, event | category | flops | bytes accessed | tf_op | source)
XLA Modules:
  0.0 26.9 jit_solution(3664929328298420672)
XLA Ops:
  0.6 0.0 copy-start
  0.6 0.9 %pack.1 = f32[8,24,128]{2,1,0:T(8,128)S(1)} custom-call(s32[4,128]{1,0:T(4,128)} %bitcast.13, s32[4,128]{1,0:T(4,128)} %bitcast.14, s32[4,128]{1,0:T(4,128)} %bitcast.15, s32[4,128]{1,0:T(4,128)} %bitcast.16, s32[4,128]{1,0:T(4,128)} %bitcast.17, s32[4,128]{1,0:T(4,128)} %bitcast.18, f32[4,256]{1,0:T(4,128)} %bitcast.12), custom_call_target="tpu_custom_call" | custom-call | tf_op jit(solution)/shard_map/pack/pallas_call | solution.py:269
  1.5 12.4 %all_to_all.10.msg = f32[8,24,128]{2,1,0:T(8,128)S(1)} all-to-all(f32[8,24,128]{2,1,0:T(8,128)S(1)} %pack.1), channel_id=1, replica_groups={{3,4,5,6,7,0,1,2},{11,12,13,14,15,8,9,10},{19,20,21,22,23,16,17,18},{27..., dimensions={0} | all-to-all | bytes 196608 | tf_op jit(solution)/shard_map/all_to_all | solution.py:236
  13.9 2.6 %pool.1 = (f32[8,4,256]{2,1,0:T(4,128)}, f32[8,16,128]{2,1,0:T(8,128)S(1)}, f32[2048,256]{1,0:T(8,128)S(1)}) custom-call(f32[8,24,128]{2,1,0:T(8,128)S(1)} %all_to_all.10.msg, f32[2048,256]{1,0:T(8,128)} %table.1), custom_call_target="tpu_custom_call" | custom-call | flops 67108864 | bytes 2097152 | tf_op jit(solution)/shard_map/pool/pallas_call | solution.py:285
  16.5 0.1 collective-permute-start.2
  16.6 4.7 %all-to-all-start.1 = ((f32[8,4,256]{2,1,0:T(4,128)}), f32[8,4,256]{2,1,0:T(4,128)S(1)}, u32[]{:S(2)}, u32[]{:S(2)}) async-start(f32[8,4,256]{2,1,0:T(4,128)} %get-tuple-element.31), calls=%async_computation.1 | async-start | bytes 65536 | tf_op jit(solution)/shard_map/all_to_all | solution.py:236
  21.3 0.0 collective-permute-done.2
  21.3 0.0 copy-done
  21.3 5.0 %conditional.1 = ((f32[2048,256]{1,0:T(8,128)}, f32[16,128]{1,0:T(8,128)S(1)})) conditional(s32[]{:T(128)} %convert_element_type.3, (f32[2048,256]{1,0:T(8,128)S(1)}, f32[16,128]{1,0:T(8,128)S(1)}) %tuple.21, (f32[8,16,128]{2,1,0:T(8,128)S(1)}, f32[8,16,128]{2,1,0:T(8,128)S(1)}, f32[2048,256]{1,0:T(8,128)S(1)}, f32[16,128]{1,0:T(8,128)S(1)}) %tuple.22), branch_computations={%region_0.0_spmd, %region_1.0_spmd} | conditional | flops 268435456 | bytes 4718680 | solution.py:381
  21.3 1.1 %collective-permute-start = (f32[8,16,128]{2,1,0:T(8,128)S(1)}, f32[8,16,128]{2,1,0:T(8,128)S(1)}, u32[]{:S(2)}, u32[]{:S(2)}) collective-permute-start(f32[8,16,128]{2,1,0:T(8,128)S(1)} %get-tuple-element.14.refs_0_), channel_id=1, source_target_pairs={{0,8},{8,0},{16,24},{24,16},{1,9},{9,1},{17,25},{25,17},{2,10},{10... | collective-permute-start | bytes 196616 | tf_op jit(solution)/shard_map/cond/branch_1_fun/ppermute | solution.py:242
  22.4 0.1 collective-permute-start.1
  22.5 0.9 %count.1 = (bf16[16,64,128]{2,1,0:T(8,128)(2,1)S(1)}, bf16[64,256]{1,0:T(8,128)(2,1)S(1)}, bf16[64,256]{1,0:T(8,128)(2,1)S(1)}) custom-call(f32[8,16,128]{2,1,0:T(8,128)S(1)} %get-tuple-element.14.refs_0_, f32[8,16,128]{2,1,0:T(8,128)S(1)} %get-tuple-element.15.refs_1_), custom_call_target="tpu_custom_call" | custom-call | flops 268435456 | bytes 4194304 | tf_op jit(solution)/shard_map/cond/branch_1_fun/count/pallas_call | solution.py:343
  23.4 0.0 collective-permute-done.refs_0_
  23.4 0.3 %collective-permute-done.1.refs_1_ = f32[8,16,128]{2,1,0:T(8,128)S(1)} collective-permute-done((f32[8,16,128]{2,1,0:T(8,128)S(1)}, f32[8,16,128]{2,1,0:T(8,128)S(1)}, u32[]{:S(2)}, u32[]{:S(2)}) %collective-permute-start.1) | collective-permute-done | bytes 65568 | tf_op jit(solution)/shard_map/cond/branch_1_fun/ppermute | solution.py:242
  23.7 2.6 %apply.1 = (f32[2048,256]{1,0:T(8,128)}, f32[16,128]{1,0:T(8,128)S(1)}) custom-call(f32[8,16,128]{2,1,0:T(8,128)S(1)} %collective-permute-done.refs_0_, f32[8,16,128]{2,1,0:T(8,128)S(1)} %collective-permute-done.1.refs_1_, bf16[16,64,128]{2,1,0:T(8,128)(2,1)S(1)} %get-tuple-element.16.refs_2_, bf16[64,256]{1,0:T(8,128)(2,1)S(1)} %get-tuple-element.17.refs_3_, ...), custom_call_target="tpu_custom_call" | custom-call | tf_op jit(solution)/shard_map/cond/branch_1_fun/apply/pallas_call | solution.py:358
  26.3 0.0 all-to-all-done.1.returned
  26.3 0.6 %finish.1 = (f32[4,256]{1,0:T(4,128)}, f32[16,128]{1,0:T(8,128)}) custom-call(f32[8,4,256]{2,1,0:T(4,128)S(1)} %all-to-all-done.1.returned, f32[16,128]{1,0:T(8,128)S(1)} %get-tuple-element.34.accum), custom_call_target="tpu_custom_call" | custom-call | tf_op jit(solution)/shard_map/finish/pallas_call | solution.py:384
Async XLA Ops:
  0.6 20.6 %copy-start = (f32[2048]{0:T(1024)S(1)}, f32[2048]{0:T(1024)}, u32[]{:S(2)}) copy-start(f32[2048]{0:T(1024)} %param.12) | copy-start | bytes 24580
  16.5 4.8 %collective-permute-start.2 = (f32[8,16,128]{2,1,0:T(8,128)S(1)}, f32[8,16,128]{2,1,0:T(8,128)S(1)}, u32[]{:S(2)}, u32[]{:S(2)}) collective-permute-start(f32[8,16,128]{2,1,0:T(8,128)S(1)} %get-tuple-element.33), channel_id=1, source_target_pairs={{0,24},{8,16},{16,8},{24,0},{1,25},{9,17},{17,9},{25,1},{2,26},{10... | collective-permute-start | bytes 196616 | tf_op jit(solution)/shard_map/ppermute | solution.py:242
  16.6 9.7 %all-to-all-start.1 = ((f32[8,4,256]{2,1,0:T(4,128)}), f32[8,4,256]{2,1,0:T(4,128)S(1)}, u32[]{:S(2)}, u32[]{:S(2)}) async-start(f32[8,4,256]{2,1,0:T(4,128)} %get-tuple-element.31), calls=%async_computation.1 | async-start | bytes 65536 | tf_op jit(solution)/shard_map/all_to_all | solution.py:236
  21.3 2.1 %collective-permute-start = (f32[8,16,128]{2,1,0:T(8,128)S(1)}, f32[8,16,128]{2,1,0:T(8,128)S(1)}, u32[]{:S(2)}, u32[]{:S(2)}) collective-permute-start(f32[8,16,128]{2,1,0:T(8,128)S(1)} %get-tuple-element.14.refs_0_), channel_id=1, source_target_pairs={{0,8},{8,0},{16,24},{24,16},{1,9},{9,1},{17,25},{25,17},{2,10},{10... | collective-permute-start | bytes 196616 | tf_op jit(solution)/shard_map/cond/branch_1_fun/ppermute | solution.py:242
  22.4 1.3 %collective-permute-start.1 = (f32[8,16,128]{2,1,0:T(8,128)S(1)}, f32[8,16,128]{2,1,0:T(8,128)S(1)}, u32[]{:S(2)}, u32[]{:S(2)}) collective-permute-start(f32[8,16,128]{2,1,0:T(8,128)S(1)} %get-tuple-element.15.refs_1_), channel_id=1, source_target_pairs={{0,8},{8,0},{16,24},{24,16},{1,9},{9,1},{17,25},{25,17},{2,10},{10... | collective-permute-start | bytes 196616 | tf_op jit(solution)/shard_map/cond/branch_1_fun/ppermute | solution.py:242

commit v19 on v18

--- a/solution.py
+++ b/solution.py
@@ -9,6 +9,17 @@
 
 learn_rate = 0.1
 LANES = 128
+
+PREV_BOUNDS = 64
+
+
+def bound_block(bags, bag_count, first):
+    lane = lax.broadcasted_iota(jnp.int32, (1, LANES), 1)
+    block = jnp.zeros((1, LANES), jnp.float32)
+    for j in range(1, bag_count):
+        start = jnp.sum((bags < j).astype(jnp.float32), axis=1, keepdims=True)
+        block = jnp.where(lane == first + j - 1, start, block)
+    return block
 
 
 def pack_kernel(rows_dev, *refs):
@@ -22,19 +33,46 @@
     for copy in copies:
         copy.wait()
     owner, row, bag, prev_owner, prev_row, prev_bag, grad = held
-    lines = row.shape[0]
+    positions = row.shape[1]
     bag_count, width = grad.shape
 
     def put(start, value):
-        shape = (out.shape[0],) + value.shape
-        out[:, start:start + value.shape[0], :] = jnp.broadcast_to(value[None], shape)
+        shape = (out.shape[0], 1, value.shape[1])
+        out[:, :, start:start + value.shape[1]] = jnp.broadcast_to(value[None], shape)
 
     put(0, (owner[...] * rows_dev + row[...]).astype(jnp.float32))
-    put(lines, bag[...].astype(jnp.float32))
-    put(2 * lines, (prev_owner[...] * rows_dev + prev_row[...]).astype(jnp.float32))
-    put(3 * lines, prev_bag[...].astype(jnp.float32))
-    for k in range(width // LANES):
-        put(4 * lines + k * bag_count, grad[:, k * LANES:(k + 1) * LANES])
+    put(positions, (prev_owner[...] * rows_dev + prev_row[...]).astype(jnp.float32))
+    put(
+        2 * positions,
+        bound_block(bag[...], bag_count, 0)
+        + bound_block(prev_bag[...], bag_count, PREV_BOUNDS),
+    )
+    for j in range(bag_count):
+        put(2 * positions + LANES + j * width, grad[j:j + 1, :])
+
+
+def unpack(msg, joined, code_ref, lane_ref, lines, bag_count, width, base):
+    devices, positions = msg.shape[0], lines * LANES
+    bounds = msg[:, 0, 2 * positions:2 * positions + LANES]
+    lane = lax.broadcasted_iota(jnp.int32, (devices, LANES), 1)
+
+    def bags(k, first):
+        place = (lane + k * LANES).astype(jnp.float32)
+        bag = jnp.zeros((devices, LANES), jnp.float32)
+        for j in range(1, bag_count):
+            bag += (place >= bounds[:, first + j - 1:first + j]).astype(jnp.float32)
+        return bag
+
+    for k in range(lines):
+        start = k * LANES
+        code_ref[:, k, :], lane_ref[:, k, :] = codes(
+            msg[:, 0, start:start + LANES], bags(k, 0), bag_count, base)
+        joined[:, k, :] = msg[:, 0, positions + start:positions + start + LANES]
+        joined[:, lines + k, :] = bags(k, PREV_BOUNDS)
+    for j in range(bag_count):
+        for k in range(width // LANES):
+            start = 2 * positions + LANES + j * width + k * LANES
+            joined[:, 2 * lines + k * bag_count + j, :] = msg[:, 0, start:start + LANES]
 
 
 def split_two(x):
@@ -84,9 +122,7 @@
         fetch.start()
     owners = msg.shape[0]
     base = lax.axis_index("rows") * rows_dev
-    code_ref[...], lane_ref[...] = codes(
-        msg[:, 0:lines, :], msg[:, lines:2 * lines, :], bag_count, base)
-    joined[...] = msg[:, 2 * lines:, :]
+    unpack(msg, joined, code_ref, lane_ref, lines, bag_count, width, base)
     count_into(counts, code_ref, lane_ref, owners, bag_count)
     blocks = rows_dev // LANES
     flat = jnp.concatenate(
@@ -255,6 +291,7 @@
     lines = row_index.shape[2] // LANES
     blocks = rows_dev // LANES
     prev_length = 2 * lines + bag_count * width // LANES
+    length = (2 * lines + 1) * LANES + bag_count * width
     vmem = pl.BlockSpec(memory_space=pltpu.VMEM)
     hbm = pl.BlockSpec(memory_space=pltpu.HBM)
     params = pltpu.CompilerParams(vmem_limit_bytes=16 * 1024 * 1024)
@@ -264,14 +301,14 @@
         return pltpu.with_memory_space_constraint(x, pltpu.HBM)
 
     def line(x):
-        return x.reshape(lines, LANES)
+        return x.reshape(1, lines * LANES)
 
     message = pl.pallas_call(
         functools.partial(pack_kernel, rows_dev),
-        out_shape=pltpu.VMEM((owners, 2 * lines + prev_length, LANES), jnp.float32),
+        out_shape=pltpu.VMEM((owners, 1, length), jnp.float32),
         in_specs=[hbm] * 7,
         out_specs=vmem,
-        scratch_shapes=[pltpu.VMEM((lines, LANES), jnp.int32)] * 6
+        scratch_shapes=[pltpu.VMEM((1, lines * LANES), jnp.int32)] * 6
         + [pltpu.VMEM((bag_count, width), jnp.float32), pltpu.SemaphoreType.DMA((7,))],
         compiler_params=params,
         name="pack",
@@ -281,7 +318,7 @@
     )])
     gathered = exchange(message, "rows", out_leader)
 
-    pieces = 8 if blocks % 8 == 0 else 1
+    pieces = 4
     partial_pooled, joined, kept = pl.pallas_call(
         functools.partial(pool_kernel, bag_count, lines, back_leader - out_leader),
         out_shape=(

time: 27.2 us -> 27.4 us (level)
  Pallas kernels: 7.53 us -> 7.84 us
where the time goes in v19:
time: 27.4 us; the launch traced here: 27.1 us
  blocking collectives  12.2 us (45%)
  Pallas kernels  7.84 us (29%)
  starting transfers between devices  6.09 us (22%)
  between operations  0.69 us (3%)
  waiting for transfers between devices  0.28 us (1%)
    all_to_all x1, blocking collectives, exchange(): lax.all_to_all(x, axis, split_axis=0, concat_axis=0, axis_index_groups=[o...  12.2 us
    all_to_all x1, starting transfers between devices, exchange(): lax.all_to_all(x, axis, split_axis=0, concat_axis=0, axis_index_groups=[o...  4.83 us
    pallas_call x1, Pallas kernels, local(): pl.pallas_call(functools.partial(pool_kernel, bag_count, lines, back_lead...  2.75 us
    pallas_call x1, Pallas kernels, hand_over(): pl.pallas_call(functools.partial(apply_kernel, bag_count, lines, number),...  2.66 us
    ppermute x3, starting transfers between devices, forward(): lax.ppermute(x, axis, [(i, ((i // 2 + step) * 2 + 1 - i % 2) % size) for...  1.26 us
    pallas_call x1, Pallas kernels, local(): pl.pallas_call(functools.partial(pack_kernel, rows_dev), out_shape=pltpu....  0.94 us
    pallas_call x1, Pallas kernels, hand_over(): pl.pallas_call(functools.partial(count_kernel, bag_count, lines), out_sha...  0.88 us
    pallas_call x1, Pallas kernels, local(): pl.pallas_call(finish_kernel, out_shape=(jax.ShapeDtypeStruct((bag_count,...  0.6 us
  transfers between devices with their start and end apart: 4, of which 1 were waited for; matrix products, arithmetic and copies ran while one was open for 0% of the time, Pallas kernels for 13%

profile of v19, /device:TPU:0, one launch (start us, length us, event | category | flops | bytes accessed | tf_op | source)
XLA Modules:
  0.0 27.1 jit_solution(9897312995564550543)
XLA Ops:
  0.6 0.0 copy-start
  0.6 0.9 %pack.1 = f32[8,1,2176]{2,1,0:T(1,128)S(1)} custom-call(s32[1,512]{1,0:T(1,128)} %bitcast.13, s32[1,512]{1,0:T(1,128)} %bitcast.14, s32[1,512]{1,0:T(1,128)} %bitcast.15, s32[1,512]{1,0:T(1,128)} %bitcast.16, s32[1,512]{1,0:T(1,128)} %bitcast.17, s32[1,512]{1,0:T(1,128)} %bitcast.18, f32[4,256]{1,0:T(4,128)} %bitcast.12), custom_call_target="tpu_custom_call" | custom-call | tf_op jit(solution)/shard_map/pack/pallas_call | solution.py:306
  1.6 12.2 %all_to_all.10.msg = f32[8,1,2176]{2,1,0:T(1,128)S(1)} all-to-all(f32[8,1,2176]{2,1,0:T(1,128)S(1)} %pack.1), channel_id=1, replica_groups={{3,4,5,6,7,0,1,2},{11,12,13,14,15,8,9,10},{19,20,21,22,23,16,17,18},{27..., dimensions={0} | all-to-all | bytes 139264 | tf_op jit(solution)/shard_map/all_to_all | solution.py:272
  13.8 2.8 %pool.1 = (f32[8,4,256]{2,1,0:T(4,128)}, f32[8,16,128]{2,1,0:T(8,128)S(1)}, f32[2048,256]{1,0:T(8,128)S(1)}) custom-call(f32[8,1,2176]{2,1,0:T(1,128)S(1)} %all_to_all.10.msg, f32[2048,256]{1,0:T(8,128)} %table.1), custom_call_target="tpu_custom_call" | custom-call | flops 67108864 | bytes 2097152 | tf_op jit(solution)/shard_map/pool/pallas_call | solution.py:322
  16.5 0.1 collective-permute-start.2
  16.6 4.8 %all-to-all-start.1 = ((f32[8,4,256]{2,1,0:T(4,128)}), f32[8,4,256]{2,1,0:T(4,128)S(1)}, u32[]{:S(2)}, u32[]{:S(2)}) async-start(f32[8,4,256]{2,1,0:T(4,128)} %get-tuple-element.31), calls=%async_computation.1 | async-start | bytes 65536 | tf_op jit(solution)/shard_map/all_to_all | solution.py:272
  21.4 0.0 collective-permute-done.2
  21.4 0.0 copy-done
  21.5 5.0 %conditional.1 = ((f32[2048,256]{1,0:T(8,128)}, f32[16,128]{1,0:T(8,128)S(1)})) conditional(s32[]{:T(128)} %convert_element_type.3, (f32[2048,256]{1,0:T(8,128)S(1)}, f32[16,128]{1,0:T(8,128)S(1)}) %tuple.21, (f32[8,16,128]{2,1,0:T(8,128)S(1)}, f32[8,16,128]{2,1,0:T(8,128)S(1)}, f32[2048,256]{1,0:T(8,128)S(1)}, f32[16,128]{1,0:T(8,128)S(1)}) %tuple.22), branch_computations={%region_0.0_spmd, %region_1.0_spmd} | conditional | flops 268435456 | bytes 4718680 | solution.py:418
  21.5 1.1 %collective-permute-start = (f32[8,16,128]{2,1,0:T(8,128)S(1)}, f32[8,16,128]{2,1,0:T(8,128)S(1)}, u32[]{:S(2)}, u32[]{:S(2)}) collective-permute-start(f32[8,16,128]{2,1,0:T(8,128)S(1)} %get-tuple-element.14.refs_0_), channel_id=1, source_target_pairs={{0,8},{8,0},{16,24},{24,16},{1,9},{9,1},{17,25},{25,17},{2,10},{10... | collective-permute-start | bytes 196616 | tf_op jit(solution)/shard_map/cond/branch_1_fun/ppermute | solution.py:278
  22.6 0.1 collective-permute-start.1
  22.7 0.9 %count.1 = (bf16[16,64,128]{2,1,0:T(8,128)(2,1)S(1)}, bf16[64,256]{1,0:T(8,128)(2,1)S(1)}, bf16[64,256]{1,0:T(8,128)(2,1)S(1)}) custom-call(f32[8,16,128]{2,1,0:T(8,128)S(1)} %get-tuple-element.14.refs_0_, f32[8,16,128]{2,1,0:T(8,128)S(1)} %get-tuple-element.15.refs_1_), custom_call_target="tpu_custom_call" | custom-call | flops 268435456 | bytes 4194304 | tf_op jit(solution)/shard_map/cond/branch_1_fun/count/pallas_call | solution.py:380
  23.5 0.0 collective-permute-done.refs_0_
  23.6 0.3 %collective-permute-done.1.refs_1_ = f32[8,16,128]{2,1,0:T(8,128)S(1)} collective-permute-done((f32[8,16,128]{2,1,0:T(8,128)S(1)}, f32[8,16,128]{2,1,0:T(8,128)S(1)}, u32[]{:S(2)}, u32[]{:S(2)}) %collective-permute-start.1) | collective-permute-done | bytes 65568 | tf_op jit(solution)/shard_map/cond/branch_1_fun/ppermute | solution.py:278
  23.8 2.7 %apply.1 = (f32[2048,256]{1,0:T(8,128)}, f32[16,128]{1,0:T(8,128)S(1)}) custom-call(f32[8,16,128]{2,1,0:T(8,128)S(1)} %collective-permute-done.refs_0_, f32[8,16,128]{2,1,0:T(8,128)S(1)} %collective-permute-done.1.refs_1_, bf16[16,64,128]{2,1,0:T(8,128)(2,1)S(1)} %get-tuple-element.16.refs_2_, bf16[64,256]{1,0:T(8,128)(2,1)S(1)} %get-tuple-element.17.refs_3_, ...), custom_call_target="tpu_custom_call" | custom-call | tf_op jit(solution)/shard_map/cond/branch_1_fun/apply/pallas_call | solution.py:395
  26.5 0.0 all-to-all-done.1.returned
  26.5 0.6 %finish.1 = (f32[4,256]{1,0:T(4,128)}, f32[16,128]{1,0:T(8,128)}) custom-call(f32[8,4,256]{2,1,0:T(4,128)S(1)} %all-to-all-done.1.returned, f32[16,128]{1,0:T(8,128)S(1)} %get-tuple-element.34.accum), custom_call_target="tpu_custom_call" | custom-call | tf_op jit(solution)/shard_map/finish/pallas_call | solution.py:421
Async XLA Ops:
  0.6 20.8 %copy-start = (f32[2048]{0:T(1024)S(1)}, f32[2048]{0:T(1024)}, u32[]{:S(2)}) copy-start(f32[2048]{0:T(1024)} %param.12) | copy-start | bytes 24580
  16.5 4.9 %collective-permute-start.2 = (f32[8,16,128]{2,1,0:T(8,128)S(1)}, f32[8,16,128]{2,1,0:T(8,128)S(1)}, u32[]{:S(2)}, u32[]{:S(2)}) collective-permute-start(f32[8,16,128]{2,1,0:T(8,128)S(1)} %get-tuple-element.33), channel_id=1, source_target_pairs={{0,24},{8,16},{16,8},{24,0},{1,25},{9,17},{17,9},{25,1},{2,26},{10... | collective-permute-start | bytes 196616 | tf_op jit(solution)/shard_map/ppermute | solution.py:278
  16.6 9.9 %all-to-all-start.1 = ((f32[8,4,256]{2,1,0:T(4,128)}), f32[8,4,256]{2,1,0:T(4,128)S(1)}, u32[]{:S(2)}, u32[]{:S(2)}) async-start(f32[8,4,256]{2,1,0:T(4,128)} %get-tuple-element.31), calls=%async_computation.1 | async-start | bytes 65536 | tf_op jit(solution)/shard_map/all_to_all | solution.py:272
  21.5 2.1 %collective-permute-start = (f32[8,16,128]{2,1,0:T(8,128)S(1)}, f32[8,16,128]{2,1,0:T(8,128)S(1)}, u32[]{:S(2)}, u32[]{:S(2)}) collective-permute-start(f32[8,16,128]{2,1,0:T(8,128)S(1)} %get-tuple-element.14.refs_0_), channel_id=1, source_target_pairs={{0,8},{8,0},{16,24},{24,16},{1,9},{9,1},{17,25},{25,17},{2,10},{10... | collective-permute-start | bytes 196616 | tf_op jit(solution)/shard_map/cond/branch_1_fun/ppermute | solution.py:278
  22.6 1.3 %collective-permute-start.1 = (f32[8,16,128]{2,1,0:T(8,128)S(1)}, f32[8,16,128]{2,1,0:T(8,128)S(1)}, u32[]{:S(2)}, u32[]{:S(2)}) collective-permute-start(f32[8,16,128]{2,1,0:T(8,128)S(1)} %get-tuple-element.15.refs_1_), channel_id=1, source_target_pairs={{0,8},{8,0},{16,24},{24,16},{1,9},{9,1},{17,25},{25,17},{2,10},{10... | collective-permute-start | bytes 196616 | tf_op jit(solution)/shard_map/cond/branch_1_fun/ppermute | solution.py:278

commit v20 on v18

--- a/solution.py
+++ b/solution.py
@@ -249,7 +249,7 @@
 ):
     owners, groups = lax.axis_size("rows"), lax.axis_size("dp")
     devices = owners * groups
-    out_leader, back_leader = owners // 2 - 1, owners // 2
+    out_leader, back_leader = 5 * owners // 8, owners // 4
     rows_dev, width = item_table.shape
     bag_count = grad_pooled.shape[2]
     lines = row_index.shape[2] // LANES
@@ -281,7 +281,7 @@
     )])
     gathered = exchange(message, "rows", out_leader)
 
-    pieces = 8 if blocks % 8 == 0 else 1
+    pieces = 4
     partial_pooled, joined, kept = pl.pallas_call(
         functools.partial(pool_kernel, bag_count, lines, back_leader - out_leader),
         out_shape=(

time: 27.2 us -> 26.2 us (0.963)
  blocking collectives: 12.4 us -> 11.5 us
    all_to_all x1, blocking collectives: 12.4 us -> 11.5 us  [exchange(): lax.all_to_all(x, axis, split_axis=0, concat_axis=0, axis_index_groups=[o...]
  transfers between devices with their start and end apart: 4 -> 4, of which waited for: 1 -> 2; matrix products, arithmetic and copies ran while one was open for 0% -> 0% of each run, Pallas kernels for 13% -> 14%
where the time goes in v20:
time: 26.2 us; the launch traced here: 25.9 us
  blocking collectives  11.5 us (44%)
  Pallas kernels  7.43 us (28%)
  starting transfers between devices  5.85 us (22%)
  between operations  0.68 us (3%)
  waiting for transfers between devices  0.46 us (2%)
    all_to_all x1, blocking collectives, exchange(): lax.all_to_all(x, axis, split_axis=0, concat_axis=0, axis_index_groups=[o...  11.5 us
    all_to_all x1, starting transfers between devices, exchange(): lax.all_to_all(x, axis, split_axis=0, concat_axis=0, axis_index_groups=[o...  4.58 us
    pallas_call x1, Pallas kernels, hand_over(): pl.pallas_call(functools.partial(apply_kernel, bag_count, lines, number),...  2.66 us
    pallas_call x1, Pallas kernels, local(): pl.pallas_call(functools.partial(pool_kernel, bag_count, lines, back_lead...  2.43 us
    ppermute x3, starting transfers between devices, forward(): lax.ppermute(x, axis, [(i, ((i // 2 + step) * 2 + 1 - i % 2) % size) for...  1.26 us
    pallas_call x1, Pallas kernels, hand_over(): pl.pallas_call(functools.partial(count_kernel, bag_count, lines), out_sha...  0.88 us
    pallas_call x1, Pallas kernels, local(): pl.pallas_call(functools.partial(pack_kernel, rows_dev), out_shape=pltpu....  0.86 us
    pallas_call x1, Pallas kernels, local(): pl.pallas_call(finish_kernel, out_shape=(jax.ShapeDtypeStruct((bag_count,...  0.6 us
  transfers between devices with their start and end apart: 4, of which 2 were waited for; matrix products, arithmetic and copies ran while one was open for 0% of the time, Pallas kernels for 14%

profile of v20, /device:TPU:0, one launch (start us, length us, event | category | flops | bytes accessed | tf_op | source)
XLA Modules:
  0.0 25.9 jit_solution(8324420586165949186)
XLA Ops:
  0.6 0.0 copy-start
  0.6 0.9 %pack.1 = f32[8,24,128]{2,1,0:T(8,128)S(1)} custom-call(s32[4,128]{1,0:T(4,128)} %bitcast.13, s32[4,128]{1,0:T(4,128)} %bitcast.14, s32[4,128]{1,0:T(4,128)} %bitcast.15, s32[4,128]{1,0:T(4,128)} %bitcast.16, s32[4,128]{1,0:T(4,128)} %bitcast.17, s32[4,128]{1,0:T(4,128)} %bitcast.18, f32[4,256]{1,0:T(4,128)} %bitcast.12), custom_call_target="tpu_custom_call" | custom-call | tf_op jit(solution)/shard_map/pack/pallas_call | solution.py:269
  1.5 11.5 %all_to_all.10.msg = f32[8,24,128]{2,1,0:T(8,128)S(1)} all-to-all(f32[8,24,128]{2,1,0:T(8,128)S(1)} %pack.1), channel_id=1, replica_groups={{5,6,7,0,1,2,3,4},{13,14,15,8,9,10,11,12},{21,22,23,16,17,18,19,20},{29..., dimensions={0} | all-to-all | bytes 196608 | tf_op jit(solution)/shard_map/all_to_all | solution.py:236
  13.0 2.4 %pool.1 = (f32[8,4,256]{2,1,0:T(4,128)}, f32[8,16,128]{2,1,0:T(8,128)S(1)}, f32[2048,256]{1,0:T(8,128)S(1)}) custom-call(f32[8,24,128]{2,1,0:T(8,128)S(1)} %all_to_all.10.msg, f32[2048,256]{1,0:T(8,128)} %table.1), custom_call_target="tpu_custom_call" | custom-call | flops 67108864 | bytes 2097152 | tf_op jit(solution)/shard_map/pool/pallas_call | solution.py:285
  15.4 0.1 collective-permute-start.2
  15.5 4.6 %all-to-all-start.1 = ((f32[8,4,256]{2,1,0:T(4,128)}), f32[8,4,256]{2,1,0:T(4,128)S(1)}, u32[]{:S(2)}, u32[]{:S(2)}) async-start(f32[8,4,256]{2,1,0:T(4,128)} %get-tuple-element.31), calls=%async_computation.1 | async-start | bytes 65536 | tf_op jit(solution)/shard_map/all_to_all | solution.py:236
  20.1 0.0 collective-permute-done.2
  20.1 0.0 copy-done
  20.1 5.0 %conditional.1 = ((f32[2048,256]{1,0:T(8,128)}, f32[16,128]{1,0:T(8,128)S(1)})) conditional(s32[]{:T(128)} %convert_element_type.3, (f32[2048,256]{1,0:T(8,128)S(1)}, f32[16,128]{1,0:T(8,128)S(1)}) %tuple.21, (f32[8,16,128]{2,1,0:T(8,128)S(1)}, f32[8,16,128]{2,1,0:T(8,128)S(1)}, f32[2048,256]{1,0:T(8,128)S(1)}, f32[16,128]{1,0:T(8,128)S(1)}) %tuple.22), branch_computations={%region_0.0_spmd, %region_1.0_spmd} | conditional | flops 268435456 | bytes 4718680 | solution.py:381
  20.1 1.1 %collective-permute-start = (f32[8,16,128]{2,1,0:T(8,128)S(1)}, f32[8,16,128]{2,1,0:T(8,128)S(1)}, u32[]{:S(2)}, u32[]{:S(2)}) collective-permute-start(f32[8,16,128]{2,1,0:T(8,128)S(1)} %get-tuple-element.14.refs_0_), channel_id=1, source_target_pairs={{0,8},{8,0},{16,24},{24,16},{1,9},{9,1},{17,25},{25,17},{2,10},{10... | collective-permute-start | bytes 196616 | tf_op jit(solution)/shard_map/cond/branch_1_fun/ppermute | solution.py:242
  21.2 0.1 collective-permute-start.1
  21.3 0.9 %count.1 = (bf16[16,64,128]{2,1,0:T(8,128)(2,1)S(1)}, bf16[64,256]{1,0:T(8,128)(2,1)S(1)}, bf16[64,256]{1,0:T(8,128)(2,1)S(1)}) custom-call(f32[8,16,128]{2,1,0:T(8,128)S(1)} %get-tuple-element.14.refs_0_, f32[8,16,128]{2,1,0:T(8,128)S(1)} %get-tuple-element.15.refs_1_), custom_call_target="tpu_custom_call" | custom-call | flops 268435456 | bytes 4194304 | tf_op jit(solution)/shard_map/cond/branch_1_fun/count/pallas_call | solution.py:343
  22.2 0.0 collective-permute-done.refs_0_
  22.2 0.3 %collective-permute-done.1.refs_1_ = f32[8,16,128]{2,1,0:T(8,128)S(1)} collective-permute-done((f32[8,16,128]{2,1,0:T(8,128)S(1)}, f32[8,16,128]{2,1,0:T(8,128)S(1)}, u32[]{:S(2)}, u32[]{:S(2)}) %collective-permute-start.1) | collective-permute-done | bytes 65568 | tf_op jit(solution)/shard_map/cond/branch_1_fun/ppermute | solution.py:242
  22.5 2.7 %apply.1 = (f32[2048,256]{1,0:T(8,128)}, f32[16,128]{1,0:T(8,128)S(1)}) custom-call(f32[8,16,128]{2,1,0:T(8,128)S(1)} %collective-permute-done.refs_0_, f32[8,16,128]{2,1,0:T(8,128)S(1)} %collective-permute-done.1.refs_1_, bf16[16,64,128]{2,1,0:T(8,128)(2,1)S(1)} %get-tuple-element.16.refs_2_, bf16[64,256]{1,0:T(8,128)(2,1)S(1)} %get-tuple-element.17.refs_3_, ...), custom_call_target="tpu_custom_call" | custom-call | tf_op jit(solution)/shard_map/cond/branch_1_fun/apply/pallas_call | solution.py:358
  25.1 0.2 all-to-all-done.1.returned
  25.3 0.6 %finish.1 = (f32[4,256]{1,0:T(4,128)}, f32[16,128]{1,0:T(8,128)}) custom-call(f32[8,4,256]{2,1,0:T(4,128)S(1)} %all-to-all-done.1.returned, f32[16,128]{1,0:T(8,128)S(1)} %get-tuple-element.34.accum), custom_call_target="tpu_custom_call" | custom-call | tf_op jit(solution)/shard_map/finish/pallas_call | solution.py:384
Async XLA Ops:
  0.6 19.5 %copy-start = (f32[2048]{0:T(1024)S(1)}, f32[2048]{0:T(1024)}, u32[]{:S(2)}) copy-start(f32[2048]{0:T(1024)} %param.12) | copy-start | bytes 24580
  15.4 4.7 %collective-permute-start.2 = (f32[8,16,128]{2,1,0:T(8,128)S(1)}, f32[8,16,128]{2,1,0:T(8,128)S(1)}, u32[]{:S(2)}, u32[]{:S(2)}) collective-permute-start(f32[8,16,128]{2,1,0:T(8,128)S(1)} %get-tuple-element.33), channel_id=1, source_target_pairs={{0,24},{8,16},{16,8},{24,0},{1,25},{9,17},{17,9},{25,1},{2,26},{10... | collective-permute-start | bytes 196616 | tf_op jit(solution)/shard_map/ppermute | solution.py:242
  15.5 9.8 %all-to-all-start.1 = ((f32[8,4,256]{2,1,0:T(4,128)}), f32[8,4,256]{2,1,0:T(4,128)S(1)}, u32[]{:S(2)}, u32[]{:S(2)}) async-start(f32[8,4,256]{2,1,0:T(4,128)} %get-tuple-element.31), calls=%async_computation.1 | async-start | bytes 65536 | tf_op jit(solution)/shard_map/all_to_all | solution.py:236
  20.1 2.1 %collective-permute-start = (f32[8,16,128]{2,1,0:T(8,128)S(1)}, f32[8,16,128]{2,1,0:T(8,128)S(1)}, u32[]{:S(2)}, u32[]{:S(2)}) collective-permute-start(f32[8,16,128]{2,1,0:T(8,128)S(1)} %get-tuple-element.14.refs_0_), channel_id=1, source_target_pairs={{0,8},{8,0},{16,24},{24,16},{1,9},{9,1},{17,25},{25,17},{2,10},{10... | collective-permute-start | bytes 196616 | tf_op jit(solution)/shard_map/cond/branch_1_fun/ppermute | solution.py:242
  21.2 1.3 %collective-permute-start.1 = (f32[8,16,128]{2,1,0:T(8,128)S(1)}, f32[8,16,128]{2,1,0:T(8,128)S(1)}, u32[]{:S(2)}, u32[]{:S(2)}) collective-permute-start(f32[8,16,128]{2,1,0:T(8,128)S(1)} %get-tuple-element.15.refs_1_), channel_id=1, source_target_pairs={{0,8},{8,0},{16,24},{24,16},{1,9},{9,1},{17,25},{25,17},{2,10},{10... | collective-permute-start | bytes 196616 | tf_op jit(solution)/shard_map/cond/branch_1_fun/ppermute | solution.py:242

commit v21 on v20

--- a/solution.py
+++ b/solution.py
@@ -166,13 +166,15 @@
 
 
 def apply_kernel(bag_count, lines, late, *refs):
-    sources, (counted, high, low, table, accum) = refs[:late], refs[late:late + 5]
-    new_table, new_accum, msg, code_ref, lane_ref, counts, grads, fresh_table, sems = refs[late + 5:]
-    owners = sources[0].shape[0]
+    swapped, met, handed = refs[0], refs[1:late], refs[late:2 * late - 1]
+    counted, high, low, table, accum, new_table, new_accum, *room = refs[2 * late - 1:]
+    msg, code_ref, lane_ref, counts, grads, fresh_table, sems = room
+    owners = swapped.shape[0]
     devices, blocks = msg.shape[0], counts.shape[0]
     base = lax.axis_index("rows") * (blocks * LANES)
-    for i, source in enumerate(sources):
-        msg[i * owners:(i + 1) * owners] = source[...]
+    msg[0:owners] = swapped[...]
+    for i, (one, other) in enumerate(zip(met, handed)):
+        msg[(i + 1) * owners:(i + 2) * owners] = one[...] + other[...]
     read_chunk(
         msg, slice(0, devices), devices, lines, bag_count, base,
         code_ref, lane_ref, counts, grads)
@@ -237,10 +239,14 @@
         x, axis, split_axis=0, concat_axis=0, axis_index_groups=[order], tiled=True)
 
 
-def forward(x, axis, step):
-    size = lax.axis_size(axis)
+def hop(x, axis, step, source, target):
+    pairs = lax.axis_size(axis) // 2
     return lax.ppermute(
-        x, axis, [(i, ((i // 2 + step) * 2 + 1 - i % 2) % size) for i in range(size)])
+        x, axis, [(2 * m + source, 2 * ((m + step) % pairs) + target) for m in range(pairs)])
+
+
+def swap(x, axis):
+    return lax.ppermute(x, axis, [(i, i + 1 - i % 2 * 2) for i in range(lax.axis_size(axis))])
 
 
 def local(
@@ -249,7 +255,7 @@
 ):
     owners, groups = lax.axis_size("rows"), lax.axis_size("dp")
     devices = owners * groups
-    out_leader, back_leader = 5 * owners // 8, owners // 4
+    out_leader, back_leader = 5 * owners // 8, owners // 2 - 1
     rows_dev, width = item_table.shape
     bag_count = grad_pooled.shape[2]
     lines = row_index.shape[2] // LANES
@@ -304,7 +310,9 @@
         name="pool",
     )(gathered, stay(item_table))
     returned = exchange(partial_pooled, "rows", back_leader)
-    there = [joined] + [forward(joined, "dp", step) for step in range(1, groups // 2)]
+    steps = range(1, groups // 2)
+    met = [hop(joined, "dp", step, 0, 1) for step in steps]
+    met = met + [hop(joined, "dp", step, 1, 1) for step in steps]
 
     segments = chunk * bag_count
     updated = (
@@ -322,12 +330,14 @@
 
     fresh_room = [
         pltpu.VMEM((rows_dev, width), jnp.float32),
-        pltpu.SemaphoreType.DMA((pieces,)),
+        pltpu.SemaphoreType.DMA((8 if blocks % 8 == 0 else 1,)),
     ]
 
-    def hand_over(there, kept, row_accum):
-        handed = [forward(x, "dp", 0) for x in there]
+    def hand_over(joined, met, kept, row_accum):
+        swapped = swap(joined, "dp")
+        handed = [hop(x, "dp", 0, 1, 0) for x in met]
         if devices > chunk:
+            rest = [x + y for x, y in zip(met, handed)]
             return pl.pallas_call(
                 functools.partial(update_kernel, bag_count, lines, groups, chunk),
                 out_shape=updated,
@@ -337,36 +347,35 @@
                 + room(chunk) + [pltpu.VMEM((blocks, LANES, width), jnp.float32)] + fresh_room,
                 compiler_params=pltpu.CompilerParams(vmem_limit_bytes=40 * 1024 * 1024),
                 name="update",
-            )(*there, *handed, kept, row_accum)
-        number = len(there)
-        count = number * owners
+            )(joined, swapped, *rest, kept, row_accum)
         counted, high, low = pl.pallas_call(
             functools.partial(count_kernel, bag_count, lines),
             out_shape=[
-                pltpu.VMEM((blocks, count * bag_count, LANES), jnp.bfloat16),
-                pltpu.VMEM((count * bag_count, width), jnp.bfloat16),
-                pltpu.VMEM((count * bag_count, width), jnp.bfloat16),
+                pltpu.VMEM((blocks, owners * bag_count, LANES), jnp.bfloat16),
+                pltpu.VMEM((owners * bag_count, width), jnp.bfloat16),
+                pltpu.VMEM((owners * bag_count, width), jnp.bfloat16),
             ],
-            in_specs=[vmem] * number,
+            in_specs=[vmem],
             out_specs=[vmem] * 3,
-            scratch_shapes=[pltpu.VMEM((count, prev_length, LANES), jnp.float32)] + room(count),
+            scratch_shapes=[pltpu.VMEM((owners, prev_length, LANES), jnp.float32)] + room(owners),
             compiler_params=params,
             cost_estimate=pl.CostEstimate(
                 flops=1 << 28, bytes_accessed=1 << 22, transcendentals=0),
             name="count",
-        )(*there)
+        )(joined)
+        late = 1 + len(met)
         return pl.pallas_call(
-            functools.partial(apply_kernel, bag_count, lines, number),
+            functools.partial(apply_kernel, bag_count, lines, late),
             out_shape=updated,
-            in_specs=[vmem] * (number + 5),
+            in_specs=[vmem] * (2 * late + 4),
             out_specs=(hbm, vmem),
-            scratch_shapes=[pltpu.VMEM((count, prev_length, LANES), jnp.float32)]
-            + room(count) + fresh_room,
+            scratch_shapes=[pltpu.VMEM((late * owners, prev_length, LANES), jnp.float32)]
+            + room(late * owners) + fresh_room,
             compiler_params=params,
             name="apply",
-        )(*handed, counted, high, low, kept, row_accum)
-
-    def skip(there, kept, row_accum):
+        )(swapped, *met, *handed, counted, high, low, kept, row_accum)
+
+    def skip(joined, met, kept, row_accum):
         return pl.pallas_call(
             pass_kernel,
             out_shape=updated,
@@ -379,7 +388,7 @@
 
     inside = lax.axis_index("dp") < groups
     new_table, new_accum = lax.cond(
-        inside, hand_over, skip, there, kept, row_accum.reshape(blocks, LANES))
+        inside, hand_over, skip, joined, met, kept, row_accum.reshape(blocks, LANES))
 
     pooled, new_accum = pl.pallas_call(
         finish_kernel,

time: 26.2 us -> 32.5 us (1.24)
  starting transfers between devices: 5.85 us -> 11.2 us
  waiting for transfers between devices: 0.46 us -> 1.33 us
    ppermute x3 -> x5, starting transfers between devices: 1.26 us -> 6.35 us  [the longest x4 6.28 us: hop(): lax.ppermute(x, axis, [(2 * m + source, 2 * ((m + step) % pairs) + target...]
    ppermute x3 -> x5, waiting for transfers between devices: 0.28 us -> 1.32 us  [the longest x4 1.32 us: hop(): lax.ppermute(x, axis, [(2 * m + source, 2 * ((m + step) % pairs) + target...]
    pallas_call x1, Pallas kernels: 0.88 us -> 0.51 us  [hand_over(): pl.pallas_call(functools.partial(count_kernel, bag_count, lines), out_sha...]
  transfers between devices with their start and end apart: 4 -> 6, of which waited for: 2 -> 1; matrix products, arithmetic and copies ran while one was open for 0% -> 0% of each run, Pallas kernels for 14% -> 11%
where the time goes in v21:
time: 32.5 us; the launch traced here: 32.2 us
  blocking collectives  11.5 us (35%)
  starting transfers between devices  11.2 us (34%)
  Pallas kernels  7.39 us (23%)
  waiting for transfers between devices  1.33 us (4%)
  between operations  0.7 us (2%)
    all_to_all x1, blocking collectives, exchange(): lax.all_to_all(x, axis, split_axis=0, concat_axis=0, axis_index_groups=[o...  11.5 us
    ppermute x4, starting transfers between devices, hop(): lax.ppermute(x, axis, [(2 * m + source, 2 * ((m + step) % pairs) + target...  6.28 us
    all_to_all x1, starting transfers between devices, exchange(): lax.all_to_all(x, axis, split_axis=0, concat_axis=0, axis_index_groups=[o...  4.87 us
    pallas_call x1, Pallas kernels, hand_over(): pl.pallas_call(functools.partial(apply_kernel, bag_count, lines, late), o...  2.98 us
    pallas_call x1, Pallas kernels, local(): pl.pallas_call(functools.partial(pool_kernel, bag_count, lines, back_lead...  2.43 us
    ppermute x4, waiting for transfers between devices, hop(): lax.ppermute(x, axis, [(2 * m + source, 2 * ((m + step) % pairs) + target...  1.32 us
    pallas_call x1, Pallas kernels, local(): pl.pallas_call(functools.partial(pack_kernel, rows_dev), out_shape=pltpu....  0.86 us
  transfers between devices with their start and end apart: 6, of which 1 were waited for; matrix products, arithmetic and copies ran while one was open for 0% of the time, Pallas kernels for 11%

profile of v21, /device:TPU:0, one launch (start us, length us, event | category | flops | bytes accessed | tf_op | source)
XLA Modules:
  0.0 32.2 jit_solution(12909306451782406235)
XLA Ops:
  0.6 0.0 copy-start
  0.6 0.9 %pack.1 = f32[8,24,128]{2,1,0:T(8,128)S(1)} custom-call(s32[4,128]{1,0:T(4,128)} %bitcast.13, s32[4,128]{1,0:T(4,128)} %bitcast.14, s32[4,128]{1,0:T(4,128)} %bitcast.15, s32[4,128]{1,0:T(4,128)} %bitcast.16, s32[4,128]{1,0:T(4,128)} %bitcast.17, s32[4,128]{1,0:T(4,128)} %bitcast.18, f32[4,256]{1,0:T(4,128)} %bitcast.12), custom_call_target="tpu_custom_call" | custom-call | tf_op jit(solution)/shard_map/pack/pallas_call | solution.py:275
  1.5 11.5 %all_to_all.10.msg = f32[8,24,128]{2,1,0:T(8,128)S(1)} all-to-all(f32[8,24,128]{2,1,0:T(8,128)S(1)} %pack.1), channel_id=1, replica_groups={{5,6,7,0,1,2,3,4},{13,14,15,8,9,10,11,12},{21,22,23,16,17,18,19,20},{29..., dimensions={0} | all-to-all | bytes 196608 | tf_op jit(solution)/shard_map/all_to_all | solution.py:238
  13.0 2.4 %pool.1 = (f32[8,4,256]{2,1,0:T(4,128)}, f32[8,16,128]{2,1,0:T(8,128)S(1)}, f32[2048,256]{1,0:T(8,128)S(1)}) custom-call(f32[8,24,128]{2,1,0:T(8,128)S(1)} %all_to_all.10.msg, f32[2048,256]{1,0:T(8,128)} %table.1), custom_call_target="tpu_custom_call" | custom-call | flops 67108864 | bytes 2097152 | tf_op jit(solution)/shard_map/pool/pallas_call | solution.py:291
  15.4 0.7 %collective-permute-start.4 = (f32[8,16,128]{2,1,0:T(8,128)S(1)}, f32[8,16,128]{2,1,0:T(8,128)S(1)}, u32[]{:S(2)}, u32[]{:S(2)}) collective-permute-start(f32[8,16,128]{2,1,0:T(8,128)S(1)} %get-tuple-element.36), channel_id=1, source_target_pairs={{8,24},{24,8},{9,25},{25,9},{10,26},{26,10},{11,27},{27,11},{12,28... | collective-permute-start | bytes 196616 | tf_op jit(solution)/shard_map/ppermute | solution.py:244
  16.1 3.0 %collective-permute-start.3 = (f32[8,16,128]{2,1,0:T(8,128)S(1)}, f32[8,16,128]{2,1,0:T(8,128)S(1)}, u32[]{:S(2)}, u32[]{:S(2)}) collective-permute-start(f32[8,16,128]{2,1,0:T(8,128)S(1)} %get-tuple-element.36), channel_id=1, source_target_pairs={{0,24},{16,8},{1,25},{17,9},{2,26},{18,10},{3,27},{19,11},{4,28},{... | collective-permute-start | bytes 196616 | tf_op jit(solution)/shard_map/ppermute | solution.py:244
  19.1 4.9 %all-to-all-start.1 = ((f32[8,4,256]{2,1,0:T(4,128)}), f32[8,4,256]{2,1,0:T(4,128)S(1)}, u32[]{:S(2)}, u32[]{:S(2)}) async-start(f32[8,4,256]{2,1,0:T(4,128)} %get-tuple-element.34), calls=%async_computation.1 | async-start | bytes 65536 | tf_op jit(solution)/shard_map/all_to_all | solution.py:238
  24.0 0.0 collective-permute-done.4
  24.0 0.0 collective-permute-done.3
  24.0 0.0 copy-done
  24.0 7.5 %conditional.1 = ((f32[2048,256]{1,0:T(8,128)}, f32[16,128]{1,0:T(8,128)S(1)})) conditional(s32[]{:T(128)} %convert_element_type.3, (f32[2048,256]{1,0:T(8,128)S(1)}, f32[16,128]{1,0:T(8,128)S(1)}) %tuple.21, (f32[8,16,128]{2,1,0:T(8,128)S(1)}, f32[8,16,128]{2,1,0:T(8,128)S(1)}, f32[8,16,128]{2,1,0:T(8,128)S(1)}, f32[2048,256]{1,0:T(8,128)S(1)}, ...), branch_computations={%region_0.0_spmd, %region_1.0_spmd} | conditional | flops 268435456 | bytes 4980864 | solution.py:390
  24.0 0.1 collective-permute-start
  24.1 1.3 %collective-permute-start.1 = (f32[8,16,128]{2,1,0:T(8,128)S(1)}, f32[8,16,128]{2,1,0:T(8,128)S(1)}, u32[]{:S(2)}, u32[]{:S(2)}) collective-permute-start(f32[8,16,128]{2,1,0:T(8,128)S(1)} %get-tuple-element.17.refs_1_), channel_id=1, source_target_pairs={{8,0},{24,16},{9,1},{25,17},{10,2},{26,18},{11,3},{27,19},{12,4},{... | collective-permute-start | bytes 196616 | tf_op jit(solution)/shard_map/cond/branch_1_fun/ppermute | solution.py:244
  25.4 1.3 %collective-permute-start.2 = (f32[8,16,128]{2,1,0:T(8,128)S(1)}, f32[8,16,128]{2,1,0:T(8,128)S(1)}, u32[]{:S(2)}, u32[]{:S(2)}) collective-permute-start(f32[8,16,128]{2,1,0:T(8,128)S(1)} %get-tuple-element.18.refs_2_), channel_id=1, source_target_pairs={{8,0},{24,16},{9,1},{25,17},{10,2},{26,18},{11,3},{27,19},{12,4},{... | collective-permute-start | bytes 196616 | tf_op jit(solution)/shard_map/cond/branch_1_fun/ppermute | solution.py:244
  26.7 0.5 %count.1 = (bf16[16,32,128]{2,1,0:T(8,128)(2,1)S(1)}, bf16[32,256]{1,0:T(8,128)(2,1)S(1)}, bf16[32,256]{1,0:T(8,128)(2,1)S(1)}) custom-call(f32[8,16,128]{2,1,0:T(8,128)S(1)} %get-tuple-element.16.refs_0_), custom_call_target="tpu_custom_call" | custom-call | flops 268435456 | bytes 4194304 | tf_op jit(solution)/shard_map/cond/branch_1_fun/count/pallas_call | solution.py:351
  27.2 0.0 collective-permute-done.refs_0_
  27.2 0.0 collective-permute-done.1.refs_3_
  27.3 1.3 %collective-permute-done.2.refs_4_ = f32[8,16,128]{2,1,0:T(8,128)S(1)} collective-permute-done((f32[8,16,128]{2,1,0:T(8,128)S(1)}, f32[8,16,128]{2,1,0:T(8,128)S(1)}, u32[]{:S(2)}, u32[]{:S(2)}) %collective-permute-start.2) | collective-permute-done | bytes 65568 | tf_op jit(solution)/shard_map/cond/branch_1_fun/ppermute | solution.py:244
  28.6 3.0 %apply.1 = (f32[2048,256]{1,0:T(8,128)}, f32[16,128]{1,0:T(8,128)S(1)}) custom-call(f32[8,16,128]{2,1,0:T(8,128)S(1)} %collective-permute-done.refs_0_, f32[8,16,128]{2,1,0:T(8,128)S(1)} %get-tuple-element.17.refs_1_, f32[8,16,128]{2,1,0:T(8,128)S(1)} %get-tuple-element.18.refs_2_, f32[8,16,128]{2,1,0:T(8,128)S(1)} %collective-permute-done.1.refs_3_, ...), custom_call_target="tpu_custom_call" | custom-call | tf_op jit(solution)/shard_map/cond/branch_1_fun/apply/pallas_call | solution.py:367
  31.5 0.0 all-to-all-done.1.returned
  31.6 0.6 %finish.1 = (f32[4,256]{1,0:T(4,128)}, f32[16,128]{1,0:T(8,128)}) custom-call(f32[8,4,256]{2,1,0:T(4,128)S(1)} %all-to-all-done.1.returned, f32[16,128]{1,0:T(8,128)S(1)} %get-tuple-element.37.accum), custom_call_target="tpu_custom_call" | custom-call | tf_op jit(solution)/shard_map/finish/pallas_call | solution.py:393
Async XLA Ops:
  0.6 23.4 %copy-start = (f32[2048]{0:T(1024)S(1)}, f32[2048]{0:T(1024)}, u32[]{:S(2)}) copy-start(f32[2048]{0:T(1024)} %param.12) | copy-start | bytes 24580
  15.4 8.6 %collective-permute-start.4 = (f32[8,16,128]{2,1,0:T(8,128)S(1)}, f32[8,16,128]{2,1,0:T(8,128)S(1)}, u32[]{:S(2)}, u32[]{:S(2)}) collective-permute-start(f32[8,16,128]{2,1,0:T(8,128)S(1)} %get-tuple-element.36), channel_id=1, source_target_pairs={{8,24},{24,8},{9,25},{25,9},{10,26},{26,10},{11,27},{27,11},{12,28... | collective-permute-start | bytes 196616 | tf_op jit(solution)/shard_map/ppermute | solution.py:244
  16.1 7.9 %collective-permute-start.3 = (f32[8,16,128]{2,1,0:T(8,128)S(1)}, f32[8,16,128]{2,1,0:T(8,128)S(1)}, u32[]{:S(2)}, u32[]{:S(2)}) collective-permute-start(f32[8,16,128]{2,1,0:T(8,128)S(1)} %get-tuple-element.36), channel_id=1, source_target_pairs={{0,24},{16,8},{1,25},{17,9},{2,26},{18,10},{3,27},{19,11},{4,28},{... | collective-permute-start | bytes 196616 | tf_op jit(solution)/shard_map/ppermute | solution.py:244
  19.1 12.4 %all-to-all-start.1 = ((f32[8,4,256]{2,1,0:T(4,128)}), f32[8,4,256]{2,1,0:T(4,128)S(1)}, u32[]{:S(2)}, u32[]{:S(2)}) async-start(f32[8,4,256]{2,1,0:T(4,128)} %get-tuple-element.34), calls=%async_computation.1 | async-start | bytes 65536 | tf_op jit(solution)/shard_map/all_to_all | solution.py:238
  24.0 3.2 %collective-permute-start = (f32[8,16,128]{2,1,0:T(8,128)S(1)}, f32[8,16,128]{2,1,0:T(8,128)S(1)}, u32[]{:S(2)}, u32[]{:S(2)}) collective-permute-start(f32[8,16,128]{2,1,0:T(8,128)S(1)} %get-tuple-element.16.refs_0_), channel_id=1, source_target_pairs={{0,8},{8,0},{16,24},{24,16},{1,9},{9,1},{17,25},{25,17},{2,10},{10... | collective-permute-start | bytes 196616 | tf_op jit(solution)/shard_map/cond/branch_1_fun/ppermute | solution.py:249
  24.1 3.1 %collective-permute-start.1 = (f32[8,16,128]{2,1,0:T(8,128)S(1)}, f32[8,16,128]{2,1,0:T(8,128)S(1)}, u32[]{:S(2)}, u32[]{:S(2)}) collective-permute-start(f32[8,16,128]{2,1,0:T(8,128)S(1)} %get-tuple-element.17.refs_1_), channel_id=1, source_target_pairs={{8,0},{24,16},{9,1},{25,17},{10,2},{26,18},{11,3},{27,19},{12,4},{... | collective-permute-start | bytes 196616 | tf_op jit(solution)/shard_map/cond/branch_1_fun/ppermute | solution.py:244
  25.4 3.1 %collective-permute-start.2 = (f32[8,16,128]{2,1,0:T(8,128)S(1)}, f32[8,16,128]{2,1,0:T(8,128)S(1)}, u32[]{:S(2)}, u32[]{:S(2)}) collective-permute-start(f32[8,16,128]{2,1,0:T(8,128)S(1)} %get-tuple-element.18.refs_2_), channel_id=1, source_target_pairs={{8,0},{24,16},{9,1},{25,17},{10,2},{26,18},{11,3},{27,19},{12,4},{... | collective-permute-start | bytes 196616 | tf_op jit(solution)/shard_map/cond/branch_1_fun/ppermute | solution.py:244

commit v22 on v20

--- a/solution.py
+++ b/solution.py
@@ -70,18 +70,9 @@
 
 
 def pool_kernel(
-    bag_count, lines, turn, msg, table, out, joined, kept, code_ref, lane_ref, counts, sems,
+    bag_count, lines, turn, msg, table, out, joined, code_ref, lane_ref, counts,
 ):
     rows_dev, width = table.shape
-    pieces = sems.shape[0]
-    rows = rows_dev // pieces
-    fetches = [
-        pltpu.make_async_copy(
-            table.at[pl.ds(i * rows, rows), :], kept.at[pl.ds(i * rows, rows), :], sems.at[i])
-        for i in range(pieces)
-    ]
-    for fetch in fetches:
-        fetch.start()
     owners = msg.shape[0]
     base = lax.axis_index("rows") * rows_dev
     code_ref[...], lane_ref[...] = codes(
@@ -92,11 +83,8 @@
     flat = jnp.concatenate(
         [counts[h].astype(jnp.bfloat16) for h in range(blocks)], axis=1)
     total = jnp.zeros((owners * bag_count, width), jnp.float32)
-    for i, fetch in enumerate(fetches):
-        fetch.wait()
-        here = slice(i * rows, (i + 1) * rows)
-        for part in split_two(kept[here, :]):
-            total += jnp.dot(flat[:, here], part, preferred_element_type=jnp.float32)
+    for part in split_two(table[...]):
+        total += jnp.dot(flat, part, preferred_element_type=jnp.float32)
     for i in range(owners):
         seen = (i + turn) % owners
         out[i] = total[seen * bag_count:(seen + 1) * bag_count, :]
@@ -274,6 +262,8 @@
         scratch_shapes=[pltpu.VMEM((lines, LANES), jnp.int32)] * 6
         + [pltpu.VMEM((bag_count, width), jnp.float32), pltpu.SemaphoreType.DMA((7,))],
         compiler_params=params,
+        cost_estimate=pl.CostEstimate(
+            flops=1 << 33, bytes_accessed=1 << 20, transcendentals=0),
         name="pack",
     )(*[stay(x) for x in (
         line(owner_map), line(row_index), line(bag_index),
@@ -281,28 +271,26 @@
     )])
     gathered = exchange(message, "rows", out_leader)
 
-    pieces = 4
-    partial_pooled, joined, kept = pl.pallas_call(
+    pieces = 8 if blocks % 8 == 0 else 1
+    partial_pooled, joined = pl.pallas_call(
         functools.partial(pool_kernel, bag_count, lines, back_leader - out_leader),
         out_shape=(
             pltpu.VMEM((owners, bag_count, width), jnp.float32),
             pltpu.VMEM((owners, prev_length, LANES), jnp.float32),
-            pltpu.VMEM((rows_dev, width), jnp.float32),
         ),
-        in_specs=[vmem, hbm],
-        out_specs=[vmem] * 3,
+        in_specs=[vmem] * 2,
+        out_specs=[vmem] * 2,
         scratch_shapes=[
             pltpu.VMEM((owners, lines, LANES), jnp.float32),
             pltpu.VMEM((owners, lines, LANES), jnp.float32),
             pltpu.VMEM((blocks, owners * bag_count, LANES), jnp.float32),
-            pltpu.SemaphoreType.DMA((pieces,)),
         ],
         compiler_params=params,
         cost_estimate=pl.CostEstimate(
             flops=4 * owners * bag_count * rows_dev * width,
             bytes_accessed=rows_dev * width * 4, transcendentals=0),
         name="pool",
-    )(gathered, stay(item_table))
+    )(gathered, item_table)
     returned = exchange(partial_pooled, "rows", back_leader)
     there = [joined] + [forward(joined, "dp", step) for step in range(1, groups // 2)]
 
@@ -379,7 +367,7 @@
 
     inside = lax.axis_index("dp") < groups
     new_table, new_accum = lax.cond(
-        inside, hand_over, skip, there, kept, row_accum.reshape(blocks, LANES))
+        inside, hand_over, skip, there, item_table, row_accum.reshape(blocks, LANES))
 
     pooled, new_accum = pl.pallas_call(
         finish_kernel,

time: 26.2 us -> 25.7 us (0.981)
  Pallas kernels: 7.43 us -> 6.97 us
    pallas_call x1, Pallas kernels: 2.43 us -> 1.88 us  [local(): pl.pallas_call(functools.partial(pool_kernel, bag_count, lines, back_lead...]
where the time goes in v22:
time: 25.7 us; the launch traced here: 25.4 us
  blocking collectives  11.5 us (45%)
  Pallas kernels  6.97 us (27%)
  starting transfers between devices  5.79 us (23%)
  between operations  0.67 us (3%)
  waiting for transfers between devices  0.49 us (2%)
    all_to_all x1, blocking collectives, exchange(): lax.all_to_all(x, axis, split_axis=0, concat_axis=0, axis_index_groups=[o...  11.5 us
    all_to_all x1, starting transfers between devices, exchange(): lax.all_to_all(x, axis, split_axis=0, concat_axis=0, axis_index_groups=[o...  4.57 us
    pallas_call x1, Pallas kernels, hand_over(): pl.pallas_call(functools.partial(apply_kernel, bag_count, lines, number),...  2.6 us
    pallas_call x1, Pallas kernels, local(): pl.pallas_call(functools.partial(pool_kernel, bag_count, lines, back_lead...  1.88 us
    ppermute x3, starting transfers between devices, forward(): lax.ppermute(x, axis, [(i, ((i // 2 + step) * 2 + 1 - i % 2) % size) for...  1.22 us
    pallas_call x1, Pallas kernels, local(): pl.pallas_call(functools.partial(pack_kernel, rows_dev), out_shape=pltpu....  1.01 us
    pallas_call x1, Pallas kernels, hand_over(): pl.pallas_call(functools.partial(count_kernel, bag_count, lines), out_sha...  0.88 us
    pallas_call x1, Pallas kernels, local(): pl.pallas_call(finish_kernel, out_shape=(jax.ShapeDtypeStruct((bag_count,...  0.6 us
  transfers between devices with their start and end apart: 4, of which 2 were waited for; matrix products, arithmetic and copies ran while one was open for 0% of the time, Pallas kernels for 14%

profile of v22, /device:TPU:0, one launch (start us, length us, event | category | flops | bytes accessed | tf_op | source)
XLA Modules:
  0.0 25.4 jit_solution(525138418817534796)
XLA Ops:
  0.6 0.0 copy-start
  0.6 1.0 %pack.1 = f32[8,24,128]{2,1,0:T(8,128)S(1)} custom-call(s32[4,128]{1,0:T(4,128)} %bitcast.15, s32[4,128]{1,0:T(4,128)} %bitcast.16, s32[4,128]{1,0:T(4,128)} %bitcast.17, s32[4,128]{1,0:T(4,128)} %bitcast.18, s32[4,128]{1,0:T(4,128)} %bitcast.19, s32[4,128]{1,0:T(4,128)} %bitcast.20, f32[4,256]{1,0:T(4,128)} %bitcast.13), custom_call_target="tpu_custom_call" | custom-call | flops 8589934592 | bytes 1048576 | tf_op jit(solution)/shard_map/pack/pallas_call | solution.py:257
  1.7 0.0 copy-start.1
  1.7 11.5 %all_to_all.10.msg = f32[8,24,128]{2,1,0:T(8,128)S(1)} all-to-all(f32[8,24,128]{2,1,0:T(8,128)S(1)} %pack.1), channel_id=1, replica_groups={{5,6,7,0,1,2,3,4},{13,14,15,8,9,10,11,12},{21,22,23,16,17,18,19,20},{29..., dimensions={0} | all-to-all | bytes 196608 | tf_op jit(solution)/shard_map/all_to_all | solution.py:224
  13.1 0.0 copy-done
  13.1 1.9 %pool.1 = (f32[8,4,256]{2,1,0:T(4,128)}, f32[8,16,128]{2,1,0:T(8,128)S(1)}) custom-call(f32[8,24,128]{2,1,0:T(8,128)S(1)} %all_to_all.10.msg, f32[2048,256]{1,0:T(8,128)S(1)} %copy-done), custom_call_target="tpu_custom_call" | custom-call | flops 67108864 | bytes 2097152 | tf_op jit(solution)/shard_map/pool/pallas_call | solution.py:275
  15.0 0.0 collective-permute-start.2
  15.0 4.6 %all-to-all-start.1 = ((f32[8,4,256]{2,1,0:T(4,128)}), f32[8,4,256]{2,1,0:T(4,128)S(1)}, u32[]{:S(2)}, u32[]{:S(2)}) async-start(f32[8,4,256]{2,1,0:T(4,128)} %get-tuple-element.30), calls=%async_computation.1 | async-start | bytes 65536 | tf_op jit(solution)/shard_map/all_to_all | solution.py:224
  19.6 0.0 collective-permute-done.2
  19.6 0.0 copy-done.1
  19.6 5.0 %conditional.1 = ((f32[2048,256]{1,0:T(8,128)}, f32[16,128]{1,0:T(8,128)S(1)})) conditional(s32[]{:T(128)} %convert_element_type.3, (f32[2048,256]{1,0:T(8,128)S(1)}, f32[16,128]{1,0:T(8,128)S(1)}) %tuple.23, (f32[8,16,128]{2,1,0:T(8,128)S(1)}, f32[8,16,128]{2,1,0:T(8,128)S(1)}, f32[2048,256]{1,0:T(8,128)S(1)}, f32[16,128]{1,0:T(8,128)S(1)}) %tuple.24), branch_computations={%region_0.0_spmd, %region_1.0_spmd} | conditional | flops 268435456 | bytes 4718680 | solution.py:369
  19.6 1.1 %collective-permute-start = (f32[8,16,128]{2,1,0:T(8,128)S(1)}, f32[8,16,128]{2,1,0:T(8,128)S(1)}, u32[]{:S(2)}, u32[]{:S(2)}) collective-permute-start(f32[8,16,128]{2,1,0:T(8,128)S(1)} %get-tuple-element.14.refs_0_), channel_id=1, source_target_pairs={{0,8},{8,0},{16,24},{24,16},{1,9},{9,1},{17,25},{25,17},{2,10},{10... | collective-permute-start | bytes 196616 | tf_op jit(solution)/shard_map/cond/branch_1_fun/ppermute | solution.py:230
  20.8 0.1 collective-permute-start.1
  20.8 0.9 %count.1 = (bf16[16,64,128]{2,1,0:T(8,128)(2,1)S(1)}, bf16[64,256]{1,0:T(8,128)(2,1)S(1)}, bf16[64,256]{1,0:T(8,128)(2,1)S(1)}) custom-call(f32[8,16,128]{2,1,0:T(8,128)S(1)} %get-tuple-element.14.refs_0_, f32[8,16,128]{2,1,0:T(8,128)S(1)} %get-tuple-element.15.refs_1_), custom_call_target="tpu_custom_call" | custom-call | flops 268435456 | bytes 4194304 | tf_op jit(solution)/shard_map/cond/branch_1_fun/count/pallas_call | solution.py:331
  21.7 0.0 collective-permute-done.refs_0_
  21.7 0.3 %collective-permute-done.1.refs_1_ = f32[8,16,128]{2,1,0:T(8,128)S(1)} collective-permute-done((f32[8,16,128]{2,1,0:T(8,128)S(1)}, f32[8,16,128]{2,1,0:T(8,128)S(1)}, u32[]{:S(2)}, u32[]{:S(2)}) %collective-permute-start.1) | collective-permute-done | bytes 65568 | tf_op jit(solution)/shard_map/cond/branch_1_fun/ppermute | solution.py:230
  22.0 2.6 %apply.1 = (f32[2048,256]{1,0:T(8,128)}, f32[16,128]{1,0:T(8,128)S(1)}) custom-call(f32[8,16,128]{2,1,0:T(8,128)S(1)} %collective-permute-done.refs_0_, f32[8,16,128]{2,1,0:T(8,128)S(1)} %collective-permute-done.1.refs_1_, bf16[16,64,128]{2,1,0:T(8,128)(2,1)S(1)} %get-tuple-element.16.refs_2_, bf16[64,256]{1,0:T(8,128)(2,1)S(1)} %get-tuple-element.17.refs_3_, ...), custom_call_target="tpu_custom_call" | custom-call | tf_op jit(solution)/shard_map/cond/branch_1_fun/apply/pallas_call | solution.py:346
  24.6 0.2 all-to-all-done.1.returned
  24.8 0.6 %finish.1 = (f32[4,256]{1,0:T(4,128)}, f32[16,128]{1,0:T(8,128)}) custom-call(f32[8,4,256]{2,1,0:T(4,128)S(1)} %all-to-all-done.1.returned, f32[16,128]{1,0:T(8,128)S(1)} %get-tuple-element.32.accum), custom_call_target="tpu_custom_call" | custom-call | tf_op jit(solution)/shard_map/finish/pallas_call | solution.py:372
Async XLA Ops:
  0.6 12.5 %copy-start = (f32[2048,256]{1,0:T(8,128)S(1)}, f32[2048,256]{1,0:T(8,128)}, u32[]{:S(2)}) copy-start(f32[2048,256]{1,0:T(8,128)} %table.1) | copy-start | bytes 6291460
  1.7 18.0 %copy-start.1 = (f32[2048]{0:T(1024)S(1)}, f32[2048]{0:T(1024)}, u32[]{:S(2)}) copy-start(f32[2048]{0:T(1024)} %param.12) | copy-start | bytes 24580
  15.0 4.6 %collective-permute-start.2 = (f32[8,16,128]{2,1,0:T(8,128)S(1)}, f32[8,16,128]{2,1,0:T(8,128)S(1)}, u32[]{:S(2)}, u32[]{:S(2)}) collective-permute-start(f32[8,16,128]{2,1,0:T(8,128)S(1)} %get-tuple-element.31), channel_id=1, source_target_pairs={{0,24},{8,16},{16,8},{24,0},{1,25},{9,17},{17,9},{25,1},{2,26},{10... | collective-permute-start | bytes 196616 | tf_op jit(solution)/shard_map/ppermute | solution.py:230
  15.0 9.8 %all-to-all-start.1 = ((f32[8,4,256]{2,1,0:T(4,128)}), f32[8,4,256]{2,1,0:T(4,128)S(1)}, u32[]{:S(2)}, u32[]{:S(2)}) async-start(f32[8,4,256]{2,1,0:T(4,128)} %get-tuple-element.30), calls=%async_computation.1 | async-start | bytes 65536 | tf_op jit(solution)/shard_map/all_to_all | solution.py:224
  19.6 2.1 %collective-permute-start = (f32[8,16,128]{2,1,0:T(8,128)S(1)}, f32[8,16,128]{2,1,0:T(8,128)S(1)}, u32[]{:S(2)}, u32[]{:S(2)}) collective-permute-start(f32[8,16,128]{2,1,0:T(8,128)S(1)} %get-tuple-element.14.refs_0_), channel_id=1, source_target_pairs={{0,8},{8,0},{16,24},{24,16},{1,9},{9,1},{17,25},{25,17},{2,10},{10... | collective-permute-start | bytes 196616 | tf_op jit(solution)/shard_map/cond/branch_1_fun/ppermute | solution.py:230
  20.8 1.3 %collective-permute-start.1 = (f32[8,16,128]{2,1,0:T(8,128)S(1)}, f32[8,16,128]{2,1,0:T(8,128)S(1)}, u32[]{:S(2)}, u32[]{:S(2)}) collective-permute-start(f32[8,16,128]{2,1,0:T(8,128)S(1)} %get-tuple-element.15.refs_1_), channel_id=1, source_target_pairs={{0,8},{8,0},{16,24},{24,16},{1,9},{9,1},{17,25},{25,17},{2,10},{10... | collective-permute-start | bytes 196616 | tf_op jit(solution)/shard_map/cond/branch_1_fun/ppermute | solution.py:230

commit v23 on v22

--- a/solution.py
+++ b/solution.py
@@ -102,11 +102,10 @@
 
 
 def block_sum(hits, parts):
-    total = jnp.zeros((hits.shape[1], parts[0].shape[1]), jnp.float32)
-    for part in parts:
-        total += lax.dot_general(
-            hits, part, (((0,), (0,)), ((), ())), preferred_element_type=jnp.float32)
-    return total
+    width = parts.shape[1] // 2
+    both = lax.dot_general(
+        hits, parts, (((0,), (0,)), ((), ())), preferred_element_type=jnp.float32)
+    return both[:, :width] + both[:, width:]
 
 
 def apply_rows(grad_of, table, accum, new_table, new_accum, fresh_table, sems):
@@ -164,10 +163,10 @@
     read_chunk(
         msg, slice(0, devices), devices, lines, bag_count, base,
         code_ref, lane_ref, counts, grads)
-    parts = [
-        jnp.concatenate([early[...], late], axis=0)
-        for early, late in zip((high, low), split_two(grads[...]))
-    ]
+    parts = jnp.concatenate([
+        jnp.concatenate([early[...], last], axis=0)
+        for early, last in zip((high, low), split_two(grads[...]))
+    ], axis=1)
 
     def grad_of(h):
         hits = jnp.concatenate([counted[h], counts[h].astype(jnp.bfloat16)], axis=0)
@@ -191,7 +190,7 @@
         read_chunk(
             msg, pl.ds(c * chunk, chunk), chunk, lines, bag_count, base,
             code_ref, lane_ref, counts, grads)
-        parts = split_two(grads[...])
+        parts = jnp.concatenate(split_two(grads[...]), axis=1)
 
         @pl.loop(0, blocks)
         def _(h):

time: 25.7 us -> 25.7 us (level)
  no operation moved by 1% of the time
where the time goes in v23:
time: 25.7 us; the launch traced here: 25.4 us
  blocking collectives  11.5 us (45%)
  Pallas kernels  6.97 us (27%)
  starting transfers between devices  5.79 us (23%)
  between operations  0.67 us (3%)
  waiting for transfers between devices  0.49 us (2%)
    all_to_all x1, blocking collectives, exchange(): lax.all_to_all(x, axis, split_axis=0, concat_axis=0, axis_index_groups=[o...  11.5 us
    all_to_all x1, starting transfers between devices, exchange(): lax.all_to_all(x, axis, split_axis=0, concat_axis=0, axis_index_groups=[o...  4.57 us
    pallas_call x1, Pallas kernels, hand_over(): pl.pallas_call(functools.partial(apply_kernel, bag_count, lines, number),...  2.6 us
    pallas_call x1, Pallas kernels, local(): pl.pallas_call(functools.partial(pool_kernel, bag_count, lines, back_lead...  1.88 us
    ppermute x3, starting transfers between devices, forward(): lax.ppermute(x, axis, [(i, ((i // 2 + step) * 2 + 1 - i % 2) % size) for...  1.22 us
    pallas_call x1, Pallas kernels, local(): pl.pallas_call(functools.partial(pack_kernel, rows_dev), out_shape=pltpu....  1.01 us
    pallas_call x1, Pallas kernels, hand_over(): pl.pallas_call(functools.partial(count_kernel, bag_count, lines), out_sha...  0.88 us
    pallas_call x1, Pallas kernels, local(): pl.pallas_call(finish_kernel, out_shape=(jax.ShapeDtypeStruct((bag_count,...  0.6 us
  transfers between devices with their start and end apart: 4, of which 2 were waited for; matrix products, arithmetic and copies ran while one was open for 0% of the time, Pallas kernels for 14%

profile of v23, /device:TPU:0, one launch (start us, length us, event | category | flops | bytes accessed | tf_op | source)
XLA Modules:
  0.0 25.4 jit_solution(7320429698702633052)
XLA Ops:
  0.6 0.0 copy-start
  0.6 1.0 %pack.1 = f32[8,24,128]{2,1,0:T(8,128)S(1)} custom-call(s32[4,128]{1,0:T(4,128)} %bitcast.15, s32[4,128]{1,0:T(4,128)} %bitcast.16, s32[4,128]{1,0:T(4,128)} %bitcast.17, s32[4,128]{1,0:T(4,128)} %bitcast.18, s32[4,128]{1,0:T(4,128)} %bitcast.19, s32[4,128]{1,0:T(4,128)} %bitcast.20, f32[4,256]{1,0:T(4,128)} %bitcast.13), custom_call_target="tpu_custom_call" | custom-call | flops 8589934592 | bytes 1048576 | tf_op jit(solution)/shard_map/pack/pallas_call | solution.py:256
  1.7 0.0 copy-start.1
  1.7 11.5 %all_to_all.10.msg = f32[8,24,128]{2,1,0:T(8,128)S(1)} all-to-all(f32[8,24,128]{2,1,0:T(8,128)S(1)} %pack.1), channel_id=1, replica_groups={{5,6,7,0,1,2,3,4},{13,14,15,8,9,10,11,12},{21,22,23,16,17,18,19,20},{29..., dimensions={0} | all-to-all | bytes 196608 | tf_op jit(solution)/shard_map/all_to_all | solution.py:223
  13.1 0.0 copy-done
  13.1 1.9 %pool.1 = (f32[8,4,256]{2,1,0:T(4,128)}, f32[8,16,128]{2,1,0:T(8,128)S(1)}) custom-call(f32[8,24,128]{2,1,0:T(8,128)S(1)} %all_to_all.10.msg, f32[2048,256]{1,0:T(8,128)S(1)} %copy-done), custom_call_target="tpu_custom_call" | custom-call | flops 67108864 | bytes 2097152 | tf_op jit(solution)/shard_map/pool/pallas_call | solution.py:274
  15.0 0.0 collective-permute-start.2
  15.0 4.6 %all-to-all-start.1 = ((f32[8,4,256]{2,1,0:T(4,128)}), f32[8,4,256]{2,1,0:T(4,128)S(1)}, u32[]{:S(2)}, u32[]{:S(2)}) async-start(f32[8,4,256]{2,1,0:T(4,128)} %get-tuple-element.30), calls=%async_computation.1 | async-start | bytes 65536 | tf_op jit(solution)/shard_map/all_to_all | solution.py:223
  19.6 0.0 collective-permute-done.2
  19.6 0.0 copy-done.1
  19.6 5.0 %conditional.1 = ((f32[2048,256]{1,0:T(8,128)}, f32[16,128]{1,0:T(8,128)S(1)})) conditional(s32[]{:T(128)} %convert_element_type.3, (f32[2048,256]{1,0:T(8,128)S(1)}, f32[16,128]{1,0:T(8,128)S(1)}) %tuple.23, (f32[8,16,128]{2,1,0:T(8,128)S(1)}, f32[8,16,128]{2,1,0:T(8,128)S(1)}, f32[2048,256]{1,0:T(8,128)S(1)}, f32[16,128]{1,0:T(8,128)S(1)}) %tuple.24), branch_computations={%region_0.0_spmd, %region_1.0_spmd} | conditional | flops 268435456 | bytes 4718680 | solution.py:368
  19.6 1.1 %collective-permute-start = (f32[8,16,128]{2,1,0:T(8,128)S(1)}, f32[8,16,128]{2,1,0:T(8,128)S(1)}, u32[]{:S(2)}, u32[]{:S(2)}) collective-permute-start(f32[8,16,128]{2,1,0:T(8,128)S(1)} %get-tuple-element.14.refs_0_), channel_id=1, source_target_pairs={{0,8},{8,0},{16,24},{24,16},{1,9},{9,1},{17,25},{25,17},{2,10},{10... | collective-permute-start | bytes 196616 | tf_op jit(solution)/shard_map/cond/branch_1_fun/ppermute | solution.py:229
  20.8 0.1 collective-permute-start.1
  20.8 0.9 %count.1 = (bf16[16,64,128]{2,1,0:T(8,128)(2,1)S(1)}, bf16[64,256]{1,0:T(8,128)(2,1)S(1)}, bf16[64,256]{1,0:T(8,128)(2,1)S(1)}) custom-call(f32[8,16,128]{2,1,0:T(8,128)S(1)} %get-tuple-element.14.refs_0_, f32[8,16,128]{2,1,0:T(8,128)S(1)} %get-tuple-element.15.refs_1_), custom_call_target="tpu_custom_call" | custom-call | flops 268435456 | bytes 4194304 | tf_op jit(solution)/shard_map/cond/branch_1_fun/count/pallas_call | solution.py:330
  21.7 0.0 collective-permute-done.refs_0_
  21.7 0.3 %collective-permute-done.1.refs_1_ = f32[8,16,128]{2,1,0:T(8,128)S(1)} collective-permute-done((f32[8,16,128]{2,1,0:T(8,128)S(1)}, f32[8,16,128]{2,1,0:T(8,128)S(1)}, u32[]{:S(2)}, u32[]{:S(2)}) %collective-permute-start.1) | collective-permute-done | bytes 65568 | tf_op jit(solution)/shard_map/cond/branch_1_fun/ppermute | solution.py:229
  22.0 2.6 %apply.1 = (f32[2048,256]{1,0:T(8,128)}, f32[16,128]{1,0:T(8,128)S(1)}) custom-call(f32[8,16,128]{2,1,0:T(8,128)S(1)} %collective-permute-done.refs_0_, f32[8,16,128]{2,1,0:T(8,128)S(1)} %collective-permute-done.1.refs_1_, bf16[16,64,128]{2,1,0:T(8,128)(2,1)S(1)} %get-tuple-element.16.refs_2_, bf16[64,256]{1,0:T(8,128)(2,1)S(1)} %get-tuple-element.17.refs_3_, ...), custom_call_target="tpu_custom_call" | custom-call | tf_op jit(solution)/shard_map/cond/branch_1_fun/apply/pallas_call | solution.py:345
  24.6 0.2 all-to-all-done.1.returned
  24.8 0.6 %finish.1 = (f32[4,256]{1,0:T(4,128)}, f32[16,128]{1,0:T(8,128)}) custom-call(f32[8,4,256]{2,1,0:T(4,128)S(1)} %all-to-all-done.1.returned, f32[16,128]{1,0:T(8,128)S(1)} %get-tuple-element.32.accum), custom_call_target="tpu_custom_call" | custom-call | tf_op jit(solution)/shard_map/finish/pallas_call | solution.py:371
Async XLA Ops:
  0.6 12.5 %copy-start = (f32[2048,256]{1,0:T(8,128)S(1)}, f32[2048,256]{1,0:T(8,128)}, u32[]{:S(2)}) copy-start(f32[2048,256]{1,0:T(8,128)} %table.1) | copy-start | bytes 6291460
  1.7 18.0 %copy-start.1 = (f32[2048]{0:T(1024)S(1)}, f32[2048]{0:T(1024)}, u32[]{:S(2)}) copy-start(f32[2048]{0:T(1024)} %param.12) | copy-start | bytes 24580
  15.0 4.6 %collective-permute-start.2 = (f32[8,16,128]{2,1,0:T(8,128)S(1)}, f32[8,16,128]{2,1,0:T(8,128)S(1)}, u32[]{:S(2)}, u32[]{:S(2)}) collective-permute-start(f32[8,16,128]{2,1,0:T(8,128)S(1)} %get-tuple-element.31), channel_id=1, source_target_pairs={{0,24},{8,16},{16,8},{24,0},{1,25},{9,17},{17,9},{25,1},{2,26},{10... | collective-permute-start | bytes 196616 | tf_op jit(solution)/shard_map/ppermute | solution.py:229
  15.0 9.8 %all-to-all-start.1 = ((f32[8,4,256]{2,1,0:T(4,128)}), f32[8,4,256]{2,1,0:T(4,128)S(1)}, u32[]{:S(2)}, u32[]{:S(2)}) async-start(f32[8,4,256]{2,1,0:T(4,128)} %get-tuple-element.30), calls=%async_computation.1 | async-start | bytes 65536 | tf_op jit(solution)/shard_map/all_to_all | solution.py:223
  19.6 2.1 %collective-permute-start = (f32[8,16,128]{2,1,0:T(8,128)S(1)}, f32[8,16,128]{2,1,0:T(8,128)S(1)}, u32[]{:S(2)}, u32[]{:S(2)}) collective-permute-start(f32[8,16,128]{2,1,0:T(8,128)S(1)} %get-tuple-element.14.refs_0_), channel_id=1, source_target_pairs={{0,8},{8,0},{16,24},{24,16},{1,9},{9,1},{17,25},{25,17},{2,10},{10... | collective-permute-start | bytes 196616 | tf_op jit(solution)/shard_map/cond/branch_1_fun/ppermute | solution.py:229
  20.8 1.3 %collective-permute-start.1 = (f32[8,16,128]{2,1,0:T(8,128)S(1)}, f32[8,16,128]{2,1,0:T(8,128)S(1)}, u32[]{:S(2)}, u32[]{:S(2)}) collective-permute-start(f32[8,16,128]{2,1,0:T(8,128)S(1)} %get-tuple-element.15.refs_1_), channel_id=1, source_target_pairs={{0,8},{8,0},{16,24},{24,16},{1,9},{9,1},{17,25},{25,17},{2,10},{10... | collective-permute-start | bytes 196616 | tf_op jit(solution)/shard_map/cond/branch_1_fun/ppermute | solution.py:229

commit v24 on v23

--- a/solution.py
+++ b/solution.py
@@ -82,9 +82,9 @@
     blocks = rows_dev // LANES
     flat = jnp.concatenate(
         [counts[h].astype(jnp.bfloat16) for h in range(blocks)], axis=1)
-    total = jnp.zeros((owners * bag_count, width), jnp.float32)
-    for part in split_two(table[...]):
-        total += jnp.dot(flat, part, preferred_element_type=jnp.float32)
+    parts = jnp.concatenate(split_two(table[...]), axis=1)
+    both = jnp.dot(flat, parts, preferred_element_type=jnp.float32)
+    total = both[:, :width] + both[:, width:]
     for i in range(owners):
         seen = (i + turn) % owners
         out[i] = total[seen * bag_count:(seen + 1) * bag_count, :]

time: 25.7 us -> 25.7 us (level)
  no operation moved by 1% of the time
where the time goes in v24:
time: 25.7 us; the launch traced here: 25.4 us
  blocking collectives  11.5 us (45%)
  Pallas kernels  6.96 us (27%)
  starting transfers between devices  5.79 us (23%)
  between operations  0.67 us (3%)
  waiting for transfers between devices  0.5 us (2%)
    all_to_all x1, blocking collectives, exchange(): lax.all_to_all(x, axis, split_axis=0, concat_axis=0, axis_index_groups=[o...  11.5 us
    all_to_all x1, starting transfers between devices, exchange(): lax.all_to_all(x, axis, split_axis=0, concat_axis=0, axis_index_groups=[o...  4.57 us
    pallas_call x1, Pallas kernels, hand_over(): pl.pallas_call(functools.partial(apply_kernel, bag_count, lines, number),...  2.6 us
    pallas_call x1, Pallas kernels, local(): pl.pallas_call(functools.partial(pool_kernel, bag_count, lines, back_lead...  1.88 us
    ppermute x3, starting transfers between devices, forward(): lax.ppermute(x, axis, [(i, ((i // 2 + step) * 2 + 1 - i % 2) % size) for...  1.22 us
    pallas_call x1, Pallas kernels, local(): pl.pallas_call(functools.partial(pack_kernel, rows_dev), out_shape=pltpu....  1.01 us
    pallas_call x1, Pallas kernels, hand_over(): pl.pallas_call(functools.partial(count_kernel, bag_count, lines), out_sha...  0.88 us
    pallas_call x1, Pallas kernels, local(): pl.pallas_call(finish_kernel, out_shape=(jax.ShapeDtypeStruct((bag_count,...  0.6 us
  transfers between devices with their start and end apart: 4, of which 2 were waited for; matrix products, arithmetic and copies ran while one was open for 0% of the time, Pallas kernels for 14%

profile of v24, /device:TPU:0, one launch (start us, length us, event | category | flops | bytes accessed | tf_op | source)
XLA Modules:
  0.0 25.4 jit_solution(2528293955384643888)
XLA Ops:
  0.6 0.0 copy-start
  0.6 1.0 %pack.1 = f32[8,24,128]{2,1,0:T(8,128)S(1)} custom-call(s32[4,128]{1,0:T(4,128)} %bitcast.15, s32[4,128]{1,0:T(4,128)} %bitcast.16, s32[4,128]{1,0:T(4,128)} %bitcast.17, s32[4,128]{1,0:T(4,128)} %bitcast.18, s32[4,128]{1,0:T(4,128)} %bitcast.19, s32[4,128]{1,0:T(4,128)} %bitcast.20, f32[4,256]{1,0:T(4,128)} %bitcast.13), custom_call_target="tpu_custom_call" | custom-call | flops 8589934592 | bytes 1048576 | tf_op jit(solution)/shard_map/pack/pallas_call | solution.py:256
  1.7 0.0 copy-start.1
  1.7 11.5 %all_to_all.10.msg = f32[8,24,128]{2,1,0:T(8,128)S(1)} all-to-all(f32[8,24,128]{2,1,0:T(8,128)S(1)} %pack.1), channel_id=1, replica_groups={{5,6,7,0,1,2,3,4},{13,14,15,8,9,10,11,12},{21,22,23,16,17,18,19,20},{29..., dimensions={0} | all-to-all | bytes 196608 | tf_op jit(solution)/shard_map/all_to_all | solution.py:223
  13.1 0.0 copy-done
  13.1 1.9 %pool.1 = (f32[8,4,256]{2,1,0:T(4,128)}, f32[8,16,128]{2,1,0:T(8,128)S(1)}) custom-call(f32[8,24,128]{2,1,0:T(8,128)S(1)} %all_to_all.10.msg, f32[2048,256]{1,0:T(8,128)S(1)} %copy-done), custom_call_target="tpu_custom_call" | custom-call | flops 67108864 | bytes 2097152 | tf_op jit(solution)/shard_map/pool/pallas_call | solution.py:274
  15.0 0.0 collective-permute-start.2
  15.0 4.6 %all-to-all-start.1 = ((f32[8,4,256]{2,1,0:T(4,128)}), f32[8,4,256]{2,1,0:T(4,128)S(1)}, u32[]{:S(2)}, u32[]{:S(2)}) async-start(f32[8,4,256]{2,1,0:T(4,128)} %get-tuple-element.30), calls=%async_computation.1 | async-start | bytes 65536 | tf_op jit(solution)/shard_map/all_to_all | solution.py:223
  19.6 0.0 collective-permute-done.2
  19.6 0.0 copy-done.1
  19.6 5.0 %conditional.1 = ((f32[2048,256]{1,0:T(8,128)}, f32[16,128]{1,0:T(8,128)S(1)})) conditional(s32[]{:T(128)} %convert_element_type.3, (f32[2048,256]{1,0:T(8,128)S(1)}, f32[16,128]{1,0:T(8,128)S(1)}) %tuple.23, (f32[8,16,128]{2,1,0:T(8,128)S(1)}, f32[8,16,128]{2,1,0:T(8,128)S(1)}, f32[2048,256]{1,0:T(8,128)S(1)}, f32[16,128]{1,0:T(8,128)S(1)}) %tuple.24), branch_computations={%region_0.0_spmd, %region_1.0_spmd} | conditional | flops 268435456 | bytes 4718680 | solution.py:368
  19.6 1.1 %collective-permute-start = (f32[8,16,128]{2,1,0:T(8,128)S(1)}, f32[8,16,128]{2,1,0:T(8,128)S(1)}, u32[]{:S(2)}, u32[]{:S(2)}) collective-permute-start(f32[8,16,128]{2,1,0:T(8,128)S(1)} %get-tuple-element.14.refs_0_), channel_id=1, source_target_pairs={{0,8},{8,0},{16,24},{24,16},{1,9},{9,1},{17,25},{25,17},{2,10},{10... | collective-permute-start | bytes 196616 | tf_op jit(solution)/shard_map/cond/branch_1_fun/ppermute | solution.py:229
  20.8 0.1 collective-permute-start.1
  20.8 0.9 %count.1 = (bf16[16,64,128]{2,1,0:T(8,128)(2,1)S(1)}, bf16[64,256]{1,0:T(8,128)(2,1)S(1)}, bf16[64,256]{1,0:T(8,128)(2,1)S(1)}) custom-call(f32[8,16,128]{2,1,0:T(8,128)S(1)} %get-tuple-element.14.refs_0_, f32[8,16,128]{2,1,0:T(8,128)S(1)} %get-tuple-element.15.refs_1_), custom_call_target="tpu_custom_call" | custom-call | flops 268435456 | bytes 4194304 | tf_op jit(solution)/shard_map/cond/branch_1_fun/count/pallas_call | solution.py:330
  21.7 0.0 collective-permute-done.refs_0_
  21.7 0.3 %collective-permute-done.1.refs_1_ = f32[8,16,128]{2,1,0:T(8,128)S(1)} collective-permute-done((f32[8,16,128]{2,1,0:T(8,128)S(1)}, f32[8,16,128]{2,1,0:T(8,128)S(1)}, u32[]{:S(2)}, u32[]{:S(2)}) %collective-permute-start.1) | collective-permute-done | bytes 65568 | tf_op jit(solution)/shard_map/cond/branch_1_fun/ppermute | solution.py:229
  22.0 2.6 %apply.1 = (f32[2048,256]{1,0:T(8,128)}, f32[16,128]{1,0:T(8,128)S(1)}) custom-call(f32[8,16,128]{2,1,0:T(8,128)S(1)} %collective-permute-done.refs_0_, f32[8,16,128]{2,1,0:T(8,128)S(1)} %collective-permute-done.1.refs_1_, bf16[16,64,128]{2,1,0:T(8,128)(2,1)S(1)} %get-tuple-element.16.refs_2_, bf16[64,256]{1,0:T(8,128)(2,1)S(1)} %get-tuple-element.17.refs_3_, ...), custom_call_target="tpu_custom_call" | custom-call | tf_op jit(solution)/shard_map/cond/branch_1_fun/apply/pallas_call | solution.py:345
  24.6 0.2 all-to-all-done.1.returned
  24.8 0.6 %finish.1 = (f32[4,256]{1,0:T(4,128)}, f32[16,128]{1,0:T(8,128)}) custom-call(f32[8,4,256]{2,1,0:T(4,128)S(1)} %all-to-all-done.1.returned, f32[16,128]{1,0:T(8,128)S(1)} %get-tuple-element.32.accum), custom_call_target="tpu_custom_call" | custom-call | tf_op jit(solution)/shard_map/finish/pallas_call | solution.py:371
Async XLA Ops:
  0.6 12.5 %copy-start = (f32[2048,256]{1,0:T(8,128)S(1)}, f32[2048,256]{1,0:T(8,128)}, u32[]{:S(2)}) copy-start(f32[2048,256]{1,0:T(8,128)} %table.1) | copy-start | bytes 6291460
  1.7 18.0 %copy-start.1 = (f32[2048]{0:T(1024)S(1)}, f32[2048]{0:T(1024)}, u32[]{:S(2)}) copy-start(f32[2048]{0:T(1024)} %param.12) | copy-start | bytes 24580
  15.0 4.6 %collective-permute-start.2 = (f32[8,16,128]{2,1,0:T(8,128)S(1)}, f32[8,16,128]{2,1,0:T(8,128)S(1)}, u32[]{:S(2)}, u32[]{:S(2)}) collective-permute-start(f32[8,16,128]{2,1,0:T(8,128)S(1)} %get-tuple-element.31), channel_id=1, source_target_pairs={{0,24},{8,16},{16,8},{24,0},{1,25},{9,17},{17,9},{25,1},{2,26},{10... | collective-permute-start | bytes 196616 | tf_op jit(solution)/shard_map/ppermute | solution.py:229
  15.0 9.8 %all-to-all-start.1 = ((f32[8,4,256]{2,1,0:T(4,128)}), f32[8,4,256]{2,1,0:T(4,128)S(1)}, u32[]{:S(2)}, u32[]{:S(2)}) async-start(f32[8,4,256]{2,1,0:T(4,128)} %get-tuple-element.30), calls=%async_computation.1 | async-start | bytes 65536 | tf_op jit(solution)/shard_map/all_to_all | solution.py:223
  19.6 2.1 %collective-permute-start = (f32[8,16,128]{2,1,0:T(8,128)S(1)}, f32[8,16,128]{2,1,0:T(8,128)S(1)}, u32[]{:S(2)}, u32[]{:S(2)}) collective-permute-start(f32[8,16,128]{2,1,0:T(8,128)S(1)} %get-tuple-element.14.refs_0_), channel_id=1, source_target_pairs={{0,8},{8,0},{16,24},{24,16},{1,9},{9,1},{17,25},{25,17},{2,10},{10... | collective-permute-start | bytes 196616 | tf_op jit(solution)/shard_map/cond/branch_1_fun/ppermute | solution.py:229
  20.8 1.3 %collective-permute-start.1 = (f32[8,16,128]{2,1,0:T(8,128)S(1)}, f32[8,16,128]{2,1,0:T(8,128)S(1)}, u32[]{:S(2)}, u32[]{:S(2)}) collective-permute-start(f32[8,16,128]{2,1,0:T(8,128)S(1)} %get-tuple-element.15.refs_1_), channel_id=1, source_target_pairs={{0,8},{8,0},{16,24},{24,16},{1,9},{9,1},{17,25},{25,17},{2,10},{10... | collective-permute-start | bytes 196616 | tf_op jit(solution)/shard_map/cond/branch_1_fun/ppermute | solution.py:229

commit v25 on v24

--- a/solution.py
+++ b/solution.py
@@ -55,10 +55,12 @@
 
     def one_hot(ref, d, size):
         numbers = lax.broadcasted_iota(jnp.int32, (size, LANES), 0).astype(jnp.bfloat16)
+        numbers = numbers.reshape(size // 16, 16, LANES)
         parts = []
         for k in range(lines):
-            row = jnp.broadcast_to(ref[d, k:k + 1, :], (size, LANES)).astype(jnp.bfloat16)
-            parts.append(jnp.where(numbers == row, one, none))
+            row = jnp.broadcast_to(ref[d, k:k + 1, :], (16, LANES)).astype(jnp.bfloat16)
+            hot = jnp.where(numbers == row[None], one, none)
+            parts.append(hot.reshape(size, LANES))
         return jnp.concatenate(parts, axis=1)
 
     for d in range(devices):

time: 25.7 us -> 25.7 us (level)
  no operation moved by 1% of the time
where the time goes in v25:
time: 25.7 us; the launch traced here: 25.4 us
  blocking collectives  11.5 us (45%)
  Pallas kernels  6.96 us (27%)
  starting transfers between devices  5.79 us (23%)
  between operations  0.67 us (3%)
  waiting for transfers between devices  0.5 us (2%)
    all_to_all x1, blocking collectives, exchange(): lax.all_to_all(x, axis, split_axis=0, concat_axis=0, axis_index_groups=[o...  11.5 us
    all_to_all x1, starting transfers between devices, exchange(): lax.all_to_all(x, axis, split_axis=0, concat_axis=0, axis_index_groups=[o...  4.57 us
    pallas_call x1, Pallas kernels, hand_over(): pl.pallas_call(functools.partial(apply_kernel, bag_count, lines, number),...  2.6 us
    pallas_call x1, Pallas kernels, local(): pl.pallas_call(functools.partial(pool_kernel, bag_count, lines, back_lead...  1.88 us
    ppermute x3, starting transfers between devices, forward(): lax.ppermute(x, axis, [(i, ((i // 2 + step) * 2 + 1 - i % 2) % size) for...  1.22 us
    pallas_call x1, Pallas kernels, local(): pl.pallas_call(functools.partial(pack_kernel, rows_dev), out_shape=pltpu....  1.01 us
    pallas_call x1, Pallas kernels, hand_over(): pl.pallas_call(functools.partial(count_kernel, bag_count, lines), out_sha...  0.88 us
    pallas_call x1, Pallas kernels, local(): pl.pallas_call(finish_kernel, out_shape=(jax.ShapeDtypeStruct((bag_count,...  0.6 us
  transfers between devices with their start and end apart: 4, of which 2 were waited for; matrix products, arithmetic and copies ran while one was open for 0% of the time, Pallas kernels for 14%

profile of v25, /device:TPU:0, one launch (start us, length us, event | category | flops | bytes accessed | tf_op | source)
XLA Modules:
  0.0 25.4 jit_solution(2528293955384643888)
XLA Ops:
  0.6 0.0 copy-start
  0.6 1.0 %pack.1 = f32[8,24,128]{2,1,0:T(8,128)S(1)} custom-call(s32[4,128]{1,0:T(4,128)} %bitcast.15, s32[4,128]{1,0:T(4,128)} %bitcast.16, s32[4,128]{1,0:T(4,128)} %bitcast.17, s32[4,128]{1,0:T(4,128)} %bitcast.18, s32[4,128]{1,0:T(4,128)} %bitcast.19, s32[4,128]{1,0:T(4,128)} %bitcast.20, f32[4,256]{1,0:T(4,128)} %bitcast.13), custom_call_target="tpu_custom_call" | custom-call | flops 8589934592 | bytes 1048576 | tf_op jit(solution)/shard_map/pack/pallas_call | solution.py:258
  1.7 0.0 copy-start.1
  1.7 11.5 %all_to_all.10.msg = f32[8,24,128]{2,1,0:T(8,128)S(1)} all-to-all(f32[8,24,128]{2,1,0:T(8,128)S(1)} %pack.1), channel_id=1, replica_groups={{5,6,7,0,1,2,3,4},{13,14,15,8,9,10,11,12},{21,22,23,16,17,18,19,20},{29..., dimensions={0} | all-to-all | bytes 196608 | tf_op jit(solution)/shard_map/all_to_all | solution.py:225
  13.1 0.0 copy-done
  13.1 1.9 %pool.1 = (f32[8,4,256]{2,1,0:T(4,128)}, f32[8,16,128]{2,1,0:T(8,128)S(1)}) custom-call(f32[8,24,128]{2,1,0:T(8,128)S(1)} %all_to_all.10.msg, f32[2048,256]{1,0:T(8,128)S(1)} %copy-done), custom_call_target="tpu_custom_call" | custom-call | flops 67108864 | bytes 2097152 | tf_op jit(solution)/shard_map/pool/pallas_call | solution.py:276
  15.0 0.0 collective-permute-start.2
  15.0 4.6 %all-to-all-start.1 = ((f32[8,4,256]{2,1,0:T(4,128)}), f32[8,4,256]{2,1,0:T(4,128)S(1)}, u32[]{:S(2)}, u32[]{:S(2)}) async-start(f32[8,4,256]{2,1,0:T(4,128)} %get-tuple-element.30), calls=%async_computation.1 | async-start | bytes 65536 | tf_op jit(solution)/shard_map/all_to_all | solution.py:225
  19.6 0.0 collective-permute-done.2
  19.6 0.0 copy-done.1
  19.6 5.0 %conditional.1 = ((f32[2048,256]{1,0:T(8,128)}, f32[16,128]{1,0:T(8,128)S(1)})) conditional(s32[]{:T(128)} %convert_element_type.3, (f32[2048,256]{1,0:T(8,128)S(1)}, f32[16,128]{1,0:T(8,128)S(1)}) %tuple.23, (f32[8,16,128]{2,1,0:T(8,128)S(1)}, f32[8,16,128]{2,1,0:T(8,128)S(1)}, f32[2048,256]{1,0:T(8,128)S(1)}, f32[16,128]{1,0:T(8,128)S(1)}) %tuple.24), branch_computations={%region_0.0_spmd, %region_1.0_spmd} | conditional | flops 268435456 | bytes 4718680 | solution.py:370
  19.6 1.1 %collective-permute-start = (f32[8,16,128]{2,1,0:T(8,128)S(1)}, f32[8,16,128]{2,1,0:T(8,128)S(1)}, u32[]{:S(2)}, u32[]{:S(2)}) collective-permute-start(f32[8,16,128]{2,1,0:T(8,128)S(1)} %get-tuple-element.14.refs_0_), channel_id=1, source_target_pairs={{0,8},{8,0},{16,24},{24,16},{1,9},{9,1},{17,25},{25,17},{2,10},{10... | collective-permute-start | bytes 196616 | tf_op jit(solution)/shard_map/cond/branch_1_fun/ppermute | solution.py:231
  20.8 0.1 collective-permute-start.1
  20.8 0.9 %count.1 = (bf16[16,64,128]{2,1,0:T(8,128)(2,1)S(1)}, bf16[64,256]{1,0:T(8,128)(2,1)S(1)}, bf16[64,256]{1,0:T(8,128)(2,1)S(1)}) custom-call(f32[8,16,128]{2,1,0:T(8,128)S(1)} %get-tuple-element.14.refs_0_, f32[8,16,128]{2,1,0:T(8,128)S(1)} %get-tuple-element.15.refs_1_), custom_call_target="tpu_custom_call" | custom-call | flops 268435456 | bytes 4194304 | tf_op jit(solution)/shard_map/cond/branch_1_fun/count/pallas_call | solution.py:332
  21.7 0.0 collective-permute-done.refs_0_
  21.7 0.3 %collective-permute-done.1.refs_1_ = f32[8,16,128]{2,1,0:T(8,128)S(1)} collective-permute-done((f32[8,16,128]{2,1,0:T(8,128)S(1)}, f32[8,16,128]{2,1,0:T(8,128)S(1)}, u32[]{:S(2)}, u32[]{:S(2)}) %collective-permute-start.1) | collective-permute-done | bytes 65568 | tf_op jit(solution)/shard_map/cond/branch_1_fun/ppermute | solution.py:231
  22.0 2.6 %apply.1 = (f32[2048,256]{1,0:T(8,128)}, f32[16,128]{1,0:T(8,128)S(1)}) custom-call(f32[8,16,128]{2,1,0:T(8,128)S(1)} %collective-permute-done.refs_0_, f32[8,16,128]{2,1,0:T(8,128)S(1)} %collective-permute-done.1.refs_1_, bf16[16,64,128]{2,1,0:T(8,128)(2,1)S(1)} %get-tuple-element.16.refs_2_, bf16[64,256]{1,0:T(8,128)(2,1)S(1)} %get-tuple-element.17.refs_3_, ...), custom_call_target="tpu_custom_call" | custom-call | tf_op jit(solution)/shard_map/cond/branch_1_fun/apply/pallas_call | solution.py:347
  24.6 0.2 all-to-all-done.1.returned
  24.8 0.6 %finish.1 = (f32[4,256]{1,0:T(4,128)}, f32[16,128]{1,0:T(8,128)}) custom-call(f32[8,4,256]{2,1,0:T(4,128)S(1)} %all-to-all-done.1.returned, f32[16,128]{1,0:T(8,128)S(1)} %get-tuple-element.32.accum), custom_call_target="tpu_custom_call" | custom-call | tf_op jit(solution)/shard_map/finish/pallas_call | solution.py:373
Async XLA Ops:
  0.6 12.5 %copy-start = (f32[2048,256]{1,0:T(8,128)S(1)}, f32[2048,256]{1,0:T(8,128)}, u32[]{:S(2)}) copy-start(f32[2048,256]{1,0:T(8,128)} %table.1) | copy-start | bytes 6291460
  1.7 18.0 %copy-start.1 = (f32[2048]{0:T(1024)S(1)}, f32[2048]{0:T(1024)}, u32[]{:S(2)}) copy-start(f32[2048]{0:T(1024)} %param.12) | copy-start | bytes 24580
  15.0 4.6 %collective-permute-start.2 = (f32[8,16,128]{2,1,0:T(8,128)S(1)}, f32[8,16,128]{2,1,0:T(8,128)S(1)}, u32[]{:S(2)}, u32[]{:S(2)}) collective-permute-start(f32[8,16,128]{2,1,0:T(8,128)S(1)} %get-tuple-element.31), channel_id=1, source_target_pairs={{0,24},{8,16},{16,8},{24,0},{1,25},{9,17},{17,9},{25,1},{2,26},{10... | collective-permute-start | bytes 196616 | tf_op jit(solution)/shard_map/ppermute | solution.py:231
  15.0 9.8 %all-to-all-start.1 = ((f32[8,4,256]{2,1,0:T(4,128)}), f32[8,4,256]{2,1,0:T(4,128)S(1)}, u32[]{:S(2)}, u32[]{:S(2)}) async-start(f32[8,4,256]{2,1,0:T(4,128)} %get-tuple-element.30), calls=%async_computation.1 | async-start | bytes 65536 | tf_op jit(solution)/shard_map/all_to_all | solution.py:225
  19.6 2.1 %collective-permute-start = (f32[8,16,128]{2,1,0:T(8,128)S(1)}, f32[8,16,128]{2,1,0:T(8,128)S(1)}, u32[]{:S(2)}, u32[]{:S(2)}) collective-permute-start(f32[8,16,128]{2,1,0:T(8,128)S(1)} %get-tuple-element.14.refs_0_), channel_id=1, source_target_pairs={{0,8},{8,0},{16,24},{24,16},{1,9},{9,1},{17,25},{25,17},{2,10},{10... | collective-permute-start | bytes 196616 | tf_op jit(solution)/shard_map/cond/branch_1_fun/ppermute | solution.py:231
  20.8 1.3 %collective-permute-start.1 = (f32[8,16,128]{2,1,0:T(8,128)S(1)}, f32[8,16,128]{2,1,0:T(8,128)S(1)}, u32[]{:S(2)}, u32[]{:S(2)}) collective-permute-start(f32[8,16,128]{2,1,0:T(8,128)S(1)} %get-tuple-element.15.refs_1_), channel_id=1, source_target_pairs={{0,8},{8,0},{16,24},{24,16},{1,9},{9,1},{17,25},{25,17},{2,10},{10... | collective-permute-start | bytes 196616 | tf_op jit(solution)/shard_map/cond/branch_1_fun/ppermute | solution.py:231

commit v26 on v25

--- a/solution.py
+++ b/solution.py
@@ -238,7 +238,7 @@
 ):
     owners, groups = lax.axis_size("rows"), lax.axis_size("dp")
     devices = owners * groups
-    out_leader, back_leader = 5 * owners // 8, owners // 4
+    out_leader, back_leader = 5 * owners // 8, owners // 2
     rows_dev, width = item_table.shape
     bag_count = grad_pooled.shape[2]
     lines = row_index.shape[2] // LANES

time: 25.7 us -> 26.1 us (1.016)
  starting transfers between devices: 5.79 us -> 6.34 us
    ppermute x3, starting transfers between devices: 1.22 us -> 1.5 us  [forward(): lax.ppermute(x, axis, [(i, ((i // 2 + step) * 2 + 1 - i % 2) % size) for...]
    all_to_all x1, starting transfers between devices: 4.57 us -> 4.84 us  [exchange(): lax.all_to_all(x, axis, split_axis=0, concat_axis=0, axis_index_groups=[o...]
  transfers between devices with their start and end apart: 4 -> 4, of which waited for: 2 -> 1; matrix products, arithmetic and copies ran while one was open for 0% -> 0% of each run, Pallas kernels for 14% -> 13%
where the time goes in v26:
time: 26.1 us; the launch traced here: 25.8 us
  blocking collectives  11.5 us (44%)
  Pallas kernels  6.97 us (27%)
  starting transfers between devices  6.34 us (24%)
  between operations  0.68 us (3%)
  waiting for transfers between devices  0.29 us (1%)
    all_to_all x1, blocking collectives, exchange(): lax.all_to_all(x, axis, split_axis=0, concat_axis=0, axis_index_groups=[o...  11.5 us
    all_to_all x1, starting transfers between devices, exchange(): lax.all_to_all(x, axis, split_axis=0, concat_axis=0, axis_index_groups=[o...  4.84 us
    pallas_call x1, Pallas kernels, hand_over(): pl.pallas_call(functools.partial(apply_kernel, bag_count, lines, number),...  2.6 us
    pallas_call x1, Pallas kernels, local(): pl.pallas_call(functools.partial(pool_kernel, bag_count, lines, back_lead...  1.88 us
    ppermute x3, starting transfers between devices, forward(): lax.ppermute(x, axis, [(i, ((i // 2 + step) * 2 + 1 - i % 2) % size) for...  1.5 us
    pallas_call x1, Pallas kernels, local(): pl.pallas_call(functools.partial(pack_kernel, rows_dev), out_shape=pltpu....  1.01 us
    pallas_call x1, Pallas kernels, hand_over(): pl.pallas_call(functools.partial(count_kernel, bag_count, lines), out_sha...  0.88 us
    pallas_call x1, Pallas kernels, local(): pl.pallas_call(finish_kernel, out_shape=(jax.ShapeDtypeStruct((bag_count,...  0.6 us
  transfers between devices with their start and end apart: 4, of which 1 were waited for; matrix products, arithmetic and copies ran while one was open for 0% of the time, Pallas kernels for 13%

profile of v26, /device:TPU:0, one launch (start us, length us, event | category | flops | bytes accessed | tf_op | source)
XLA Modules:
  0.0 25.8 jit_solution(7542246809135601782)
XLA Ops:
  0.6 0.0 copy-start
  0.6 1.0 %pack.1 = f32[8,24,128]{2,1,0:T(8,128)S(1)} custom-call(s32[4,128]{1,0:T(4,128)} %bitcast.15, s32[4,128]{1,0:T(4,128)} %bitcast.16, s32[4,128]{1,0:T(4,128)} %bitcast.17, s32[4,128]{1,0:T(4,128)} %bitcast.18, s32[4,128]{1,0:T(4,128)} %bitcast.19, s32[4,128]{1,0:T(4,128)} %bitcast.20, f32[4,256]{1,0:T(4,128)} %bitcast.13), custom_call_target="tpu_custom_call" | custom-call | flops 8589934592 | bytes 1048576 | tf_op jit(solution)/shard_map/pack/pallas_call | solution.py:258
  1.7 0.0 copy-start.1
  1.7 11.5 %all_to_all.10.msg = f32[8,24,128]{2,1,0:T(8,128)S(1)} all-to-all(f32[8,24,128]{2,1,0:T(8,128)S(1)} %pack.1), channel_id=1, replica_groups={{5,6,7,0,1,2,3,4},{13,14,15,8,9,10,11,12},{21,22,23,16,17,18,19,20},{29..., dimensions={0} | all-to-all | bytes 196608 | tf_op jit(solution)/shard_map/all_to_all | solution.py:225
  13.1 0.0 copy-done
  13.1 1.9 %pool.1 = (f32[8,4,256]{2,1,0:T(4,128)}, f32[8,16,128]{2,1,0:T(8,128)S(1)}) custom-call(f32[8,24,128]{2,1,0:T(8,128)S(1)} %all_to_all.10.msg, f32[2048,256]{1,0:T(8,128)S(1)} %copy-done), custom_call_target="tpu_custom_call" | custom-call | flops 67108864 | bytes 2097152 | tf_op jit(solution)/shard_map/pool/pallas_call | solution.py:276
  15.0 0.0 collective-permute-start.2
  15.0 4.8 %all-to-all-start.1 = ((f32[8,4,256]{2,1,0:T(4,128)}), f32[8,4,256]{2,1,0:T(4,128)S(1)}, u32[]{:S(2)}, u32[]{:S(2)}) async-start(f32[8,4,256]{2,1,0:T(4,128)} %get-tuple-element.30), calls=%async_computation.1 | async-start | bytes 65536 | tf_op jit(solution)/shard_map/all_to_all | solution.py:225
  19.9 0.0 collective-permute-done.2
  19.9 0.0 copy-done.1
  19.9 5.3 %conditional.1 = ((f32[2048,256]{1,0:T(8,128)}, f32[16,128]{1,0:T(8,128)S(1)})) conditional(s32[]{:T(128)} %convert_element_type.3, (f32[2048,256]{1,0:T(8,128)S(1)}, f32[16,128]{1,0:T(8,128)S(1)}) %tuple.23, (f32[8,16,128]{2,1,0:T(8,128)S(1)}, f32[8,16,128]{2,1,0:T(8,128)S(1)}, f32[2048,256]{1,0:T(8,128)S(1)}, f32[16,128]{1,0:T(8,128)S(1)}) %tuple.24), branch_computations={%region_0.0_spmd, %region_1.0_spmd} | conditional | flops 268435456 | bytes 4718680 | solution.py:370
  19.9 1.4 %collective-permute-start = (f32[8,16,128]{2,1,0:T(8,128)S(1)}, f32[8,16,128]{2,1,0:T(8,128)S(1)}, u32[]{:S(2)}, u32[]{:S(2)}) collective-permute-start(f32[8,16,128]{2,1,0:T(8,128)S(1)} %get-tuple-element.14.refs_0_), channel_id=1, source_target_pairs={{0,8},{8,0},{16,24},{24,16},{1,9},{9,1},{17,25},{25,17},{2,10},{10... | collective-permute-start | bytes 196616 | tf_op jit(solution)/shard_map/cond/branch_1_fun/ppermute | solution.py:231
  21.3 0.1 collective-permute-start.1
  21.4 0.9 %count.1 = (bf16[16,64,128]{2,1,0:T(8,128)(2,1)S(1)}, bf16[64,256]{1,0:T(8,128)(2,1)S(1)}, bf16[64,256]{1,0:T(8,128)(2,1)S(1)}) custom-call(f32[8,16,128]{2,1,0:T(8,128)S(1)} %get-tuple-element.14.refs_0_, f32[8,16,128]{2,1,0:T(8,128)S(1)} %get-tuple-element.15.refs_1_), custom_call_target="tpu_custom_call" | custom-call | flops 268435456 | bytes 4194304 | tf_op jit(solution)/shard_map/cond/branch_1_fun/count/pallas_call | solution.py:332
  22.3 0.0 collective-permute-done.refs_0_
  22.3 0.3 %collective-permute-done.1.refs_1_ = f32[8,16,128]{2,1,0:T(8,128)S(1)} collective-permute-done((f32[8,16,128]{2,1,0:T(8,128)S(1)}, f32[8,16,128]{2,1,0:T(8,128)S(1)}, u32[]{:S(2)}, u32[]{:S(2)}) %collective-permute-start.1) | collective-permute-done | bytes 65568 | tf_op jit(solution)/shard_map/cond/branch_1_fun/ppermute | solution.py:231
  22.6 2.6 %apply.1 = (f32[2048,256]{1,0:T(8,128)}, f32[16,128]{1,0:T(8,128)S(1)}) custom-call(f32[8,16,128]{2,1,0:T(8,128)S(1)} %collective-permute-done.refs_0_, f32[8,16,128]{2,1,0:T(8,128)S(1)} %collective-permute-done.1.refs_1_, bf16[16,64,128]{2,1,0:T(8,128)(2,1)S(1)} %get-tuple-element.16.refs_2_, bf16[64,256]{1,0:T(8,128)(2,1)S(1)} %get-tuple-element.17.refs_3_, ...), custom_call_target="tpu_custom_call" | custom-call | tf_op jit(solution)/shard_map/cond/branch_1_fun/apply/pallas_call | solution.py:347
  25.2 0.0 all-to-all-done.1.returned
  25.2 0.6 %finish.1 = (f32[4,256]{1,0:T(4,128)}, f32[16,128]{1,0:T(8,128)}) custom-call(f32[8,4,256]{2,1,0:T(4,128)S(1)} %all-to-all-done.1.returned, f32[16,128]{1,0:T(8,128)S(1)} %get-tuple-element.32.accum), custom_call_target="tpu_custom_call" | custom-call | tf_op jit(solution)/shard_map/finish/pallas_call | solution.py:373
Async XLA Ops:
  0.6 12.5 %copy-start = (f32[2048,256]{1,0:T(8,128)S(1)}, f32[2048,256]{1,0:T(8,128)}, u32[]{:S(2)}) copy-start(f32[2048,256]{1,0:T(8,128)} %table.1) | copy-start | bytes 6291460
  1.7 18.2 %copy-start.1 = (f32[2048]{0:T(1024)S(1)}, f32[2048]{0:T(1024)}, u32[]{:S(2)}) copy-start(f32[2048]{0:T(1024)} %param.12) | copy-start | bytes 24580
  15.0 4.9 %collective-permute-start.2 = (f32[8,16,128]{2,1,0:T(8,128)S(1)}, f32[8,16,128]{2,1,0:T(8,128)S(1)}, u32[]{:S(2)}, u32[]{:S(2)}) collective-permute-start(f32[8,16,128]{2,1,0:T(8,128)S(1)} %get-tuple-element.31), channel_id=1, source_target_pairs={{0,24},{8,16},{16,8},{24,0},{1,25},{9,17},{17,9},{25,1},{2,26},{10... | collective-permute-start | bytes 196616 | tf_op jit(solution)/shard_map/ppermute | solution.py:231
  15.0 10.1 %all-to-all-start.1 = ((f32[8,4,256]{2,1,0:T(4,128)}), f32[8,4,256]{2,1,0:T(4,128)S(1)}, u32[]{:S(2)}, u32[]{:S(2)}) async-start(f32[8,4,256]{2,1,0:T(4,128)} %get-tuple-element.30), calls=%async_computation.1 | async-start | bytes 65536 | tf_op jit(solution)/shard_map/all_to_all | solution.py:225
  19.9 2.4 %collective-permute-start = (f32[8,16,128]{2,1,0:T(8,128)S(1)}, f32[8,16,128]{2,1,0:T(8,128)S(1)}, u32[]{:S(2)}, u32[]{:S(2)}) collective-permute-start(f32[8,16,128]{2,1,0:T(8,128)S(1)} %get-tuple-element.14.refs_0_), channel_id=1, source_target_pairs={{0,8},{8,0},{16,24},{24,16},{1,9},{9,1},{17,25},{25,17},{2,10},{10... | collective-permute-start | bytes 196616 | tf_op jit(solution)/shard_map/cond/branch_1_fun/ppermute | solution.py:231
  21.3 1.3 %collective-permute-start.1 = (f32[8,16,128]{2,1,0:T(8,128)S(1)}, f32[8,16,128]{2,1,0:T(8,128)S(1)}, u32[]{:S(2)}, u32[]{:S(2)}) collective-permute-start(f32[8,16,128]{2,1,0:T(8,128)S(1)} %get-tuple-element.15.refs_1_), channel_id=1, source_target_pairs={{0,8},{8,0},{16,24},{24,16},{1,9},{9,1},{17,25},{25,17},{2,10},{10... | collective-permute-start | bytes 196616 | tf_op jit(solution)/shard_map/cond/branch_1_fun/ppermute | solution.py:231

commit v27 on v26

--- a/solution.py
+++ b/solution.py
@@ -238,7 +238,7 @@
 ):
     owners, groups = lax.axis_size("rows"), lax.axis_size("dp")
     devices = owners * groups
-    out_leader, back_leader = 5 * owners // 8, owners // 2
+    out_leader, back_leader = owners // 2, owners // 4
     rows_dev, width = item_table.shape
     bag_count = grad_pooled.shape[2]
     lines = row_index.shape[2] // LANES

time: 26.1 us -> 26.1 us (level)
  starting transfers between devices: 6.34 us -> 5.09 us
  blocking collectives: 11.5 us -> 12.4 us
  waiting for transfers between devices: 0.29 us -> 0.7 us
    all_to_all x1, blocking collectives: 11.5 us -> 12.4 us  [exchange(): lax.all_to_all(x, axis, split_axis=0, concat_axis=0, axis_index_groups=[o...]
    all_to_all x1, starting transfers between devices: 4.84 us -> 4.07 us  [exchange(): lax.all_to_all(x, axis, split_axis=0, concat_axis=0, axis_index_groups=[o...]
    ppermute x3, starting transfers between devices: 1.5 us -> 1.02 us  [forward(): lax.ppermute(x, axis, [(i, ((i // 2 + step) * 2 + 1 - i % 2) % size) for...]
  transfers between devices with their start and end apart: 4 -> 4, of which waited for: 1 -> 3; matrix products, arithmetic and copies ran while one was open for 0% -> 0% of each run, Pallas kernels for 13% -> 13%
where the time goes in v27:
time: 26.1 us; the launch traced here: 25.8 us
  blocking collectives  12.4 us (48%)
  Pallas kernels  6.97 us (27%)
  starting transfers between devices  5.09 us (20%)
  waiting for transfers between devices  0.7 us (3%)
  between operations  0.67 us (3%)
    all_to_all x1, blocking collectives, exchange(): lax.all_to_all(x, axis, split_axis=0, concat_axis=0, axis_index_groups=[o...  12.4 us
    all_to_all x1, starting transfers between devices, exchange(): lax.all_to_all(x, axis, split_axis=0, concat_axis=0, axis_index_groups=[o...  4.07 us
    pallas_call x1, Pallas kernels, hand_over(): pl.pallas_call(functools.partial(apply_kernel, bag_count, lines, number),...  2.6 us
    pallas_call x1, Pallas kernels, local(): pl.pallas_call(functools.partial(pool_kernel, bag_count, lines, back_lead...  1.88 us
    ppermute x3, starting transfers between devices, forward(): lax.ppermute(x, axis, [(i, ((i // 2 + step) * 2 + 1 - i % 2) % size) for...  1.02 us
    pallas_call x1, Pallas kernels, local(): pl.pallas_call(functools.partial(pack_kernel, rows_dev), out_shape=pltpu....  1.01 us
    pallas_call x1, Pallas kernels, hand_over(): pl.pallas_call(functools.partial(count_kernel, bag_count, lines), out_sha...  0.88 us
    pallas_call x1, Pallas kernels, local(): pl.pallas_call(finish_kernel, out_shape=(jax.ShapeDtypeStruct((bag_count,...  0.6 us
  transfers between devices with their start and end apart: 4, of which 3 were waited for; matrix products, arithmetic and copies ran while one was open for 0% of the time, Pallas kernels for 13%

profile of v27, /device:TPU:0, one launch (start us, length us, event | category | flops | bytes accessed | tf_op | source)
XLA Modules:
  0.0 25.8 jit_solution(14947963449571326371)
XLA Ops:
  0.6 0.0 copy-start
  0.6 1.0 %pack.1 = f32[8,24,128]{2,1,0:T(8,128)S(1)} custom-call(s32[4,128]{1,0:T(4,128)} %bitcast.15, s32[4,128]{1,0:T(4,128)} %bitcast.16, s32[4,128]{1,0:T(4,128)} %bitcast.17, s32[4,128]{1,0:T(4,128)} %bitcast.18, s32[4,128]{1,0:T(4,128)} %bitcast.19, s32[4,128]{1,0:T(4,128)} %bitcast.20, f32[4,256]{1,0:T(4,128)} %bitcast.13), custom_call_target="tpu_custom_call" | custom-call | flops 8589934592 | bytes 1048576 | tf_op jit(solution)/shard_map/pack/pallas_call | solution.py:258
  1.7 0.0 copy-start.1
  1.7 12.4 %all_to_all.10.msg = f32[8,24,128]{2,1,0:T(8,128)S(1)} all-to-all(f32[8,24,128]{2,1,0:T(8,128)S(1)} %pack.1), channel_id=1, replica_groups={{4,5,6,7,0,1,2,3},{12,13,14,15,8,9,10,11},{20,21,22,23,16,17,18,19},{28..., dimensions={0} | all-to-all | bytes 196608 | tf_op jit(solution)/shard_map/all_to_all | solution.py:225
  14.0 0.0 copy-done
  14.0 1.9 %pool.1 = (f32[8,4,256]{2,1,0:T(4,128)}, f32[8,16,128]{2,1,0:T(8,128)S(1)}) custom-call(f32[8,24,128]{2,1,0:T(8,128)S(1)} %all_to_all.10.msg, f32[2048,256]{1,0:T(8,128)S(1)} %copy-done), custom_call_target="tpu_custom_call" | custom-call | flops 67108864 | bytes 2097152 | tf_op jit(solution)/shard_map/pool/pallas_call | solution.py:276
  15.9 0.0 collective-permute-start.2
  15.9 4.1 %all-to-all-start.1 = ((f32[8,4,256]{2,1,0:T(4,128)}), f32[8,4,256]{2,1,0:T(4,128)S(1)}, u32[]{:S(2)}, u32[]{:S(2)}) async-start(f32[8,4,256]{2,1,0:T(4,128)} %get-tuple-element.30), calls=%async_computation.1 | async-start | bytes 65536 | tf_op jit(solution)/shard_map/all_to_all | solution.py:225
  20.0 0.2 collective-permute-done.2
  20.2 0.0 copy-done.1
  20.3 4.8 %conditional.1 = ((f32[2048,256]{1,0:T(8,128)}, f32[16,128]{1,0:T(8,128)S(1)})) conditional(s32[]{:T(128)} %convert_element_type.3, (f32[2048,256]{1,0:T(8,128)S(1)}, f32[16,128]{1,0:T(8,128)S(1)}) %tuple.23, (f32[8,16,128]{2,1,0:T(8,128)S(1)}, f32[8,16,128]{2,1,0:T(8,128)S(1)}, f32[2048,256]{1,0:T(8,128)S(1)}, f32[16,128]{1,0:T(8,128)S(1)}) %tuple.24), branch_computations={%region_0.0_spmd, %region_1.0_spmd} | conditional | flops 268435456 | bytes 4718680 | solution.py:370
  20.3 0.9 %collective-permute-start = (f32[8,16,128]{2,1,0:T(8,128)S(1)}, f32[8,16,128]{2,1,0:T(8,128)S(1)}, u32[]{:S(2)}, u32[]{:S(2)}) collective-permute-start(f32[8,16,128]{2,1,0:T(8,128)S(1)} %get-tuple-element.14.refs_0_), channel_id=1, source_target_pairs={{0,8},{8,0},{16,24},{24,16},{1,9},{9,1},{17,25},{25,17},{2,10},{10... | collective-permute-start | bytes 196616 | tf_op jit(solution)/shard_map/cond/branch_1_fun/ppermute | solution.py:231
  21.2 0.1 collective-permute-start.1
  21.3 0.9 %count.1 = (bf16[16,64,128]{2,1,0:T(8,128)(2,1)S(1)}, bf16[64,256]{1,0:T(8,128)(2,1)S(1)}, bf16[64,256]{1,0:T(8,128)(2,1)S(1)}) custom-call(f32[8,16,128]{2,1,0:T(8,128)S(1)} %get-tuple-element.14.refs_0_, f32[8,16,128]{2,1,0:T(8,128)S(1)} %get-tuple-element.15.refs_1_), custom_call_target="tpu_custom_call" | custom-call | flops 268435456 | bytes 4194304 | tf_op jit(solution)/shard_map/cond/branch_1_fun/count/pallas_call | solution.py:332
  22.2 0.0 collective-permute-done.refs_0_
  22.2 0.3 %collective-permute-done.1.refs_1_ = f32[8,16,128]{2,1,0:T(8,128)S(1)} collective-permute-done((f32[8,16,128]{2,1,0:T(8,128)S(1)}, f32[8,16,128]{2,1,0:T(8,128)S(1)}, u32[]{:S(2)}, u32[]{:S(2)}) %collective-permute-start.1) | collective-permute-done | bytes 65568 | tf_op jit(solution)/shard_map/cond/branch_1_fun/ppermute | solution.py:231
  22.4 2.6 %apply.1 = (f32[2048,256]{1,0:T(8,128)}, f32[16,128]{1,0:T(8,128)S(1)}) custom-call(f32[8,16,128]{2,1,0:T(8,128)S(1)} %collective-permute-done.refs_0_, f32[8,16,128]{2,1,0:T(8,128)S(1)} %collective-permute-done.1.refs_1_, bf16[16,64,128]{2,1,0:T(8,128)(2,1)S(1)} %get-tuple-element.16.refs_2_, bf16[64,256]{1,0:T(8,128)(2,1)S(1)} %get-tuple-element.17.refs_3_, ...), custom_call_target="tpu_custom_call" | custom-call | tf_op jit(solution)/shard_map/cond/branch_1_fun/apply/pallas_call | solution.py:347
  25.1 0.2 all-to-all-done.1.returned
  25.2 0.6 %finish.1 = (f32[4,256]{1,0:T(4,128)}, f32[16,128]{1,0:T(8,128)}) custom-call(f32[8,4,256]{2,1,0:T(4,128)S(1)} %all-to-all-done.1.returned, f32[16,128]{1,0:T(8,128)S(1)} %get-tuple-element.32.accum), custom_call_target="tpu_custom_call" | custom-call | tf_op jit(solution)/shard_map/finish/pallas_call | solution.py:373
Async XLA Ops:
  0.6 13.4 %copy-start = (f32[2048,256]{1,0:T(8,128)S(1)}, f32[2048,256]{1,0:T(8,128)}, u32[]{:S(2)}) copy-start(f32[2048,256]{1,0:T(8,128)} %table.1) | copy-start | bytes 6291460
  1.7 18.6 %copy-start.1 = (f32[2048]{0:T(1024)S(1)}, f32[2048]{0:T(1024)}, u32[]{:S(2)}) copy-start(f32[2048]{0:T(1024)} %param.12) | copy-start | bytes 24580
  15.9 4.3 %collective-permute-start.2 = (f32[8,16,128]{2,1,0:T(8,128)S(1)}, f32[8,16,128]{2,1,0:T(8,128)S(1)}, u32[]{:S(2)}, u32[]{:S(2)}) collective-permute-start(f32[8,16,128]{2,1,0:T(8,128)S(1)} %get-tuple-element.31), channel_id=1, source_target_pairs={{0,24},{8,16},{16,8},{24,0},{1,25},{9,17},{17,9},{25,1},{2,26},{10... | collective-permute-start | bytes 196616 | tf_op jit(solution)/shard_map/ppermute | solution.py:231
  15.9 9.3 %all-to-all-start.1 = ((f32[8,4,256]{2,1,0:T(4,128)}), f32[8,4,256]{2,1,0:T(4,128)S(1)}, u32[]{:S(2)}, u32[]{:S(2)}) async-start(f32[8,4,256]{2,1,0:T(4,128)} %get-tuple-element.30), calls=%async_computation.1 | async-start | bytes 65536 | tf_op jit(solution)/shard_map/all_to_all | solution.py:225
  20.3 1.9 %collective-permute-start = (f32[8,16,128]{2,1,0:T(8,128)S(1)}, f32[8,16,128]{2,1,0:T(8,128)S(1)}, u32[]{:S(2)}, u32[]{:S(2)}) collective-permute-start(f32[8,16,128]{2,1,0:T(8,128)S(1)} %get-tuple-element.14.refs_0_), channel_id=1, source_target_pairs={{0,8},{8,0},{16,24},{24,16},{1,9},{9,1},{17,25},{25,17},{2,10},{10... | collective-permute-start | bytes 196616 | tf_op jit(solution)/shard_map/cond/branch_1_fun/ppermute | solution.py:231
  21.2 1.3 %collective-permute-start.1 = (f32[8,16,128]{2,1,0:T(8,128)S(1)}, f32[8,16,128]{2,1,0:T(8,128)S(1)}, u32[]{:S(2)}, u32[]{:S(2)}) collective-permute-start(f32[8,16,128]{2,1,0:T(8,128)S(1)} %get-tuple-element.15.refs_1_), channel_id=1, source_target_pairs={{0,8},{8,0},{16,24},{24,16},{1,9},{9,1},{17,25},{25,17},{2,10},{10... | collective-permute-start | bytes 196616 | tf_op jit(solution)/shard_map/cond/branch_1_fun/ppermute | solution.py:231
